TPU v7x, 32 devices: a whole 2x2x4 slice. The times are simulated.
32 devices in a mesh: seq: 8 (over y, x, core), trk: 4 (over z).
Axes of the slice: x: 2, y: 2, z: 4, core: 2. Of those that a mesh axis runs over, the one named last changes fastest.
Arguments:
- trunk_input: bfloat16 [3072, 1536], P('seq', 'trk'), may hold values from -6 to 6
- conv_in: bfloat16 [6, 3, 768, 1536], P(None, None, 'trk'), may hold values from -0.09375 to 0.09375
- conv_bias: bfloat16 [6, 768], P(None, 'trk'), may hold values from -3 to 3
- conv_out: bfloat16 [6, 768, 1536], P(None, 'trk'), may hold values from -0.21875 to 0.21875
- projection_bias: bfloat16 [6, 1536], P(None, 'trk'), may hold values from -3 to 3
- head_weight: bfloat16 [1536, 4096], P(None, 'trk'), may hold values from -0.15625 to 0.15625
- head_bias: bfloat16 [4096], P('trk'), may hold values from -4 to 4
- exon_bins: int32 [64, 64], P('seq'), may hold values from -1 to 3071, as said below
Outputs:
- coverage: bfloat16 [3072, 4096], P('seq', 'trk')
- gene_cov: float32 [64, 4096], P('seq', 'trk')
Inputs may be any that keep to these rules, and one draw needn't show every extreme that they name: `exon_bins`: row g lists gene g's exon bins in increasing order, then -1 in the unused entries; every gene has at least one exon bin and some gene has exactly 64. The genes of rows 8 * o to 8 * (o + 1) - 1 are owned by index o of seq.
All inputs are finite; a program needn't handle non-finite values.
Results may differ from a plain program's by a relative error of at most 0.024.
Values may be sent and summed in bfloat16 or wider, within the bound.
No kernel may reach another device: no remote copies, remote signals or barrier semaphores. Data moves between devices by JAX's collectives and lax.ppermute only.
A program may use at most 128 MiB of HBM per device.

v0:
```python
import jax
import jax.numpy as jnp
from jax import lax
from jax.sharding import PartitionSpec as P

RESIDUAL_BLOCKS = 6
BASE_DILATION = 2


def extended(cells, sides, width):
    for axis, dim in sides:
        count = lax.axis_size(axis)
        ends = count - 1
        head = lax.slice_in_dim(cells, 0, width, axis=dim)
        tail = lax.slice_in_dim(cells, cells.shape[dim] - width, cells.shape[dim], axis=dim)
        cells = jnp.concatenate(
            [
                lax.ppermute(tail, axis, [(i, (i + 1) % count) for i in range(ends)]),
                cells,
                lax.ppermute(head, axis, [((i + 1) % count, i) for i in range(ends)]),
            ],
            axis=dim,
        )
    return cells


def contract_last(rows, kernel):
    return lax.dot_general(
        rows, kernel, (((1,), (1,)), ((), ())), preferred_element_type=jnp.float32
    )


def dilated_inner(trunk, conv_in, block_layer_index, dilation_step):
    bin_rows = trunk.shape[0]
    gathered = lax.all_gather(trunk, "trk", axis=1, tiled=True)
    padded = extended(gathered, (("seq", 0),), dilation_step)
    inner = jnp.zeros((bin_rows, conv_in.shape[2]), jnp.float32)
    for tap_index in range(3):
        window = padded[tap_index * dilation_step : tap_index * dilation_step + bin_rows]
        inner = inner + contract_last(window, conv_in[block_layer_index, tap_index])
    return inner


def exon_onehot(gene_block, first_bin, width_now):
    exon_matches = (
        gene_block[:, :, None] - first_bin == jnp.arange(width_now, dtype=jnp.int32)[None, None, :]
    )
    return jnp.sum(exon_matches.astype(jnp.float32), axis=1).astype(jnp.bfloat16)


def shards(
    trunk_input, conv_in, conv_bias, conv_out, projection_bias, head_weight, head_bias, exon_bins
):
    trunk = trunk_input
    bin_rows = trunk.shape[0]
    for block_layer_index in range(RESIDUAL_BLOCKS):
        dilation_step = BASE_DILATION * 2**block_layer_index
        inner = dilated_inner(trunk, conv_in, block_layer_index, dilation_step)
        activation = jax.nn.gelu(
            inner + conv_bias[block_layer_index].astype(jnp.float32), approximate=True
        ).astype(jnp.bfloat16)
        partial_value = jnp.dot(
            activation, conv_out[block_layer_index], preferred_element_type=jnp.float32
        )
        summed = lax.psum_scatter(
            partial_value.astype(jnp.bfloat16), "trk", scatter_dimension=1, tiled=True
        ).astype(jnp.float32)
        trunk = (
            trunk.astype(jnp.float32)
            + summed
            + projection_bias[block_layer_index].astype(jnp.float32)
        ).astype(jnp.bfloat16)
    logits = jnp.dot(
        lax.all_gather(trunk, "trk", axis=1, tiled=True),
        head_weight,
        preferred_element_type=jnp.float32,
    )
    coverage = jax.nn.softplus(logits + head_bias.astype(jnp.float32)).astype(jnp.bfloat16)
    gene_lists = lax.all_gather(exon_bins, "seq", axis=0, tiled=True)
    first_bin = lax.axis_index("seq") * bin_rows
    onehot = exon_onehot(gene_lists, first_bin, bin_rows)
    gene_sum = lax.psum_scatter(
        jnp.dot(onehot, coverage, preferred_element_type=jnp.float32).astype(jnp.bfloat16),
        "seq",
        scatter_dimension=0,
        tiled=True,
    ).astype(jnp.float32)
    counts = jnp.sum((exon_bins >= 0).astype(jnp.float32), axis=1)
    gene_cov = gene_sum / counts[:, None]
    return (coverage, gene_cov)


def solution(mesh):
    in_specs = (
        P("seq", "trk"),
        P(None, None, "trk", None),
        P(None, "trk"),
        P(None, "trk", None),
        P(None, "trk"),
        P(None, "trk"),
        P("trk"),
        P("seq", None),
    )
    out_specs = (P("seq", "trk"), P("seq", "trk"))
    return jax.shard_map(shards, mesh=mesh, in_specs=in_specs, out_specs=out_specs, check_vma=False)
```

profile of v0, /device:TPU:8, one launch (start us, length us, event | category | flops | bytes accessed | tf_op | source)
XLA Modules:
  0.0 560.2 jit_solution(3758645301963879392)
XLA Ops:
  8.9 32.1 %all-gather.8.cloned.1.call-done = bf16[384,1536]{1,0:T(8,128)(2,1)} async-done(((bf16[384,384]{1,0:T(8,128)(2,1)}), bf16[384,1536]{1,0:T(8,128)(2,1)}) %all-gather.8.cloned.1.call-update) | async-done | bytes 1179664 | tf_op jit(solution)/shard_map/all_gather | solution.py:35
  43.2 3.0 collective-permute-start
  50.6 3.9 convolution_convert_fusion.5
  57.6 26.9 %reduce-scatter.22.cloned.1.call-done = bf16[384,384]{1,0:T(8,128)(2,1)} async-done(((bf16[1536,384]{1,0:T(8,128)(2,1)}), bf16[384,384]{1,0:T(8,128)(2,1)}) %reduce-scatter.22.cloned.1.call-update) | async-done | bytes 294928
  88.1 31.0 %all-gather.10.cloned.1.call-done = bf16[384,1536]{1,0:T(8,128)(2,1)} async-done(((bf16[384,384]{1,0:T(8,128)(2,1)}), bf16[384,1536]{1,0:T(8,128)(2,1)}) %all-gather.10.cloned.1.call-update) | async-done | bytes 1179664 | tf_op jit(solution)/shard_map/all_gather | solution.py:35
  121.3 3.0 collective-permute-start.2
  124.3 2.7 fusion.65
  129.4 4.0 convolution_convert_fusion.4
  135.8 27.5 %reduce-scatter.24.cloned.1.call-done = bf16[384,384]{1,0:T(8,128)(2,1)} async-done(((bf16[1536,384]{1,0:T(8,128)(2,1)}), bf16[384,384]{1,0:T(8,128)(2,1)}) %reduce-scatter.24.cloned.1.call-update) | async-done | bytes 294928
  167.0 31.0 %all-gather.12.cloned.1.call-done = bf16[384,1536]{1,0:T(8,128)(2,1)} async-done(((bf16[384,384]{1,0:T(8,128)(2,1)}), bf16[384,1536]{1,0:T(8,128)(2,1)}) %all-gather.12.cloned.1.call-update) | async-done | bytes 1179664 | tf_op jit(solution)/shard_map/all_gather | solution.py:35
  200.2 3.0 collective-permute-start.4
  203.2 2.7 fusion.60
  208.3 4.0 convolution_convert_fusion.3
  214.7 27.5 %reduce-scatter.26.cloned.1.call-done = bf16[384,384]{1,0:T(8,128)(2,1)} async-done(((bf16[1536,384]{1,0:T(8,128)(2,1)}), bf16[384,384]{1,0:T(8,128)(2,1)}) %reduce-scatter.26.cloned.1.call-update) | async-done | bytes 294928
  245.9 31.0 %all-gather.14.cloned.1.call-done = bf16[384,1536]{1,0:T(8,128)(2,1)} async-done(((bf16[384,384]{1,0:T(8,128)(2,1)}), bf16[384,1536]{1,0:T(8,128)(2,1)}) %all-gather.14.cloned.1.call-update) | async-done | bytes 1179664 | tf_op jit(solution)/shard_map/all_gather | solution.py:35
  279.1 3.0 collective-permute-start.6
  287.2 4.0 convolution_convert_fusion.2
  293.6 27.5 %reduce-scatter.28.cloned.1.call-done = bf16[384,384]{1,0:T(8,128)(2,1)} async-done(((bf16[1536,384]{1,0:T(8,128)(2,1)}), bf16[384,384]{1,0:T(8,128)(2,1)}) %reduce-scatter.28.cloned.1.call-update) | async-done | bytes 294928
  324.8 31.0 %all-gather.16.cloned.1.call-done = bf16[384,1536]{1,0:T(8,128)(2,1)} async-done(((bf16[384,384]{1,0:T(8,128)(2,1)}), bf16[384,1536]{1,0:T(8,128)(2,1)}) %all-gather.16.cloned.1.call-update) | async-done | bytes 1179664 | tf_op jit(solution)/shard_map/all_gather | solution.py:35
  358.2 3.2 collective-permute-start.8
  361.4 2.7 fusion.50
  366.5 3.9 convolution_convert_fusion.1
  372.9 27.5 %reduce-scatter.30.cloned.1.call-done = bf16[384,384]{1,0:T(8,128)(2,1)} async-done(((bf16[1536,384]{1,0:T(8,128)(2,1)}), bf16[384,384]{1,0:T(8,128)(2,1)}) %reduce-scatter.30.cloned.1.call-update) | async-done | bytes 294928
  404.1 31.0 %all-gather.18.cloned.1.call-done = bf16[384,1536]{1,0:T(8,128)(2,1)} async-done(((bf16[384,384]{1,0:T(8,128)(2,1)}), bf16[384,1536]{1,0:T(8,128)(2,1)}) %all-gather.18.cloned.1.call-update) | async-done | bytes 1179664 | tf_op jit(solution)/shard_map/all_gather | solution.py:35
  437.6 3.0 collective-permute-start.10
  440.6 2.7 fusion.45
  445.7 3.9 convolution_convert_fusion
  452.1 27.5 %reduce-scatter.32.cloned.1.call-done = bf16[384,384]{1,0:T(8,128)(2,1)} async-done(((bf16[1536,384]{1,0:T(8,128)(2,1)}), bf16[384,384]{1,0:T(8,128)(2,1)}) %reduce-scatter.32.cloned.1.call-update) | async-done | bytes 294928
  483.3 9.0 %all_gather.31 = s32[64,64]{1,0:T(8,128)S(1)} all-gather(s32[8,64]{1,0:T(8,128)S(1)} %copy-done.10), channel_id=1, replica_groups=mesh['seq'=8,'trk'=4] {'seq'}, dimensions={0}, use_global_device_ids=true | all-gather | bytes 18432 | tf_op jit(solution)/shard_map/all_gather | solution.py:79
  493.4 20.8 %all-gather.20.cloned.1.call-done = bf16[384,1536]{1,0:T(8,128)(2,1)} async-done(((bf16[384,384]{1,0:T(8,128)(2,1)}), bf16[384,1536]{1,0:T(8,128)(2,1)}) %all-gather.20.cloned.1.call-update) | async-done | bytes 1179664 | tf_op jit(solution)/shard_map/all_gather | solution.py:74
  514.2 3.3 fusion
  519.5 32.8 %reduce-scatter.20.cloned.1.call-done = bf16[8,1024]{1,0:T(8,128)(2,1)} async-done(((bf16[64,1024]{1,0:T(8,128)(2,1)}), bf16[8,1024]{1,0:T(8,128)(2,1)}) %reduce-scatter.20.cloned.1.call-update) | async-done | bytes 16400 | tf_op jit(solution)/shard_map/reduce_scatter | solution.py:82
  (120 shorter events, 75.9 us)
Async XLA Ops:
  7.2 507.1 %copy-start = (bf16[1536,1024]{1,0:T(8,128)(2,1)S(1)}, bf16[1536,1024]{1,0:T(8,128)(2,1)}, u32[]{:S(2)}) copy-start(bf16[1536,1024]{1,0:T(8,128)(2,1)} %param.13) | copy-start | bytes 9437188
  7.2 33.8 %all-gather.8.cloned.1.call-start = ((), (), s32[]{:S(2)}) async-start(), calls=%async_computation.7 | async-start | bytes 1474560 | tf_op jit(solution)/shard_map/all_gather | solution.py:35
  7.9 76.5 %reduce-scatter.22.cloned.1.call-start = ((), (), s32[]{:S(2)}) async-start(), calls=%async_computation.15 | async-start | bytes 1474560
  41.9 6.3 %collective-permute-start.1 = (bf16[2,1536]{1,0:T(2,128)(2,1)S(1)}, bf16[2,1536]{1,0:T(2,128)(2,1)S(1)}, u32[]{:S(2)}, u32[]{:S(2)}) collective-permute-start(bf16[2,1536]{1,0:T(2,128)(2,1)S(1)} %get-tuple-element.19), channel_id=1, source_target_pairs={{4,0},{8,4},{12,8},{16,12},{20,16},{24,20},{28,24},{5,1},{9,5},{13... | collective-permute-start | bytes 18440 | tf_op jit(solution)/shard_map/ppermute | solution.py:20
  43.2 7.4 %collective-permute-start = (bf16[2,1536]{1,0:T(2,128)(2,1)S(1)}, bf16[2,1536]{1,0:T(2,128)(2,1)S(1)}, u32[]{:S(2)}, u32[]{:S(2)}) collective-permute-start(bf16[2,1536]{1,0:T(2,128)(2,1)S(1)} %get-tuple-element.18), channel_id=1, source_target_pairs={{0,4},{4,8},{8,12},{12,16},{16,20},{20,24},{24,28},{1,5},{5,9},{9,... | collective-permute-start | bytes 18440 | tf_op jit(solution)/shard_map/ppermute | solution.py:18
  56.9 29.4 %copy-start.6 = (bf16[384,384]{1,0:T(8,128)(2,1)S(1)}, bf16[384,384]{1,0:T(8,128)(2,1)}, u32[]{:S(2)}) copy-start(bf16[384,384]{1,0:T(8,128)(2,1)} %param.8) | copy-start | bytes 884740
  56.9 62.2 %all-gather.10.cloned.1.call-start = ((), (), s32[]{:S(2)}) async-start(), calls=%async_computation.8 | async-start | bytes 1474560 | tf_op jit(solution)/shard_map/all_gather | solution.py:35
  88.1 75.3 %reduce-scatter.24.cloned.1.call-start = ((), (), s32[]{:S(2)}) async-start(), calls=%async_computation.16 | async-start | bytes 1474560
  120.0 7.0 %collective-permute-start.3 = (bf16[4,1536]{1,0:T(4,128)(2,1)S(1)}, bf16[4,1536]{1,0:T(4,128)(2,1)S(1)}, u32[]{:S(2)}, u32[]{:S(2)}) collective-permute-start(bf16[4,1536]{1,0:T(4,128)(2,1)S(1)} %get-tuple-element.17), channel_id=1, source_target_pairs={{4,0},{8,4},{12,8},{16,12},{20,16},{24,20},{28,24},{5,1},{9,5},{13... | collective-permute-start | bytes 36872 | tf_op jit(solution)/shard_map/ppermute | solution.py:20
  121.3 8.1 %collective-permute-start.2 = (bf16[4,1536]{1,0:T(4,128)(2,1)S(1)}, bf16[4,1536]{1,0:T(4,128)(2,1)S(1)}, u32[]{:S(2)}, u32[]{:S(2)}) collective-permute-start(bf16[4,1536]{1,0:T(4,128)(2,1)S(1)} %get-tuple-element.16), channel_id=1, source_target_pairs={{0,4},{4,8},{8,12},{12,16},{16,20},{20,24},{24,28},{1,5},{5,9},{9,... | collective-permute-start | bytes 36872 | tf_op jit(solution)/shard_map/ppermute | solution.py:18
  135.8 29.4 %copy-start.5 = (bf16[384,384]{1,0:T(8,128)(2,1)S(1)}, bf16[384,384]{1,0:T(8,128)(2,1)}, u32[]{:S(2)}) copy-start(bf16[384,384]{1,0:T(8,128)(2,1)} %add_convert_fusion.5) | copy-start | bytes 884740
  135.8 62.3 %all-gather.12.cloned.1.call-start = ((), (), s32[]{:S(2)}) async-start(), calls=%async_computation.9 | async-start | bytes 1474560 | tf_op jit(solution)/shard_map/all_gather | solution.py:35
  167.0 75.2 %reduce-scatter.26.cloned.1.call-start = ((), (), s32[]{:S(2)}) async-start(), calls=%async_computation.17 | async-start | bytes 1474560
  198.9 7.0 %collective-permute-start.5 = (bf16[8,1536]{1,0:T(8,128)(2,1)S(1)}, bf16[8,1536]{1,0:T(8,128)(2,1)S(1)}, u32[]{:S(2)}, u32[]{:S(2)}) collective-permute-start(bf16[8,1536]{1,0:T(8,128)(2,1)S(1)} %get-tuple-element.15), channel_id=1, source_target_pairs={{4,0},{8,4},{12,8},{16,12},{20,16},{24,20},{28,24},{5,1},{9,5},{13... | collective-permute-start | bytes 73736 | tf_op jit(solution)/shard_map/ppermute | solution.py:20
  200.2 8.1 %collective-permute-start.4 = (bf16[8,1536]{1,0:T(8,128)(2,1)S(1)}, bf16[8,1536]{1,0:T(8,128)(2,1)S(1)}, u32[]{:S(2)}, u32[]{:S(2)}) collective-permute-start(bf16[8,1536]{1,0:T(8,128)(2,1)S(1)} %get-tuple-element.14), channel_id=1, source_target_pairs={{0,4},{4,8},{8,12},{12,16},{16,20},{20,24},{24,28},{1,5},{5,9},{9,... | collective-permute-start | bytes 73736 | tf_op jit(solution)/shard_map/ppermute | solution.py:18
  214.6 29.4 %copy-start.2 = (bf16[384,384]{1,0:T(8,128)(2,1)S(1)}, bf16[384,384]{1,0:T(8,128)(2,1)}, u32[]{:S(2)}) copy-start(bf16[384,384]{1,0:T(8,128)(2,1)} %add_convert_fusion.4) | copy-start | bytes 884740
  214.7 62.2 %all-gather.14.cloned.1.call-start = ((), (), s32[]{:S(2)}) async-start(), calls=%async_computation.10 | async-start | bytes 1474560 | tf_op jit(solution)/shard_map/all_gather | solution.py:35
  245.9 75.3 %reduce-scatter.28.cloned.1.call-start = ((), (), s32[]{:S(2)}) async-start(), calls=%async_computation.18 | async-start | bytes 1474560
  277.8 7.0 %collective-permute-start.7 = (bf16[16,1536]{1,0:T(8,128)(2,1)S(1)}, bf16[16,1536]{1,0:T(8,128)(2,1)S(1)}, u32[]{:S(2)}, u32[]{:S(2)}) collective-permute-start(bf16[16,1536]{1,0:T(8,128)(2,1)S(1)} %get-tuple-element.13), channel_id=1, source_target_pairs={{4,0},{8,4},{12,8},{16,12},{20,16},{24,20},{28,24},{5,1},{9,5},{13... | collective-permute-start | bytes 147464 | tf_op jit(solution)/shard_map/ppermute | solution.py:20
  279.1 8.1 %collective-permute-start.6 = (bf16[16,1536]{1,0:T(8,128)(2,1)S(1)}, bf16[16,1536]{1,0:T(8,128)(2,1)S(1)}, u32[]{:S(2)}, u32[]{:S(2)}) collective-permute-start(bf16[16,1536]{1,0:T(8,128)(2,1)S(1)} %get-tuple-element.12), channel_id=1, source_target_pairs={{0,4},{4,8},{8,12},{12,16},{16,20},{20,24},{24,28},{1,5},{5,9},{9,... | collective-permute-start | bytes 147464 | tf_op jit(solution)/shard_map/ppermute | solution.py:18
  293.6 62.2 %all-gather.16.cloned.1.call-start = ((), (), s32[]{:S(2)}) async-start(), calls=%async_computation.11 | async-start | bytes 1474560 | tf_op jit(solution)/shard_map/all_gather | solution.py:35
  324.8 75.6 %reduce-scatter.30.cloned.1.call-start = ((), (), s32[]{:S(2)}) async-start(), calls=%async_computation.19 | async-start | bytes 1474560
  356.8 7.3 %collective-permute-start.9 = (bf16[32,1536]{1,0:T(8,128)(2,1)S(1)}, bf16[32,1536]{1,0:T(8,128)(2,1)S(1)}, u32[]{:S(2)}, u32[]{:S(2)}) collective-permute-start(bf16[32,1536]{1,0:T(8,128)(2,1)S(1)} %get-tuple-element.11), channel_id=1, source_target_pairs={{4,0},{8,4},{12,8},{16,12},{20,16},{24,20},{28,24},{5,1},{9,5},{13... | collective-permute-start | bytes 294920 | tf_op jit(solution)/shard_map/ppermute | solution.py:20
  358.2 8.3 %collective-permute-start.8 = (bf16[32,1536]{1,0:T(8,128)(2,1)S(1)}, bf16[32,1536]{1,0:T(8,128)(2,1)S(1)}, u32[]{:S(2)}, u32[]{:S(2)}) collective-permute-start(bf16[32,1536]{1,0:T(8,128)(2,1)S(1)} %get-tuple-element.10), channel_id=1, source_target_pairs={{0,4},{4,8},{8,12},{12,16},{16,20},{20,24},{24,28},{1,5},{5,9},{9,... | collective-permute-start | bytes 294920 | tf_op jit(solution)/shard_map/ppermute | solution.py:18
  372.8 62.2 %all-gather.18.cloned.1.call-start = ((), (), s32[]{:S(2)}) async-start(), calls=%async_computation.12 | async-start | bytes 1474560 | tf_op jit(solution)/shard_map/all_gather | solution.py:35
  404.0 75.5 %reduce-scatter.32.cloned.1.call-start = ((), (), s32[]{:S(2)}) async-start(), calls=%async_computation.20 | async-start | bytes 1474560
  436.1 7.2 %collective-permute-start.11 = (bf16[64,1536]{1,0:T(8,128)(2,1)S(1)}, bf16[64,1536]{1,0:T(8,128)(2,1)S(1)}, u32[]{:S(2)}, u32[]{:S(2)}) collective-permute-start(bf16[64,1536]{1,0:T(8,128)(2,1)S(1)} %get-tuple-element.9), channel_id=1, source_target_pairs={{4,0},{8,4},{12,8},{16,12},{20,16},{24,20},{28,24},{5,1},{9,5},{13... | collective-permute-start | bytes 589832 | tf_op jit(solution)/shard_map/ppermute | solution.py:20
  437.6 8.1 %collective-permute-start.10 = (bf16[64,1536]{1,0:T(8,128)(2,1)S(1)}, bf16[64,1536]{1,0:T(8,128)(2,1)S(1)}, u32[]{:S(2)}, u32[]{:S(2)}) collective-permute-start(bf16[64,1536]{1,0:T(8,128)(2,1)S(1)} %get-tuple-element.8), channel_id=1, source_target_pairs={{0,4},{4,8},{8,12},{12,16},{16,20},{20,24},{24,28},{1,5},{5,9},{9,... | collective-permute-start | bytes 589832 | tf_op jit(solution)/shard_map/ppermute | solution.py:18
  452.0 31.3 %copy-start.13 = (bf16[1024]{0:T(1024)(128)(2,1)S(1)}, bf16[1024]{0:T(1024)(128)(2,1)}, u32[]{:S(2)}) copy-start(bf16[1024]{0:T(1024)(128)(2,1)} %param.14) | copy-start | bytes 6148
  452.0 31.3 %copy-start.10 = (s32[8,64]{1,0:T(8,128)S(1)}, s32[8,64]{1,0:T(8,128)}, u32[]{:S(2)}) copy-start(s32[8,64]{1,0:T(8,128)} %param.15) | copy-start | bytes 6148
  452.0 62.2 %all-gather.20.cloned.1.call-start = ((), (), s32[]{:S(2)}) async-start(), calls=%async_computation.13 | async-start | bytes 1474560 | tf_op jit(solution)/shard_map/all_gather | solution.py:74
  483.2 69.1 %reduce-scatter.20.cloned.1.call-start = ((), (), s32[]{:S(2)}) async-start(), calls=%async_computation.14 | async-start | bytes 147456 | tf_op jit(solution)/shard_map/reduce_scatter | solution.py:82
  (11 other events, 135.3 us)
Sparse Core Ops, SparseCore 0:
  9.6 31.3 all-gather.7
  57.0 27.4 reduce-scatter.21
  88.2 30.8 all-gather.9
  135.9 27.4 reduce-scatter.23
  167.1 30.8 all-gather.11
  214.8 27.4 reduce-scatter.25
  246.0 30.8 all-gather.13
  293.7 27.4 reduce-scatter.27
  324.9 30.8 all-gather.15
  373.0 27.4 reduce-scatter.29
  404.2 30.8 all-gather.17
  452.1 27.4 reduce-scatter.31
  483.3 30.8 all-gather.19
  519.5 32.7 reduce-scatter.19
where the time goes:
time: 564 us; the launch traced here: 560 us
  waiting for transfers between devices  406 us (72%)
  matrix products  57.4 us (10%)
  local copies, waits for them, and re-layouts  32.4 us (6%)
  starting transfers between devices  27 us (5%)
  other arithmetic  14.2 us (3%)
  between operations  14.2 us (3%)
  blocking collectives  9.03 us (2%)
    all_gather x6, waiting for transfers between devices, dilated_inner(): gathered = lax.all_gather(trunk, 'trk', axis=1, tiled=True)  187 us
    unnamed x20, waiting for transfers between devices  165 us
    reduce_scatter x1, waiting for transfers between devices, shards(): lax.psum_scatter(jnp.dot(onehot, coverage, preferred_element_type=jnp.flo...  32.8 us
    dot_general x12, matrix products, contract_last(): lax.dot_general(rows, kernel, (((1,), (1,)), ((), ())), preferred_element...  29.5 us
    unnamed x46, local copies, waits for them, and re-layouts  26.9 us
    dot_general x6, matrix products, shards(): jnp.dot(activation, conv_out[block_layer_index], preferred_element_type=j...  23.7 us
    all_gather x1, waiting for transfers between devices, shards(): lax.all_gather(trunk, 'trk', axis=1, tiled=True)  20.8 us
    ppermute x6, starting transfers between devices, extended(): lax.ppermute(tail, axis, [(i, (i + 1) % count) for i in range(ends)])  18.4 us
  transfers between devices with their start and end apart: 26, of which 14 were waited for; matrix products, arithmetic and copies ran while one was open for 6% of the time, Pallas kernels for 0%

commit v1 on v0

v1 whole, which is shorter than its diff:
```python
import jax
import jax.numpy as jnp
from jax import lax
from jax.sharding import PartitionSpec as P

RESIDUAL_BLOCKS = 6
BASE_DILATION = 2
BLOCKS_PER_LOAD = 2


def shifted(cells, axis, step):
    count = lax.axis_size(axis)
    return lax.ppermute(cells, axis, [(i, (i + step) % count) for i in range(count)])


def halo(cells, width):
    count = lax.axis_size("seq")
    head = cells[:width]
    tail = cells[cells.shape[0] - width :]
    above = lax.ppermute(tail, "seq", [(i, i + 1) for i in range(count - 1)])
    below = lax.ppermute(head, "seq", [(i + 1, i) for i in range(count - 1)])
    return above, below


def contract_last(rows, kernel):
    return lax.dot_general(
        rows, kernel, (((1,), (1,)), ((), ())), preferred_element_type=jnp.float32
    )


def group_size(rows, count):
    size = 1
    for g in range(1, count + 1):
        if count % g == 0 and rows % (16 * g) == 0:
            size = g
    return size


def spread_projection(conv_out):
    blocks, hidden, channels = conv_out.shape
    count = lax.axis_size("seq")
    rows = BLOCKS_PER_LOAD * hidden
    size = group_size(rows, count)
    share = rows // size
    groups = [[g * size + i for i in range(size)] for g in range(count // size)]
    mine = lax.rem(lax.axis_index("seq"), size)
    loads = []
    for first in range(0, blocks, BLOCKS_PER_LOAD):
        flat = conv_out[first : first + BLOCKS_PER_LOAD].reshape(rows, channels)
        part = lax.dynamic_slice_in_dim(flat, mine * share, share, 0)
        column = lax.all_gather(part, "trk", axis=0, tiled=False)
        whole = lax.all_gather(column, "seq", axis=0, tiled=False, axis_index_groups=groups)
        loads.append(whole)
    return loads


def block_projection(loads, block, hidden):
    whole = loads[block // BLOCKS_PER_LOAD]
    size, quarters, share, channels = whole.shape
    per = hidden // share
    first = (block % BLOCKS_PER_LOAD) * per
    part = whole[first : first + per]
    return jnp.transpose(part, (1, 0, 2, 3)).reshape(quarters, hidden, channels)


def exon_onehot(gene_block, first_bin, width_now):
    exon_matches = (
        gene_block[:, :, None] - first_bin == jnp.arange(width_now, dtype=jnp.int32)[None, None, :]
    )
    return jnp.sum(exon_matches.astype(jnp.float32), axis=1).astype(jnp.bfloat16)


def shards(
    trunk_input, conv_in, conv_bias, conv_out, projection_bias, head_weight, head_bias, exon_bins
):
    quarters = lax.axis_size("trk")
    place = lax.axis_index("trk")
    bin_rows = trunk_input.shape[0]
    hidden = conv_out.shape[1]
    gene_lists = lax.all_gather(exon_bins, "seq", axis=0, tiled=True)
    trunk = lax.all_gather(trunk_input, "trk", axis=1, tiled=True)
    biases = lax.all_gather(projection_bias, "trk", axis=1, tiled=True)
    loads = spread_projection(conv_out)
    for block in range(RESIDUAL_BLOCKS):
        step = BASE_DILATION * 2**block
        above, below = halo(trunk, step)
        padded = jnp.concatenate([above, trunk, below], axis=0)
        inner = conv_bias[block].astype(jnp.float32)
        for tap in range(3):
            inner = inner + contract_last(
                padded[tap * step : tap * step + bin_rows], conv_in[block, tap]
            )
        activation = jax.nn.gelu(inner, approximate=True).astype(jnp.bfloat16)
        weight = block_projection(loads, block, hidden)
        total = trunk.astype(jnp.float32) + biases[block].astype(jnp.float32)
        others = [activation] + [shifted(activation, "trk", k) for k in range(1, quarters)]
        for k in range(quarters):
            owner = lax.rem(place - k + quarters, quarters)
            total = total + jnp.dot(
                others[k],
                lax.dynamic_index_in_dim(weight, owner, 0, keepdims=False),
                preferred_element_type=jnp.float32,
            )
        trunk = total.astype(jnp.bfloat16)
    logits = jnp.dot(trunk, head_weight, preferred_element_type=jnp.float32)
    coverage = jax.nn.softplus(logits + head_bias.astype(jnp.float32)).astype(jnp.bfloat16)
    first_bin = lax.axis_index("seq") * bin_rows
    onehot = exon_onehot(gene_lists, first_bin, bin_rows)
    partial = jnp.dot(onehot, coverage, preferred_element_type=jnp.float32).astype(jnp.bfloat16)
    count = lax.axis_size("seq")
    parts = lax.all_to_all(
        partial.reshape(count, exon_bins.shape[0], partial.shape[1]), "seq", 0, 0, tiled=False
    )
    gene_sum = jnp.sum(parts.astype(jnp.float32), axis=0)
    counts = jnp.sum((exon_bins >= 0).astype(jnp.float32), axis=1)
    gene_cov = gene_sum / counts[:, None]
    return (coverage, gene_cov)


def solution(mesh):
    in_specs = (
        P("seq", "trk"),
        P(None, None, "trk", None),
        P(None, "trk"),
        P(None, "trk", None),
        P(None, "trk"),
        P(None, "trk"),
        P("trk"),
        P("seq", None),
    )
    out_specs = (P("seq", "trk"), P("seq", "trk"))
    return jax.shard_map(shards, mesh=mesh, in_specs=in_specs, out_specs=out_specs, check_vma=False)
```

time: 564 us -> 333 us (0.59)
  waiting for transfers between devices: 406 us -> 89.3 us
  blocking collectives: 9.03 us -> 81.8 us
  starting transfers between devices: 27 us -> 71.5 us
  other arithmetic: 14.2 us -> 2.65 us
  matrix products: 57.4 us -> 46.5 us
  local copies, waits for them, and re-layouts: 32.4 us -> 25.1 us
    all_gather x7 -> x4, waiting for transfers between devices: 208 us -> 37.2 us  [the longest x3 37.2 us: spread_projection(): lax.all_gather(column, 'seq', axis=0, tiled=False, axis_index_groups=groups)]
    unnamed x20 -> x4, waiting for transfers between devices: 165 us -> 0.73 us
    all_gather x0 -> x4, blocking collectives: none -> 72.9 us  [the longest x3 59.6 us: spread_projection(): column = lax.all_gather(part, 'trk', axis=0, tiled=False)]
    ppermute x12 -> x30, waiting for transfers between devices: 0.03 us -> 46 us  [the longest x18 45.2 us: shifted(): lax.ppermute(cells, axis, [(i, (i + step) % count) for i in range(count)])]
    reduce_scatter x1 -> x0, waiting for transfers between devices: 32.8 us -> none  [shards(): lax.psum_scatter(jnp.dot(onehot, coverage, preferred_element_type=jnp.flo...]
    ppermute x12 -> x30, starting transfers between devices: 26.4 us -> 52.2 us  [the longest x6 23.5 us: halo(): above = lax.ppermute(tail, 'seq', [(i, i + 1) for i in range(count - 1)])]
    unnamed x46 -> x42, local copies, waits for them, and re-layouts: 26.9 us -> 5.78 us
    all_to_all x0 -> x1, starting transfers between devices: none -> 19.1 us  [shards(): lax.all_to_all(partial.reshape(count, exon_bins.shape[0], partial.shape[1...]
  transfers between devices with their start and end apart: 26 -> 35, of which waited for: 14 -> 19; matrix products, arithmetic and copies ran while one was open for 6% -> 15% of each run, Pallas kernels for 0% -> 0%
where the time goes in v1:
time: 333 us; the launch traced here: 331 us
  waiting for transfers between devices  89.3 us (27%)
  blocking collectives  81.8 us (25%)
  starting transfers between devices  71.5 us (21%)
  matrix products  46.5 us (14%)
  local copies, waits for them, and re-layouts  25.1 us (8%)
  between operations  14.6 us (4%)
    all_gather x3, blocking collectives, spread_projection(): column = lax.all_gather(part, 'trk', axis=0, tiled=False)  59.6 us
    ppermute x18, waiting for transfers between devices, shifted(): lax.ppermute(cells, axis, [(i, (i + step) % count) for i in range(count)])  45.2 us
    all_gather x3, waiting for transfers between devices, spread_projection(): lax.all_gather(column, 'seq', axis=0, tiled=False, axis_index_groups=groups)  37.2 us
    ppermute x6, starting transfers between devices, halo(): above = lax.ppermute(tail, 'seq', [(i, i + 1) for i in range(count - 1)])  23.5 us
    ppermute x18, starting transfers between devices, shifted(): lax.ppermute(cells, axis, [(i, (i + step) % count) for i in range(count)])  21 us
    all_to_all x1, starting transfers between devices, shards(): lax.all_to_all(partial.reshape(count, exon_bins.shape[0], partial.shape[1...  19.1 us
    dot_general x18, matrix products, contract_last(): lax.dot_general(rows, kernel, (((1,), (1,)), ((), ())), preferred_element...  18.7 us
    dot_general x23, matrix products, shards(): jnp.dot(others[k], lax.dynamic_index_in_dim(weight, owner, 0, keepdims=Fa...  18.7 us
  transfers between devices with their start and end apart: 35, of which 19 were waited for; matrix products, arithmetic and copies ran while one was open for 15% of the time, Pallas kernels for 0%

profile of v1, /device:TPU:8, one launch (start us, length us, event | category | flops | bytes accessed | tf_op | source)
XLA Modules:
  0.0 331.5 jit_solution(11259037252919530827)
XLA Ops:
  8.0 3.8 %fusion.290 = (bf16[2,192,1536]{2,1,0:T(8,128)(2,1)}, bf16[2,192,1536]{2,1,0:T(8,128)(2,1)S(1)}, bf16[2,192,1536]{2,1,0:T(8,128)(2,1)}) fusion(bf16[6,192,1536]{2,1,0:T(8,128)(2,1)} %param.11), kind=kLoop, calls=%fused_computation.311 | loop fusion | bytes 7077888 | tf_op jit(solution)/shard_map/slice | solution.py:49
  11.9 22.0 %all-gather = bf16[192,1536]{1,0:T(8,128)(2,1)} all-gather(bf16[48,1536]{1,0:T(8,128)(2,1)S(1)} %constant_dynamic-slice_fusion.2), channel_id=2, replica_groups=mesh['seq'=8,'trk'=4] {'trk'}, dimensions={0}, use_global_device_ids=true | all-gather | bytes 737280 | tf_op jit(solution)/shard_map/all_gather | solution.py:51
  34.8 21.8 %all-gather.4 = bf16[192,1536]{1,0:T(8,128)(2,1)} all-gather(bf16[48,1536]{1,0:T(8,128)(2,1)S(1)} %constant_dynamic-slice_fusion), channel_id=6, replica_groups=mesh['seq'=8,'trk'=4] {'trk'}, dimensions={0}, use_global_device_ids=true | all-gather | bytes 737280 | tf_op jit(solution)/shard_map/all_gather | solution.py:51
  57.6 15.9 %all-gather.2 = bf16[192,1536]{1,0:T(8,128)(2,1)} all-gather(bf16[48,1536]{1,0:T(8,128)(2,1)S(1)} %constant_dynamic-slice_fusion.1), channel_id=4, replica_groups=mesh['seq'=8,'trk'=4] {'trk'}, dimensions={0}, use_global_device_ids=true | all-gather | bytes 737280 | tf_op jit(solution)/shard_map/all_gather | solution.py:51
  73.6 8.8 %all_gather.59 = s32[64,64]{1,0:T(8,128)S(1)} all-gather(s32[8,64]{1,0:T(8,128)S(1)} %copy-done.10), channel_id=1, replica_groups=mesh['seq'=8,'trk'=4] {'seq'}, dimensions={0}, use_global_device_ids=true | all-gather | bytes 18432 | tf_op jit(solution)/shard_map/all_gather | solution.py:80
  82.4 13.3 %all_gather.46 = bf16[6,1536]{1,0:T(8,128)(2,1)S(1)} all-gather(bf16[6,384]{1,0:T(8,128)(2,1)S(1)} %copy-done.12), channel_id=1, replica_groups=mesh['seq'=8,'trk'=4] {'trk'}, dimensions={1}, use_global_device_ids=true | all-gather | bytes 23040 | tf_op jit(solution)/shard_map/all_gather | solution.py:82
  99.7 3.2 collective-permute-start
  108.8 2.4 collective-permute-start.3
  113.6 4.1 %fusion.289 = (bf16[16,48,1536]{2,1,0:T(8,128)(2,1)}, bf16[16,48,1536]{2,1,0:T(8,128)(2,1)S(1)}) fusion(bf16[32,48,1536]{2,1,0:T(8,128)(2,1)} %all-gather.13.cloned.1.call-done), kind=kLoop, calls=%fused_computation.310 | loop fusion | bytes 9437184 | tf_op jit(solution)/shard_map/slice | solution.py:62
  119.5 2.4 collective-permute-done.3
  123.3 2.8 collective-permute-done.4
  129.3 3.0 collective-permute-start.5
  135.9 4.8 %fusion.287 = (bf16[16,48,1536]{2,1,0:T(8,128)(2,1)}, bf16[16,48,1536]{2,1,0:T(8,128)(2,1)}) fusion(bf16[32,48,1536]{2,1,0:T(8,128)(2,1)} %all-gather.17.cloned.1.call-done), kind=kLoop, calls=%fused_computation.308 | loop fusion | bytes 9437184 | tf_op jit(solution)/shard_map/slice | solution.py:62
  140.7 36.0 %all-gather.15.cloned.1.call-done = bf16[32,48,1536]{2,1,0:T(8,128)(2,1)} async-done(((bf16[4,48,1536]{2,1,0:T(8,128)(2,1)}), bf16[32,48,1536]{2,1,0:T(8,128)(2,1)}) %all-gather.15.cloned.1.call-update) | async-done | bytes 4718608 | tf_op jit(solution)/shard_map/all_gather | solution.py:52
  176.7 2.8 fusion.288
  188.7 2.5 collective-permute-start.8
  193.7 7.4 %collective-permute-done.8 = bf16[384,192]{0,1:T(8,128)(2,1)S(1)} collective-permute-done((bf16[384,192]{0,1:T(8,128)(2,1)S(1)}, bf16[384,192]{0,1:T(8,128)(2,1)S(1)}, u32[]{:S(2)}, u32[]{:S(2)}) %collective-permute-start.8) | collective-permute-done | bytes 147488 | tf_op jit(solution)/shard_map/ppermute | solution.py:13
  201.6 2.6 collective-permute-done.9
  207.4 3.2 collective-permute-start.10
  212.8 2.6 collective-permute-start.14
  215.9 7.0 %collective-permute-done.13 = bf16[384,192]{0,1:T(8,128)(2,1)S(1)} collective-permute-done((bf16[384,192]{0,1:T(8,128)(2,1)S(1)}, bf16[384,192]{0,1:T(8,128)(2,1)S(1)}, u32[]{:S(2)}, u32[]{:S(2)}) %collective-permute-start.13) | collective-permute-done | bytes 147488 | tf_op jit(solution)/shard_map/ppermute | solution.py:13
  223.5 4.1 %collective-permute-done.14 = bf16[384,192]{0,1:T(8,128)(2,1)S(1)} collective-permute-done((bf16[384,192]{0,1:T(8,128)(2,1)S(1)}, bf16[384,192]{0,1:T(8,128)(2,1)S(1)}, u32[]{:S(2)}, u32[]{:S(2)}) %collective-permute-start.14) | collective-permute-done | bytes 147488 | tf_op jit(solution)/shard_map/ppermute | solution.py:13
  230.7 3.0 collective-permute-start.15
  238.0 3.5 %collective-permute-done.18 = bf16[384,192]{0,1:T(8,128)(2,1)S(1)} collective-permute-done((bf16[384,192]{0,1:T(8,128)(2,1)S(1)}, bf16[384,192]{0,1:T(8,128)(2,1)S(1)}, u32[]{:S(2)}, u32[]{:S(2)}) %collective-permute-start.18) | collective-permute-done | bytes 147488 | tf_op jit(solution)/shard_map/ppermute | solution.py:13
  242.0 4.0 %collective-permute-done.19 = bf16[384,192]{0,1:T(8,128)(2,1)S(1)} collective-permute-done((bf16[384,192]{0,1:T(8,128)(2,1)S(1)}, bf16[384,192]{0,1:T(8,128)(2,1)S(1)}, u32[]{:S(2)}, u32[]{:S(2)}) %collective-permute-start.19) | collective-permute-done | bytes 147488 | tf_op jit(solution)/shard_map/ppermute | solution.py:13
  250.3 5.6 %collective-permute-start.20 = (bf16[32,1536]{1,0:T(8,128)(2,1)S(1)}, bf16[32,1536]{1,0:T(8,128)(2,1)S(1)}, u32[]{:S(2)}, u32[]{:S(2)}) collective-permute-start(bf16[32,1536]{1,0:T(8,128)(2,1)S(1)} %get-tuple-element.19), channel_id=1, source_target_pairs={{0,4},{4,8},{8,12},{12,16},{16,20},{20,24},{24,28},{1,5},{5,9},{9,... | collective-permute-start | bytes 294920 | tf_op jit(solution)/shard_map/ppermute | solution.py:20
  261.1 3.4 %collective-permute-done.23 = bf16[384,192]{0,1:T(8,128)(2,1)S(1)} collective-permute-done((bf16[384,192]{0,1:T(8,128)(2,1)S(1)}, bf16[384,192]{0,1:T(8,128)(2,1)S(1)}, u32[]{:S(2)}, u32[]{:S(2)}) %collective-permute-start.23) | collective-permute-done | bytes 147488 | tf_op jit(solution)/shard_map/ppermute | solution.py:13
  265.8 5.1 %collective-permute-done.22 = bf16[384,192]{0,1:T(8,128)(2,1)S(1)} collective-permute-done((bf16[384,192]{0,1:T(8,128)(2,1)S(1)}, bf16[384,192]{0,1:T(8,128)(2,1)S(1)}, u32[]{:S(2)}, u32[]{:S(2)}) %collective-permute-start.22) | collective-permute-done | bytes 147488 | tf_op jit(solution)/shard_map/ppermute | solution.py:13
  273.1 5.5 %collective-permute-start.25 = (bf16[64,1536]{1,0:T(8,128)(2,1)S(1)}, bf16[64,1536]{1,0:T(8,128)(2,1)S(1)}, u32[]{:S(2)}, u32[]{:S(2)}) collective-permute-start(bf16[64,1536]{1,0:T(8,128)(2,1)S(1)} %get-tuple-element.17), channel_id=1, source_target_pairs={{0,4},{4,8},{8,12},{12,16},{16,20},{20,24},{24,28},{1,5},{5,9},{9,... | collective-permute-start | bytes 589832 | tf_op jit(solution)/shard_map/ppermute | solution.py:20
  290.4 7.1 %fusion.18 = bf16[384,1024]{1,0:T(8,128)(2,1)} fusion(bf16[1536,1024]{1,0:T(8,128)(2,1)S(1)} %copy-done, f32[1024]{0:T(1024)S(1)} %convert_element_type.117, f32[384,1536]{1,0:T(8,128)} %fusion.62, f32[384,1536]{1,0:T(8,128)} %fusion.64, bf16[384,192]{0,1:T(8,128)(2,1)S(1)} %collective-permute-done.27, f32[384,1536]{1,0:T(8,128)} %fusion.68, ...), kind=kOutput, calls=%fused_computation.28 | convolution fusion | flops 1441726464 | bytes 12937220 | tf_op jit(solution)/shard_map/dot_general | solution.py:105
  299.6 19.1 %all-to-all-start = ((bf16[8,8,1024]{2,1,0:T(8,128)(2,1)}), bf16[8,8,1024]{2,1,0:T(8,128)(2,1)S(1)}, u32[]{:S(2)}, u32[]{:S(2)}) async-start(bf16[8,8,1024]{2,1,0:T(8,128)(2,1)} %fusion.61), calls=%async_computation | async-start | bytes 262144 | tf_op jit(solution)/shard_map/all_to_all | solution.py:111
  318.8 5.4 %all-to-all-done = bf16[8,8,1024]{2,1,0:T(8,128)(2,1)S(1)} async-done(((bf16[8,8,1024]{2,1,0:T(8,128)(2,1)}), bf16[8,8,1024]{2,1,0:T(8,128)(2,1)S(1)}, u32[]{:S(2)}, u32[]{:S(2)}) %all-to-all-start) | async-done | bytes 131104 | tf_op jit(solution)/shard_map/all_to_all | solution.py:111
  (160 shorter events, 78.4 us)
Async XLA Ops:
  7.2 90.4 %all-gather.11.cloned.1.call-start = ((), (), s32[]{:S(2)}) async-start(), calls=%async_computation.1 | async-start | bytes 1474560 | tf_op jit(solution)/shard_map/all_gather | solution.py:81
  7.9 105.6 %all-gather.13.cloned.1.call-start = ((), (), s32[]{:S(2)}) async-start(), calls=%async_computation.2 | async-start | bytes 5308416 | tf_op jit(solution)/shard_map/all_gather | solution.py:52
  33.8 102.0 %all-gather.17.cloned.1.call-start = ((), (), s32[]{:S(2)}) async-start(), calls=%async_computation.4 | async-start | bytes 5308416 | tf_op jit(solution)/shard_map/all_gather | solution.py:52
  56.6 120.1 %all-gather.15.cloned.1.call-start = ((), (), s32[]{:S(2)}) async-start(), calls=%async_computation.3 | async-start | bytes 5308416 | tf_op jit(solution)/shard_map/all_gather | solution.py:52
  98.4 6.6 %collective-permute-start.1 = (bf16[2,1536]{1,0:T(2,128)(2,1)S(1)}, bf16[2,1536]{1,0:T(2,128)(2,1)S(1)}, u32[]{:S(2)}, u32[]{:S(2)}) collective-permute-start(bf16[2,1536]{1,0:T(2,128)(2,1)S(1)} %get-tuple-element.28), channel_id=1, source_target_pairs={{4,0},{8,4},{12,8},{16,12},{20,16},{24,20},{28,24},{5,1},{9,5},{13... | collective-permute-start | bytes 18440 | tf_op jit(solution)/shard_map/ppermute | solution.py:21
  99.7 7.4 %collective-permute-start = (bf16[2,1536]{1,0:T(2,128)(2,1)S(1)}, bf16[2,1536]{1,0:T(2,128)(2,1)S(1)}, u32[]{:S(2)}, u32[]{:S(2)}) collective-permute-start(bf16[2,1536]{1,0:T(2,128)(2,1)S(1)} %get-tuple-element.27), channel_id=1, source_target_pairs={{0,4},{4,8},{8,12},{12,16},{16,20},{20,24},{24,28},{1,5},{5,9},{9,... | collective-permute-start | bytes 18440 | tf_op jit(solution)/shard_map/ppermute | solution.py:20
  108.8 13.0 %collective-permute-start.3 = (bf16[384,192]{0,1:T(8,128)(2,1)S(1)}, bf16[384,192]{0,1:T(8,128)(2,1)}, u32[]{:S(2)}, u32[]{:S(2)}) collective-permute-start(bf16[384,192]{0,1:T(8,128)(2,1)S(1)} %fusion.180), channel_id=1, source_target_pairs={{0,2},{1,3},{2,0},{3,1},{4,6},{5,7},{6,4},{7,5},{8,10},{9,11},{10,... | collective-permute-start | bytes 442376 | tf_op jit(solution)/shard_map/ppermute | solution.py:13
  111.3 14.8 %collective-permute-start.4 = (bf16[384,192]{0,1:T(8,128)(2,1)S(1)}, bf16[384,192]{0,1:T(8,128)(2,1)S(1)}, u32[]{:S(2)}, u32[]{:S(2)}) collective-permute-start(bf16[384,192]{0,1:T(8,128)(2,1)S(1)} %fusion.180), channel_id=1, source_target_pairs={{0,3},{1,0},{2,1},{3,2},{4,7},{5,4},{6,5},{7,6},{8,11},{9,8},{10,9... | collective-permute-start | bytes 442376 | tf_op jit(solution)/shard_map/ppermute | solution.py:13
  112.8 13.7 %collective-permute-start.2 = (bf16[384,192]{0,1:T(8,128)(2,1)S(1)}, bf16[384,192]{0,1:T(8,128)(2,1)}, u32[]{:S(2)}, u32[]{:S(2)}) collective-permute-start(bf16[384,192]{0,1:T(8,128)(2,1)S(1)} %fusion.180), channel_id=1, source_target_pairs={{0,1},{1,2},{2,3},{3,0},{4,5},{5,6},{6,7},{7,4},{8,9},{9,10},{10,1... | collective-permute-start | bytes 442376 | tf_op jit(solution)/shard_map/ppermute | solution.py:13
  128.0 55.7 %collective-permute-start.6 = (bf16[4,1536]{1,0:T(4,128)(2,1)S(1)}, bf16[4,1536]{1,0:T(4,128)(2,1)S(1)}, u32[]{:S(2)}, u32[]{:S(2)}) collective-permute-start(bf16[4,1536]{1,0:T(4,128)(2,1)S(1)} %get-tuple-element.26), channel_id=1, source_target_pairs={{4,0},{8,4},{12,8},{16,12},{20,16},{24,20},{28,24},{5,1},{9,5},{13... | collective-permute-start | bytes 36872 | tf_op jit(solution)/shard_map/ppermute | solution.py:21
  129.3 57.4 %collective-permute-start.5 = (bf16[4,1536]{1,0:T(4,128)(2,1)S(1)}, bf16[4,1536]{1,0:T(4,128)(2,1)S(1)}, u32[]{:S(2)}, u32[]{:S(2)}) collective-permute-start(bf16[4,1536]{1,0:T(4,128)(2,1)S(1)} %get-tuple-element.25), channel_id=1, source_target_pairs={{0,4},{4,8},{8,12},{12,16},{16,20},{20,24},{24,28},{1,5},{5,9},{9,... | collective-permute-start | bytes 36872 | tf_op jit(solution)/shard_map/ppermute | solution.py:20
  188.7 12.4 %collective-permute-start.8 = (bf16[384,192]{0,1:T(8,128)(2,1)S(1)}, bf16[384,192]{0,1:T(8,128)(2,1)S(1)}, u32[]{:S(2)}, u32[]{:S(2)}) collective-permute-start(bf16[384,192]{0,1:T(8,128)(2,1)S(1)} %fusion.192), channel_id=1, source_target_pairs={{0,2},{1,3},{2,0},{3,1},{4,6},{5,7},{6,4},{7,5},{8,10},{9,11},{10,... | collective-permute-start | bytes 442376 | tf_op jit(solution)/shard_map/ppermute | solution.py:13
  191.2 13.1 %collective-permute-start.9 = (bf16[384,192]{0,1:T(8,128)(2,1)S(1)}, bf16[384,192]{0,1:T(8,128)(2,1)S(1)}, u32[]{:S(2)}, u32[]{:S(2)}) collective-permute-start(bf16[384,192]{0,1:T(8,128)(2,1)S(1)} %fusion.192), channel_id=1, source_target_pairs={{0,3},{1,0},{2,1},{3,2},{4,7},{5,4},{6,5},{7,6},{8,11},{9,8},{10,9... | collective-permute-start | bytes 442376 | tf_op jit(solution)/shard_map/ppermute | solution.py:13
  191.7 13.0 %collective-permute-start.7 = (bf16[384,192]{0,1:T(8,128)(2,1)S(1)}, bf16[384,192]{0,1:T(8,128)(2,1)S(1)}, u32[]{:S(2)}, u32[]{:S(2)}) collective-permute-start(bf16[384,192]{0,1:T(8,128)(2,1)S(1)} %fusion.192), channel_id=1, source_target_pairs={{0,1},{1,2},{2,3},{3,0},{4,5},{5,6},{6,7},{7,4},{8,9},{9,10},{10,1... | collective-permute-start | bytes 442376 | tf_op jit(solution)/shard_map/ppermute | solution.py:13
  205.6 5.1 %collective-permute-start.11 = (bf16[8,1536]{1,0:T(8,128)(2,1)S(1)}, bf16[8,1536]{1,0:T(8,128)(2,1)S(1)}, u32[]{:S(2)}, u32[]{:S(2)}) collective-permute-start(bf16[8,1536]{1,0:T(8,128)(2,1)S(1)} %get-tuple-element.24), channel_id=1, source_target_pairs={{4,0},{8,4},{12,8},{16,12},{20,16},{24,20},{28,24},{5,1},{9,5},{13... | collective-permute-start | bytes 73736 | tf_op jit(solution)/shard_map/ppermute | solution.py:21
  212.0 11.0 %collective-permute-start.13 = (bf16[384,192]{0,1:T(8,128)(2,1)S(1)}, bf16[384,192]{0,1:T(8,128)(2,1)S(1)}, u32[]{:S(2)}, u32[]{:S(2)}) collective-permute-start(bf16[384,192]{0,1:T(8,128)(2,1)S(1)} %fusion.204), channel_id=1, source_target_pairs={{0,2},{1,3},{2,0},{3,1},{4,6},{5,7},{6,4},{7,5},{8,10},{9,11},{10,... | collective-permute-start | bytes 442376 | tf_op jit(solution)/shard_map/ppermute | solution.py:13
  212.8 14.7 %collective-permute-start.14 = (bf16[384,192]{0,1:T(8,128)(2,1)S(1)}, bf16[384,192]{0,1:T(8,128)(2,1)S(1)}, u32[]{:S(2)}, u32[]{:S(2)}) collective-permute-start(bf16[384,192]{0,1:T(8,128)(2,1)S(1)} %fusion.204), channel_id=1, source_target_pairs={{0,3},{1,0},{2,1},{3,2},{4,7},{5,4},{6,5},{7,6},{8,11},{9,8},{10,9... | collective-permute-start | bytes 442376 | tf_op jit(solution)/shard_map/ppermute | solution.py:13
  215.4 12.6 %collective-permute-start.12 = (bf16[384,192]{0,1:T(8,128)(2,1)S(1)}, bf16[384,192]{0,1:T(8,128)(2,1)S(1)}, u32[]{:S(2)}, u32[]{:S(2)}) collective-permute-start(bf16[384,192]{0,1:T(8,128)(2,1)S(1)} %fusion.204), channel_id=1, source_target_pairs={{0,1},{1,2},{2,3},{3,0},{4,5},{5,6},{6,7},{7,4},{8,9},{9,10},{10,1... | collective-permute-start | bytes 442376 | tf_op jit(solution)/shard_map/ppermute | solution.py:13
  235.3 6.2 %collective-permute-start.18 = (bf16[384,192]{0,1:T(8,128)(2,1)S(1)}, bf16[384,192]{0,1:T(8,128)(2,1)S(1)}, u32[]{:S(2)}, u32[]{:S(2)}) collective-permute-start(bf16[384,192]{0,1:T(8,128)(2,1)S(1)} %fusion.216), channel_id=1, source_target_pairs={{0,2},{1,3},{2,0},{3,1},{4,6},{5,7},{6,4},{7,5},{8,10},{9,11},{10,... | collective-permute-start | bytes 442376 | tf_op jit(solution)/shard_map/ppermute | solution.py:13
  235.4 10.7 %collective-permute-start.19 = (bf16[384,192]{0,1:T(8,128)(2,1)S(1)}, bf16[384,192]{0,1:T(8,128)(2,1)S(1)}, u32[]{:S(2)}, u32[]{:S(2)}) collective-permute-start(bf16[384,192]{0,1:T(8,128)(2,1)S(1)} %fusion.216), channel_id=1, source_target_pairs={{0,3},{1,0},{2,1},{3,2},{4,7},{5,4},{6,5},{7,6},{8,11},{9,8},{10,9... | collective-permute-start | bytes 442376 | tf_op jit(solution)/shard_map/ppermute | solution.py:13
  237.5 10.1 %collective-permute-start.17 = (bf16[384,192]{0,1:T(8,128)(2,1)S(1)}, bf16[384,192]{0,1:T(8,128)(2,1)S(1)}, u32[]{:S(2)}, u32[]{:S(2)}) collective-permute-start(bf16[384,192]{0,1:T(8,128)(2,1)S(1)} %fusion.216), channel_id=1, source_target_pairs={{0,1},{1,2},{2,3},{3,0},{4,5},{5,6},{6,7},{7,4},{8,9},{9,10},{10,1... | collective-permute-start | bytes 442376 | tf_op jit(solution)/shard_map/ppermute | solution.py:13
  248.4 7.5 %collective-permute-start.21 = (bf16[32,1536]{1,0:T(8,128)(2,1)S(1)}, bf16[32,1536]{1,0:T(8,128)(2,1)S(1)}, u32[]{:S(2)}, u32[]{:S(2)}) collective-permute-start(bf16[32,1536]{1,0:T(8,128)(2,1)S(1)} %get-tuple-element.20), channel_id=1, source_target_pairs={{4,0},{8,4},{12,8},{16,12},{20,16},{24,20},{28,24},{5,1},{9,5},{13... | collective-permute-start | bytes 294920 | tf_op jit(solution)/shard_map/ppermute | solution.py:21
  250.3 6.5 %collective-permute-start.20 = (bf16[32,1536]{1,0:T(8,128)(2,1)S(1)}, bf16[32,1536]{1,0:T(8,128)(2,1)S(1)}, u32[]{:S(2)}, u32[]{:S(2)}) collective-permute-start(bf16[32,1536]{1,0:T(8,128)(2,1)S(1)} %get-tuple-element.19), channel_id=1, source_target_pairs={{0,4},{4,8},{8,12},{12,16},{16,20},{20,24},{24,28},{1,5},{5,9},{9,... | collective-permute-start | bytes 294920 | tf_op jit(solution)/shard_map/ppermute | solution.py:20
  257.4 7.1 %collective-permute-start.23 = (bf16[384,192]{0,1:T(8,128)(2,1)S(1)}, bf16[384,192]{0,1:T(8,128)(2,1)S(1)}, u32[]{:S(2)}, u32[]{:S(2)}) collective-permute-start(bf16[384,192]{0,1:T(8,128)(2,1)S(1)} %fusion.228), channel_id=1, source_target_pairs={{0,2},{1,3},{2,0},{3,1},{4,6},{5,7},{6,4},{7,5},{8,10},{9,11},{10,... | collective-permute-start | bytes 442376 | tf_op jit(solution)/shard_map/ppermute | solution.py:13
  258.6 6.8 %collective-permute-start.24 = (bf16[384,192]{0,1:T(8,128)(2,1)S(1)}, bf16[384,192]{0,1:T(8,128)(2,1)S(1)}, u32[]{:S(2)}, u32[]{:S(2)}) collective-permute-start(bf16[384,192]{0,1:T(8,128)(2,1)S(1)} %fusion.228), channel_id=1, source_target_pairs={{0,3},{1,0},{2,1},{3,2},{4,7},{5,4},{6,5},{7,6},{8,11},{9,8},{10,9... | collective-permute-start | bytes 442376 | tf_op jit(solution)/shard_map/ppermute | solution.py:13
  259.7 11.3 %collective-permute-start.22 = (bf16[384,192]{0,1:T(8,128)(2,1)S(1)}, bf16[384,192]{0,1:T(8,128)(2,1)S(1)}, u32[]{:S(2)}, u32[]{:S(2)}) collective-permute-start(bf16[384,192]{0,1:T(8,128)(2,1)S(1)} %fusion.228), channel_id=1, source_target_pairs={{0,1},{1,2},{2,3},{3,0},{4,5},{5,6},{6,7},{7,4},{8,9},{9,10},{10,1... | collective-permute-start | bytes 442376 | tf_op jit(solution)/shard_map/ppermute | solution.py:13
  271.8 7.3 %collective-permute-start.26 = (bf16[64,1536]{1,0:T(8,128)(2,1)S(1)}, bf16[64,1536]{1,0:T(8,128)(2,1)S(1)}, u32[]{:S(2)}, u32[]{:S(2)}) collective-permute-start(bf16[64,1536]{1,0:T(8,128)(2,1)S(1)} %get-tuple-element.18), channel_id=1, source_target_pairs={{4,0},{8,4},{12,8},{16,12},{20,16},{24,20},{28,24},{5,1},{9,5},{13... | collective-permute-start | bytes 589832 | tf_op jit(solution)/shard_map/ppermute | solution.py:21
  273.1 6.6 %collective-permute-start.25 = (bf16[64,1536]{1,0:T(8,128)(2,1)S(1)}, bf16[64,1536]{1,0:T(8,128)(2,1)S(1)}, u32[]{:S(2)}, u32[]{:S(2)}) collective-permute-start(bf16[64,1536]{1,0:T(8,128)(2,1)S(1)} %get-tuple-element.17), channel_id=1, source_target_pairs={{0,4},{4,8},{8,12},{12,16},{16,20},{20,24},{24,28},{1,5},{5,9},{9,... | collective-permute-start | bytes 589832 | tf_op jit(solution)/shard_map/ppermute | solution.py:20
  280.4 6.2 %collective-permute-start.28 = (bf16[384,192]{0,1:T(8,128)(2,1)S(1)}, bf16[384,192]{0,1:T(8,128)(2,1)S(1)}, u32[]{:S(2)}, u32[]{:S(2)}) collective-permute-start(bf16[384,192]{0,1:T(8,128)(2,1)S(1)} %fusion.240), channel_id=1, source_target_pairs={{0,2},{1,3},{2,0},{3,1},{4,6},{5,7},{6,4},{7,5},{8,10},{9,11},{10,... | collective-permute-start | bytes 442376 | tf_op jit(solution)/shard_map/ppermute | solution.py:13
  281.3 7.2 %collective-permute-start.29 = (bf16[384,192]{0,1:T(8,128)(2,1)S(1)}, bf16[384,192]{0,1:T(8,128)(2,1)S(1)}, u32[]{:S(2)}, u32[]{:S(2)}) collective-permute-start(bf16[384,192]{0,1:T(8,128)(2,1)S(1)} %fusion.240), channel_id=1, source_target_pairs={{0,3},{1,0},{2,1},{3,2},{4,7},{5,4},{6,5},{7,6},{8,11},{9,8},{10,9... | collective-permute-start | bytes 442376 | tf_op jit(solution)/shard_map/ppermute | solution.py:13
  282.6 7.8 %collective-permute-start.27 = (bf16[384,192]{0,1:T(8,128)(2,1)S(1)}, bf16[384,192]{0,1:T(8,128)(2,1)S(1)}, u32[]{:S(2)}, u32[]{:S(2)}) collective-permute-start(bf16[384,192]{0,1:T(8,128)(2,1)S(1)} %fusion.240), channel_id=1, source_target_pairs={{0,1},{1,2},{2,3},{3,0},{4,5},{5,6},{6,7},{7,4},{8,9},{9,10},{10,1... | collective-permute-start | bytes 442376 | tf_op jit(solution)/shard_map/ppermute | solution.py:13
  299.6 24.6 %all-to-all-start = ((bf16[8,8,1024]{2,1,0:T(8,128)(2,1)}), bf16[8,8,1024]{2,1,0:T(8,128)(2,1)S(1)}, u32[]{:S(2)}, u32[]{:S(2)}) async-start(bf16[8,8,1024]{2,1,0:T(8,128)(2,1)} %fusion.61), calls=%async_computation | async-start | bytes 262144 | tf_op jit(solution)/shard_map/all_to_all | solution.py:111
  (24 other events, 762.1 us)
Sparse Core Ops, SparseCore 0:
  9.6 44.1 all-gather.10
  55.7 39.3 all-gather.12
  96.9 38.9 all-gather.16
  137.6 39.0 all-gather.14

commit v2 on v1

v2 whole, which is shorter than its diff:
```python
import jax
import jax.numpy as jnp
from jax import lax
from jax.sharding import PartitionSpec as P

RESIDUAL_BLOCKS = 6
BASE_DILATION = 2
BLOCKS_PER_LOAD = 2
HALO_GROUPS = ((0, 1, 2, 3), (4,), (5,))
DIGIT = 128


def dilation(block):
    return BASE_DILATION * 2**block


def after(cells, *earlier):
    return lax.optimization_barrier((cells,) + earlier)[0]


def from_others(cells):
    count = lax.axis_size("trk")
    return [cells] + [
        lax.ppermute(cells, "trk", [(i, (i + k) % count) for i in range(count)])
        for k in range(1, count)
    ]


def halo(cells, width):
    count = lax.axis_size("seq")
    head = cells[:width]
    tail = cells[cells.shape[0] - width :]
    above = lax.ppermute(tail, "seq", [(i, i + 1) for i in range(count - 1)])
    below = lax.ppermute(head, "seq", [(i + 1, i) for i in range(count - 1)])
    return above, below


def contract_last(rows, kernel):
    return lax.dot_general(
        rows, kernel, (((1,), (1,)), ((), ())), preferred_element_type=jnp.float32
    )


def group_size(rows, count):
    size = 1
    for g in range(1, count + 1):
        if count % g == 0 and rows % (16 * g) == 0:
            size = g
    return size


def exon_digits(exon_bins, channels):
    digits = jnp.concatenate([exon_bins >> 7, exon_bins & (DIGIT - 1)], axis=1)
    genes, width = digits.shape
    return jnp.pad(
        digits.astype(jnp.bfloat16), ((0, -genes % 16), (0, channels - width))
    )


def exon_lists(rows, genes, entries):
    digits = rows[:, :genes, : 2 * entries].astype(jnp.int32)
    lists = digits[:, :, :entries] * DIGIT + digits[:, :, entries:]
    return lists.reshape(-1, entries)


def exon_onehot(gene_block, first_bin, width_now):
    exon_matches = (
        gene_block[:, :, None] - first_bin == jnp.arange(width_now, dtype=jnp.int32)[None, None, :]
    )
    return jnp.sum(exon_matches.astype(jnp.float32), axis=1).astype(jnp.bfloat16)


def shards(
    trunk_input, conv_in, conv_bias, conv_out, projection_bias, head_weight, head_bias, exon_bins
):
    quarters = lax.axis_size("trk")
    place = lax.axis_index("trk")
    count = lax.axis_size("seq")
    lane = lax.axis_index("seq")
    bin_rows, channels_here = trunk_input.shape
    blocks, hidden, channels = conv_out.shape
    genes_here, entries = exon_bins.shape

    load_rows = BLOCKS_PER_LOAD * hidden
    size = group_size(load_rows, count)
    share = load_rows // size
    per_block = hidden // share
    groups = [[g * size + i for i in range(size)] for g in range(count // size)]
    mine = lax.rem(lane, size)
    packed = size == count and 2 * entries <= channels

    def column(load):
        first = load * BLOCKS_PER_LOAD
        flat = conv_out[first : first + BLOCKS_PER_LOAD].reshape(load_rows, channels)
        return lax.dynamic_slice_in_dim(flat, mine * share, share, 0)

    def gather(parts):
        return lax.all_gather(
            jnp.concatenate(parts, axis=0), "seq", axis=0, tiled=False, axis_index_groups=groups
        )

    start_width = sum(dilation(b) for b in HALO_GROUPS[0])
    above, below = halo(trunk_input, start_width)
    loads = []
    first_column = from_others(column(0))
    loads.append(gather(first_column))

    own = jnp.concatenate(
        [above, trunk_input, below, jnp.pad(projection_bias, ((0, -blocks % 4), (0, 0)))], axis=0
    )
    own = after(own, *first_column)
    quarter_cells = from_others(own)
    whole = jnp.zeros((own.shape[0], channels), own.dtype)
    for k in range(quarters):
        owner = lax.rem(place - k + quarters, quarters)
        whole = lax.dynamic_update_slice_in_dim(
            whole, quarter_cells[k], owner * channels_here, 1
        )
    wide = bin_rows + 2 * start_width
    trunk = whole[:wide]
    biases = whole[wide : wide + blocks]
    second_column = from_others(after(column(1), *quarter_cells))
    loads.append(gather(second_column))

    for group in HALO_GROUPS:
        reach = sum(dilation(b) for b in group)
        if group is not HALO_GROUPS[0]:
            above, below = halo(trunk, reach)
            trunk = jnp.concatenate([above, trunk, below], axis=0)
        for block in group:
            step = dilation(block)
            reach -= step
            rows = bin_rows + 2 * reach
            inner = conv_bias[block].astype(jnp.float32)
            for tap in range(3):
                inner = inner + contract_last(
                    trunk[tap * step : tap * step + rows], conv_in[block, tap]
                )
            activation = jax.nn.gelu(inner, approximate=True).astype(jnp.bfloat16)
            others = from_others(activation)
            if block == 0:
                last = column(2)
                third_column = from_others(after(last, *others))
                tail = [exon_digits(exon_bins, channels)] if packed else []
                loads.append(gather(third_column + tail))
            load = loads[block // BLOCKS_PER_LOAD]
            first = (block % BLOCKS_PER_LOAD) * per_block
            total = trunk[step : step + rows].astype(jnp.float32) + biases[block].astype(
                jnp.float32
            )
            for k in range(quarters):
                weight = load[first : first + per_block, k * share : (k + 1) * share]
                total = total + jnp.dot(
                    others[k],
                    weight.reshape(hidden, channels),
                    preferred_element_type=jnp.float32,
                )
            if reach > 0:
                bins = lane * bin_rows - reach + jnp.arange(rows, dtype=jnp.int32)
                inside = (bins >= 0) & (bins < count * bin_rows)
                total = jnp.where(inside[:, None], total, 0.0)
            trunk = total.astype(jnp.bfloat16)

    logits = jnp.dot(trunk, head_weight, preferred_element_type=jnp.float32)
    coverage = jax.nn.softplus(logits + head_bias.astype(jnp.float32)).astype(jnp.bfloat16)
    if packed:
        gene_lists = exon_lists(loads[-1][:, quarters * share :], genes_here, entries)
    else:
        gene_lists = lax.all_gather(exon_bins, "seq", axis=0, tiled=True)
    onehot = exon_onehot(gene_lists, lane * bin_rows, bin_rows)
    partial = jnp.dot(onehot, coverage, preferred_element_type=jnp.float32).astype(jnp.bfloat16)
    parts = lax.all_to_all(
        partial.reshape(count, genes_here, partial.shape[1]), "seq", 0, 0, tiled=False
    )
    gene_sum = jnp.sum(parts.astype(jnp.float32), axis=0)
    counts = jnp.sum((exon_bins >= 0).astype(jnp.float32), axis=1)
    gene_cov = gene_sum / counts[:, None]
    return (coverage, gene_cov)


def solution(mesh):
    in_specs = (
        P("seq", "trk"),
        P(None, None, "trk", None),
        P(None, "trk"),
        P(None, "trk", None),
        P(None, "trk"),
        P(None, "trk"),
        P("trk"),
        P("seq", None),
    )
    out_specs = (P("seq", "trk"), P("seq", "trk"))
    return jax.shard_map(shards, mesh=mesh, in_specs=in_specs, out_specs=out_specs, check_vma=False)
```

time: 333 us -> 296 us (0.89); the launches traced: 331 us -> 291 us
  blocking collectives: 81.8 us -> 0 us
  waiting for transfers between devices: 89.3 us -> 121 us
  matrix products: 46.5 us -> 62.4 us
  starting transfers between devices: 71.5 us -> 61.8 us
  other arithmetic: 2.65 us -> 9.77 us
  local copies, waits for them, and re-layouts: 25.1 us -> 21 us
    all_gather x5 -> x0, blocking collectives: 81.8 us -> none  [the longest x3 59.6 us: spread_projection(): column = lax.all_gather(part, 'trk', axis=0, tiled=False)]
    ppermute x18 -> x30, waiting for transfers between devices: 45.2 us -> 115 us  [from_others(): lax.ppermute(cells, 'trk', [(i, (i + k) % count) for i in range(count)])]
    all_gather x4 -> x3, waiting for transfers between devices: 37.2 us -> 0.02 us  [gather(): lax.all_gather(jnp.concatenate(parts, axis=0), 'seq', axis=0, tiled=False...]
    ppermute x18 -> x30, starting transfers between devices: 21 us -> 40.5 us  [from_others(): lax.ppermute(cells, 'trk', [(i, (i + k) % count) for i in range(count)])]
    ppermute x6 -> x3, starting transfers between devices: 23.5 us -> 9.1 us  [halo(): above = lax.ppermute(tail, 'seq', [(i, i + 1) for i in range(count - 1)])]
    dot_general x18, matrix products: 18.7 us -> 31.1 us  [contract_last(): lax.dot_general(rows, kernel, (((1,), (1,)), ((), ())), preferred_element...]
    all_to_all x1, starting transfers between devices: 19.1 us -> 8.2 us  [shards(): lax.all_to_all(partial.reshape(count, genes_here, partial.shape[1]), 'seq...]
    ppermute x6 -> x3, starting transfers between devices: 7.75 us -> 3.86 us  [halo(): below = lax.ppermute(head, 'seq', [(i + 1, i) for i in range(count - 1)])]
  transfers between devices with their start and end apart: 35 -> 40, of which waited for: 19 -> 24; matrix products, arithmetic and copies ran while one was open for 15% -> 24% of each run, Pallas kernels for 0% -> 0%
where the time goes in v2:
time: 296 us; the launch traced here: 291 us
  waiting for transfers between devices  121 us (41%)
  matrix products  62.4 us (21%)
  starting transfers between devices  61.8 us (21%)
  local copies, waits for them, and re-layouts  21 us (7%)
  between operations  14.6 us (5%)
  other arithmetic  9.77 us (3%)
    ppermute x30, waiting for transfers between devices, from_others(): lax.ppermute(cells, 'trk', [(i, (i + k) % count) for i in range(count)])  115 us
    ppermute x30, starting transfers between devices, from_others(): lax.ppermute(cells, 'trk', [(i, (i + k) % count) for i in range(count)])  40.5 us
    dot_general x18, matrix products, contract_last(): lax.dot_general(rows, kernel, (((1,), (1,)), ((), ())), preferred_element...  31.1 us
    dot_general x23, matrix products, shards(): jnp.dot(others[k], weight.reshape(hidden, channels), preferred_element_ty...  22.1 us
    ppermute x3, starting transfers between devices, halo(): above = lax.ppermute(tail, 'seq', [(i, i + 1) for i in range(count - 1)])  9.1 us
    slice x3, local copies, waits for them, and re-layouts, shards(): weight = load[first:first + per_block, k * share:(k + 1) * share]  8.69 us
    all_to_all x1, starting transfers between devices, shards(): lax.all_to_all(partial.reshape(count, genes_here, partial.shape[1]), 'seq...  8.2 us
    dot_general x1, matrix products, shards(): logits = jnp.dot(trunk, head_weight, preferred_element_type=jnp.float32)  7.11 us
  transfers between devices with their start and end apart: 40, of which 24 were waited for; matrix products, arithmetic and copies ran while one was open for 24% of the time, Pallas kernels for 0%

profile of v2, /device:TPU:8, one launch (start us, length us, event | category | flops | bytes accessed | tf_op | source)
XLA Modules:
  0.0 290.6 jit_solution(3678972044672930395)
XLA Ops:
  7.2 4.0 %fusion.249 = (bf16[2,192,1536]{2,1,0:T(8,128)(2,1)}, bf16[2,192,1536]{2,1,0:T(8,128)(2,1)}, bf16[2,192,1536]{2,1,0:T(8,128)(2,1)}) fusion(bf16[6,192,1536]{2,1,0:T(8,128)(2,1)} %param.11), kind=kLoop, calls=%fused_computation.248 | loop fusion | bytes 7077888 | tf_op jit(solution)/shard_map/slice | solution.py:94
  16.8 7.5 %collective-permute-done.2 = bf16[48,1536]{1,0:T(8,128)(2,1)S(1)} collective-permute-done((bf16[48,1536]{1,0:T(8,128)(2,1)S(1)}, bf16[48,1536]{1,0:T(8,128)(2,1)S(1)}, u32[]{:S(2)}, u32[]{:S(2)}) %collective-permute-start.2) | collective-permute-done | bytes 147488 | tf_op jit(solution)/shard_map/ppermute | solution.py:24
  31.1 3.0 %collective-permute-start = (bf16[30,384]{1,0:T(8,128)(2,1)S(1)}, bf16[30,384]{1,0:T(8,128)(2,1)S(1)}, u32[]{:S(2)}, u32[]{:S(2)}) collective-permute-start(bf16[30,384]{1,0:T(8,128)(2,1)S(1)} %get-tuple-element.45), channel_id=1, source_target_pairs={{0,4},{4,8},{8,12},{12,16},{16,20},{20,24},{24,28},{1,5},{5,9},{9,... | collective-permute-start | bytes 69128 | tf_op jit(solution)/shard_map/ppermute | solution.py:33
  40.7 6.2 %collective-permute-done.5 = bf16[452,384]{1,0:T(8,128)(2,1)S(1)} collective-permute-done((bf16[452,384]{1,0:T(8,128)(2,1)S(1)}, bf16[452,384]{1,0:T(8,128)(2,1)S(1)}, u32[]{:S(2)}, u32[]{:S(2)}) %collective-permute-start.5) | collective-permute-done | bytes 347168 | tf_op jit(solution)/shard_map/ppermute | solution.py:24
  46.9 19.7 %collective-permute-done.6 = bf16[452,384]{1,0:T(8,128)(2,1)S(1)} collective-permute-done((bf16[452,384]{1,0:T(8,128)(2,1)S(1)}, bf16[452,384]{1,0:T(8,128)(2,1)S(1)}, u32[]{:S(2)}, u32[]{:S(2)}) %collective-permute-start.6) | collective-permute-done | bytes 347168 | tf_op jit(solution)/shard_map/ppermute | solution.py:24
  66.6 2.8 collective-permute-done.7
  70.4 2.6 collective-permute-start.14
  73.0 9.4 %collective-permute-done.16 = bf16[48,1536]{1,0:T(8,128)(2,1)S(1)} collective-permute-done((bf16[48,1536]{1,0:T(8,128)(2,1)S(1)}, bf16[48,1536]{1,0:T(8,128)(2,1)S(1)}, u32[]{:S(2)}, u32[]{:S(2)}) %collective-permute-start.16) | collective-permute-done | bytes 147488 | tf_op jit(solution)/shard_map/ppermute | solution.py:24
  93.9 3.4 %collective-permute-start.8 = (bf16[440,192]{0,1:T(8,128)(2,1)S(1)}, bf16[440,192]{0,1:T(8,128)(2,1)S(1)}, u32[]{:S(2)}, u32[]{:S(2)}) collective-permute-start(bf16[440,192]{0,1:T(8,128)(2,1)S(1)} %fusion.139), channel_id=1, source_target_pairs={{0,1},{1,2},{2,3},{3,0},{4,5},{5,6},{6,7},{7,4},{8,9},{9,10},{10,1... | collective-permute-start | bytes 506888 | tf_op jit(solution)/shard_map/ppermute | solution.py:24
  99.2 3.1 %collective-permute-done.9 = bf16[440,192]{0,1:T(8,128)(2,1)S(1)} collective-permute-done((bf16[440,192]{0,1:T(8,128)(2,1)S(1)}, bf16[440,192]{0,1:T(8,128)(2,1)S(1)}, u32[]{:S(2)}, u32[]{:S(2)}) %collective-permute-start.9) | collective-permute-done | bytes 168992 | tf_op jit(solution)/shard_map/ppermute | solution.py:24
  102.3 7.4 %collective-permute-done.8 = bf16[440,192]{0,1:T(8,128)(2,1)S(1)} collective-permute-done((bf16[440,192]{0,1:T(8,128)(2,1)S(1)}, bf16[440,192]{0,1:T(8,128)(2,1)S(1)}, u32[]{:S(2)}, u32[]{:S(2)}) %collective-permute-start.8) | collective-permute-done | bytes 168992 | tf_op jit(solution)/shard_map/ppermute | solution.py:24
  109.7 3.0 %collective-permute-done.10 = bf16[440,192]{0,1:T(8,128)(2,1)S(1)} collective-permute-done((bf16[440,192]{0,1:T(8,128)(2,1)S(1)}, bf16[440,192]{0,1:T(8,128)(2,1)S(1)}, u32[]{:S(2)}, u32[]{:S(2)}) %collective-permute-start.10) | collective-permute-done | bytes 168992 | tf_op jit(solution)/shard_map/ppermute | solution.py:24
  115.4 4.0 %collective-permute-done.25 = bf16[48,1536]{1,0:T(8,128)(2,1)S(1)} collective-permute-done((bf16[48,1536]{1,0:T(8,128)(2,1)S(1)}, bf16[48,1536]{1,0:T(8,128)(2,1)S(1)}, u32[]{:S(2)}, u32[]{:S(2)}) %collective-permute-start.25) | collective-permute-done | bytes 147488 | tf_op jit(solution)/shard_map/ppermute | solution.py:24
  120.1 5.8 %collective-permute-done.26 = bf16[48,1536]{1,0:T(8,128)(2,1)S(1)} collective-permute-done((bf16[48,1536]{1,0:T(8,128)(2,1)S(1)}, bf16[48,1536]{1,0:T(8,128)(2,1)S(1)}, u32[]{:S(2)}, u32[]{:S(2)}) %collective-permute-start.26) | collective-permute-done | bytes 147488 | tf_op jit(solution)/shard_map/ppermute | solution.py:24
  128.0 2.6 fusion.248
  139.6 3.5 %collective-permute-start.12 = (bf16[432,192]{0,1:T(8,128)(2,1)S(1)}, bf16[432,192]{0,1:T(8,128)(2,1)S(1)}, u32[]{:S(2)}, u32[]{:S(2)}) collective-permute-start(bf16[432,192]{0,1:T(8,128)(2,1)S(1)} %fusion.155), channel_id=1, source_target_pairs={{0,2},{1,3},{2,0},{3,1},{4,6},{5,7},{6,4},{7,5},{8,10},{9,11},{10,... | collective-permute-start | bytes 497672 | tf_op jit(solution)/shard_map/ppermute | solution.py:24
  143.1 2.8 collective-permute-start.11
  147.7 8.7 %collective-permute-done.12 = bf16[432,192]{0,1:T(8,128)(2,1)S(1)} collective-permute-done((bf16[432,192]{0,1:T(8,128)(2,1)S(1)}, bf16[432,192]{0,1:T(8,128)(2,1)S(1)}, u32[]{:S(2)}, u32[]{:S(2)}) %collective-permute-start.12) | collective-permute-done | bytes 165920 | tf_op jit(solution)/shard_map/ppermute | solution.py:24
  156.9 2.7 collective-permute-done.11
  167.3 2.6 collective-permute-start.18
  169.9 2.6 fusion.247
  173.0 9.7 %collective-permute-done.19 = bf16[416,192]{0,1:T(8,128)(2,1)} collective-permute-done((bf16[416,192]{0,1:T(8,128)(2,1)S(1)}, bf16[416,192]{0,1:T(8,128)(2,1)}, u32[]{:S(2)}, u32[]{:S(2)}) %collective-permute-start.19) | collective-permute-done | bytes 159776 | tf_op jit(solution)/shard_map/ppermute | solution.py:24
  196.4 8.5 %collective-permute-done.22 = bf16[384,192]{0,1:T(8,128)(2,1)S(1)} collective-permute-done((bf16[384,192]{0,1:T(8,128)(2,1)S(1)}, bf16[384,192]{0,1:T(8,128)(2,1)S(1)}, u32[]{:S(2)}, u32[]{:S(2)}) %collective-permute-start.22) | collective-permute-done | bytes 147488 | tf_op jit(solution)/shard_map/ppermute | solution.py:24
  209.7 3.0 %collective-permute-start.23 = (bf16[32,1536]{1,0:T(8,128)(2,1)S(1)}, bf16[32,1536]{1,0:T(8,128)(2,1)S(1)}, u32[]{:S(2)}, u32[]{:S(2)}) collective-permute-start(bf16[32,1536]{1,0:T(8,128)(2,1)S(1)} %get-tuple-element.43), channel_id=1, source_target_pairs={{0,4},{4,8},{8,12},{12,16},{16,20},{20,24},{24,28},{1,5},{5,9},{9,... | collective-permute-start | bytes 294920 | tf_op jit(solution)/shard_map/ppermute | solution.py:33
  220.2 3.4 %fusion.246 = (bf16[4,48,1536]{2,1,0:T(8,128)(2,1)S(1)}, bf16[4,48,1536]{2,1,0:T(8,128)(2,1)S(1)}, bf16[4,48,1536]{2,1,0:T(8,128)(2,1)S(1)}, bf16[4,48,1536]{2,1...) fusion(bf16[8,208,1536]{2,1,0:T(8,128)(2,1)} %bitcast.173), kind=kLoop, calls=%fused_computation.245 | loop fusion | bytes 9437184 | tf_op jit(solution)/shard_map/slice | solution.py:152
  225.7 2.9 collective-permute-done.29
  229.1 2.7 collective-permute-done.28
  237.6 3.0 %collective-permute-start.31 = (bf16[64,1536]{1,0:T(8,128)(2,1)S(1)}, bf16[64,1536]{1,0:T(8,128)(2,1)S(1)}, u32[]{:S(2)}, u32[]{:S(2)}) collective-permute-start(bf16[64,1536]{1,0:T(8,128)(2,1)S(1)} %get-tuple-element.41), channel_id=1, source_target_pairs={{0,4},{4,8},{8,12},{12,16},{16,20},{20,24},{24,28},{1,5},{5,9},{9,... | collective-permute-start | bytes 589832 | tf_op jit(solution)/shard_map/ppermute | solution.py:33
  253.1 4.0 %collective-permute-done.34 = bf16[384,192]{0,1:T(8,128)(2,1)S(1)} collective-permute-done((bf16[384,192]{0,1:T(8,128)(2,1)S(1)}, bf16[384,192]{0,1:T(8,128)(2,1)S(1)}, u32[]{:S(2)}, u32[]{:S(2)}) %collective-permute-start.34) | collective-permute-done | bytes 147488 | tf_op jit(solution)/shard_map/ppermute | solution.py:24
  260.4 7.1 %fusion.17 = bf16[384,1024]{1,0:T(8,128)(2,1)} fusion(bf16[1536,1024]{1,0:T(8,128)(2,1)S(1)} %copy-done, f32[1024]{0:T(1024)S(1)} %copy-done.26, f32[384,1536]{1,0:T(8,128)} %fusion.269, f32[384,1536]{1,0:T(8,128)} %fusion.268, bf16[384,192]{0,1:T(8,128)(2,1)S(1)} %collective-permute-done.33, bf16[192,1536]{1,0:T(8,128)(2,1)} %bitcast.200, ...), kind=kOutput, calls=%fused_computation.27 | convolution fusion | flops 1441726464 | bytes 12937216 | tf_op jit(solution)/shard_map/dot_general | solution.py:164
  269.6 8.2 %all-to-all-start = ((bf16[8,8,1024]{2,1,0:T(8,128)(2,1)}), bf16[8,8,1024]{2,1,0:T(8,128)(2,1)S(1)}, u32[]{:S(2)}, u32[]{:S(2)}) async-start(bf16[8,8,1024]{2,1,0:T(8,128)(2,1)} %fusion.85), calls=%async_computation | async-start | bytes 262144 | tf_op jit(solution)/shard_map/all_to_all | solution.py:172
  277.9 5.4 %all-to-all-done = bf16[8,8,1024]{2,1,0:T(8,128)(2,1)S(1)} async-done(((bf16[8,8,1024]{2,1,0:T(8,128)(2,1)}), bf16[8,8,1024]{2,1,0:T(8,128)(2,1)S(1)}, u32[]{:S(2)}, u32[]{:S(2)}) %all-to-all-start) | async-done | bytes 131104 | tf_op jit(solution)/shard_map/all_to_all | solution.py:172
  (202 shorter events, 110.5 us)
Async XLA Ops:
  7.2 120.8 %all-gather.7.cloned.1.call-start = ((), (), s32[]{:S(2)}) async-start(), calls=%async_computation.1 | async-start | bytes 5308416 | tf_op jit(solution)/shard_map/all_gather | solution.py:98
  12.2 12.2 %collective-permute-start.2 = (bf16[48,1536]{1,0:T(8,128)(2,1)S(1)}, bf16[48,1536]{1,0:T(8,128)(2,1)S(1)}, u32[]{:S(2)}, u32[]{:S(2)}) collective-permute-start(bf16[48,1536]{1,0:T(8,128)(2,1)S(1)} %constant_dynamic-slice_fusion.2), channel_id=1, source_target_pairs={{0,1},{1,2},{2,3},{3,0},{4,5},{5,6},{6,7},{7,4},{8,9},{9,10},{10,1... | collective-permute-start | bytes 442376 | tf_op jit(solution)/shard_map/ppermute | solution.py:24
  13.8 12.6 %collective-permute-start.3 = (bf16[48,1536]{1,0:T(8,128)(2,1)S(1)}, bf16[48,1536]{1,0:T(8,128)(2,1)S(1)}, u32[]{:S(2)}, u32[]{:S(2)}) collective-permute-start(bf16[48,1536]{1,0:T(8,128)(2,1)S(1)} %constant_dynamic-slice_fusion.2), channel_id=1, source_target_pairs={{0,2},{1,3},{2,0},{3,1},{4,6},{5,7},{6,4},{7,5},{8,10},{9,11},{10,... | collective-permute-start | bytes 442376 | tf_op jit(solution)/shard_map/ppermute | solution.py:24
  14.9 13.2 %collective-permute-start.4 = (bf16[48,1536]{1,0:T(8,128)(2,1)S(1)}, bf16[48,1536]{1,0:T(8,128)(2,1)S(1)}, u32[]{:S(2)}, u32[]{:S(2)}) collective-permute-start(bf16[48,1536]{1,0:T(8,128)(2,1)S(1)} %constant_dynamic-slice_fusion.2), channel_id=1, source_target_pairs={{0,3},{1,0},{2,1},{3,2},{4,7},{5,4},{6,5},{7,6},{8,11},{9,8},{10,9... | collective-permute-start | bytes 442376 | tf_op jit(solution)/shard_map/ppermute | solution.py:24
  29.0 140.9 %all-gather.9.cloned.1.call-start = ((), (), s32[]{:S(2)}) async-start(), calls=%async_computation.2 | async-start | bytes 5308416 | tf_op jit(solution)/shard_map/all_gather | solution.py:98
  36.1 10.8 %collective-permute-start.5 = (bf16[452,384]{1,0:T(8,128)(2,1)S(1)}, bf16[452,384]{1,0:T(8,128)(2,1)S(1)}, u32[]{:S(2)}, u32[]{:S(2)}) collective-permute-start(bf16[452,384]{1,0:T(8,128)(2,1)S(1)} %fusion.176), channel_id=1, source_target_pairs={{0,1},{1,2},{2,3},{3,0},{4,5},{5,6},{6,7},{7,4},{8,9},{9,10},{10,1... | collective-permute-start | bytes 1041416 | tf_op jit(solution)/shard_map/ppermute | solution.py:24
  36.1 30.5 %collective-permute-start.6 = (bf16[452,384]{1,0:T(8,128)(2,1)S(1)}, bf16[452,384]{1,0:T(8,128)(2,1)S(1)}, u32[]{:S(2)}, u32[]{:S(2)}) collective-permute-start(bf16[452,384]{1,0:T(8,128)(2,1)S(1)} %fusion.176), channel_id=1, source_target_pairs={{0,2},{1,3},{2,0},{3,1},{4,6},{5,7},{6,4},{7,5},{8,10},{9,11},{10,... | collective-permute-start | bytes 1041416 | tf_op jit(solution)/shard_map/ppermute | solution.py:24
  37.8 31.5 %collective-permute-start.7 = (bf16[452,384]{1,0:T(8,128)(2,1)S(1)}, bf16[452,384]{1,0:T(8,128)(2,1)S(1)}, u32[]{:S(2)}, u32[]{:S(2)}) collective-permute-start(bf16[452,384]{1,0:T(8,128)(2,1)S(1)} %fusion.176), channel_id=1, source_target_pairs={{0,3},{1,0},{2,1},{3,2},{4,7},{5,4},{6,5},{7,6},{8,11},{9,8},{10,9... | collective-permute-start | bytes 1041416 | tf_op jit(solution)/shard_map/ppermute | solution.py:24
  69.3 13.0 %collective-permute-start.16 = (bf16[48,1536]{1,0:T(8,128)(2,1)S(1)}, bf16[48,1536]{1,0:T(8,128)(2,1)S(1)}, u32[]{:S(2)}, u32[]{:S(2)}) collective-permute-start(bf16[48,1536]{1,0:T(8,128)(2,1)S(1)} %constant_dynamic-slice_fusion.1), channel_id=1, source_target_pairs={{0,3},{1,0},{2,1},{3,2},{4,7},{5,4},{6,5},{7,6},{8,11},{9,8},{10,9... | collective-permute-start | bytes 442376 | tf_op jit(solution)/shard_map/ppermute | solution.py:24
  69.4 13.0 %collective-permute-start.15 = (bf16[48,1536]{1,0:T(8,128)(2,1)S(1)}, bf16[48,1536]{1,0:T(8,128)(2,1)S(1)}, u32[]{:S(2)}, u32[]{:S(2)}) collective-permute-start(bf16[48,1536]{1,0:T(8,128)(2,1)S(1)} %constant_dynamic-slice_fusion.1), channel_id=1, source_target_pairs={{0,2},{1,3},{2,0},{3,1},{4,6},{5,7},{6,4},{7,5},{8,10},{9,11},{10,... | collective-permute-start | bytes 442376 | tf_op jit(solution)/shard_map/ppermute | solution.py:24
  70.4 13.0 %collective-permute-start.14 = (bf16[48,1536]{1,0:T(8,128)(2,1)S(1)}, bf16[48,1536]{1,0:T(8,128)(2,1)S(1)}, u32[]{:S(2)}, u32[]{:S(2)}) collective-permute-start(bf16[48,1536]{1,0:T(8,128)(2,1)S(1)} %constant_dynamic-slice_fusion.1), channel_id=1, source_target_pairs={{0,1},{1,2},{2,3},{3,0},{4,5},{5,6},{6,7},{7,4},{8,9},{9,10},{10,1... | collective-permute-start | bytes 442376 | tf_op jit(solution)/shard_map/ppermute | solution.py:24
  84.2 136.0 %all-gather.11.cloned.1.call-start = ((), (), s32[]{:S(2)}) async-start(), calls=%async_computation.3 | async-start | bytes 5750784 | tf_op jit(solution)/shard_map/all_gather | solution.py:98
  92.9 9.4 %collective-permute-start.9 = (bf16[440,192]{0,1:T(8,128)(2,1)S(1)}, bf16[440,192]{0,1:T(8,128)(2,1)S(1)}, u32[]{:S(2)}, u32[]{:S(2)}) collective-permute-start(bf16[440,192]{0,1:T(8,128)(2,1)S(1)} %fusion.139), channel_id=1, source_target_pairs={{0,2},{1,3},{2,0},{3,1},{4,6},{5,7},{6,4},{7,5},{8,10},{9,11},{10,... | collective-permute-start | bytes 506888 | tf_op jit(solution)/shard_map/ppermute | solution.py:24
  93.9 15.8 %collective-permute-start.8 = (bf16[440,192]{0,1:T(8,128)(2,1)S(1)}, bf16[440,192]{0,1:T(8,128)(2,1)S(1)}, u32[]{:S(2)}, u32[]{:S(2)}) collective-permute-start(bf16[440,192]{0,1:T(8,128)(2,1)S(1)} %fusion.139), channel_id=1, source_target_pairs={{0,1},{1,2},{2,3},{3,0},{4,5},{5,6},{6,7},{7,4},{8,9},{9,10},{10,1... | collective-permute-start | bytes 506888 | tf_op jit(solution)/shard_map/ppermute | solution.py:24
  97.3 15.4 %collective-permute-start.10 = (bf16[440,192]{0,1:T(8,128)(2,1)S(1)}, bf16[440,192]{0,1:T(8,128)(2,1)S(1)}, u32[]{:S(2)}, u32[]{:S(2)}) collective-permute-start(bf16[440,192]{0,1:T(8,128)(2,1)S(1)} %fusion.139), channel_id=1, source_target_pairs={{0,3},{1,0},{2,1},{3,2},{4,7},{5,4},{6,5},{7,6},{8,11},{9,8},{10,9... | collective-permute-start | bytes 506888 | tf_op jit(solution)/shard_map/ppermute | solution.py:24
  112.7 13.2 %collective-permute-start.26 = (bf16[48,1536]{1,0:T(8,128)(2,1)S(1)}, bf16[48,1536]{1,0:T(8,128)(2,1)S(1)}, u32[]{:S(2)}, u32[]{:S(2)}) collective-permute-start(bf16[48,1536]{1,0:T(8,128)(2,1)S(1)} %constant_dynamic-slice_fusion), channel_id=1, source_target_pairs={{0,2},{1,3},{2,0},{3,1},{4,6},{5,7},{6,4},{7,5},{8,10},{9,11},{10,... | collective-permute-start | bytes 442376 | tf_op jit(solution)/shard_map/ppermute | solution.py:24
  113.8 12.7 %collective-permute-start.27 = (bf16[48,1536]{1,0:T(8,128)(2,1)S(1)}, bf16[48,1536]{1,0:T(8,128)(2,1)S(1)}, u32[]{:S(2)}, u32[]{:S(2)}) collective-permute-start(bf16[48,1536]{1,0:T(8,128)(2,1)S(1)} %constant_dynamic-slice_fusion), channel_id=1, source_target_pairs={{0,3},{1,0},{2,1},{3,2},{4,7},{5,4},{6,5},{7,6},{8,11},{9,8},{10,9... | collective-permute-start | bytes 442376 | tf_op jit(solution)/shard_map/ppermute | solution.py:24
  139.5 7.6 %collective-permute-start.13 = (bf16[432,192]{0,1:T(8,128)(2,1)S(1)}, bf16[432,192]{0,1:T(8,128)(2,1)S(1)}, u32[]{:S(2)}, u32[]{:S(2)}) collective-permute-start(bf16[432,192]{0,1:T(8,128)(2,1)S(1)} %fusion.155), channel_id=1, source_target_pairs={{0,3},{1,0},{2,1},{3,2},{4,7},{5,4},{6,5},{7,6},{8,11},{9,8},{10,9... | collective-permute-start | bytes 497672 | tf_op jit(solution)/shard_map/ppermute | solution.py:24
  139.6 16.8 %collective-permute-start.12 = (bf16[432,192]{0,1:T(8,128)(2,1)S(1)}, bf16[432,192]{0,1:T(8,128)(2,1)S(1)}, u32[]{:S(2)}, u32[]{:S(2)}) collective-permute-start(bf16[432,192]{0,1:T(8,128)(2,1)S(1)} %fusion.155), channel_id=1, source_target_pairs={{0,2},{1,3},{2,0},{3,1},{4,6},{5,7},{6,4},{7,5},{8,10},{9,11},{10,... | collective-permute-start | bytes 497672 | tf_op jit(solution)/shard_map/ppermute | solution.py:24
  143.1 16.5 %collective-permute-start.11 = (bf16[432,192]{0,1:T(8,128)(2,1)S(1)}, bf16[432,192]{0,1:T(8,128)(2,1)S(1)}, u32[]{:S(2)}, u32[]{:S(2)}) collective-permute-start(bf16[432,192]{0,1:T(8,128)(2,1)S(1)} %fusion.155), channel_id=1, source_target_pairs={{0,1},{1,2},{2,3},{3,0},{4,5},{5,6},{6,7},{7,4},{8,9},{9,10},{10,1... | collective-permute-start | bytes 497672 | tf_op jit(solution)/shard_map/ppermute | solution.py:24
  165.9 16.9 %collective-permute-start.19 = (bf16[416,192]{0,1:T(8,128)(2,1)S(1)}, bf16[416,192]{0,1:T(8,128)(2,1)}, u32[]{:S(2)}, u32[]{:S(2)}) collective-permute-start(bf16[416,192]{0,1:T(8,128)(2,1)S(1)} %fusion.171), channel_id=1, source_target_pairs={{0,3},{1,0},{2,1},{3,2},{4,7},{5,4},{6,5},{7,6},{8,11},{9,8},{10,9... | collective-permute-start | bytes 479240 | tf_op jit(solution)/shard_map/ppermute | solution.py:24
  167.3 17.0 %collective-permute-start.18 = (bf16[416,192]{0,1:T(8,128)(2,1)S(1)}, bf16[416,192]{0,1:T(8,128)(2,1)S(1)}, u32[]{:S(2)}, u32[]{:S(2)}) collective-permute-start(bf16[416,192]{0,1:T(8,128)(2,1)S(1)} %fusion.171), channel_id=1, source_target_pairs={{0,2},{1,3},{2,0},{3,1},{4,6},{5,7},{6,4},{7,5},{8,10},{9,11},{10,... | collective-permute-start | bytes 479240 | tf_op jit(solution)/shard_map/ppermute | solution.py:24
  169.9 14.9 %collective-permute-start.17 = (bf16[416,192]{0,1:T(8,128)(2,1)S(1)}, bf16[416,192]{0,1:T(8,128)(2,1)}, u32[]{:S(2)}, u32[]{:S(2)}) collective-permute-start(bf16[416,192]{0,1:T(8,128)(2,1)S(1)} %fusion.171), channel_id=1, source_target_pairs={{0,1},{1,2},{2,3},{3,0},{4,5},{5,6},{6,7},{7,4},{8,9},{9,10},{10,1... | collective-permute-start | bytes 479240 | tf_op jit(solution)/shard_map/ppermute | solution.py:24
  192.4 12.4 %collective-permute-start.22 = (bf16[384,192]{0,1:T(8,128)(2,1)S(1)}, bf16[384,192]{0,1:T(8,128)(2,1)S(1)}, u32[]{:S(2)}, u32[]{:S(2)}) collective-permute-start(bf16[384,192]{0,1:T(8,128)(2,1)S(1)} %fusion.188), channel_id=1, source_target_pairs={{0,3},{1,0},{2,1},{3,2},{4,7},{5,4},{6,5},{7,6},{8,11},{9,8},{10,9... | collective-permute-start | bytes 442376 | tf_op jit(solution)/shard_map/ppermute | solution.py:24
  194.3 11.0 %collective-permute-start.21 = (bf16[384,192]{0,1:T(8,128)(2,1)S(1)}, bf16[384,192]{0,1:T(8,128)(2,1)S(1)}, u32[]{:S(2)}, u32[]{:S(2)}) collective-permute-start(bf16[384,192]{0,1:T(8,128)(2,1)S(1)} %fusion.188), channel_id=1, source_target_pairs={{0,2},{1,3},{2,0},{3,1},{4,6},{5,7},{6,4},{7,5},{8,10},{9,11},{10,... | collective-permute-start | bytes 442376 | tf_op jit(solution)/shard_map/ppermute | solution.py:24
  194.4 11.5 %collective-permute-start.20 = (bf16[384,192]{0,1:T(8,128)(2,1)S(1)}, bf16[384,192]{0,1:T(8,128)(2,1)S(1)}, u32[]{:S(2)}, u32[]{:S(2)}) collective-permute-start(bf16[384,192]{0,1:T(8,128)(2,1)S(1)} %fusion.188), channel_id=1, source_target_pairs={{0,1},{1,2},{2,3},{3,0},{4,5},{5,6},{6,7},{7,4},{8,9},{9,10},{10,1... | collective-permute-start | bytes 442376 | tf_op jit(solution)/shard_map/ppermute | solution.py:24
  216.1 8.0 %collective-permute-start.30 = (bf16[384,192]{0,1:T(8,128)(2,1)S(1)}, bf16[384,192]{0,1:T(8,128)(2,1)}, u32[]{:S(2)}, u32[]{:S(2)}) collective-permute-start(bf16[384,192]{0,1:T(8,128)(2,1)S(1)} %fusion.202), channel_id=1, source_target_pairs={{0,3},{1,0},{2,1},{3,2},{4,7},{5,4},{6,5},{7,6},{8,11},{9,8},{10,9... | collective-permute-start | bytes 442376 | tf_op jit(solution)/shard_map/ppermute | solution.py:24
  218.7 9.9 %collective-permute-start.29 = (bf16[384,192]{0,1:T(8,128)(2,1)S(1)}, bf16[384,192]{0,1:T(8,128)(2,1)S(1)}, u32[]{:S(2)}, u32[]{:S(2)}) collective-permute-start(bf16[384,192]{0,1:T(8,128)(2,1)S(1)} %fusion.202), channel_id=1, source_target_pairs={{0,2},{1,3},{2,0},{3,1},{4,6},{5,7},{6,4},{7,5},{8,10},{9,11},{10,... | collective-permute-start | bytes 442376 | tf_op jit(solution)/shard_map/ppermute | solution.py:24
  219.7 12.0 %collective-permute-start.28 = (bf16[384,192]{0,1:T(8,128)(2,1)S(1)}, bf16[384,192]{0,1:T(8,128)(2,1)}, u32[]{:S(2)}, u32[]{:S(2)}) collective-permute-start(bf16[384,192]{0,1:T(8,128)(2,1)S(1)} %fusion.202), channel_id=1, source_target_pairs={{0,1},{1,2},{2,3},{3,0},{4,5},{5,6},{6,7},{7,4},{8,9},{9,10},{10,1... | collective-permute-start | bytes 442376 | tf_op jit(solution)/shard_map/ppermute | solution.py:24
  247.4 9.7 %collective-permute-start.34 = (bf16[384,192]{0,1:T(8,128)(2,1)S(1)}, bf16[384,192]{0,1:T(8,128)(2,1)S(1)}, u32[]{:S(2)}, u32[]{:S(2)}) collective-permute-start(bf16[384,192]{0,1:T(8,128)(2,1)S(1)} %fusion.214), channel_id=1, source_target_pairs={{0,2},{1,3},{2,0},{3,1},{4,6},{5,7},{6,4},{7,5},{8,10},{9,11},{10,... | collective-permute-start | bytes 442376 | tf_op jit(solution)/shard_map/ppermute | solution.py:24
  249.3 11.1 %collective-permute-start.33 = (bf16[384,192]{0,1:T(8,128)(2,1)S(1)}, bf16[384,192]{0,1:T(8,128)(2,1)S(1)}, u32[]{:S(2)}, u32[]{:S(2)}) collective-permute-start(bf16[384,192]{0,1:T(8,128)(2,1)S(1)} %fusion.214), channel_id=1, source_target_pairs={{0,1},{1,2},{2,3},{3,0},{4,5},{5,6},{6,7},{7,4},{8,9},{9,10},{10,1... | collective-permute-start | bytes 442376 | tf_op jit(solution)/shard_map/ppermute | solution.py:24
  269.6 13.7 %all-to-all-start = ((bf16[8,8,1024]{2,1,0:T(8,128)(2,1)}), bf16[8,8,1024]{2,1,0:T(8,128)(2,1)S(1)}, u32[]{:S(2)}, u32[]{:S(2)}) async-start(bf16[8,8,1024]{2,1,0:T(8,128)(2,1)} %fusion.85), calls=%async_computation | async-start | bytes 262144 | tf_op jit(solution)/shard_map/all_to_all | solution.py:172
  (44 other events, 717.2 us)
Sparse Core Ops, SparseCore 0:
  29.1 39.1 all-gather.6
  84.4 40.4 all-gather.8
  128.1 42.7 all-gather.10

commit v3 on v2

v3 whole, which is shorter than its diff:
```python
import functools
import math

import jax
import jax.numpy as jnp
from jax import lax
from jax.experimental import pallas as pl
from jax.experimental.pallas import tpu as pltpu
from jax.sharding import PartitionSpec as P

RESIDUAL_BLOCKS = 6
BASE_DILATION = 2
BLOCKS_PER_LOAD = 2
FRAMED_BLOCKS = 4
DIGIT = 128
VMEM_BYTES = 24 * 2**20


def dilation(block):
    return BASE_DILATION * 2**block


def after(cells, *earlier):
    return lax.optimization_barrier((cells,) + earlier)[0]


def after_all(cells, *earlier):
    return list(lax.optimization_barrier(tuple(cells) + earlier)[: len(cells)])


def from_others(cells):
    count = lax.axis_size("trk")
    return [cells] + [
        lax.ppermute(cells, "trk", [(i, (i + k) % count) for i in range(count)])
        for k in range(1, count)
    ]


def halo(cells, width):
    count = lax.axis_size("seq")
    head = cells[:width]
    tail = cells[cells.shape[0] - width :]
    above = lax.ppermute(tail, "seq", [(i, i + 1) for i in range(count - 1)])
    below = lax.ppermute(head, "seq", [(i + 1, i) for i in range(count - 1)])
    return above, below


def group_size(rows, count):
    size = 1
    for g in range(1, count + 1):
        if count % g == 0 and rows % (16 * g) == 0:
            size = g
    return size


def tile_of(channels):
    for width in (512, 256, 384, 128):
        if channels % width == 0:
            return width
    return channels


def dot(a, b):
    return jnp.dot(a, b, preferred_element_type=jnp.float32)


def dot_last(a, b):
    return lax.dot_general(a, b, (((1,), (1,)), ((), ())), preferred_element_type=jnp.float32)


def gelu(x):
    cubic = x + 0.044715 * (x * x * x)
    return 0.5 * x * (1.0 + jnp.tanh(math.sqrt(2.0 / math.pi) * cubic))


def gelu_of_taps(sums, bias, step, rows):
    total = sums.shape[1]
    inner = sums[1] + pltpu.roll(sums[0], step, 0) + pltpu.roll(sums[2], total - step, 0)
    margin = (total - rows) // 2
    inner = inner[margin : margin + rows] + bias.astype(jnp.float32)
    return gelu(inner).astype(jnp.bfloat16)


def first_kernel(step, own_rows, order_ref, c0, c1, c2, c3, w_ref, bias_ref, act_ref, trunk_ref, sums):
    k = pl.program_id(0)
    rows = trunk_ref.shape[0]
    for j, cell in enumerate((c0, c1, c2, c3)):

        @pl.when(k == j)
        def _():
            trunk_ref[...] = cell[:rows]

    tile = trunk_ref[...]
    for t in range(3):
        part = dot_last(tile, w_ref[0, t])
        sums[t] = jnp.where(k == 0, part, sums[t] + part)

    @pl.when(k == pl.num_programs(0) - 1)
    def _():
        act_ref[...] = gelu_of_taps(sums, bias_ref[...], step, act_ref.shape[0])


def first_conv(cells, rows, order, conv_in, bias, step):
    quarters = len(cells)
    _, _, hidden, channels = conv_in.shape
    width = cells[0].shape[1]
    full = pl.BlockSpec(cells[0].shape, lambda k, order: (0, 0))
    return pl.pallas_call(
        functools.partial(first_kernel, step, rows),
        grid_spec=pltpu.PrefetchScalarGridSpec(
            num_scalar_prefetch=1,
            grid=(quarters,),
            in_specs=[full] * quarters
            + [
                pl.BlockSpec((1, 3, hidden, width), lambda k, order: (0, 0, 0, order[k])),
                pl.BlockSpec((1, hidden), lambda k, order: (0, 0)),
            ],
            out_specs=[
                pl.BlockSpec((rows, hidden), lambda k, order: (0, 0)),
                pl.BlockSpec((rows, width), lambda k, order: (0, order[k])),
            ],
            scratch_shapes=[pltpu.VMEM((3, rows, hidden), jnp.float32)],
        ),
        out_shape=[
            jax.ShapeDtypeStruct((rows, hidden), jnp.bfloat16),
            jax.ShapeDtypeStruct((rows, channels), jnp.bfloat16),
        ],
        compiler_params=pltpu.CompilerParams(vmem_limit_bytes=VMEM_BYTES),
        cost_estimate=pl.CostEstimate(
            flops=6 * rows * hidden * channels,
            bytes_accessed=2 * (3 * hidden * channels + 2 * rows * channels),
            transcendentals=rows * hidden,
        ),
    )(order, *cells, conv_in, bias)


def project(acts, weights, trunk, bias):
    whole = jnp.concatenate([w[...].reshape(-1, w.shape[-1]) for w in weights], axis=0)
    return trunk.astype(jnp.float32) + bias.astype(jnp.float32) + dot(acts[...], whole)


def keep_acts(acts_ref, acts):
    acts_ref[...] = jnp.concatenate([a[...] for a in acts], axis=1)


def fused_kernel(
    step, edge_ref, a0, a1, a2, a3, w0, w1, w2, w3, trunk_ref, pbias_ref, w_ref, bias_ref,
    act_ref, out_ref, acts_ref, sums
):
    c = pl.program_id(0)

    @pl.when(c == 0)
    def _():
        keep_acts(acts_ref, (a0, a1, a2, a3))

    total = project(acts_ref, (w0, w1, w2, w3), trunk_ref[...], pbias_ref[...])
    row = lax.broadcasted_iota(jnp.int32, total.shape, 0)
    inside = (row >= edge_ref[0]) & (row < edge_ref[1])
    tile = jnp.where(inside, total, 0.0).astype(jnp.bfloat16)
    out_ref[...] = tile
    for t in range(3):
        part = dot_last(tile, w_ref[0, t])
        sums[t] = jnp.where(c == 0, part, sums[t] + part)

    @pl.when(c == pl.num_programs(0) - 1)
    def _():
        act_ref[...] = gelu_of_taps(sums, bias_ref[...], step, act_ref.shape[0])


def projection_specs(load, part, acts, per_block, share, width):
    specs = [pl.BlockSpec(acts[0].shape, lambda c, *_: (0, 0))] * len(acts)
    for j in range(len(acts)):
        specs.append(
            pl.BlockSpec((per_block, share, width), lambda c, *_, j=j: (part, j, c))
        )
    return specs


def fused(acts, load, part, per_block, share, trunk, pbias, conv_in, block, bias, edge, rows_out):
    rows, channels = trunk.shape
    hidden = conv_in.shape[2]
    width = tile_of(channels)
    return pl.pallas_call(
        functools.partial(fused_kernel, dilation(block)),
        grid_spec=pltpu.PrefetchScalarGridSpec(
            num_scalar_prefetch=1,
            grid=(channels // width,),
            in_specs=projection_specs(load, part, acts, per_block, share, width)
            + [
                pl.BlockSpec((rows, width), lambda c, *_: (0, c)),
                pl.BlockSpec((1, width), lambda c, *_: (0, c)),
                pl.BlockSpec((1, 3, hidden, width), lambda c, *_: (block, 0, 0, c)),
                pl.BlockSpec((1, hidden), lambda c, *_: (0, 0)),
            ],
            out_specs=[
                pl.BlockSpec((rows_out, hidden), lambda c, *_: (0, 0)),
                pl.BlockSpec((rows, width), lambda c, *_: (0, c)),
            ],
            scratch_shapes=[
                pltpu.VMEM((rows, len(acts) * hidden), jnp.bfloat16),
                pltpu.VMEM((3, rows, hidden), jnp.float32),
            ],
        ),
        out_shape=[
            jax.ShapeDtypeStruct((rows_out, hidden), jnp.bfloat16),
            jax.ShapeDtypeStruct((rows, channels), jnp.bfloat16),
        ],
        compiler_params=pltpu.CompilerParams(vmem_limit_bytes=VMEM_BYTES),
        cost_estimate=pl.CostEstimate(
            flops=14 * rows * hidden * channels,
            bytes_accessed=2 * (7 * hidden * channels + 2 * rows * channels),
            transcendentals=rows * hidden,
        ),
    )(edge, *acts, *[load] * len(acts), trunk, pbias, conv_in, bias)


def projection_kernel(margin, a0, a1, a2, a3, w0, w1, w2, w3, trunk_ref, pbias_ref, out_ref, acts_ref):
    @pl.when(pl.program_id(0) == 0)
    def _():
        keep_acts(acts_ref, (a0, a1, a2, a3))

    rows = out_ref.shape[0]
    total = project(
        acts_ref, (w0, w1, w2, w3), trunk_ref[margin : margin + rows], pbias_ref[...]
    )
    out_ref[...] = total.astype(jnp.bfloat16)


def projection(acts, load, part, per_block, share, trunk, pbias):
    frame, channels = trunk.shape
    rows, hidden = acts[0].shape
    width = tile_of(channels)
    return pl.pallas_call(
        functools.partial(projection_kernel, (frame - rows) // 2),
        grid=(channels // width,),
        in_specs=projection_specs(load, part, acts, per_block, share, width)
        + [
            pl.BlockSpec((frame, width), lambda c: (0, c)),
            pl.BlockSpec((1, width), lambda c: (0, c)),
        ],
        out_specs=pl.BlockSpec((rows, width), lambda c: (0, c)),
        scratch_shapes=[pltpu.VMEM((rows, len(acts) * hidden), jnp.bfloat16)],
        out_shape=jax.ShapeDtypeStruct((rows, channels), jnp.bfloat16),
        compiler_params=pltpu.CompilerParams(vmem_limit_bytes=VMEM_BYTES),
        cost_estimate=pl.CostEstimate(
            flops=8 * rows * hidden * channels,
            bytes_accessed=2 * (4 * hidden * channels + 2 * rows * channels),
            transcendentals=0,
        ),
    )(*acts, *[load] * len(acts), trunk, pbias)


def conv_kernel(step, above_ref, trunk_ref, below_ref, w_ref, bias_ref, act_ref, sums):
    c = pl.program_id(0)
    tile = jnp.concatenate([above_ref[...], trunk_ref[...], below_ref[...]], axis=0)
    for t in range(3):
        part = dot_last(tile, w_ref[0, t])
        sums[t] = jnp.where(c == 0, part, sums[t] + part)

    @pl.when(c == pl.num_programs(0) - 1)
    def _():
        act_ref[...] = gelu_of_taps(sums, bias_ref[...], step, act_ref.shape[0])


def conv(above, trunk, below, conv_in, block, bias):
    rows, channels = trunk.shape
    hidden = conv_in.shape[2]
    step = dilation(block)
    width = tile_of(channels)
    return pl.pallas_call(
        functools.partial(conv_kernel, step),
        grid=(channels // width,),
        in_specs=[
            pl.BlockSpec((step, width), lambda c: (0, c)),
            pl.BlockSpec((rows, width), lambda c: (0, c)),
            pl.BlockSpec((step, width), lambda c: (0, c)),
            pl.BlockSpec((1, 3, hidden, width), lambda c: (block, 0, 0, c)),
            pl.BlockSpec((1, hidden), lambda c: (0, 0)),
        ],
        out_specs=pl.BlockSpec((rows, hidden), lambda c: (0, 0)),
        scratch_shapes=[pltpu.VMEM((3, rows + 2 * step, hidden), jnp.float32)],
        out_shape=jax.ShapeDtypeStruct((rows, hidden), jnp.bfloat16),
        compiler_params=pltpu.CompilerParams(vmem_limit_bytes=VMEM_BYTES),
        cost_estimate=pl.CostEstimate(
            flops=6 * rows * hidden * channels,
            bytes_accessed=2 * (3 * hidden * channels + rows * channels),
            transcendentals=rows * hidden,
        ),
    )(above, trunk, below, conv_in, bias)


def head_kernel(
    a0, a1, a2, a3, w0, w1, w2, w3, trunk_ref, pbias_ref, head_ref, hbias_ref, onehot_ref,
    cover_ref, gene_ref, acts_ref, logits
):
    c = pl.program_id(0)

    @pl.when(c == 0)
    def _():
        keep_acts(acts_ref, (a0, a1, a2, a3))

    total = project(acts_ref, (w0, w1, w2, w3), trunk_ref[...], pbias_ref[...])
    part = dot(total.astype(jnp.bfloat16), head_ref[...])
    logits[...] = jnp.where(c == 0, part, logits[...] + part)

    @pl.when(c == pl.num_programs(0) - 1)
    def _():
        x = logits[...] + hbias_ref[...].astype(jnp.float32)
        cover = (jnp.maximum(x, 0.0) + jnp.log1p(jnp.exp(-jnp.abs(x)))).astype(jnp.bfloat16)
        cover_ref[...] = cover
        gene_ref[...] = dot(onehot_ref[...], cover).astype(jnp.bfloat16)


def head(acts, load, part, per_block, share, trunk, pbias, head_weight, head_bias, onehot):
    rows, channels = trunk.shape
    hidden = acts[0].shape[1]
    tracks = head_weight.shape[1]
    genes = onehot.shape[0]
    width = tile_of(channels)
    return pl.pallas_call(
        head_kernel,
        grid=(channels // width,),
        in_specs=projection_specs(load, part, acts, per_block, share, width)
        + [
            pl.BlockSpec((rows, width), lambda c: (0, c)),
            pl.BlockSpec((1, width), lambda c: (0, c)),
            pl.BlockSpec((width, tracks), lambda c: (c, 0)),
            pl.BlockSpec((1, tracks), lambda c: (0, 0)),
            pl.BlockSpec((genes, rows), lambda c: (0, 0)),
        ],
        out_specs=[
            pl.BlockSpec((rows, tracks), lambda c: (0, 0)),
            pl.BlockSpec((genes, tracks), lambda c: (0, 0)),
        ],
        scratch_shapes=[
            pltpu.VMEM((rows, len(acts) * hidden), jnp.bfloat16),
            pltpu.VMEM((rows, tracks), jnp.float32),
        ],
        out_shape=[
            jax.ShapeDtypeStruct((rows, tracks), jnp.bfloat16),
            jax.ShapeDtypeStruct((genes, tracks), jnp.bfloat16),
        ],
        compiler_params=pltpu.CompilerParams(vmem_limit_bytes=VMEM_BYTES),
        cost_estimate=pl.CostEstimate(
            flops=8 * rows * hidden * channels + 2 * rows * channels * tracks,
            bytes_accessed=2 * (4 * hidden * channels + rows * channels + channels * tracks),
            transcendentals=2 * rows * tracks,
        ),
    )(*acts, *[load] * len(acts), trunk, pbias, head_weight, head_bias, onehot)


def exon_digits(exon_bins, channels):
    digits = jnp.concatenate([exon_bins >> 7, exon_bins & (DIGIT - 1)], axis=1)
    genes, width = digits.shape
    return jnp.pad(digits.astype(jnp.bfloat16), ((0, -genes % 16), (0, channels - width)))


def exon_lists(rows, genes, entries):
    digits = rows[:, :genes, : 2 * entries].astype(jnp.int32)
    lists = digits[:, :, :entries] * DIGIT + digits[:, :, entries:]
    return lists.reshape(-1, entries)


def exon_onehot(gene_block, first_bin, width_now):
    exon_matches = (
        gene_block[:, :, None] - first_bin == jnp.arange(width_now, dtype=jnp.int32)[None, None, :]
    )
    return jnp.sum(exon_matches.astype(jnp.float32), axis=1).astype(jnp.bfloat16)


def shards(
    trunk_input, conv_in, conv_bias, conv_out, projection_bias, head_weight, head_bias, exon_bins
):
    quarters = lax.axis_size("trk")
    place = lax.axis_index("trk")
    count = lax.axis_size("seq")
    lane = lax.axis_index("seq")
    bin_rows, channels_here = trunk_input.shape
    blocks, hidden, channels = conv_out.shape
    genes_here, entries = exon_bins.shape

    load_rows = BLOCKS_PER_LOAD * hidden
    size = group_size(load_rows, count)
    share = load_rows // size
    per_block = hidden // share
    groups = [[g * size + i for i in range(size)] for g in range(count // size)]
    mine = lax.rem(lane, size)
    packed = size == count and 2 * entries <= channels

    def column(load):
        first = load * BLOCKS_PER_LOAD
        flat = conv_out[first : first + BLOCKS_PER_LOAD].reshape(load_rows, channels)
        return lax.dynamic_slice_in_dim(flat, mine * share, share, 0)

    def gather(parts):
        return lax.all_gather(
            jnp.concatenate(parts, axis=0), "seq", axis=0, tiled=False, axis_index_groups=groups
        )

    margin = dilation(FRAMED_BLOCKS)
    frame = bin_rows + 2 * margin
    order = lax.rem(place - jnp.arange(quarters, dtype=jnp.int32) + quarters, quarters)
    edge = jnp.stack(
        [
            jnp.where(lane == 0, margin, 0),
            jnp.where(lane == count - 1, margin + bin_rows, frame),
        ]
    ).astype(jnp.int32)

    above, below = halo(trunk_input, margin)
    first_column = from_others(column(0))
    loads = [gather(first_column)]
    own = jnp.concatenate(
        [above, trunk_input, below, jnp.pad(projection_bias, ((0, -blocks % 16), (0, 0)))], axis=0
    )
    own = after(own, *first_column)
    cells = from_others(own)
    second = from_others(after(column(1), *cells))

    act, trunk = first_conv(cells, frame, order, conv_in, conv_bias[:1], dilation(0))
    biases = jnp.zeros((blocks, channels), jnp.bfloat16)
    for k in range(quarters):
        biases = lax.dynamic_update_slice_in_dim(
            biases, cells[k][frame : frame + blocks], order[k] * channels_here, 1
        )

    onehot = None
    for block in range(RESIDUAL_BLOCKS):
        others = from_others(act)
        if block == 0:
            loads.append(gather(after_all(second, *others)))
            third = from_others(after(column(2), *others))
        if block == 1:
            tail = [exon_digits(exon_bins, channels)] if packed else []
            loads.append(gather(after_all(third, *others) + tail))
        if block == 4:
            if packed:
                gene_lists = exon_lists(loads[2][:, quarters * share :], genes_here, entries)
            else:
                gene_lists = lax.all_gather(exon_bins, "seq", axis=0, tiled=True)
            onehot = exon_onehot(gene_lists, lane * bin_rows, bin_rows)
        load = loads[block // BLOCKS_PER_LOAD]
        part = block % BLOCKS_PER_LOAD
        where = (load, part, per_block, share, trunk, biases[block : block + 1])
        later = block + 1
        if later < FRAMED_BLOCKS:
            rows_out = frame if later < FRAMED_BLOCKS - 1 else bin_rows
            act, trunk = fused(
                others, *where, conv_in, later, conv_bias[later : later + 1], edge, rows_out
            )
        elif later < RESIDUAL_BLOCKS:
            trunk = projection(others, *where)
            above, below = halo(trunk, dilation(later))
            act = conv(above, trunk, below, conv_in, later, conv_bias[later : later + 1])
        else:
            coverage, partial = head(others, *where, head_weight, head_bias[None, :], onehot)

    parts = lax.all_to_all(
        partial.reshape(count, genes_here, partial.shape[1]), "seq", 0, 0, tiled=False
    )
    gene_sum = jnp.sum(parts.astype(jnp.float32), axis=0)
    counts = jnp.sum((exon_bins >= 0).astype(jnp.float32), axis=1)
    gene_cov = gene_sum / counts[:, None]
    return (coverage, gene_cov)


def solution(mesh):
    in_specs = (
        P("seq", "trk"),
        P(None, None, "trk", None),
        P(None, "trk"),
        P(None, "trk", None),
        P(None, "trk"),
        P(None, "trk"),
        P("trk"),
        P("seq", None),
    )
    out_specs = (P("seq", "trk"), P("seq", "trk"))
    return jax.shard_map(shards, mesh=mesh, in_specs=in_specs, out_specs=out_specs, check_vma=False)
```

time: 296 us -> 316 us (1.068); the launches traced: 291 us -> 315 us
  matrix products: 62.4 us -> 0 us
  waiting for transfers between devices: 121 us -> 158 us
  Pallas kernels: 0 us -> 31 us
  local copies, waits for them, and re-layouts: 21 us -> 48.8 us
  starting transfers between devices: 61.8 us -> 55.3 us
  other arithmetic: 9.77 us -> 4.67 us
    dot_general x43 -> x0, matrix products: 62.4 us -> none  [the longest x18 31.1 us: contract_last(): lax.dot_general(rows, kernel, (((1,), (1,)), ((), ())), preferred_element...]
    unnamed x76 -> x74, local copies, waits for them, and re-layouts: 4.39 us -> 43.7 us
    pallas_call x0 -> x9, Pallas kernels: none -> 31 us  [the longest x3 13.8 us: fused(): pl.pallas_call(functools.partial(fused_kernel, dilation(block)), grid_spe...]
    ppermute x30, waiting for transfers between devices: 115 us -> 144 us  [from_others(): lax.ppermute(cells, 'trk', [(i, (i + k) % count) for i in range(count)])]
    ppermute x3, waiting for transfers between devices: 0.01 us -> 7.98 us  [halo(): below = lax.ppermute(head, 'seq', [(i + 1, i) for i in range(count - 1)])]
    slice x3 -> x5, local copies, waits for them, and re-layouts: 8.69 us -> 0.75 us  [the longest x1 0.67 us: shards(): order[k] * channels_here]
    ppermute x30, starting transfers between devices: 40.5 us -> 36.8 us  [from_others(): lax.ppermute(cells, 'trk', [(i, (i + k) % count) for i in range(count)])]
  transfers between devices with their start and end apart: 40 -> 40, of which waited for: 24 -> 27; matrix products, arithmetic and copies ran while one was open for 24% -> 2% of each run, Pallas kernels for 0% -> 7%
where the time goes in v3:
time: 316 us; the launch traced here: 315 us
  waiting for transfers between devices  158 us (50%)
  starting transfers between devices  55.3 us (18%)
  local copies, waits for them, and re-layouts  48.8 us (15%)
  Pallas kernels  31 us (10%)
  between operations  16.8 us (5%)
  other arithmetic  4.67 us (1%)
    ppermute x30, waiting for transfers between devices, from_others(): lax.ppermute(cells, 'trk', [(i, (i + k) % count) for i in range(count)])  144 us
    unnamed x74, local copies, waits for them, and re-layouts  43.7 us
    ppermute x30, starting transfers between devices, from_others(): lax.ppermute(cells, 'trk', [(i, (i + k) % count) for i in range(count)])  36.8 us
    pallas_call x3, Pallas kernels, fused(): pl.pallas_call(functools.partial(fused_kernel, dilation(block)), grid_spe...  13.8 us
    ppermute x3, waiting for transfers between devices, halo(): below = lax.ppermute(head, 'seq', [(i + 1, i) for i in range(count - 1)])  7.98 us
    all_to_all x1, starting transfers between devices, shards(): lax.all_to_all(partial.reshape(count, genes_here, partial.shape[1]), 'seq...  7.3 us
    ppermute x3, starting transfers between devices, halo(): above = lax.ppermute(tail, 'seq', [(i, i + 1) for i in range(count - 1)])  6.99 us
  transfers between devices with their start and end apart: 40, of which 27 were waited for; matrix products, arithmetic and copies ran while one was open for 2% of the time, Pallas kernels for 7%

profile of v3, /device:TPU:8, one launch (start us, length us, event | category | flops | bytes accessed | tf_op | source)
XLA Modules:
  0.0 315.0 jit_solution(17388572290778523693)
XLA Ops:
  7.2 3.3 %fusion.12 = (bf16[2,192,1536]{2,1,0:T(8,128)(2,1)}, bf16[2,192,1536]{2,1,0:T(8,128)(2,1)S(1)}, bf16[2,192,1536]{2,1,0:T(8,128)(2,1)S(1)}) fusion(bf16[6,192,1536]{2,1,0:T(8,128)(2,1)} %param.11), kind=kLoop, calls=%fused_computation.41 | loop fusion | bytes 7077888 | tf_op jit(solution)/shard_map/slice | solution.py:392
  15.2 7.5 %collective-permute-done.2 = bf16[48,1536]{1,0:T(8,128)(2,1)S(1)} collective-permute-done((bf16[48,1536]{1,0:T(8,128)(2,1)S(1)}, bf16[48,1536]{1,0:T(8,128)(2,1)S(1)}, u32[]{:S(2)}, u32[]{:S(2)}) %collective-permute-start.2) | collective-permute-done | bytes 147488 | tf_op jit(solution)/shard_map/ppermute | solution.py:34
  28.7 3.0 collective-permute-start
  36.4 7.2 %collective-permute-done.5.c1 = bf16[464,384]{1,0:T(8,128)(2,1)S(1)} collective-permute-done((bf16[464,384]{1,0:T(8,128)(2,1)S(1)}, bf16[464,384]{1,0:T(8,128)(2,1)S(1)}, u32[]{:S(2)}, u32[]{:S(2)}) %collective-permute-start.5) | collective-permute-done | bytes 356384 | tf_op jit(solution)/shard_map/ppermute | solution.py:34
  43.6 20.1 %collective-permute-done.6.c2 = bf16[464,384]{1,0:T(8,128)(2,1)S(1)} collective-permute-done((bf16[464,384]{1,0:T(8,128)(2,1)S(1)}, bf16[464,384]{1,0:T(8,128)(2,1)S(1)}, u32[]{:S(2)}, u32[]{:S(2)}) %collective-permute-start.6) | collective-permute-done | bytes 356384 | tf_op jit(solution)/shard_map/ppermute | solution.py:34
  66.5 4.0 %copy-done = bf16[6,3,192,1536]{3,2,1,0:T(8,128)(2,1)S(1)} copy-done((bf16[6,3,192,1536]{3,2,1,0:T(8,128)(2,1)S(1)}, bf16[6,3,192,1536]{3,2,1,0:T(8,128)(2,1)}, u32[]{:S(2)}) %copy-start) | copy-done | bytes 10616856
  70.5 3.6 %shard_map.95 = (bf16[448,192]{1,0:T(8,128)(2,1)S(1)}, bf16[448,1536]{1,0:T(8,128)(2,1)S(1)}) custom-call(s32[4]{0:T(128)S(1)} %compare_select_fusion.order_ref, bf16[464,384]{1,0:T(8,128)(2,1)S(1)} %fusion.1.c0, bf16[464,384]{1,0:T(8,128)(2,1)S(1)} %collective-permute-done.5.c1, bf16[464,384]{1,0:T(8,128)(2,1)S(1)} %collective-permute-done.6.c2, ...), custom_call_target="tpu_custom_call" | custom-call | flops 792723456 | bytes 4521984 | tf_op jit(solution)/shard_map/pallas_call | solution.py:108
  75.3 3.2 %collective-permute-start.9 = (bf16[448,192]{1,0:T(8,128)(2,1)S(1)}, bf16[448,192]{1,0:T(8,128)(2,1)S(1)}, u32[]{:S(2)}, u32[]{:S(2)}) collective-permute-start(bf16[448,192]{1,0:T(8,128)(2,1)S(1)} %get-tuple-element.24.a0), channel_id=1, source_target_pairs={{0,2},{1,3},{2,0},{3,1},{4,6},{5,7},{6,4},{7,5},{8,10},{9,11},{10,... | collective-permute-start | bytes 516104 | tf_op jit(solution)/shard_map/ppermute | solution.py:34
  79.1 2.8 collective-permute-start.19
  82.0 22.8 %collective-permute-done.18 = bf16[48,1536]{1,0:T(8,128)(2,1)S(1)} collective-permute-done((bf16[48,1536]{1,0:T(8,128)(2,1)S(1)}, bf16[48,1536]{1,0:T(8,128)(2,1)S(1)}, u32[]{:S(2)}, u32[]{:S(2)}) %collective-permute-start.18) | collective-permute-done | bytes 147488 | tf_op jit(solution)/shard_map/ppermute | solution.py:34
  117.0 4.4 %copy-done.1 = bf16[6,3,192,1536]{3,2,1,0:T(8,128)(2,1)S(1)} copy-done((bf16[6,3,192,1536]{3,2,1,0:T(8,128)(2,1)S(1)}, bf16[6,3,192,1536]{3,2,1,0:T(8,128)(2,1)}, u32[]{:S(2)}) %copy-start.1) | copy-done | bytes 10616856
  126.6 4.7 %shard_map.96 = (bf16[448,192]{1,0:T(8,128)(2,1)S(1)}, bf16[448,1536]{1,0:T(8,128)(2,1)S(1)}) custom-call(s32[2]{0:T(128)S(1)} %pad_add_fusion.edge_ref, bf16[448,192]{1,0:T(8,128)(2,1)S(1)} %get-tuple-element.24.a0, bf16[448,192]{1,0:T(8,128)(2,1)S(1)} %copy-done.11, bf16[448,192]{1,0:T(8,128)(2,1)S(1)} %copy-done.13, bf16[448,192]{1,0:T(8,128)(2,1)S(1)} %copy-done.15, ...), custom_call_target="tpu_custom_call" | custom-call | flops 1849688064 | bytes 6881280 | tf_op jit(solution)/shard_map/pallas_call | solution.py:183
  136.2 11.5 %collective-permute-done.11.a1 = bf16[448,192]{1,0:T(8,128)(2,1)S(1)} collective-permute-done((bf16[448,192]{1,0:T(8,128)(2,1)S(1)}, bf16[448,192]{1,0:T(8,128)(2,1)S(1)}, u32[]{:S(2)}, u32[]{:S(2)}) %collective-permute-start.11) | collective-permute-done | bytes 172064 | tf_op jit(solution)/shard_map/ppermute | solution.py:34
  147.6 2.9 collective-permute-done.12.a2
  157.9 4.0 %copy-done.2 = bf16[6,3,192,1536]{3,2,1,0:T(8,128)(2,1)S(1)} copy-done((bf16[6,3,192,1536]{3,2,1,0:T(8,128)(2,1)S(1)}, bf16[6,3,192,1536]{3,2,1,0:T(8,128)(2,1)}, u32[]{:S(2)}) %copy-start.2) | copy-done | bytes 10616856
  166.2 4.6 %shard_map.97 = (bf16[448,192]{1,0:T(8,128)(2,1)S(1)}, bf16[448,1536]{1,0:T(8,128)(2,1)S(1)}) custom-call(s32[2]{0:T(128)S(1)} %pad_add_fusion.edge_ref, bf16[448,192]{1,0:T(8,128)(2,1)S(1)} %copy-done.17, bf16[448,192]{1,0:T(8,128)(2,1)S(1)} %collective-permute-done.11.a1, bf16[448,192]{1,0:T(8,128)(2,1)S(1)} %copy-done.19, ...), custom_call_target="tpu_custom_call" | custom-call | flops 1849688064 | bytes 6881280 | tf_op jit(solution)/shard_map/pallas_call | solution.py:183
  174.6 4.8 %collective-permute-done.14.a1 = bf16[448,192]{1,0:T(8,128)(2,1)S(1)} collective-permute-done((bf16[448,192]{1,0:T(8,128)(2,1)S(1)}, bf16[448,192]{1,0:T(8,128)(2,1)S(1)}, u32[]{:S(2)}, u32[]{:S(2)}) %collective-permute-start.14) | collective-permute-done | bytes 172064 | tf_op jit(solution)/shard_map/ppermute | solution.py:34
  179.4 10.8 %collective-permute-done.15.a2 = bf16[448,192]{1,0:T(8,128)(2,1)S(1)} collective-permute-done((bf16[448,192]{1,0:T(8,128)(2,1)S(1)}, bf16[448,192]{1,0:T(8,128)(2,1)S(1)}, u32[]{:S(2)}, u32[]{:S(2)}) %collective-permute-start.15) | collective-permute-done | bytes 172064 | tf_op jit(solution)/shard_map/ppermute | solution.py:34
  190.6 4.1 %copy-done.3 = bf16[6,3,192,1536]{3,2,1,0:T(8,128)(2,1)S(1)} copy-done((bf16[6,3,192,1536]{3,2,1,0:T(8,128)(2,1)S(1)}, bf16[6,3,192,1536]{3,2,1,0:T(8,128)(2,1)}, u32[]{:S(2)}) %copy-start.3) | copy-done | bytes 10616856
  198.1 4.6 %shard_map.98 = (bf16[384,192]{1,0:T(8,128)(2,1)S(1)}, bf16[448,1536]{1,0:T(8,128)(2,1)S(1)}) custom-call(s32[2]{0:T(128)S(1)} %pad_add_fusion.edge_ref, bf16[448,192]{1,0:T(8,128)(2,1)S(1)} %copy-done.23, bf16[448,192]{1,0:T(8,128)(2,1)S(1)} %collective-permute-done.14.a1, bf16[448,192]{1,0:T(8,128)(2,1)S(1)} %collective-permute-done.15.a2, ...), custom_call_target="tpu_custom_call" | custom-call | flops 1849688064 | bytes 6881280 | tf_op jit(solution)/shard_map/pallas_call | solution.py:183
  202.7 3.0 collective-permute-start.21
  207.7 2.8 collective-permute-done.20.a1
  210.5 9.6 %collective-permute-done.21.a2 = bf16[384,192]{1,0:T(8,128)(2,1)S(1)} collective-permute-done((bf16[384,192]{1,0:T(8,128)(2,1)S(1)}, bf16[384,192]{1,0:T(8,128)(2,1)S(1)}, u32[]{:S(2)}, u32[]{:S(2)}) %collective-permute-start.21) | collective-permute-done | bytes 147488 | tf_op jit(solution)/shard_map/ppermute | solution.py:34
  227.4 3.6 %collective-permute-done.24.below_ref = bf16[32,1536]{1,0:T(8,128)(2,1)S(1)} collective-permute-done((bf16[32,1536]{1,0:T(8,128)(2,1)S(1)}, bf16[32,1536]{1,0:T(8,128)(2,1)S(1)}, u32[]{:S(2)}, u32[]{:S(2)}) %collective-permute-start.24) | collective-permute-done | bytes 98336 | tf_op jit(solution)/shard_map/ppermute | solution.py:44
  231.0 4.0 %copy-done.4 = bf16[6,3,192,1536]{3,2,1,0:T(8,128)(2,1)S(1)} copy-done((bf16[6,3,192,1536]{3,2,1,0:T(8,128)(2,1)S(1)}, bf16[6,3,192,1536]{3,2,1,0:T(8,128)(2,1)}, u32[]{:S(2)}) %copy-start.4) | copy-done | bytes 10616856
  242.8 3.2 %collective-permute-done.26.a2 = bf16[384,192]{1,0:T(8,128)(2,1)S(1)} collective-permute-done((bf16[384,192]{1,0:T(8,128)(2,1)S(1)}, bf16[384,192]{1,0:T(8,128)(2,1)S(1)}, u32[]{:S(2)}, u32[]{:S(2)}) %collective-permute-start.26) | collective-permute-done | bytes 147488 | tf_op jit(solution)/shard_map/ppermute | solution.py:34
  246.0 10.6 %collective-permute-done.27.a3 = bf16[384,192]{1,0:T(8,128)(2,1)S(1)} collective-permute-done((bf16[384,192]{1,0:T(8,128)(2,1)S(1)}, bf16[384,192]{1,0:T(8,128)(2,1)S(1)}, u32[]{:S(2)}, u32[]{:S(2)}) %collective-permute-start.27) | collective-permute-done | bytes 147488 | tf_op jit(solution)/shard_map/ppermute | solution.py:34
  264.9 4.3 %collective-permute-done.32.below_ref = bf16[64,1536]{1,0:T(8,128)(2,1)S(1)} collective-permute-done((bf16[64,1536]{1,0:T(8,128)(2,1)S(1)}, bf16[64,1536]{1,0:T(8,128)(2,1)S(1)}, u32[]{:S(2)}, u32[]{:S(2)}) %collective-permute-start.32) | collective-permute-done | bytes 196640 | tf_op jit(solution)/shard_map/ppermute | solution.py:44
  280.0 9.6 %collective-permute-done.35.a3 = bf16[384,192]{1,0:T(8,128)(2,1)S(1)} collective-permute-done((bf16[384,192]{1,0:T(8,128)(2,1)S(1)}, bf16[384,192]{1,0:T(8,128)(2,1)S(1)}, u32[]{:S(2)}, u32[]{:S(2)}) %collective-permute-start.35) | collective-permute-done | bytes 147488 | tf_op jit(solution)/shard_map/ppermute | solution.py:34
  289.5 5.3 %shard_map.103 = (bf16[384,1024]{1,0:T(8,128)(2,1)}, bf16[64,1024]{1,0:T(8,128)(2,1)}) custom-call(bf16[384,192]{1,0:T(8,128)(2,1)S(1)} %shard_map.102.a0, bf16[384,192]{1,0:T(8,128)(2,1)S(1)} %collective-permute-done.33.a1, bf16[384,192]{1,0:T(8,128)(2,1)S(1)} %collective-permute-done.34.a2, bf16[384,192]{1,0:T(8,128)(2,1)S(1)} %collective-permute-done.35.a3, ...), custom_call_target="tpu_custom_call" | custom-call | flops 2113929216 | bytes 6684672 | tf_op jit(solution)/shard_map/pallas_call | solution.py:320
  294.9 7.3 %all-to-all-start = ((bf16[8,8,1024]{2,1,0:T(8,128)(2,1)}), bf16[8,8,1024]{2,1,0:T(8,128)(2,1)S(1)}, u32[]{:S(2)}, u32[]{:S(2)}) async-start(bf16[8,8,1024]{2,1,0:T(8,128)(2,1)} %bitcast.13), calls=%async_computation | async-start | bytes 262144 | tf_op jit(solution)/shard_map/all_to_all | solution.py:458
  302.3 5.4 %all-to-all-done = bf16[8,8,1024]{2,1,0:T(8,128)(2,1)S(1)} async-done(((bf16[8,8,1024]{2,1,0:T(8,128)(2,1)}), bf16[8,8,1024]{2,1,0:T(8,128)(2,1)S(1)}, u32[]{:S(2)}, u32[]{:S(2)}) %all-to-all-start) | async-done | bytes 131104 | tf_op jit(solution)/shard_map/all_to_all | solution.py:458
  (165 shorter events, 95.5 us)
Async XLA Ops:
  7.2 109.8 %all-gather.7.cloned.1.call-start = ((), (), s32[]{:S(2)}) async-start(), calls=%async_computation.1 | async-start | bytes 5308416 | tf_op jit(solution)/shard_map/all_gather | solution.py:396
  10.5 12.2 %collective-permute-start.2 = (bf16[48,1536]{1,0:T(8,128)(2,1)S(1)}, bf16[48,1536]{1,0:T(8,128)(2,1)S(1)}, u32[]{:S(2)}, u32[]{:S(2)}) collective-permute-start(bf16[48,1536]{1,0:T(8,128)(2,1)S(1)} %constant_dynamic-slice_fusion.2), channel_id=1, source_target_pairs={{0,1},{1,2},{2,3},{3,0},{4,5},{5,6},{6,7},{7,4},{8,9},{9,10},{10,1... | collective-permute-start | bytes 442376 | tf_op jit(solution)/shard_map/ppermute | solution.py:34
  12.1 12.6 %collective-permute-start.3 = (bf16[48,1536]{1,0:T(8,128)(2,1)S(1)}, bf16[48,1536]{1,0:T(8,128)(2,1)S(1)}, u32[]{:S(2)}, u32[]{:S(2)}) collective-permute-start(bf16[48,1536]{1,0:T(8,128)(2,1)S(1)} %constant_dynamic-slice_fusion.2), channel_id=1, source_target_pairs={{0,2},{1,3},{2,0},{3,1},{4,6},{5,7},{6,4},{7,5},{8,10},{9,11},{10,... | collective-permute-start | bytes 442376 | tf_op jit(solution)/shard_map/ppermute | solution.py:34
  13.2 13.2 %collective-permute-start.4 = (bf16[48,1536]{1,0:T(8,128)(2,1)S(1)}, bf16[48,1536]{1,0:T(8,128)(2,1)S(1)}, u32[]{:S(2)}, u32[]{:S(2)}) collective-permute-start(bf16[48,1536]{1,0:T(8,128)(2,1)S(1)} %constant_dynamic-slice_fusion.2), channel_id=1, source_target_pairs={{0,3},{1,0},{2,1},{3,2},{4,7},{5,4},{6,5},{7,6},{8,11},{9,8},{10,9... | collective-permute-start | bytes 442376 | tf_op jit(solution)/shard_map/ppermute | solution.py:34
  27.4 163.2 %all-gather.9.cloned.1.call-start = ((), (), s32[]{:S(2)}) async-start(), calls=%async_computation.2 | async-start | bytes 5308416 | tf_op jit(solution)/shard_map/all_gather | solution.py:396
  32.7 11.0 %collective-permute-start.5 = (bf16[464,384]{1,0:T(8,128)(2,1)S(1)}, bf16[464,384]{1,0:T(8,128)(2,1)S(1)}, u32[]{:S(2)}, u32[]{:S(2)}) collective-permute-start(bf16[464,384]{1,0:T(8,128)(2,1)S(1)} %fusion.1.c0), channel_id=1, source_target_pairs={{0,1},{1,2},{2,3},{3,0},{4,5},{5,6},{6,7},{7,4},{8,9},{9,10},{10,1... | collective-permute-start | bytes 1069064 | tf_op jit(solution)/shard_map/ppermute | solution.py:34
  32.7 31.0 %collective-permute-start.6 = (bf16[464,384]{1,0:T(8,128)(2,1)S(1)}, bf16[464,384]{1,0:T(8,128)(2,1)S(1)}, u32[]{:S(2)}, u32[]{:S(2)}) collective-permute-start(bf16[464,384]{1,0:T(8,128)(2,1)S(1)} %fusion.1.c0), channel_id=1, source_target_pairs={{0,2},{1,3},{2,0},{3,1},{4,6},{5,7},{6,4},{7,5},{8,10},{9,11},{10,... | collective-permute-start | bytes 1069064 | tf_op jit(solution)/shard_map/ppermute | solution.py:34
  34.4 32.0 %collective-permute-start.7 = (bf16[464,384]{1,0:T(8,128)(2,1)S(1)}, bf16[464,384]{1,0:T(8,128)(2,1)S(1)}, u32[]{:S(2)}, u32[]{:S(2)}) collective-permute-start(bf16[464,384]{1,0:T(8,128)(2,1)S(1)} %fusion.1.c0), channel_id=1, source_target_pairs={{0,3},{1,0},{2,1},{3,2},{4,7},{5,4},{6,5},{7,6},{8,11},{9,8},{10,9... | collective-permute-start | bytes 1069064 | tf_op jit(solution)/shard_map/ppermute | solution.py:34
  66.5 12.7 %collective-permute-start.17 = (bf16[48,1536]{1,0:T(8,128)(2,1)S(1)}, bf16[48,1536]{1,0:T(8,128)(2,1)S(1)}, u32[]{:S(2)}, u32[]{:S(2)}) collective-permute-start(bf16[48,1536]{1,0:T(8,128)(2,1)S(1)} %constant_dynamic-slice_fusion.1), channel_id=1, source_target_pairs={{0,1},{1,2},{2,3},{3,0},{4,5},{5,6},{6,7},{7,4},{8,9},{9,10},{10,1... | collective-permute-start | bytes 442376 | tf_op jit(solution)/shard_map/ppermute | solution.py:34
  74.1 33.2 %collective-permute-start.8 = (bf16[448,192]{1,0:T(8,128)(2,1)S(1)}, bf16[448,192]{1,0:T(8,128)(2,1)S(1)}, u32[]{:S(2)}, u32[]{:S(2)}) collective-permute-start(bf16[448,192]{1,0:T(8,128)(2,1)S(1)} %get-tuple-element.24.a0), channel_id=1, source_target_pairs={{0,1},{1,2},{2,3},{3,0},{4,5},{5,6},{6,7},{7,4},{8,9},{9,10},{10,1... | collective-permute-start | bytes 516104 | tf_op jit(solution)/shard_map/ppermute | solution.py:34
  75.3 32.0 %collective-permute-start.9 = (bf16[448,192]{1,0:T(8,128)(2,1)S(1)}, bf16[448,192]{1,0:T(8,128)(2,1)S(1)}, u32[]{:S(2)}, u32[]{:S(2)}) collective-permute-start(bf16[448,192]{1,0:T(8,128)(2,1)S(1)} %get-tuple-element.24.a0), channel_id=1, source_target_pairs={{0,2},{1,3},{2,0},{3,1},{4,6},{5,7},{6,4},{7,5},{8,10},{9,11},{10,... | collective-permute-start | bytes 516104 | tf_op jit(solution)/shard_map/ppermute | solution.py:34
  78.5 29.6 %collective-permute-start.10 = (bf16[448,192]{1,0:T(8,128)(2,1)S(1)}, bf16[448,192]{1,0:T(8,128)(2,1)S(1)}, u32[]{:S(2)}, u32[]{:S(2)}) collective-permute-start(bf16[448,192]{1,0:T(8,128)(2,1)S(1)} %get-tuple-element.24.a0), channel_id=1, source_target_pairs={{0,3},{1,0},{2,1},{3,2},{4,7},{5,4},{6,5},{7,6},{8,11},{9,8},{10,9... | collective-permute-start | bytes 516104 | tf_op jit(solution)/shard_map/ppermute | solution.py:34
  78.5 26.3 %collective-permute-start.18 = (bf16[48,1536]{1,0:T(8,128)(2,1)S(1)}, bf16[48,1536]{1,0:T(8,128)(2,1)S(1)}, u32[]{:S(2)}, u32[]{:S(2)}) collective-permute-start(bf16[48,1536]{1,0:T(8,128)(2,1)S(1)} %constant_dynamic-slice_fusion.1), channel_id=1, source_target_pairs={{0,2},{1,3},{2,0},{3,1},{4,6},{5,7},{6,4},{7,5},{8,10},{9,11},{10,... | collective-permute-start | bytes 442376 | tf_op jit(solution)/shard_map/ppermute | solution.py:34
  79.1 28.2 %collective-permute-start.19 = (bf16[48,1536]{1,0:T(8,128)(2,1)S(1)}, bf16[48,1536]{1,0:T(8,128)(2,1)S(1)}, u32[]{:S(2)}, u32[]{:S(2)}) collective-permute-start(bf16[48,1536]{1,0:T(8,128)(2,1)S(1)} %constant_dynamic-slice_fusion.1), channel_id=1, source_target_pairs={{0,3},{1,0},{2,1},{3,2},{4,7},{5,4},{6,5},{7,6},{8,11},{9,8},{10,9... | collective-permute-start | bytes 442376 | tf_op jit(solution)/shard_map/ppermute | solution.py:34
  109.7 130.7 %all-gather.11.cloned.1.call-start = ((), (), s32[]{:S(2)}) async-start(), calls=%async_computation.3 | async-start | bytes 5750784 | tf_op jit(solution)/shard_map/all_gather | solution.py:396
  114.0 20.9 %collective-permute-start.28 = (bf16[48,1536]{1,0:T(8,128)(2,1)S(1)}, bf16[48,1536]{1,0:T(8,128)(2,1)}, u32[]{:S(2)}, u32[]{:S(2)}) collective-permute-start(bf16[48,1536]{1,0:T(8,128)(2,1)S(1)} %constant_dynamic-slice_fusion), channel_id=1, source_target_pairs={{0,1},{1,2},{2,3},{3,0},{4,5},{5,6},{6,7},{7,4},{8,9},{9,10},{10,1... | collective-permute-start | bytes 442376 | tf_op jit(solution)/shard_map/ppermute | solution.py:34
  114.1 22.0 %collective-permute-start.29 = (bf16[48,1536]{1,0:T(8,128)(2,1)S(1)}, bf16[48,1536]{1,0:T(8,128)(2,1)}, u32[]{:S(2)}, u32[]{:S(2)}) collective-permute-start(bf16[48,1536]{1,0:T(8,128)(2,1)S(1)} %constant_dynamic-slice_fusion), channel_id=1, source_target_pairs={{0,2},{1,3},{2,0},{3,1},{4,6},{5,7},{6,4},{7,5},{8,10},{9,11},{10,... | collective-permute-start | bytes 442376 | tf_op jit(solution)/shard_map/ppermute | solution.py:34
  115.7 20.4 %collective-permute-start.30 = (bf16[48,1536]{1,0:T(8,128)(2,1)S(1)}, bf16[48,1536]{1,0:T(8,128)(2,1)}, u32[]{:S(2)}, u32[]{:S(2)}) collective-permute-start(bf16[48,1536]{1,0:T(8,128)(2,1)S(1)} %constant_dynamic-slice_fusion), channel_id=1, source_target_pairs={{0,3},{1,0},{2,1},{3,2},{4,7},{5,4},{6,5},{7,6},{8,11},{9,8},{10,9... | collective-permute-start | bytes 442376 | tf_op jit(solution)/shard_map/ppermute | solution.py:34
  131.2 16.4 %collective-permute-start.11 = (bf16[448,192]{1,0:T(8,128)(2,1)S(1)}, bf16[448,192]{1,0:T(8,128)(2,1)S(1)}, u32[]{:S(2)}, u32[]{:S(2)}) collective-permute-start(bf16[448,192]{1,0:T(8,128)(2,1)S(1)} %get-tuple-element.26.a0), channel_id=1, source_target_pairs={{0,1},{1,2},{2,3},{3,0},{4,5},{5,6},{6,7},{7,4},{8,9},{9,10},{10,1... | collective-permute-start | bytes 516104 | tf_op jit(solution)/shard_map/ppermute | solution.py:34
  132.2 18.3 %collective-permute-start.12 = (bf16[448,192]{1,0:T(8,128)(2,1)S(1)}, bf16[448,192]{1,0:T(8,128)(2,1)S(1)}, u32[]{:S(2)}, u32[]{:S(2)}) collective-permute-start(bf16[448,192]{1,0:T(8,128)(2,1)S(1)} %get-tuple-element.26.a0), channel_id=1, source_target_pairs={{0,2},{1,3},{2,0},{3,1},{4,6},{5,7},{6,4},{7,5},{8,10},{9,11},{10,... | collective-permute-start | bytes 516104 | tf_op jit(solution)/shard_map/ppermute | solution.py:34
  135.0 18.5 %collective-permute-start.13 = (bf16[448,192]{1,0:T(8,128)(2,1)S(1)}, bf16[448,192]{1,0:T(8,128)(2,1)S(1)}, u32[]{:S(2)}, u32[]{:S(2)}) collective-permute-start(bf16[448,192]{1,0:T(8,128)(2,1)S(1)} %get-tuple-element.26.a0), channel_id=1, source_target_pairs={{0,3},{1,0},{2,1},{3,2},{4,7},{5,4},{6,5},{7,6},{8,11},{9,8},{10,9... | collective-permute-start | bytes 516104 | tf_op jit(solution)/shard_map/ppermute | solution.py:34
  170.8 8.6 %collective-permute-start.14 = (bf16[448,192]{1,0:T(8,128)(2,1)S(1)}, bf16[448,192]{1,0:T(8,128)(2,1)S(1)}, u32[]{:S(2)}, u32[]{:S(2)}) collective-permute-start(bf16[448,192]{1,0:T(8,128)(2,1)S(1)} %get-tuple-element.28.a0), channel_id=1, source_target_pairs={{0,1},{1,2},{2,3},{3,0},{4,5},{5,6},{6,7},{7,4},{8,9},{9,10},{10,1... | collective-permute-start | bytes 516104 | tf_op jit(solution)/shard_map/ppermute | solution.py:34
  170.9 19.3 %collective-permute-start.15 = (bf16[448,192]{1,0:T(8,128)(2,1)S(1)}, bf16[448,192]{1,0:T(8,128)(2,1)S(1)}, u32[]{:S(2)}, u32[]{:S(2)}) collective-permute-start(bf16[448,192]{1,0:T(8,128)(2,1)S(1)} %get-tuple-element.28.a0), channel_id=1, source_target_pairs={{0,2},{1,3},{2,0},{3,1},{4,6},{5,7},{6,4},{7,5},{8,10},{9,11},{10,... | collective-permute-start | bytes 516104 | tf_op jit(solution)/shard_map/ppermute | solution.py:34
  171.9 18.7 %collective-permute-start.16 = (bf16[448,192]{1,0:T(8,128)(2,1)S(1)}, bf16[448,192]{1,0:T(8,128)(2,1)S(1)}, u32[]{:S(2)}, u32[]{:S(2)}) collective-permute-start(bf16[448,192]{1,0:T(8,128)(2,1)S(1)} %get-tuple-element.28.a0), channel_id=1, source_target_pairs={{0,3},{1,0},{2,1},{3,2},{4,7},{5,4},{6,5},{7,6},{8,11},{9,8},{10,9... | collective-permute-start | bytes 516104 | tf_op jit(solution)/shard_map/ppermute | solution.py:34
  202.7 7.8 %collective-permute-start.20 = (bf16[384,192]{1,0:T(8,128)(2,1)S(1)}, bf16[384,192]{1,0:T(8,128)(2,1)S(1)}, u32[]{:S(2)}, u32[]{:S(2)}) collective-permute-start(bf16[384,192]{1,0:T(8,128)(2,1)S(1)} %get-tuple-element.35.a0), channel_id=1, source_target_pairs={{0,1},{1,2},{2,3},{3,0},{4,5},{5,6},{6,7},{7,4},{8,9},{9,10},{10,1... | collective-permute-start | bytes 442376 | tf_op jit(solution)/shard_map/ppermute | solution.py:34
  202.7 17.3 %collective-permute-start.21 = (bf16[384,192]{1,0:T(8,128)(2,1)S(1)}, bf16[384,192]{1,0:T(8,128)(2,1)S(1)}, u32[]{:S(2)}, u32[]{:S(2)}) collective-permute-start(bf16[384,192]{1,0:T(8,128)(2,1)S(1)} %get-tuple-element.35.a0), channel_id=1, source_target_pairs={{0,2},{1,3},{2,0},{3,1},{4,6},{5,7},{6,4},{7,5},{8,10},{9,11},{10,... | collective-permute-start | bytes 442376 | tf_op jit(solution)/shard_map/ppermute | solution.py:34
  205.7 16.3 %collective-permute-start.22 = (bf16[384,192]{1,0:T(8,128)(2,1)S(1)}, bf16[384,192]{1,0:T(8,128)(2,1)S(1)}, u32[]{:S(2)}, u32[]{:S(2)}) collective-permute-start(bf16[384,192]{1,0:T(8,128)(2,1)S(1)} %get-tuple-element.35.a0), channel_id=1, source_target_pairs={{0,3},{1,0},{2,1},{3,2},{4,7},{5,4},{6,5},{7,6},{8,11},{9,8},{10,9... | collective-permute-start | bytes 442376 | tf_op jit(solution)/shard_map/ppermute | solution.py:34
  237.1 8.9 %collective-permute-start.26 = (bf16[384,192]{1,0:T(8,128)(2,1)S(1)}, bf16[384,192]{1,0:T(8,128)(2,1)S(1)}, u32[]{:S(2)}, u32[]{:S(2)}) collective-permute-start(bf16[384,192]{1,0:T(8,128)(2,1)S(1)} %shard_map.100.a0), channel_id=1, source_target_pairs={{0,2},{1,3},{2,0},{3,1},{4,6},{5,7},{6,4},{7,5},{8,10},{9,11},{10,... | collective-permute-start | bytes 442376 | tf_op jit(solution)/shard_map/ppermute | solution.py:34
  238.4 18.3 %collective-permute-start.27 = (bf16[384,192]{1,0:T(8,128)(2,1)S(1)}, bf16[384,192]{1,0:T(8,128)(2,1)S(1)}, u32[]{:S(2)}, u32[]{:S(2)}) collective-permute-start(bf16[384,192]{1,0:T(8,128)(2,1)S(1)} %shard_map.100.a0), channel_id=1, source_target_pairs={{0,3},{1,0},{2,1},{3,2},{4,7},{5,4},{6,5},{7,6},{8,11},{9,8},{10,9... | collective-permute-start | bytes 442376 | tf_op jit(solution)/shard_map/ppermute | solution.py:34
  271.6 8.4 %collective-permute-start.34 = (bf16[384,192]{1,0:T(8,128)(2,1)S(1)}, bf16[384,192]{1,0:T(8,128)(2,1)S(1)}, u32[]{:S(2)}, u32[]{:S(2)}) collective-permute-start(bf16[384,192]{1,0:T(8,128)(2,1)S(1)} %shard_map.102.a0), channel_id=1, source_target_pairs={{0,2},{1,3},{2,0},{3,1},{4,6},{5,7},{6,4},{7,5},{8,10},{9,11},{10,... | collective-permute-start | bytes 442376 | tf_op jit(solution)/shard_map/ppermute | solution.py:34
  271.7 17.9 %collective-permute-start.35 = (bf16[384,192]{1,0:T(8,128)(2,1)S(1)}, bf16[384,192]{1,0:T(8,128)(2,1)S(1)}, u32[]{:S(2)}, u32[]{:S(2)}) collective-permute-start(bf16[384,192]{1,0:T(8,128)(2,1)S(1)} %shard_map.102.a0), channel_id=1, source_target_pairs={{0,3},{1,0},{2,1},{3,2},{4,7},{5,4},{6,5},{7,6},{8,11},{9,8},{10,9... | collective-permute-start | bytes 442376 | tf_op jit(solution)/shard_map/ppermute | solution.py:34
  294.9 12.8 %all-to-all-start = ((bf16[8,8,1024]{2,1,0:T(8,128)(2,1)}), bf16[8,8,1024]{2,1,0:T(8,128)(2,1)S(1)}, u32[]{:S(2)}, u32[]{:S(2)}) async-start(bf16[8,8,1024]{2,1,0:T(8,128)(2,1)} %bitcast.13), calls=%async_computation | async-start | bytes 262144 | tf_op jit(solution)/shard_map/all_to_all | solution.py:458
  (43 other events, 283.0 us)
Sparse Core Ops, SparseCore 0:
  27.5 39.1 all-gather.6
  109.8 39.1 all-gather.8
  158.0 41.3 all-gather.10

commit v4 on v3

--- a/solution.py
+++ b/solution.py
@@ -13,7 +13,7 @@
 BLOCKS_PER_LOAD = 2
 FRAMED_BLOCKS = 4
 DIGIT = 128
-VMEM_BYTES = 24 * 2**20
+VMEM_BYTES = 56 * 2**20
 
 
 def dilation(block):
@@ -81,6 +81,16 @@
     return gelu(inner).astype(jnp.bfloat16)
 
 
+def pack(act):
+    half = act.shape[0] // 2
+    return jnp.concatenate([act[:half], act[half:]], axis=1)
+
+
+def unpack(cells):
+    half = cells.shape[1] // 2
+    return jnp.concatenate([cells[:, :half], cells[:, half:]], axis=0)
+
+
 def first_kernel(step, own_rows, order_ref, c0, c1, c2, c3, w_ref, bias_ref, act_ref, trunk_ref, sums):
     k = pl.program_id(0)
     rows = trunk_ref.shape[0]
@@ -97,7 +107,7 @@
 
     @pl.when(k == pl.num_programs(0) - 1)
     def _():
-        act_ref[...] = gelu_of_taps(sums, bias_ref[...], step, act_ref.shape[0])
+        act_ref[...] = pack(gelu_of_taps(sums, bias_ref[...], step, 2 * act_ref.shape[0]))
 
 
 def first_conv(cells, rows, order, conv_in, bias, step):
@@ -116,13 +126,13 @@
                 pl.BlockSpec((1, hidden), lambda k, order: (0, 0)),
             ],
             out_specs=[
-                pl.BlockSpec((rows, hidden), lambda k, order: (0, 0)),
+                pl.BlockSpec((rows // 2, 2 * hidden), lambda k, order: (0, 0)),
                 pl.BlockSpec((rows, width), lambda k, order: (0, order[k])),
             ],
             scratch_shapes=[pltpu.VMEM((3, rows, hidden), jnp.float32)],
         ),
         out_shape=[
-            jax.ShapeDtypeStruct((rows, hidden), jnp.bfloat16),
+            jax.ShapeDtypeStruct((rows // 2, 2 * hidden), jnp.bfloat16),
             jax.ShapeDtypeStruct((rows, channels), jnp.bfloat16),
         ],
         compiler_params=pltpu.CompilerParams(vmem_limit_bytes=VMEM_BYTES),
@@ -140,7 +150,7 @@
 
 
 def keep_acts(acts_ref, acts):
-    acts_ref[...] = jnp.concatenate([a[...] for a in acts], axis=1)
+    acts_ref[...] = jnp.concatenate([unpack(a[...]) for a in acts], axis=1)
 
 
 def fused_kernel(
@@ -164,7 +174,7 @@
 
     @pl.when(c == pl.num_programs(0) - 1)
     def _():
-        act_ref[...] = gelu_of_taps(sums, bias_ref[...], step, act_ref.shape[0])
+        act_ref[...] = pack(gelu_of_taps(sums, bias_ref[...], step, 2 * act_ref.shape[0]))
 
 
 def projection_specs(load, part, acts, per_block, share, width):
@@ -193,7 +203,7 @@
                 pl.BlockSpec((1, hidden), lambda c, *_: (0, 0)),
             ],
             out_specs=[
-                pl.BlockSpec((rows_out, hidden), lambda c, *_: (0, 0)),
+                pl.BlockSpec((rows_out // 2, 2 * hidden), lambda c, *_: (0, 0)),
                 pl.BlockSpec((rows, width), lambda c, *_: (0, c)),
             ],
             scratch_shapes=[
@@ -202,7 +212,7 @@
             ],
         ),
         out_shape=[
-            jax.ShapeDtypeStruct((rows_out, hidden), jnp.bfloat16),
+            jax.ShapeDtypeStruct((rows_out // 2, 2 * hidden), jnp.bfloat16),
             jax.ShapeDtypeStruct((rows, channels), jnp.bfloat16),
         ],
         compiler_params=pltpu.CompilerParams(vmem_limit_bytes=VMEM_BYTES),
@@ -228,7 +238,7 @@
 
 def projection(acts, load, part, per_block, share, trunk, pbias):
     frame, channels = trunk.shape
-    rows, hidden = acts[0].shape
+    rows, hidden = 2 * acts[0].shape[0], acts[0].shape[1] // 2
     width = tile_of(channels)
     return pl.pallas_call(
         functools.partial(projection_kernel, (frame - rows) // 2),
@@ -259,7 +269,7 @@
 
     @pl.when(c == pl.num_programs(0) - 1)
     def _():
-        act_ref[...] = gelu_of_taps(sums, bias_ref[...], step, act_ref.shape[0])
+        act_ref[...] = pack(gelu_of_taps(sums, bias_ref[...], step, 2 * act_ref.shape[0]))
 
 
 def conv(above, trunk, below, conv_in, block, bias):
@@ -277,9 +287,9 @@
             pl.BlockSpec((1, 3, hidden, width), lambda c: (block, 0, 0, c)),
             pl.BlockSpec((1, hidden), lambda c: (0, 0)),
         ],
-        out_specs=pl.BlockSpec((rows, hidden), lambda c: (0, 0)),
+        out_specs=pl.BlockSpec((rows // 2, 2 * hidden), lambda c: (0, 0)),
         scratch_shapes=[pltpu.VMEM((3, rows + 2 * step, hidden), jnp.float32)],
-        out_shape=jax.ShapeDtypeStruct((rows, hidden), jnp.bfloat16),
+        out_shape=jax.ShapeDtypeStruct((rows // 2, 2 * hidden), jnp.bfloat16),
         compiler_params=pltpu.CompilerParams(vmem_limit_bytes=VMEM_BYTES),
         cost_estimate=pl.CostEstimate(
             flops=6 * rows * hidden * channels,
@@ -313,7 +323,7 @@
 
 def head(acts, load, part, per_block, share, trunk, pbias, head_weight, head_bias, onehot):
     rows, channels = trunk.shape
-    hidden = acts[0].shape[1]
+    hidden = acts[0].shape[1] // 2
     tracks = head_weight.shape[1]
     genes = onehot.shape[0]
     width = tile_of(channels)
@@ -409,7 +419,7 @@
 
     above, below = halo(trunk_input, margin)
     first_column = from_others(column(0))
-    loads = [gather(first_column)]
+    loads = [gather(after_all(first_column, above, below))]
     own = jnp.concatenate(
         [above, trunk_input, below, jnp.pad(projection_bias, ((0, -blocks % 16), (0, 0)))], axis=0
     )

time: 316 us -> 278 us (0.88)
  local copies, waits for them, and re-layouts: 48.8 us -> 15.3 us
  waiting for transfers between devices: 158 us -> 127 us
  Pallas kernels: 31 us -> 56.3 us
    unnamed x74 -> x70, local copies, waits for them, and re-layouts: 43.7 us -> 5 us
    ppermute x30, waiting for transfers between devices: 144 us -> 114 us  [from_others(): lax.ppermute(cells, 'trk', [(i, (i + k) % count) for i in range(count)])]
    pallas_call x3, Pallas kernels: 13.8 us -> 23 us  [fused(): pl.pallas_call(functools.partial(fused_kernel, dilation(block)), grid_spe...]
    pallas_call x2, Pallas kernels: 4 us -> 10.4 us  [projection(): pl.pallas_call(functools.partial(projection_kernel, (frame - rows) // 2),...]
    pallas_call x2, Pallas kernels: 4.28 us -> 8.86 us  [conv(): pl.pallas_call(functools.partial(conv_kernel, step), grid=(channels // wi...]
  transfers between devices with their start and end apart: 40 -> 40, of which waited for: 27 -> 28; matrix products, arithmetic and copies ran while one was open for 2% -> 4% of each run, Pallas kernels for 7% -> 14%
where the time goes in v4:
time: 278 us; the launch traced here: 277 us
  waiting for transfers between devices  127 us (46%)
  Pallas kernels  56.3 us (20%)
  starting transfers between devices  55.4 us (20%)
  between operations  16.7 us (6%)
  local copies, waits for them, and re-layouts  15.3 us (6%)
  other arithmetic  6.53 us (2%)
    ppermute x30, waiting for transfers between devices, from_others(): lax.ppermute(cells, 'trk', [(i, (i + k) % count) for i in range(count)])  114 us
    ppermute x30, starting transfers between devices, from_others(): lax.ppermute(cells, 'trk', [(i, (i + k) % count) for i in range(count)])  36.1 us
    pallas_call x3, Pallas kernels, fused(): pl.pallas_call(functools.partial(fused_kernel, dilation(block)), grid_spe...  23 us
    pallas_call x2, Pallas kernels, projection(): pl.pallas_call(functools.partial(projection_kernel, (frame - rows) // 2),...  10.4 us
    pallas_call x2, Pallas kernels, conv(): pl.pallas_call(functools.partial(conv_kernel, step), grid=(channels // wi...  8.86 us
    all_to_all x1, starting transfers between devices, shards(): lax.all_to_all(partial.reshape(count, genes_here, partial.shape[1]), 'seq...  8.14 us
    pallas_call x1, Pallas kernels, head(): pl.pallas_call(head_kernel, grid=(channels // width,), in_specs=projectio...  7.75 us
    ppermute x3, starting transfers between devices, halo(): above = lax.ppermute(tail, 'seq', [(i, i + 1) for i in range(count - 1)])  6.99 us
  transfers between devices with their start and end apart: 40, of which 28 were waited for; matrix products, arithmetic and copies ran while one was open for 4% of the time, Pallas kernels for 14%

profile of v4, /device:TPU:8, one launch (start us, length us, event | category | flops | bytes accessed | tf_op | source)
XLA Modules:
  0.0 277.1 jit_solution(14866677204184350277)
XLA Ops:
  7.2 2.2 fusion.12
  16.2 3.0 %collective-permute-start = (bf16[32,384]{1,0:T(8,128)(2,1)S(1)}, bf16[32,384]{1,0:T(8,128)(2,1)S(1)}, u32[]{:S(2)}, u32[]{:S(2)}) collective-permute-start(bf16[32,384]{1,0:T(8,128)(2,1)S(1)} %get-tuple-element.59), channel_id=1, source_target_pairs={{0,4},{4,8},{8,12},{12,16},{16,20},{20,24},{24,28},{1,5},{5,9},{9,... | collective-permute-start | bytes 73736 | tf_op jit(solution)/shard_map/ppermute | solution.py:43
  30.8 6.9 %collective-permute-done.5.c1 = bf16[464,384]{1,0:T(8,128)(2,1)S(1)} collective-permute-done((bf16[464,384]{1,0:T(8,128)(2,1)S(1)}, bf16[464,384]{1,0:T(8,128)(2,1)S(1)}, u32[]{:S(2)}, u32[]{:S(2)}) %collective-permute-start.5) | collective-permute-done | bytes 356384 | tf_op jit(solution)/shard_map/ppermute | solution.py:34
  37.7 19.8 %collective-permute-done.6.c2 = bf16[464,384]{1,0:T(8,128)(2,1)S(1)} collective-permute-done((bf16[464,384]{1,0:T(8,128)(2,1)S(1)}, bf16[464,384]{1,0:T(8,128)(2,1)S(1)}, u32[]{:S(2)}, u32[]{:S(2)}) %collective-permute-start.6) | collective-permute-done | bytes 356384 | tf_op jit(solution)/shard_map/ppermute | solution.py:34
  59.3 6.2 %shard_map.95 = (bf16[224,384]{1,0:T(8,128)(2,1)}, bf16[448,1536]{1,0:T(8,128)(2,1)}) custom-call(s32[4]{0:T(128)} %compare_select_fusion.order_ref, bf16[464,384]{1,0:T(8,128)(2,1)} %copy-done, bf16[464,384]{1,0:T(8,128)(2,1)} %copy-done.3, bf16[464,384]{1,0:T(8,128)(2,1)} %copy-done.4, bf16[464,384]{1,0:T(8,128)(2,1)} %copy-done.5, ...), custom_call_target="tpu_custom_call" | custom-call | flops 792723456 | bytes 4521984 | tf_op jit(solution)/shard_map/pallas_call | solution.py:118
  65.5 2.9 %collective-permute-start.8 = (bf16[224,384]{1,0:T(8,128)(2,1)}, bf16[224,384]{1,0:T(8,128)(2,1)S(1)}, u32[]{:S(2)}, u32[]{:S(2)}) collective-permute-start(bf16[224,384]{1,0:T(8,128)(2,1)} %get-tuple-element.28.a0), channel_id=1, source_target_pairs={{0,1},{1,2},{2,3},{3,0},{4,5},{5,6},{6,7},{7,4},{8,9},{9,10},{10,1... | collective-permute-start | bytes 516104 | tf_op jit(solution)/shard_map/ppermute | solution.py:34
  71.4 2.0 collective-permute-start.19
  73.4 18.7 %collective-permute-done.18 = bf16[48,1536]{1,0:T(8,128)(2,1)S(1)} collective-permute-done((bf16[48,1536]{1,0:T(8,128)(2,1)S(1)}, bf16[48,1536]{1,0:T(8,128)(2,1)S(1)}, u32[]{:S(2)}, u32[]{:S(2)}) %collective-permute-start.18) | collective-permute-done | bytes 147488 | tf_op jit(solution)/shard_map/ppermute | solution.py:34
  106.0 7.7 %shard_map.96 = (bf16[224,384]{1,0:T(8,128)(2,1)}, bf16[448,1536]{1,0:T(8,128)(2,1)}) custom-call(s32[2]{0:T(128)} %pad_add_fusion.edge_ref, bf16[224,384]{1,0:T(8,128)(2,1)} %get-tuple-element.28.a0, bf16[224,384]{1,0:T(8,128)(2,1)} %copy-done.8, bf16[224,384]{1,0:T(8,128)(2,1)} %copy-done.9, bf16[224,384]{1,0:T(8,128)(2,1)} %copy-done.10, ...), custom_call_target="tpu_custom_call" | custom-call | flops 1849688064 | bytes 6881280 | tf_op jit(solution)/shard_map/pallas_call | solution.py:193
  113.7 3.1 %collective-permute-start.12 = (bf16[224,384]{1,0:T(8,128)(2,1)}, bf16[224,384]{1,0:T(8,128)(2,1)S(1)}, u32[]{:S(2)}, u32[]{:S(2)}) collective-permute-start(bf16[224,384]{1,0:T(8,128)(2,1)} %get-tuple-element.34.a0), channel_id=1, source_target_pairs={{0,2},{1,3},{2,0},{3,1},{4,6},{5,7},{6,4},{7,5},{8,10},{9,11},{10,... | collective-permute-start | bytes 516104 | tf_op jit(solution)/shard_map/ppermute | solution.py:34
  118.1 9.1 %collective-permute-done.11.a1 = bf16[224,384]{1,0:T(8,128)(2,1)S(1)} collective-permute-done((bf16[224,384]{1,0:T(8,128)(2,1)}, bf16[224,384]{1,0:T(8,128)(2,1)S(1)}, u32[]{:S(2)}, u32[]{:S(2)}) %collective-permute-start.11) | collective-permute-done | bytes 172064 | tf_op jit(solution)/shard_map/ppermute | solution.py:34
  127.2 2.1 collective-permute-done.12.a2
  131.8 7.7 %shard_map.97 = (bf16[224,384]{1,0:T(8,128)(2,1)}, bf16[448,1536]{1,0:T(8,128)(2,1)}) custom-call(s32[2]{0:T(128)} %pad_add_fusion.edge_ref, bf16[224,384]{1,0:T(8,128)(2,1)} %get-tuple-element.34.a0, bf16[224,384]{1,0:T(8,128)(2,1)} %copy-done.11, bf16[224,384]{1,0:T(8,128)(2,1)} %copy-done.12, bf16[224,384]{1,0:T(8,128)(2,1)} %copy-done.13, ...), custom_call_target="tpu_custom_call" | custom-call | flops 1849688064 | bytes 6881280 | tf_op jit(solution)/shard_map/pallas_call | solution.py:193
  143.3 3.6 %collective-permute-done.14.a1 = bf16[224,384]{1,0:T(8,128)(2,1)S(1)} collective-permute-done((bf16[224,384]{1,0:T(8,128)(2,1)}, bf16[224,384]{1,0:T(8,128)(2,1)S(1)}, u32[]{:S(2)}, u32[]{:S(2)}) %collective-permute-start.14) | collective-permute-done | bytes 172064 | tf_op jit(solution)/shard_map/ppermute | solution.py:34
  147.0 7.9 %collective-permute-done.15.a2 = bf16[224,384]{1,0:T(8,128)(2,1)S(1)} collective-permute-done((bf16[224,384]{1,0:T(8,128)(2,1)}, bf16[224,384]{1,0:T(8,128)(2,1)S(1)}, u32[]{:S(2)}, u32[]{:S(2)}) %collective-permute-start.15) | collective-permute-done | bytes 172064 | tf_op jit(solution)/shard_map/ppermute | solution.py:34
  156.6 7.6 %shard_map.98 = (bf16[192,384]{1,0:T(8,128)(2,1)}, bf16[448,1536]{1,0:T(8,128)(2,1)}) custom-call(s32[2]{0:T(128)} %pad_add_fusion.edge_ref, bf16[224,384]{1,0:T(8,128)(2,1)} %get-tuple-element.36.a0, bf16[224,384]{1,0:T(8,128)(2,1)} %copy-done.14, bf16[224,384]{1,0:T(8,128)(2,1)} %copy-done.15, bf16[224,384]{1,0:T(8,128)(2,1)} %copy-done.16, ...), custom_call_target="tpu_custom_call" | custom-call | flops 1849688064 | bytes 6881280 | tf_op jit(solution)/shard_map/pallas_call | solution.py:193
  164.2 2.3 collective-permute-start.21
  168.5 2.6 collective-permute-done.20.a1
  171.2 6.4 %collective-permute-done.21.a2 = bf16[192,384]{1,0:T(8,128)(2,1)S(1)} collective-permute-done((bf16[192,384]{1,0:T(8,128)(2,1)}, bf16[192,384]{1,0:T(8,128)(2,1)S(1)}, u32[]{:S(2)}, u32[]{:S(2)}) %collective-permute-start.21) | collective-permute-done | bytes 147488 | tf_op jit(solution)/shard_map/ppermute | solution.py:34
  177.6 2.6 collective-permute-done.22.a3
  180.9 5.2 %shard_map.99.trunk_ref = bf16[384,1536]{1,0:T(8,128)(2,1)} custom-call(bf16[192,384]{1,0:T(8,128)(2,1)} %get-tuple-element.43.a0, bf16[192,384]{1,0:T(8,128)(2,1)} %copy-done.18, bf16[192,384]{1,0:T(8,128)(2,1)} %copy-done.20, bf16[192,384]{1,0:T(8,128)(2,1)} %copy-done.22, bf16[8,192,1536]{2,1,0:T(8,128)(2,1)} %bitcast.36, bf16[8,192,1536]{2,1,0:T(8,128)(2,1)} %bitcast.37, ...), custom_call_target="tpu_custom_call" | custom-call | flops 905969664 | bytes 4718592 | tf_op jit(solution)/shard_map/pallas_call | solution.py:243
  190.9 2.4 collective-permute-done.24.below_ref
  193.9 4.4 %shard_map.100.a0 = bf16[192,384]{1,0:T(8,128)(2,1)} custom-call(bf16[32,1536]{1,0:T(8,128)(2,1)} %copy-done.26, bf16[384,1536]{1,0:T(8,128)(2,1)} %shard_map.99.trunk_ref, bf16[32,1536]{1,0:T(8,128)(2,1)} %copy-done.27, bf16[6,3,192,1536]{3,2,1,0:T(8,128)(2,1)} %w_ref.11, bf16[1,192]{1,0:T(2,128)(2,1)} %get-tuple-element.72.bias_ref), custom_call_target="tpu_custom_call" | custom-call | flops 679477248 | bytes 2949120 | tf_op jit(solution)/shard_map/pallas_call | solution.py:280
  203.6 2.3 collective-permute-done.26.a2
  205.9 8.0 %collective-permute-done.27.a3 = bf16[192,384]{1,0:T(8,128)(2,1)S(1)} collective-permute-done((bf16[192,384]{1,0:T(8,128)(2,1)}, bf16[192,384]{1,0:T(8,128)(2,1)S(1)}, u32[]{:S(2)}, u32[]{:S(2)}) %collective-permute-start.27) | collective-permute-done | bytes 147488 | tf_op jit(solution)/shard_map/ppermute | solution.py:34
  214.5 5.2 %shard_map.101.trunk_ref = bf16[384,1536]{1,0:T(8,128)(2,1)} custom-call(bf16[192,384]{1,0:T(8,128)(2,1)} %shard_map.100.a0, bf16[192,384]{1,0:T(8,128)(2,1)} %copy-done.17, bf16[192,384]{1,0:T(8,128)(2,1)} %copy-done.19, bf16[192,384]{1,0:T(8,128)(2,1)} %copy-done.21, bf16[8,208,1536]{2,1,0:T(8,128)(2,1)} %bitcast.16, bf16[8,208,1536]{2,1,0:T(8,128)(2,1)} %bitcast.17, ...), custom_call_target="tpu_custom_call" | custom-call | flops 905969664 | bytes 4718592 | tf_op jit(solution)/shard_map/pallas_call | solution.py:243
  224.4 4.0 %collective-permute-done.32.below_ref = bf16[64,1536]{1,0:T(8,128)(2,1)S(1)} collective-permute-done((bf16[64,1536]{1,0:T(8,128)(2,1)S(1)}, bf16[64,1536]{1,0:T(8,128)(2,1)S(1)}, u32[]{:S(2)}, u32[]{:S(2)}) %collective-permute-start.32) | collective-permute-done | bytes 196640 | tf_op jit(solution)/shard_map/ppermute | solution.py:44
  229.1 4.5 %shard_map.102.a0 = bf16[192,384]{1,0:T(8,128)(2,1)} custom-call(bf16[64,1536]{1,0:T(8,128)(2,1)} %copy-done.6, bf16[384,1536]{1,0:T(8,128)(2,1)} %shard_map.101.trunk_ref, bf16[64,1536]{1,0:T(8,128)(2,1)} %copy-done.7, bf16[6,3,192,1536]{3,2,1,0:T(8,128)(2,1)} %w_ref.11, bf16[1,192]{1,0:T(2,128)(2,1)} %get-tuple-element.67.bias_ref), custom_call_target="tpu_custom_call" | custom-call | flops 679477248 | bytes 2949120 | tf_op jit(solution)/shard_map/pallas_call | solution.py:280
  240.0 7.8 %collective-permute-done.35.a3 = bf16[192,384]{1,0:T(8,128)(2,1)S(1)} collective-permute-done((bf16[192,384]{1,0:T(8,128)(2,1)}, bf16[192,384]{1,0:T(8,128)(2,1)S(1)}, u32[]{:S(2)}, u32[]{:S(2)}) %collective-permute-start.35) | collective-permute-done | bytes 147488 | tf_op jit(solution)/shard_map/ppermute | solution.py:34
  248.4 7.7 %shard_map.103 = (bf16[384,1024]{1,0:T(8,128)(2,1)}, bf16[64,1024]{1,0:T(8,128)(2,1)}) custom-call(bf16[192,384]{1,0:T(8,128)(2,1)} %shard_map.102.a0, bf16[192,384]{1,0:T(8,128)(2,1)} %copy-done.23, bf16[192,384]{1,0:T(8,128)(2,1)} %copy-done.24, bf16[192,384]{1,0:T(8,128)(2,1)} %copy-done.25, bf16[8,208,1536]{2,1,0:T(8,128)(2,1)} %bitcast.20, ...), custom_call_target="tpu_custom_call" | custom-call | flops 2113929216 | bytes 6684672 | tf_op jit(solution)/shard_map/pallas_call | solution.py:330
  256.2 8.1 %all-to-all-start = ((bf16[8,8,1024]{2,1,0:T(8,128)(2,1)}), bf16[8,8,1024]{2,1,0:T(8,128)(2,1)S(1)}, u32[]{:S(2)}, u32[]{:S(2)}) async-start(bf16[8,8,1024]{2,1,0:T(8,128)(2,1)} %bitcast.43), calls=%async_computation | async-start | bytes 262144 | tf_op jit(solution)/shard_map/all_to_all | solution.py:468
  264.4 5.4 %all-to-all-done = bf16[8,8,1024]{2,1,0:T(8,128)(2,1)S(1)} async-done(((bf16[8,8,1024]{2,1,0:T(8,128)(2,1)}), bf16[8,8,1024]{2,1,0:T(8,128)(2,1)S(1)}, u32[]{:S(2)}, u32[]{:S(2)}) %all-to-all-start) | async-done | bytes 131104 | tf_op jit(solution)/shard_map/all_to_all | solution.py:468
  (159 shorter events, 70.7 us)
Async XLA Ops:
  7.2 98.8 %all-gather.7.cloned.1.call-start = ((), (), s32[]{:S(2)}) async-start(), calls=%async_computation.1 | async-start | bytes 5308416 | tf_op jit(solution)/shard_map/all_gather | solution.py:406
  9.5 12.2 %collective-permute-start.2 = (bf16[48,1536]{1,0:T(8,128)(2,1)S(1)}, bf16[48,1536]{1,0:T(8,128)(2,1)S(1)}, u32[]{:S(2)}, u32[]{:S(2)}) collective-permute-start(bf16[48,1536]{1,0:T(8,128)(2,1)S(1)} %constant_dynamic-slice_fusion.2), channel_id=1, source_target_pairs={{0,1},{1,2},{2,3},{3,0},{4,5},{5,6},{6,7},{7,4},{8,9},{9,10},{10,1... | collective-permute-start | bytes 442376 | tf_op jit(solution)/shard_map/ppermute | solution.py:34
  11.1 12.6 %collective-permute-start.3 = (bf16[48,1536]{1,0:T(8,128)(2,1)S(1)}, bf16[48,1536]{1,0:T(8,128)(2,1)S(1)}, u32[]{:S(2)}, u32[]{:S(2)}) collective-permute-start(bf16[48,1536]{1,0:T(8,128)(2,1)S(1)} %constant_dynamic-slice_fusion.2), channel_id=1, source_target_pairs={{0,2},{1,3},{2,0},{3,1},{4,6},{5,7},{6,4},{7,5},{8,10},{9,11},{10,... | collective-permute-start | bytes 442376 | tf_op jit(solution)/shard_map/ppermute | solution.py:34
  12.2 13.2 %collective-permute-start.4 = (bf16[48,1536]{1,0:T(8,128)(2,1)S(1)}, bf16[48,1536]{1,0:T(8,128)(2,1)S(1)}, u32[]{:S(2)}, u32[]{:S(2)}) collective-permute-start(bf16[48,1536]{1,0:T(8,128)(2,1)S(1)} %constant_dynamic-slice_fusion.2), channel_id=1, source_target_pairs={{0,3},{1,0},{2,1},{3,2},{4,7},{5,4},{6,5},{7,6},{8,11},{9,8},{10,9... | collective-permute-start | bytes 442376 | tf_op jit(solution)/shard_map/ppermute | solution.py:34
  26.3 129.6 %all-gather.9.cloned.1.call-start = ((), (), s32[]{:S(2)}) async-start(), calls=%async_computation.2 | async-start | bytes 5308416 | tf_op jit(solution)/shard_map/all_gather | solution.py:406
  26.5 11.2 %collective-permute-start.5 = (bf16[464,384]{1,0:T(8,128)(2,1)S(1)}, bf16[464,384]{1,0:T(8,128)(2,1)S(1)}, u32[]{:S(2)}, u32[]{:S(2)}) collective-permute-start(bf16[464,384]{1,0:T(8,128)(2,1)S(1)} %fusion.1.c0), channel_id=1, source_target_pairs={{0,1},{1,2},{2,3},{3,0},{4,5},{5,6},{6,7},{7,4},{8,9},{9,10},{10,1... | collective-permute-start | bytes 1069064 | tf_op jit(solution)/shard_map/ppermute | solution.py:34
  26.5 30.9 %collective-permute-start.6 = (bf16[464,384]{1,0:T(8,128)(2,1)S(1)}, bf16[464,384]{1,0:T(8,128)(2,1)S(1)}, u32[]{:S(2)}, u32[]{:S(2)}) collective-permute-start(bf16[464,384]{1,0:T(8,128)(2,1)S(1)} %fusion.1.c0), channel_id=1, source_target_pairs={{0,2},{1,3},{2,0},{3,1},{4,6},{5,7},{6,4},{7,5},{8,10},{9,11},{10,... | collective-permute-start | bytes 1069064 | tf_op jit(solution)/shard_map/ppermute | solution.py:34
  28.2 30.3 %collective-permute-start.7 = (bf16[464,384]{1,0:T(8,128)(2,1)S(1)}, bf16[464,384]{1,0:T(8,128)(2,1)S(1)}, u32[]{:S(2)}, u32[]{:S(2)}) collective-permute-start(bf16[464,384]{1,0:T(8,128)(2,1)S(1)} %fusion.1.c0), channel_id=1, source_target_pairs={{0,3},{1,0},{2,1},{3,2},{4,7},{5,4},{6,5},{7,6},{8,11},{9,8},{10,9... | collective-permute-start | bytes 1069064 | tf_op jit(solution)/shard_map/ppermute | solution.py:34
  58.6 12.8 %collective-permute-start.17 = (bf16[48,1536]{1,0:T(8,128)(2,1)S(1)}, bf16[48,1536]{1,0:T(8,128)(2,1)S(1)}, u32[]{:S(2)}, u32[]{:S(2)}) collective-permute-start(bf16[48,1536]{1,0:T(8,128)(2,1)S(1)} %constant_dynamic-slice_fusion.1), channel_id=1, source_target_pairs={{0,1},{1,2},{2,3},{3,0},{4,5},{5,6},{6,7},{7,4},{8,9},{9,10},{10,1... | collective-permute-start | bytes 442376 | tf_op jit(solution)/shard_map/ppermute | solution.py:34
  65.5 28.4 %collective-permute-start.8 = (bf16[224,384]{1,0:T(8,128)(2,1)}, bf16[224,384]{1,0:T(8,128)(2,1)S(1)}, u32[]{:S(2)}, u32[]{:S(2)}) collective-permute-start(bf16[224,384]{1,0:T(8,128)(2,1)} %get-tuple-element.28.a0), channel_id=1, source_target_pairs={{0,1},{1,2},{2,3},{3,0},{4,5},{5,6},{6,7},{7,4},{8,9},{9,10},{10,1... | collective-permute-start | bytes 516104 | tf_op jit(solution)/shard_map/ppermute | solution.py:34
  68.4 25.5 %collective-permute-start.9 = (bf16[224,384]{1,0:T(8,128)(2,1)}, bf16[224,384]{1,0:T(8,128)(2,1)S(1)}, u32[]{:S(2)}, u32[]{:S(2)}) collective-permute-start(bf16[224,384]{1,0:T(8,128)(2,1)} %get-tuple-element.28.a0), channel_id=1, source_target_pairs={{0,2},{1,3},{2,0},{3,1},{4,6},{5,7},{6,4},{7,5},{8,10},{9,11},{10,... | collective-permute-start | bytes 516104 | tf_op jit(solution)/shard_map/ppermute | solution.py:34
  69.9 24.0 %collective-permute-start.10 = (bf16[224,384]{1,0:T(8,128)(2,1)}, bf16[224,384]{1,0:T(8,128)(2,1)S(1)}, u32[]{:S(2)}, u32[]{:S(2)}) collective-permute-start(bf16[224,384]{1,0:T(8,128)(2,1)} %get-tuple-element.28.a0), channel_id=1, source_target_pairs={{0,3},{1,0},{2,1},{3,2},{4,7},{5,4},{6,5},{7,6},{8,11},{9,8},{10,9... | collective-permute-start | bytes 516104 | tf_op jit(solution)/shard_map/ppermute | solution.py:34
  70.0 22.1 %collective-permute-start.18 = (bf16[48,1536]{1,0:T(8,128)(2,1)S(1)}, bf16[48,1536]{1,0:T(8,128)(2,1)S(1)}, u32[]{:S(2)}, u32[]{:S(2)}) collective-permute-start(bf16[48,1536]{1,0:T(8,128)(2,1)S(1)} %constant_dynamic-slice_fusion.1), channel_id=1, source_target_pairs={{0,2},{1,3},{2,0},{3,1},{4,6},{5,7},{6,4},{7,5},{8,10},{9,11},{10,... | collective-permute-start | bytes 442376 | tf_op jit(solution)/shard_map/ppermute | solution.py:34
  71.4 22.5 %collective-permute-start.19 = (bf16[48,1536]{1,0:T(8,128)(2,1)S(1)}, bf16[48,1536]{1,0:T(8,128)(2,1)S(1)}, u32[]{:S(2)}, u32[]{:S(2)}) collective-permute-start(bf16[48,1536]{1,0:T(8,128)(2,1)S(1)} %constant_dynamic-slice_fusion.1), channel_id=1, source_target_pairs={{0,3},{1,0},{2,1},{3,2},{4,7},{5,4},{6,5},{7,6},{8,11},{9,8},{10,9... | collective-permute-start | bytes 442376 | tf_op jit(solution)/shard_map/ppermute | solution.py:34
  94.9 106.1 %all-gather.11.cloned.1.call-start = ((), (), s32[]{:S(2)}) async-start(), calls=%async_computation.3 | async-start | bytes 5750784 | tf_op jit(solution)/shard_map/all_gather | solution.py:406
  102.3 14.5 %collective-permute-start.28 = (bf16[48,1536]{1,0:T(8,128)(2,1)S(1)}, bf16[48,1536]{1,0:T(8,128)(2,1)S(1)}, u32[]{:S(2)}, u32[]{:S(2)}) collective-permute-start(bf16[48,1536]{1,0:T(8,128)(2,1)S(1)} %constant_dynamic-slice_fusion), channel_id=1, source_target_pairs={{0,1},{1,2},{2,3},{3,0},{4,5},{5,6},{6,7},{7,4},{8,9},{9,10},{10,1... | collective-permute-start | bytes 442376 | tf_op jit(solution)/shard_map/ppermute | solution.py:34
  102.3 15.9 %collective-permute-start.29 = (bf16[48,1536]{1,0:T(8,128)(2,1)S(1)}, bf16[48,1536]{1,0:T(8,128)(2,1)S(1)}, u32[]{:S(2)}, u32[]{:S(2)}) collective-permute-start(bf16[48,1536]{1,0:T(8,128)(2,1)S(1)} %constant_dynamic-slice_fusion), channel_id=1, source_target_pairs={{0,2},{1,3},{2,0},{3,1},{4,6},{5,7},{6,4},{7,5},{8,10},{9,11},{10,... | collective-permute-start | bytes 442376 | tf_op jit(solution)/shard_map/ppermute | solution.py:34
  104.0 14.2 %collective-permute-start.30 = (bf16[48,1536]{1,0:T(8,128)(2,1)S(1)}, bf16[48,1536]{1,0:T(8,128)(2,1)S(1)}, u32[]{:S(2)}, u32[]{:S(2)}) collective-permute-start(bf16[48,1536]{1,0:T(8,128)(2,1)S(1)} %constant_dynamic-slice_fusion), channel_id=1, source_target_pairs={{0,3},{1,0},{2,1},{3,2},{4,7},{5,4},{6,5},{7,6},{8,11},{9,8},{10,9... | collective-permute-start | bytes 442376 | tf_op jit(solution)/shard_map/ppermute | solution.py:34
  113.7 13.6 %collective-permute-start.11 = (bf16[224,384]{1,0:T(8,128)(2,1)}, bf16[224,384]{1,0:T(8,128)(2,1)S(1)}, u32[]{:S(2)}, u32[]{:S(2)}) collective-permute-start(bf16[224,384]{1,0:T(8,128)(2,1)} %get-tuple-element.34.a0), channel_id=1, source_target_pairs={{0,1},{1,2},{2,3},{3,0},{4,5},{5,6},{6,7},{7,4},{8,9},{9,10},{10,1... | collective-permute-start | bytes 516104 | tf_op jit(solution)/shard_map/ppermute | solution.py:34
  113.7 15.6 %collective-permute-start.12 = (bf16[224,384]{1,0:T(8,128)(2,1)}, bf16[224,384]{1,0:T(8,128)(2,1)S(1)}, u32[]{:S(2)}, u32[]{:S(2)}) collective-permute-start(bf16[224,384]{1,0:T(8,128)(2,1)} %get-tuple-element.34.a0), channel_id=1, source_target_pairs={{0,2},{1,3},{2,0},{3,1},{4,6},{5,7},{6,4},{7,5},{8,10},{9,11},{10,... | collective-permute-start | bytes 516104 | tf_op jit(solution)/shard_map/ppermute | solution.py:34
  116.8 14.0 %collective-permute-start.13 = (bf16[224,384]{1,0:T(8,128)(2,1)}, bf16[224,384]{1,0:T(8,128)(2,1)S(1)}, u32[]{:S(2)}, u32[]{:S(2)}) collective-permute-start(bf16[224,384]{1,0:T(8,128)(2,1)} %get-tuple-element.34.a0), channel_id=1, source_target_pairs={{0,3},{1,0},{2,1},{3,2},{4,7},{5,4},{6,5},{7,6},{8,11},{9,8},{10,9... | collective-permute-start | bytes 516104 | tf_op jit(solution)/shard_map/ppermute | solution.py:34
  139.5 7.5 %collective-permute-start.14 = (bf16[224,384]{1,0:T(8,128)(2,1)}, bf16[224,384]{1,0:T(8,128)(2,1)S(1)}, u32[]{:S(2)}, u32[]{:S(2)}) collective-permute-start(bf16[224,384]{1,0:T(8,128)(2,1)} %get-tuple-element.36.a0), channel_id=1, source_target_pairs={{0,1},{1,2},{2,3},{3,0},{4,5},{5,6},{6,7},{7,4},{8,9},{9,10},{10,1... | collective-permute-start | bytes 516104 | tf_op jit(solution)/shard_map/ppermute | solution.py:34
  139.5 15.4 %collective-permute-start.15 = (bf16[224,384]{1,0:T(8,128)(2,1)}, bf16[224,384]{1,0:T(8,128)(2,1)S(1)}, u32[]{:S(2)}, u32[]{:S(2)}) collective-permute-start(bf16[224,384]{1,0:T(8,128)(2,1)} %get-tuple-element.36.a0), channel_id=1, source_target_pairs={{0,2},{1,3},{2,0},{3,1},{4,6},{5,7},{6,4},{7,5},{8,10},{9,11},{10,... | collective-permute-start | bytes 516104 | tf_op jit(solution)/shard_map/ppermute | solution.py:34
  141.4 14.6 %collective-permute-start.16 = (bf16[224,384]{1,0:T(8,128)(2,1)}, bf16[224,384]{1,0:T(8,128)(2,1)S(1)}, u32[]{:S(2)}, u32[]{:S(2)}) collective-permute-start(bf16[224,384]{1,0:T(8,128)(2,1)} %get-tuple-element.36.a0), channel_id=1, source_target_pairs={{0,3},{1,0},{2,1},{3,2},{4,7},{5,4},{6,5},{7,6},{8,11},{9,8},{10,9... | collective-permute-start | bytes 516104 | tf_op jit(solution)/shard_map/ppermute | solution.py:34
  164.2 6.9 %collective-permute-start.20 = (bf16[192,384]{1,0:T(8,128)(2,1)}, bf16[192,384]{1,0:T(8,128)(2,1)S(1)}, u32[]{:S(2)}, u32[]{:S(2)}) collective-permute-start(bf16[192,384]{1,0:T(8,128)(2,1)} %get-tuple-element.43.a0), channel_id=1, source_target_pairs={{0,1},{1,2},{2,3},{3,0},{4,5},{5,6},{6,7},{7,4},{8,9},{9,10},{10,1... | collective-permute-start | bytes 442376 | tf_op jit(solution)/shard_map/ppermute | solution.py:34
  164.2 13.4 %collective-permute-start.21 = (bf16[192,384]{1,0:T(8,128)(2,1)}, bf16[192,384]{1,0:T(8,128)(2,1)S(1)}, u32[]{:S(2)}, u32[]{:S(2)}) collective-permute-start(bf16[192,384]{1,0:T(8,128)(2,1)} %get-tuple-element.43.a0), channel_id=1, source_target_pairs={{0,2},{1,3},{2,0},{3,1},{4,6},{5,7},{6,4},{7,5},{8,10},{9,11},{10,... | collective-permute-start | bytes 442376 | tf_op jit(solution)/shard_map/ppermute | solution.py:34
  166.6 13.6 %collective-permute-start.22 = (bf16[192,384]{1,0:T(8,128)(2,1)}, bf16[192,384]{1,0:T(8,128)(2,1)S(1)}, u32[]{:S(2)}, u32[]{:S(2)}) collective-permute-start(bf16[192,384]{1,0:T(8,128)(2,1)} %get-tuple-element.43.a0), channel_id=1, source_target_pairs={{0,3},{1,0},{2,1},{3,2},{4,7},{5,4},{6,5},{7,6},{8,11},{9,8},{10,9... | collective-permute-start | bytes 442376 | tf_op jit(solution)/shard_map/ppermute | solution.py:34
  198.2 7.7 %collective-permute-start.26 = (bf16[192,384]{1,0:T(8,128)(2,1)}, bf16[192,384]{1,0:T(8,128)(2,1)S(1)}, u32[]{:S(2)}, u32[]{:S(2)}) collective-permute-start(bf16[192,384]{1,0:T(8,128)(2,1)} %shard_map.100.a0), channel_id=1, source_target_pairs={{0,2},{1,3},{2,0},{3,1},{4,6},{5,7},{6,4},{7,5},{8,10},{9,11},{10,... | collective-permute-start | bytes 442376 | tf_op jit(solution)/shard_map/ppermute | solution.py:34
  199.1 14.8 %collective-permute-start.27 = (bf16[192,384]{1,0:T(8,128)(2,1)}, bf16[192,384]{1,0:T(8,128)(2,1)S(1)}, u32[]{:S(2)}, u32[]{:S(2)}) collective-permute-start(bf16[192,384]{1,0:T(8,128)(2,1)} %shard_map.100.a0), channel_id=1, source_target_pairs={{0,3},{1,0},{2,1},{3,2},{4,7},{5,4},{6,5},{7,6},{8,11},{9,8},{10,9... | collective-permute-start | bytes 442376 | tf_op jit(solution)/shard_map/ppermute | solution.py:34
  233.6 6.4 %collective-permute-start.34 = (bf16[192,384]{1,0:T(8,128)(2,1)}, bf16[192,384]{1,0:T(8,128)(2,1)S(1)}, u32[]{:S(2)}, u32[]{:S(2)}) collective-permute-start(bf16[192,384]{1,0:T(8,128)(2,1)} %shard_map.102.a0), channel_id=1, source_target_pairs={{0,2},{1,3},{2,0},{3,1},{4,6},{5,7},{6,4},{7,5},{8,10},{9,11},{10,... | collective-permute-start | bytes 442376 | tf_op jit(solution)/shard_map/ppermute | solution.py:34
  234.4 13.4 %collective-permute-start.35 = (bf16[192,384]{1,0:T(8,128)(2,1)}, bf16[192,384]{1,0:T(8,128)(2,1)S(1)}, u32[]{:S(2)}, u32[]{:S(2)}) collective-permute-start(bf16[192,384]{1,0:T(8,128)(2,1)} %shard_map.102.a0), channel_id=1, source_target_pairs={{0,3},{1,0},{2,1},{3,2},{4,7},{5,4},{6,5},{7,6},{8,11},{9,8},{10,9... | collective-permute-start | bytes 442376 | tf_op jit(solution)/shard_map/ppermute | solution.py:34
  256.2 13.7 %all-to-all-start = ((bf16[8,8,1024]{2,1,0:T(8,128)(2,1)}), bf16[8,8,1024]{2,1,0:T(8,128)(2,1)S(1)}, u32[]{:S(2)}, u32[]{:S(2)}) async-start(bf16[8,8,1024]{2,1,0:T(8,128)(2,1)} %bitcast.43), calls=%async_computation | async-start | bytes 262144 | tf_op jit(solution)/shard_map/all_to_all | solution.py:468
  (41 other events, 302.5 us)
Sparse Core Ops, SparseCore 0:
  26.5 39.1 all-gather.6
  95.0 39.0 all-gather.8
  136.6 40.5 all-gather.10

commit v5 on v2

v5 whole, which is shorter than its diff:
```python
import functools
import math

import jax
import jax.numpy as jnp
from jax import lax
from jax.experimental import pallas as pl
from jax.experimental.pallas import tpu as pltpu
from jax.sharding import PartitionSpec as P

RESIDUAL_BLOCKS = 6
BASE_DILATION = 2
BLOCKS_PER_LOAD = 2
FRAMED_BLOCKS = 4
DIGIT = 128
VMEM_BYTES = 24 * 2**20


def dilation(block):
    return BASE_DILATION * 2**block


def after(cells, *earlier):
    return lax.optimization_barrier((cells,) + earlier)[0]


def after_all(cells, *earlier):
    return list(lax.optimization_barrier(tuple(cells) + earlier)[: len(cells)])


def from_others(cells):
    count = lax.axis_size("trk")
    return [cells] + [
        lax.ppermute(cells, "trk", [(i, (i + k) % count) for i in range(count)])
        for k in range(1, count)
    ]


def halo(cells, width):
    count = lax.axis_size("seq")
    head = cells[:width]
    tail = cells[cells.shape[0] - width :]
    above = lax.ppermute(tail, "seq", [(i, i + 1) for i in range(count - 1)])
    below = lax.ppermute(head, "seq", [(i + 1, i) for i in range(count - 1)])
    return above, below


def group_size(rows, count):
    size = 1
    for g in range(1, count + 1):
        if count % g == 0 and rows % (16 * g) == 0:
            size = g
    return size


def tile_of(channels):
    for width in (512, 256, 384, 128):
        if channels % width == 0:
            return width
    return channels


def dot(a, b):
    return jnp.dot(a, b, preferred_element_type=jnp.float32)


def dot_last(a, b):
    return lax.dot_general(a, b, (((1,), (1,)), ((), ())), preferred_element_type=jnp.float32)


def gelu(x):
    cubic = x + 0.044715 * (x * x * x)
    return 0.5 * x * (1.0 + jnp.tanh(math.sqrt(2.0 / math.pi) * cubic))


def pack(act):
    half = act.shape[0] // 2
    return jnp.concatenate([act[:half], act[half:]], axis=1)


def unpack(cells):
    half = cells.shape[1] // 2
    return jnp.concatenate([cells[:, :half], cells[:, half:]], axis=0)


class Copies:
    def __init__(self, sems):
        self.sems = sems
        self.used = 0

    def start(self, source, target):
        copy = pltpu.make_async_copy(source, target, self.sems.at[self.used])
        self.used += 1
        copy.start()
        return copy


def wait(copies):
    for copy in copies:
        copy.wait()


def columns(tile, width):
    return pl.ds(tile * width, width)


def start_acts(copies, acts, raw):
    return [copies.start(act, raw.at[j]) for j, act in enumerate(acts)]


def start_projection(copies, load, part, raw):
    quarters, per_block, share, channels = raw.shape
    width = tile_of(channels)
    tiles = []
    for c in range(channels // width):
        tiles.append(
            [
                copies.start(
                    load.at[
                        pl.ds(part * per_block, per_block), pl.ds(j * share, share), columns(c, width)
                    ],
                    raw.at[j, :, :, columns(c, width)],
                )
                for j in range(quarters)
            ]
        )
    return tiles


def start_trunk(copies, trunk, margin, target):
    rows, channels = target.shape
    width = tile_of(channels)
    return [
        copies.start(trunk.at[pl.ds(margin, rows), columns(c, width)], target.at[:, columns(c, width)])
        for c in range(channels // width)
    ]


def start_taps(copies, conv_in, block, target):
    half = target.shape[1] // 2
    return [
        [
            copies.start(conv_in.at[block, t, pl.ds(h * half, half)], target.at[t, pl.ds(h * half, half)])
            for h in range(2)
        ]
        for t in range(3)
    ]


def project(acts, weights, trunk, bias, c):
    channels = trunk.shape[1]
    cols = columns(c, tile_of(channels))
    part = dot(acts, weights[:, :, :, cols].reshape(-1, tile_of(channels)))
    total = trunk[:, cols].astype(jnp.float32) + bias[:, cols].astype(jnp.float32) + part
    trunk[:, cols] = total.astype(jnp.bfloat16)


def project_all(raw, act_copies, weights, weight_copies, trunk, trunk_copies, bias):
    wait(act_copies)
    acts = jnp.concatenate([unpack(raw[j]) for j in range(raw.shape[0])], axis=1)
    for c in range(len(weight_copies)):
        wait(weight_copies[c])
        trunk_copies[c].wait()
        project(acts, weights, trunk, bias, c)


def convolve(trunk, rows, taps, tap_copies, bias, step, act_ref):
    cells = trunk[:rows]
    sums = []
    for t in range(3):
        wait(tap_copies[t])
        sums.append(dot_last(cells, taps[t]))
    inner = sums[1] + pltpu.roll(sums[0], step, 0) + pltpu.roll(sums[2], rows - step, 0)
    keep = 2 * act_ref.shape[0]
    margin = (rows - keep) // 2
    inner = inner[margin : margin + keep] + bias.astype(jnp.float32)
    act_ref[...] = pack(gelu(inner).astype(jnp.bfloat16))


def first_kernel(
    step, order_ref, c0, c1, c2, c3, conv_in, bias_ref, act_ref, trunk_out, pbias_out, trunk, taps, sems
):
    copies = Copies(sems)
    width = c0.shape[1]
    cells = [
        copies.start(cell, trunk.at[:, pl.ds(pl.multiple_of(order_ref[k] * width, 128), width)])
        for k, cell in enumerate((c0, c1, c2, c3))
    ]
    tap_copies = start_taps(copies, conv_in, 0, taps)
    wait(cells)
    rows = trunk_out.shape[0]
    out = [
        copies.start(trunk.at[pl.ds(0, rows)], trunk_out),
        copies.start(trunk.at[pl.ds(rows, pbias_out.shape[0])], pbias_out),
    ]
    convolve(trunk, rows, taps, tap_copies, bias_ref[0:1], step, act_ref)
    wait(out)


ANY = pl.BlockSpec(memory_space=pl.ANY)
HBM = pl.BlockSpec(memory_space=pltpu.HBM)
SMEM = pl.BlockSpec(memory_space=pltpu.SMEM)
VMEM = pl.BlockSpec(memory_space=pltpu.VMEM)
BF16 = jnp.bfloat16


def shape(*dims):
    return jax.ShapeDtypeStruct(dims, BF16)


def kernel_call(body, ins, outs, out_specs, specs, scratch, flops, moved, special=0):
    return pl.pallas_call(
        body,
        in_specs=specs,
        out_specs=out_specs,
        out_shape=outs,
        scratch_shapes=scratch + [pltpu.SemaphoreType.DMA((48,))],
        compiler_params=pltpu.CompilerParams(vmem_limit_bytes=VMEM_BYTES),
        cost_estimate=pl.CostEstimate(
            flops=flops, bytes_accessed=2 * moved, transcendentals=special
        ),
    )(*ins)


def first_conv(cells, rows, order, conv_in, conv_bias, step):
    _, _, hidden, channels = conv_in.shape
    total = cells[0].shape[0]
    return kernel_call(
        functools.partial(first_kernel, step),
        (order, *cells, conv_in, conv_bias),
        [shape(rows // 2, 2 * hidden), shape(rows, channels), shape(total - rows, channels)],
        [VMEM, ANY, ANY],
        [SMEM] + [ANY] * len(cells) + [HBM, VMEM],
        [pltpu.VMEM((total, channels), BF16), pltpu.VMEM((3, hidden, channels), BF16)],
        6 * rows * hidden * channels,
        3 * hidden * channels + 2 * rows * channels,
        rows * hidden,
    )


def fused_kernel(
    block, part, edge_ref, a0, a1, a2, a3, load, trunk_in, pbias_ref, conv_in, bias_ref,
    act_ref, trunk_out, raw, weights, trunk, taps, sems
):
    copies = Copies(sems)
    act_copies = start_acts(copies, (a0, a1, a2, a3), raw)
    weight_copies = start_projection(copies, load, part, weights)
    trunk_copies = start_trunk(copies, trunk_in, 0, trunk)
    tap_copies = start_taps(copies, conv_in, block + 1, taps)
    pbias = pbias_ref[block : block + 1]
    project_all(raw, act_copies, weights, weight_copies, trunk, trunk_copies, pbias)
    rows = trunk.shape[0]
    margin = dilation(FRAMED_BLOCKS)

    @pl.when(edge_ref[0] == 1)
    def _():
        trunk[:margin] = jnp.zeros((margin, trunk.shape[1]), BF16)

    @pl.when(edge_ref[1] == 1)
    def _():
        trunk[rows - margin :] = jnp.zeros((margin, trunk.shape[1]), BF16)

    out = copies.start(trunk, trunk_out)
    bias = bias_ref[block + 1 : block + 2]
    convolve(trunk, rows, taps, tap_copies, bias, dilation(block + 1), act_ref)
    out.wait()


def projection_scratch(acts, per_block, share, channels):
    return [
        pltpu.VMEM((len(acts),) + acts[0].shape, BF16),
        pltpu.VMEM((len(acts), per_block, share, channels), BF16),
    ]


def fused(acts, load, part, per_block, share, trunk, pbias, conv_in, conv_bias, block, edge, rows_out):
    rows, channels = trunk.shape
    hidden = conv_in.shape[2]
    return kernel_call(
        functools.partial(fused_kernel, block, part),
        (edge, *acts, load, trunk, pbias, conv_in, conv_bias),
        [shape(rows_out // 2, 2 * hidden), shape(rows, channels)],
        [VMEM, ANY],
        [SMEM] + [ANY] * len(acts) + [HBM, ANY, VMEM, HBM, VMEM],
        projection_scratch(acts, per_block, share, channels)
        + [pltpu.VMEM((rows, channels), BF16), pltpu.VMEM((3, hidden, channels), BF16)],
        14 * rows * hidden * channels,
        7 * hidden * channels + 2 * rows * channels,
        rows * hidden,
    )


def projection_kernel(block, part, a0, a1, a2, a3, load, trunk_in, pbias_ref, trunk, raw, weights, sems):
    copies = Copies(sems)
    act_copies = start_acts(copies, (a0, a1, a2, a3), raw)
    weight_copies = start_projection(copies, load, part, weights)
    margin = (trunk_in.shape[0] - trunk.shape[0]) // 2
    trunk_copies = start_trunk(copies, trunk_in, margin, trunk)
    pbias = pbias_ref[block : block + 1]
    project_all(raw, act_copies, weights, weight_copies, trunk, trunk_copies, pbias)


def projection(acts, load, part, per_block, share, trunk, pbias, block):
    channels = trunk.shape[1]
    rows, hidden = 2 * acts[0].shape[0], acts[0].shape[1] // 2
    return kernel_call(
        functools.partial(projection_kernel, block, part),
        (*acts, load, trunk, pbias),
        shape(rows, channels),
        VMEM,
        [ANY] * len(acts) + [HBM, ANY, VMEM],
        projection_scratch(acts, per_block, share, channels),
        8 * rows * hidden * channels,
        4 * hidden * channels + 2 * rows * channels,
    )


def conv_kernel(block, above, trunk_in, below, conv_in, bias_ref, act_ref, trunk, taps, sems):
    copies = Copies(sems)
    step = dilation(block)
    rows = trunk_in.shape[0]
    cells = [
        copies.start(trunk_in, trunk.at[pl.ds(step, rows)]),
        copies.start(above, trunk.at[pl.ds(0, step)]),
        copies.start(below, trunk.at[pl.ds(step + rows, step)]),
    ]
    tap_copies = start_taps(copies, conv_in, block, taps)
    wait(cells)
    bias = bias_ref[block : block + 1]
    convolve(trunk, trunk.shape[0], taps, tap_copies, bias, step, act_ref)


def conv(above, trunk, below, conv_in, block, conv_bias):
    rows, channels = trunk.shape
    hidden = conv_in.shape[2]
    frame = rows + 2 * dilation(block)
    return kernel_call(
        functools.partial(conv_kernel, block),
        (above, trunk, below, conv_in, conv_bias),
        shape(rows // 2, 2 * hidden),
        VMEM,
        [ANY] * 3 + [HBM, VMEM],
        [pltpu.VMEM((frame, channels), BF16), pltpu.VMEM((3, hidden, channels), BF16)],
        6 * frame * hidden * channels,
        3 * hidden * channels + frame * channels,
        rows * hidden,
    )


def head_kernel(
    block, part, a0, a1, a2, a3, load, trunk_in, pbias_ref, head_ref, hbias_ref, onehot_ref,
    cover_out, gene_ref, raw, weights, trunk, head_w, cover, sems
):
    copies = Copies(sems)
    act_copies = start_acts(copies, (a0, a1, a2, a3), raw)
    weight_copies = start_projection(copies, load, part, weights)
    trunk_copies = start_trunk(copies, trunk_in, 0, trunk)
    channels, tracks = head_w.shape
    width = tile_of(tracks)
    band = channels // 4
    head_copies = [
        [
            copies.start(
                head_ref.at[pl.ds(r * band, band), columns(c, width)],
                head_w.at[pl.ds(r * band, band), columns(c, width)],
            )
            for r in range(4)
        ]
        for c in range(tracks // width)
    ]
    pbias = pbias_ref[block : block + 1]
    project_all(raw, act_copies, weights, weight_copies, trunk, trunk_copies, pbias)
    out = []
    for c in range(tracks // width):
        cols = columns(c, width)
        wait(head_copies[c])
        x = dot(trunk[...], head_w[:, cols]) + hbias_ref[:, cols].astype(jnp.float32)
        tile = (jnp.maximum(x, 0.0) + jnp.log1p(jnp.exp(-jnp.abs(x)))).astype(BF16)
        cover[:, cols] = tile
        out.append(copies.start(cover.at[:, cols], cover_out.at[:, cols]))
        gene_ref[:, cols] = dot(onehot_ref[...], tile).astype(BF16)
    wait(out)


def head(acts, load, part, per_block, share, trunk, pbias, block, head_weight, head_bias, onehot):
    rows, channels = trunk.shape
    hidden = acts[0].shape[1] // 2
    tracks = head_weight.shape[1]
    genes = onehot.shape[0]
    return kernel_call(
        functools.partial(head_kernel, block, part),
        (*acts, load, trunk, pbias, head_weight, head_bias, onehot),
        [shape(rows, tracks), shape(genes, tracks)],
        [ANY, VMEM],
        [ANY] * len(acts) + [HBM, ANY, VMEM, HBM, VMEM, VMEM],
        projection_scratch(acts, per_block, share, channels)
        + [
            pltpu.VMEM((rows, channels), BF16),
            pltpu.VMEM((channels, tracks), BF16),
            pltpu.VMEM((rows, tracks), BF16),
        ],
        8 * rows * hidden * channels + 2 * rows * channels * tracks,
        4 * hidden * channels + rows * channels + channels * tracks,
        2 * rows * tracks,
    )


def exon_digits(exon_bins, channels):
    digits = jnp.concatenate([exon_bins >> 7, exon_bins & (DIGIT - 1)], axis=1)
    genes, width = digits.shape
    return jnp.pad(digits.astype(jnp.bfloat16), ((0, -genes % 16), (0, channels - width)))


def exon_lists(rows, genes, entries):
    digits = rows[:, :genes, : 2 * entries].astype(jnp.int32)
    lists = digits[:, :, :entries] * DIGIT + digits[:, :, entries:]
    return lists.reshape(-1, entries)


def exon_onehot(gene_block, first_bin, width_now):
    exon_matches = (
        gene_block[:, :, None] - first_bin == jnp.arange(width_now, dtype=jnp.int32)[None, None, :]
    )
    return jnp.sum(exon_matches.astype(jnp.float32), axis=1).astype(jnp.bfloat16)


def shards(
    trunk_input, conv_in, conv_bias, conv_out, projection_bias, head_weight, head_bias, exon_bins
):
    quarters = lax.axis_size("trk")
    place = lax.axis_index("trk")
    count = lax.axis_size("seq")
    lane = lax.axis_index("seq")
    bin_rows, channels_here = trunk_input.shape
    blocks, hidden, channels = conv_out.shape
    genes_here, entries = exon_bins.shape

    load_rows = BLOCKS_PER_LOAD * hidden
    size = group_size(load_rows, count)
    share = load_rows // size
    per_block = hidden // share
    groups = [[g * size + i for i in range(size)] for g in range(count // size)]
    mine = lax.rem(lane, size)
    packed = size == count and 2 * entries <= channels

    def column(load):
        first = load * BLOCKS_PER_LOAD
        flat = conv_out[first : first + BLOCKS_PER_LOAD].reshape(load_rows, channels)
        return lax.dynamic_slice_in_dim(flat, mine * share, share, 0)

    def gather(parts):
        return lax.all_gather(
            jnp.concatenate(parts, axis=0), "seq", axis=0, tiled=False, axis_index_groups=groups
        )

    margin = dilation(FRAMED_BLOCKS)
    frame = bin_rows + 2 * margin
    order = lax.rem(place - jnp.arange(quarters, dtype=jnp.int32) + quarters, quarters)
    edge = jnp.stack([lane == 0, lane == count - 1]).astype(jnp.int32)

    above, below = halo(trunk_input, margin)
    first_column = from_others(column(0))
    loads = [gather(after_all(first_column, above, below))]
    own = jnp.concatenate(
        [above, trunk_input, below, jnp.pad(projection_bias, ((0, -blocks % 16), (0, 0)))], axis=0
    )
    own = after(own, *first_column)
    cells = from_others(own)
    second = from_others(after(column(1), *cells))

    act, trunk, biases = first_conv(cells, frame, order, conv_in, conv_bias, dilation(0))

    onehot = None
    for block in range(RESIDUAL_BLOCKS):
        others = from_others(act)
        if block == 0:
            third = from_others(after(column(2), *others))
        if block == 1:
            loads.append(gather(after_all(second, act)))
        if block == 2:
            tail = [exon_digits(exon_bins, channels)] if packed else []
            loads.append(gather(after_all(third, act) + tail))
        if block == 4:
            if packed:
                gene_lists = exon_lists(loads[2][:, quarters * share :], genes_here, entries)
            else:
                gene_lists = lax.all_gather(exon_bins, "seq", axis=0, tiled=True)
            onehot = exon_onehot(gene_lists, lane * bin_rows, bin_rows)
        load = loads[block // BLOCKS_PER_LOAD]
        part = block % BLOCKS_PER_LOAD
        where = (load, part, per_block, share, trunk, biases)
        later = block + 1
        if later < FRAMED_BLOCKS:
            rows_out = frame if later < FRAMED_BLOCKS - 1 else bin_rows
            act, trunk = fused(others, *where, conv_in, conv_bias, block, edge, rows_out)
        elif later < RESIDUAL_BLOCKS:
            trunk = projection(others, *where, block)
            above, below = halo(trunk, dilation(later))
            act = conv(above, trunk, below, conv_in, later, conv_bias)
        else:
            coverage, partial = head(
                others, *where, block, head_weight, head_bias[None, :], onehot
            )

    parts = lax.all_to_all(
        partial.reshape(count, genes_here, partial.shape[1]), "seq", 0, 0, tiled=False
    )
    gene_sum = jnp.sum(parts.astype(jnp.float32), axis=0)
    counts = jnp.sum((exon_bins >= 0).astype(jnp.float32), axis=1)
    gene_cov = gene_sum / counts[:, None]
    return (coverage, gene_cov)


def solution(mesh):
    in_specs = (
        P("seq", "trk"),
        P(None, None, "trk", None),
        P(None, "trk"),
        P(None, "trk", None),
        P(None, "trk"),
        P(None, "trk"),
        P("trk"),
        P("seq", None),
    )
    out_specs = (P("seq", "trk"), P("seq", "trk"))
    return jax.shard_map(shards, mesh=mesh, in_specs=in_specs, out_specs=out_specs, check_vma=False)
```

time: 296 us -> 289 us (0.976); the launches traced: 291 us -> 288 us
  matrix products: 62.4 us -> 0 us
  Pallas kernels: 0 us -> 46.9 us
  local copies, waits for them, and re-layouts: 21 us -> 43.8 us
  starting transfers between devices: 61.8 us -> 53.7 us
  other arithmetic: 9.77 us -> 5.81 us
  waiting for transfers between devices: 121 us -> 124 us
    dot_general x43 -> x0, matrix products: 62.4 us -> none  [the longest x18 31.1 us: contract_last(): lax.dot_general(rows, kernel, (((1,), (1,)), ((), ())), preferred_element...]
    pallas_call x0 -> x9, Pallas kernels: none -> 46.9 us  [kernel_call(): pl.pallas_call(body, in_specs=specs, out_specs=out_specs, out_shape=outs,...]
    unnamed x76 -> x48, local copies, waits for them, and re-layouts: 4.39 us -> 38.9 us
    slice x3 -> x2, local copies, waits for them, and re-layouts: 8.69 us -> 0.04 us  [halo(): head = cells[:width]]
    ppermute x3, waiting for transfers between devices: 0.01 us -> 6.97 us  [halo(): below = lax.ppermute(head, 'seq', [(i + 1, i) for i in range(count - 1)])]
    ppermute x30, starting transfers between devices: 40.5 us -> 34.4 us  [from_others(): lax.ppermute(cells, 'trk', [(i, (i + k) % count) for i in range(count)])]
    ppermute x30, waiting for transfers between devices: 115 us -> 111 us  [from_others(): lax.ppermute(cells, 'trk', [(i, (i + k) % count) for i in range(count)])]
  transfers between devices with their start and end apart: 40 -> 40, of which waited for: 24 -> 26; matrix products, arithmetic and copies ran while one was open for 24% -> 1% of each run, Pallas kernels for 0% -> 11%
where the time goes in v5:
time: 289 us; the launch traced here: 288 us
  waiting for transfers between devices  124 us (43%)
  starting transfers between devices  53.7 us (19%)
  Pallas kernels  46.9 us (16%)
  local copies, waits for them, and re-layouts  43.8 us (15%)
  between operations  14.2 us (5%)
  other arithmetic  5.81 us (2%)
    ppermute x30, waiting for transfers between devices, from_others(): lax.ppermute(cells, 'trk', [(i, (i + k) % count) for i in range(count)])  111 us
    pallas_call x9, Pallas kernels, kernel_call(): pl.pallas_call(body, in_specs=specs, out_specs=out_specs, out_shape=outs,...  46.9 us
    unnamed x48, local copies, waits for them, and re-layouts  38.9 us
    ppermute x30, starting transfers between devices, from_others(): lax.ppermute(cells, 'trk', [(i, (i + k) % count) for i in range(count)])  34.4 us
    all_to_all x1, starting transfers between devices, shards(): lax.all_to_all(partial.reshape(count, genes_here, partial.shape[1]), 'seq...  8.32 us
    ppermute x3, starting transfers between devices, halo(): above = lax.ppermute(tail, 'seq', [(i, i + 1) for i in range(count - 1)])  6.99 us
    ppermute x3, waiting for transfers between devices, halo(): below = lax.ppermute(head, 'seq', [(i + 1, i) for i in range(count - 1)])  6.97 us
  transfers between devices with their start and end apart: 40, of which 26 were waited for; matrix products, arithmetic and copies ran while one was open for 1% of the time, Pallas kernels for 11%

profile of v5, /device:TPU:8, one launch (start us, length us, event | category | flops | bytes accessed | tf_op | source)
XLA Modules:
  0.0 288.5 jit_solution(13549564355850558654)
XLA Ops:
  7.2 3.3 %fusion.12 = (bf16[2,192,1536]{2,1,0:T(8,128)(2,1)S(1)}, bf16[2,192,1536]{2,1,0:T(8,128)(2,1)S(1)}, bf16[2,192,1536]{2,1,0:T(8,128)(2,1)}) fusion(bf16[6,192,1536]{2,1,0:T(8,128)(2,1)} %param.11), kind=kLoop, calls=%fused_computation.37 | loop fusion | bytes 7077888 | tf_op jit(solution)/shard_map/slice | solution.py:448
  31.3 7.4 %collective-permute-done.5.c1 = bf16[464,384]{1,0:T(8,128)(2,1)S(1)} collective-permute-done((bf16[464,384]{1,0:T(8,128)(2,1)S(1)}, bf16[464,384]{1,0:T(8,128)(2,1)S(1)}, u32[]{:S(2)}, u32[]{:S(2)}) %collective-permute-start.5) | collective-permute-done | bytes 356384 | tf_op jit(solution)/shard_map/ppermute | solution.py:34
  38.7 19.8 %collective-permute-done.6.c2 = bf16[464,384]{1,0:T(8,128)(2,1)S(1)} collective-permute-done((bf16[464,384]{1,0:T(8,128)(2,1)S(1)}, bf16[464,384]{1,0:T(8,128)(2,1)S(1)}, u32[]{:S(2)}, u32[]{:S(2)}) %collective-permute-start.6) | collective-permute-done | bytes 356384 | tf_op jit(solution)/shard_map/ppermute | solution.py:34
  59.6 4.1 %copy-done = bf16[6,3,192,1536]{3,2,1,0:T(8,128)(2,1)S(1)} copy-done((bf16[6,3,192,1536]{3,2,1,0:T(8,128)(2,1)S(1)}, bf16[6,3,192,1536]{3,2,1,0:T(8,128)(2,1)}, u32[]{:S(2)}) %copy-start) | copy-done | bytes 10616856
  63.7 3.4 %shard_map.95 = (bf16[224,384]{1,0:T(8,128)(2,1)S(1)}, bf16[448,1536]{1,0:T(8,128)(2,1)S(1)}, bf16[16,1536]{1,0:T(8,128)(2,1)S(1)}) custom-call(s32[4]{0:T(128)S(1)} %compare_select_fusion.order_ref, bf16[464,384]{1,0:T(8,128)(2,1)S(1)} %fusion.1.c0, bf16[464,384]{1,0:T(8,128)(2,1)S(1)} %collective-permute-done.5.c1, ...), custom_call_target="tpu_custom_call" | custom-call | flops 792723456 | bytes 4521984 | tf_op jit(solution)/shard_map/pallas_call | solution.py:212
  77.4 6.8 %collective-permute-done.9.a2 = bf16[224,384]{1,0:T(8,128)(2,1)S(1)} collective-permute-done((bf16[224,384]{1,0:T(8,128)(2,1)S(1)}, bf16[224,384]{1,0:T(8,128)(2,1)S(1)}, u32[]{:S(2)}, u32[]{:S(2)}) %collective-permute-start.9) | collective-permute-done | bytes 172064 | tf_op jit(solution)/shard_map/ppermute | solution.py:34
  84.2 7.9 %collective-permute-done.10.a3 = bf16[224,384]{1,0:T(8,128)(2,1)S(1)} collective-permute-done((bf16[224,384]{1,0:T(8,128)(2,1)S(1)}, bf16[224,384]{1,0:T(8,128)(2,1)S(1)}, u32[]{:S(2)}, u32[]{:S(2)}) %collective-permute-start.10) | collective-permute-done | bytes 172064 | tf_op jit(solution)/shard_map/ppermute | solution.py:34
  92.1 4.0 %copy-done.1 = bf16[6,3,192,1536]{3,2,1,0:T(8,128)(2,1)S(1)} copy-done((bf16[6,3,192,1536]{3,2,1,0:T(8,128)(2,1)S(1)}, bf16[6,3,192,1536]{3,2,1,0:T(8,128)(2,1)}, u32[]{:S(2)}) %copy-start.1) | copy-done | bytes 10616856
  99.8 6.9 %shard_map.96 = (bf16[224,384]{1,0:T(8,128)(2,1)S(1)}, bf16[448,1536]{1,0:T(8,128)(2,1)S(1)}) custom-call(s32[2]{0:T(128)S(1)} %add_convert_fusion.edge_ref, bf16[224,384]{1,0:T(8,128)(2,1)S(1)} %get-tuple-element.29.a0, bf16[224,384]{1,0:T(8,128)(2,1)S(1)} %collective-permute-done.8.a1, bf16[224,384]{1,0:T(8,128)(2,1)S(1)} %collective-permute-done.9.a2, ...), custom_call_target="tpu_custom_call" | custom-call | flops 1849688064 | bytes 6881280 | tf_op jit(solution)/shard_map/pallas_call | solution.py:212
  112.5 3.3 %collective-permute-start.29 = (bf16[48,1536]{1,0:T(8,128)(2,1)S(1)}, bf16[48,1536]{1,0:T(8,128)(2,1)S(1)}, u32[]{:S(2)}, u32[]{:S(2)}) collective-permute-start(bf16[48,1536]{1,0:T(8,128)(2,1)S(1)} %constant_dynamic-slice_fusion), channel_id=1, source_target_pairs={{0,2},{1,3},{2,0},{3,1},{4,6},{5,7},{6,4},{7,5},{8,10},{9,11},{10,... | collective-permute-start | bytes 442376 | tf_op jit(solution)/shard_map/ppermute | solution.py:34
  116.2 9.1 %collective-permute-done.12.a2 = bf16[224,384]{1,0:T(8,128)(2,1)S(1)} collective-permute-done((bf16[224,384]{1,0:T(8,128)(2,1)S(1)}, bf16[224,384]{1,0:T(8,128)(2,1)S(1)}, u32[]{:S(2)}, u32[]{:S(2)}) %collective-permute-start.12) | collective-permute-done | bytes 172064 | tf_op jit(solution)/shard_map/ppermute | solution.py:34
  125.3 4.6 %collective-permute-done.13.a3 = bf16[224,384]{1,0:T(8,128)(2,1)S(1)} collective-permute-done((bf16[224,384]{1,0:T(8,128)(2,1)S(1)}, bf16[224,384]{1,0:T(8,128)(2,1)S(1)}, u32[]{:S(2)}, u32[]{:S(2)}) %collective-permute-start.13) | collective-permute-done | bytes 172064 | tf_op jit(solution)/shard_map/ppermute | solution.py:34
  129.9 4.8 %copy-done.2 = bf16[6,3,192,1536]{3,2,1,0:T(8,128)(2,1)S(1)} copy-done((bf16[6,3,192,1536]{3,2,1,0:T(8,128)(2,1)S(1)}, bf16[6,3,192,1536]{3,2,1,0:T(8,128)(2,1)}, u32[]{:S(2)}) %copy-start.2) | copy-done | bytes 10616856
  137.1 7.4 %shard_map.97 = (bf16[224,384]{1,0:T(8,128)(2,1)S(1)}, bf16[448,1536]{1,0:T(8,128)(2,1)S(1)}) custom-call(s32[2]{0:T(128)S(1)} %add_convert_fusion.edge_ref, bf16[224,384]{1,0:T(8,128)(2,1)S(1)} %get-tuple-element.36.a0, bf16[224,384]{1,0:T(8,128)(2,1)S(1)} %collective-permute-done.11.a1, bf16[224,384]{1,0:T(8,128)(2,1)S(1)} %collective-permute-done.12.a2, ...), custom_call_target="tpu_custom_call" | custom-call | flops 1849688064 | bytes 6881280 | tf_op jit(solution)/shard_map/pallas_call | solution.py:212
  148.6 5.2 %collective-permute-done.14.a1 = bf16[224,384]{1,0:T(8,128)(2,1)S(1)} collective-permute-done((bf16[224,384]{1,0:T(8,128)(2,1)S(1)}, bf16[224,384]{1,0:T(8,128)(2,1)S(1)}, u32[]{:S(2)}, u32[]{:S(2)}) %collective-permute-start.14) | collective-permute-done | bytes 172064 | tf_op jit(solution)/shard_map/ppermute | solution.py:34
  153.8 7.8 %collective-permute-done.15.a2 = bf16[224,384]{1,0:T(8,128)(2,1)S(1)} collective-permute-done((bf16[224,384]{1,0:T(8,128)(2,1)S(1)}, bf16[224,384]{1,0:T(8,128)(2,1)S(1)}, u32[]{:S(2)}, u32[]{:S(2)}) %collective-permute-start.15) | collective-permute-done | bytes 172064 | tf_op jit(solution)/shard_map/ppermute | solution.py:34
  161.7 4.0 %copy-done.3 = bf16[6,3,192,1536]{3,2,1,0:T(8,128)(2,1)S(1)} copy-done((bf16[6,3,192,1536]{3,2,1,0:T(8,128)(2,1)S(1)}, bf16[6,3,192,1536]{3,2,1,0:T(8,128)(2,1)}, u32[]{:S(2)}) %copy-start.3) | copy-done | bytes 10616856
  168.0 8.0 %shard_map.98 = (bf16[192,384]{1,0:T(8,128)(2,1)S(1)}, bf16[448,1536]{1,0:T(8,128)(2,1)S(1)}) custom-call(s32[2]{0:T(128)S(1)} %add_convert_fusion.edge_ref, bf16[224,384]{1,0:T(8,128)(2,1)S(1)} %get-tuple-element.38.a0, bf16[224,384]{1,0:T(8,128)(2,1)S(1)} %collective-permute-done.14.a1, bf16[224,384]{1,0:T(8,128)(2,1)S(1)} %collective-permute-done.15.a2, ...), custom_call_target="tpu_custom_call" | custom-call | flops 1849688064 | bytes 6881280 | tf_op jit(solution)/shard_map/pallas_call | solution.py:212
  176.1 3.4 %collective-permute-start.21 = (bf16[192,384]{1,0:T(8,128)(2,1)S(1)}, bf16[192,384]{1,0:T(8,128)(2,1)S(1)}, u32[]{:S(2)}, u32[]{:S(2)}) collective-permute-start(bf16[192,384]{1,0:T(8,128)(2,1)S(1)} %get-tuple-element.45.a0), channel_id=1, source_target_pairs={{0,2},{1,3},{2,0},{3,1},{4,6},{5,7},{6,4},{7,5},{8,10},{9,11},{10,... | collective-permute-start | bytes 442376 | tf_op jit(solution)/shard_map/ppermute | solution.py:34
  181.7 7.1 %collective-permute-done.21.a2 = bf16[192,384]{1,0:T(8,128)(2,1)S(1)} collective-permute-done((bf16[192,384]{1,0:T(8,128)(2,1)S(1)}, bf16[192,384]{1,0:T(8,128)(2,1)S(1)}, u32[]{:S(2)}, u32[]{:S(2)}) %collective-permute-start.21) | collective-permute-done | bytes 147488 | tf_op jit(solution)/shard_map/ppermute | solution.py:34
  188.8 3.6 %collective-permute-done.22.a3 = bf16[192,384]{1,0:T(8,128)(2,1)S(1)} collective-permute-done((bf16[192,384]{1,0:T(8,128)(2,1)S(1)}, bf16[192,384]{1,0:T(8,128)(2,1)S(1)}, u32[]{:S(2)}, u32[]{:S(2)}) %collective-permute-start.22) | collective-permute-done | bytes 147488 | tf_op jit(solution)/shard_map/ppermute | solution.py:34
  192.4 3.1 %shard_map.99.trunk_in = bf16[384,1536]{1,0:T(8,128)(2,1)S(1)} custom-call(bf16[192,384]{1,0:T(8,128)(2,1)S(1)} %get-tuple-element.45.a0, bf16[192,384]{1,0:T(8,128)(2,1)S(1)} %collective-permute-done.20.a1, bf16[192,384]{1,0:T(8,128)(2,1)S(1)} %collective-permute-done.21.a2, bf16[192,384]{1,0:T(8,128)(2,1)S(1)} %collective-permute-done.22.a3, ...), custom_call_target="tpu_custom_call" | custom-call | flops 905969664 | bytes 4718592 | tf_op jit(solution)/shard_map/pallas_call | solution.py:212
  201.9 4.0 %copy-done.4 = bf16[6,3,192,1536]{3,2,1,0:T(8,128)(2,1)S(1)} copy-done((bf16[6,3,192,1536]{3,2,1,0:T(8,128)(2,1)S(1)}, bf16[6,3,192,1536]{3,2,1,0:T(8,128)(2,1)}, u32[]{:S(2)}) %copy-start.4) | copy-done | bytes 10616856
  205.9 3.6 %shard_map.100.a0 = bf16[192,384]{1,0:T(8,128)(2,1)S(1)} custom-call(bf16[32,1536]{1,0:T(8,128)(2,1)S(1)} %collective-permute-done.23.above, bf16[384,1536]{1,0:T(8,128)(2,1)S(1)} %shard_map.99.trunk_in, bf16[32,1536]{1,0:T(8,128)(2,1)S(1)} %collective-permute-done.24.below, bf16[6,3,192,1536]{3,2,1,0:T(8,128)(2,1)S(1)} %copy-done.4, ...), custom_call_target="tpu_custom_call" | custom-call | flops 792723456 | bytes 3145728 | tf_op jit(solution)/shard_map/pallas_call | solution.py:212
  217.3 7.7 %collective-permute-done.27.a3 = bf16[192,384]{1,0:T(8,128)(2,1)S(1)} collective-permute-done((bf16[192,384]{1,0:T(8,128)(2,1)S(1)}, bf16[192,384]{1,0:T(8,128)(2,1)S(1)}, u32[]{:S(2)}, u32[]{:S(2)}) %collective-permute-start.27) | collective-permute-done | bytes 147488 | tf_op jit(solution)/shard_map/ppermute | solution.py:34
  234.1 3.9 %collective-permute-done.32.below = bf16[64,1536]{1,0:T(8,128)(2,1)S(1)} collective-permute-done((bf16[64,1536]{1,0:T(8,128)(2,1)S(1)}, bf16[64,1536]{1,0:T(8,128)(2,1)S(1)}, u32[]{:S(2)}, u32[]{:S(2)}) %collective-permute-start.32) | collective-permute-done | bytes 196640 | tf_op jit(solution)/shard_map/ppermute | solution.py:44
  238.0 4.0 %copy-done.5 = bf16[6,3,192,1536]{3,2,1,0:T(8,128)(2,1)S(1)} copy-done((bf16[6,3,192,1536]{3,2,1,0:T(8,128)(2,1)S(1)}, bf16[6,3,192,1536]{3,2,1,0:T(8,128)(2,1)}, u32[]{:S(2)}) %copy-start.5) | copy-done | bytes 10616856
  242.0 4.1 %shard_map.102.a0 = bf16[192,384]{1,0:T(8,128)(2,1)S(1)} custom-call(bf16[64,1536]{1,0:T(8,128)(2,1)S(1)} %collective-permute-done.31.above, bf16[384,1536]{1,0:T(8,128)(2,1)S(1)} %shard_map.101.trunk_in, bf16[64,1536]{1,0:T(8,128)(2,1)S(1)} %collective-permute-done.32.below, bf16[6,3,192,1536]{3,2,1,0:T(8,128)(2,1)S(1)} %copy-done.5, ...), custom_call_target="tpu_custom_call" | custom-call | flops 905969664 | bytes 3342336 | tf_op jit(solution)/shard_map/pallas_call | solution.py:212
  252.5 7.8 %collective-permute-done.35.a3 = bf16[192,384]{1,0:T(8,128)(2,1)S(1)} collective-permute-done((bf16[192,384]{1,0:T(8,128)(2,1)S(1)}, bf16[192,384]{1,0:T(8,128)(2,1)S(1)}, u32[]{:S(2)}, u32[]{:S(2)}) %collective-permute-start.35) | collective-permute-done | bytes 147488 | tf_op jit(solution)/shard_map/ppermute | solution.py:34
  260.2 7.1 %shard_map.103 = (bf16[384,1024]{1,0:T(8,128)(2,1)}, bf16[64,1024]{1,0:T(8,128)(2,1)}) custom-call(bf16[192,384]{1,0:T(8,128)(2,1)S(1)} %shard_map.102.a0, bf16[192,384]{1,0:T(8,128)(2,1)S(1)} %collective-permute-done.33.a1, bf16[192,384]{1,0:T(8,128)(2,1)S(1)} %collective-permute-done.34.a2, bf16[192,384]{1,0:T(8,128)(2,1)S(1)} %collective-permute-done.35.a3, ...), custom_call_target="tpu_custom_call" | custom-call | flops 2113929216 | bytes 6684672 | tf_op jit(solution)/shard_map/pallas_call | solution.py:212
  267.4 8.3 %all-to-all-start = ((bf16[8,8,1024]{2,1,0:T(8,128)(2,1)}), bf16[8,8,1024]{2,1,0:T(8,128)(2,1)S(1)}, u32[]{:S(2)}, u32[]{:S(2)}) async-start(bf16[8,8,1024]{2,1,0:T(8,128)(2,1)} %bitcast.9), calls=%async_computation | async-start | bytes 262144 | tf_op jit(solution)/shard_map/all_to_all | solution.py:505
  275.8 5.4 %all-to-all-done = bf16[8,8,1024]{2,1,0:T(8,128)(2,1)S(1)} async-done(((bf16[8,8,1024]{2,1,0:T(8,128)(2,1)}), bf16[8,8,1024]{2,1,0:T(8,128)(2,1)S(1)}, u32[]{:S(2)}, u32[]{:S(2)}) %all-to-all-start) | async-done | bytes 131104 | tf_op jit(solution)/shard_map/all_to_all | solution.py:505
  (129 shorter events, 82.9 us)
Async XLA Ops:
  7.2 84.9 %all-gather.7.cloned.1.call-start = ((), (), s32[]{:S(2)}) async-start(), calls=%async_computation.1 | async-start | bytes 5308416 | tf_op jit(solution)/shard_map/all_gather | solution.py:452
  10.6 12.2 %collective-permute-start.2 = (bf16[48,1536]{1,0:T(8,128)(2,1)S(1)}, bf16[48,1536]{1,0:T(8,128)(2,1)S(1)}, u32[]{:S(2)}, u32[]{:S(2)}) collective-permute-start(bf16[48,1536]{1,0:T(8,128)(2,1)S(1)} %constant_dynamic-slice_fusion.2), channel_id=1, source_target_pairs={{0,1},{1,2},{2,3},{3,0},{4,5},{5,6},{6,7},{7,4},{8,9},{9,10},{10,1... | collective-permute-start | bytes 442376 | tf_op jit(solution)/shard_map/ppermute | solution.py:34
  12.2 12.6 %collective-permute-start.3 = (bf16[48,1536]{1,0:T(8,128)(2,1)S(1)}, bf16[48,1536]{1,0:T(8,128)(2,1)S(1)}, u32[]{:S(2)}, u32[]{:S(2)}) collective-permute-start(bf16[48,1536]{1,0:T(8,128)(2,1)S(1)} %constant_dynamic-slice_fusion.2), channel_id=1, source_target_pairs={{0,2},{1,3},{2,0},{3,1},{4,6},{5,7},{6,4},{7,5},{8,10},{9,11},{10,... | collective-permute-start | bytes 442376 | tf_op jit(solution)/shard_map/ppermute | solution.py:34
  13.3 13.2 %collective-permute-start.4 = (bf16[48,1536]{1,0:T(8,128)(2,1)S(1)}, bf16[48,1536]{1,0:T(8,128)(2,1)S(1)}, u32[]{:S(2)}, u32[]{:S(2)}) collective-permute-start(bf16[48,1536]{1,0:T(8,128)(2,1)S(1)} %constant_dynamic-slice_fusion.2), channel_id=1, source_target_pairs={{0,3},{1,0},{2,1},{3,2},{4,7},{5,4},{6,5},{7,6},{8,11},{9,8},{10,9... | collective-permute-start | bytes 442376 | tf_op jit(solution)/shard_map/ppermute | solution.py:34
  27.4 134.3 %all-gather.9.cloned.1.call-start = ((), (), s32[]{:S(2)}) async-start(), calls=%async_computation.2 | async-start | bytes 5308416 | tf_op jit(solution)/shard_map/all_gather | solution.py:452
  27.5 11.2 %collective-permute-start.5 = (bf16[464,384]{1,0:T(8,128)(2,1)S(1)}, bf16[464,384]{1,0:T(8,128)(2,1)S(1)}, u32[]{:S(2)}, u32[]{:S(2)}) collective-permute-start(bf16[464,384]{1,0:T(8,128)(2,1)S(1)} %fusion.1.c0), channel_id=1, source_target_pairs={{0,1},{1,2},{2,3},{3,0},{4,5},{5,6},{6,7},{7,4},{8,9},{9,10},{10,1... | collective-permute-start | bytes 1069064 | tf_op jit(solution)/shard_map/ppermute | solution.py:34
  27.6 30.9 %collective-permute-start.6 = (bf16[464,384]{1,0:T(8,128)(2,1)S(1)}, bf16[464,384]{1,0:T(8,128)(2,1)S(1)}, u32[]{:S(2)}, u32[]{:S(2)}) collective-permute-start(bf16[464,384]{1,0:T(8,128)(2,1)S(1)} %fusion.1.c0), channel_id=1, source_target_pairs={{0,2},{1,3},{2,0},{3,1},{4,6},{5,7},{6,4},{7,5},{8,10},{9,11},{10,... | collective-permute-start | bytes 1069064 | tf_op jit(solution)/shard_map/ppermute | solution.py:34
  29.3 30.3 %collective-permute-start.7 = (bf16[464,384]{1,0:T(8,128)(2,1)S(1)}, bf16[464,384]{1,0:T(8,128)(2,1)S(1)}, u32[]{:S(2)}, u32[]{:S(2)}) collective-permute-start(bf16[464,384]{1,0:T(8,128)(2,1)S(1)} %fusion.1.c0), channel_id=1, source_target_pairs={{0,3},{1,0},{2,1},{3,2},{4,7},{5,4},{6,5},{7,6},{8,11},{9,8},{10,9... | collective-permute-start | bytes 1069064 | tf_op jit(solution)/shard_map/ppermute | solution.py:34
  68.3 8.3 %collective-permute-start.8 = (bf16[224,384]{1,0:T(8,128)(2,1)S(1)}, bf16[224,384]{1,0:T(8,128)(2,1)S(1)}, u32[]{:S(2)}, u32[]{:S(2)}) collective-permute-start(bf16[224,384]{1,0:T(8,128)(2,1)S(1)} %get-tuple-element.29.a0), channel_id=1, source_target_pairs={{0,1},{1,2},{2,3},{3,0},{4,5},{5,6},{6,7},{7,4},{8,9},{9,10},{10,1... | collective-permute-start | bytes 516104 | tf_op jit(solution)/shard_map/ppermute | solution.py:34
  68.3 15.9 %collective-permute-start.9 = (bf16[224,384]{1,0:T(8,128)(2,1)S(1)}, bf16[224,384]{1,0:T(8,128)(2,1)S(1)}, u32[]{:S(2)}, u32[]{:S(2)}) collective-permute-start(bf16[224,384]{1,0:T(8,128)(2,1)S(1)} %get-tuple-element.29.a0), channel_id=1, source_target_pairs={{0,2},{1,3},{2,0},{3,1},{4,6},{5,7},{6,4},{7,5},{8,10},{9,11},{10,... | collective-permute-start | bytes 516104 | tf_op jit(solution)/shard_map/ppermute | solution.py:34
  70.6 21.5 %collective-permute-start.10 = (bf16[224,384]{1,0:T(8,128)(2,1)S(1)}, bf16[224,384]{1,0:T(8,128)(2,1)S(1)}, u32[]{:S(2)}, u32[]{:S(2)}) collective-permute-start(bf16[224,384]{1,0:T(8,128)(2,1)S(1)} %get-tuple-element.29.a0), channel_id=1, source_target_pairs={{0,3},{1,0},{2,1},{3,2},{4,7},{5,4},{6,5},{7,6},{8,11},{9,8},{10,9... | collective-permute-start | bytes 516104 | tf_op jit(solution)/shard_map/ppermute | solution.py:34
  74.2 32.5 %collective-permute-start.17 = (bf16[48,1536]{1,0:T(8,128)(2,1)}, bf16[48,1536]{1,0:T(8,128)(2,1)}, u32[]{:S(2)}, u32[]{:S(2)}) collective-permute-start(bf16[48,1536]{1,0:T(8,128)(2,1)} %constant_dynamic-slice_fusion.1), channel_id=1, source_target_pairs={{0,1},{1,2},{2,3},{3,0},{4,5},{5,6},{6,7},{7,4},{8,9},{9,10},{10,1... | collective-permute-start | bytes 442376 | tf_op jit(solution)/shard_map/ppermute | solution.py:34
  74.2 32.5 %collective-permute-start.18 = (bf16[48,1536]{1,0:T(8,128)(2,1)}, bf16[48,1536]{1,0:T(8,128)(2,1)}, u32[]{:S(2)}, u32[]{:S(2)}) collective-permute-start(bf16[48,1536]{1,0:T(8,128)(2,1)} %constant_dynamic-slice_fusion.1), channel_id=1, source_target_pairs={{0,2},{1,3},{2,0},{3,1},{4,6},{5,7},{6,4},{7,5},{8,10},{9,11},{10,... | collective-permute-start | bytes 442376 | tf_op jit(solution)/shard_map/ppermute | solution.py:34
  76.6 30.1 %collective-permute-start.19 = (bf16[48,1536]{1,0:T(8,128)(2,1)}, bf16[48,1536]{1,0:T(8,128)(2,1)}, u32[]{:S(2)}, u32[]{:S(2)}) collective-permute-start(bf16[48,1536]{1,0:T(8,128)(2,1)} %constant_dynamic-slice_fusion.1), channel_id=1, source_target_pairs={{0,3},{1,0},{2,1},{3,2},{4,7},{5,4},{6,5},{7,6},{8,11},{9,8},{10,9... | collective-permute-start | bytes 442376 | tf_op jit(solution)/shard_map/ppermute | solution.py:34
  108.8 102.8 %all-gather.11.cloned.1.call-start = ((), (), s32[]{:S(2)}) async-start(), calls=%async_computation.3 | async-start | bytes 5750784 | tf_op jit(solution)/shard_map/all_gather | solution.py:452
  108.8 7.3 %collective-permute-start.11 = (bf16[224,384]{1,0:T(8,128)(2,1)S(1)}, bf16[224,384]{1,0:T(8,128)(2,1)S(1)}, u32[]{:S(2)}, u32[]{:S(2)}) collective-permute-start(bf16[224,384]{1,0:T(8,128)(2,1)S(1)} %get-tuple-element.36.a0), channel_id=1, source_target_pairs={{0,1},{1,2},{2,3},{3,0},{4,5},{5,6},{6,7},{7,4},{8,9},{9,10},{10,1... | collective-permute-start | bytes 516104 | tf_op jit(solution)/shard_map/ppermute | solution.py:34
  108.9 16.4 %collective-permute-start.12 = (bf16[224,384]{1,0:T(8,128)(2,1)S(1)}, bf16[224,384]{1,0:T(8,128)(2,1)S(1)}, u32[]{:S(2)}, u32[]{:S(2)}) collective-permute-start(bf16[224,384]{1,0:T(8,128)(2,1)S(1)} %get-tuple-element.36.a0), channel_id=1, source_target_pairs={{0,2},{1,3},{2,0},{3,1},{4,6},{5,7},{6,4},{7,5},{8,10},{9,11},{10,... | collective-permute-start | bytes 516104 | tf_op jit(solution)/shard_map/ppermute | solution.py:34
  109.0 20.9 %collective-permute-start.13 = (bf16[224,384]{1,0:T(8,128)(2,1)S(1)}, bf16[224,384]{1,0:T(8,128)(2,1)S(1)}, u32[]{:S(2)}, u32[]{:S(2)}) collective-permute-start(bf16[224,384]{1,0:T(8,128)(2,1)S(1)} %get-tuple-element.36.a0), channel_id=1, source_target_pairs={{0,3},{1,0},{2,1},{3,2},{4,7},{5,4},{6,5},{7,6},{8,11},{9,8},{10,9... | collective-permute-start | bytes 516104 | tf_op jit(solution)/shard_map/ppermute | solution.py:34
  110.9 34.6 %collective-permute-start.28 = (bf16[48,1536]{1,0:T(8,128)(2,1)S(1)}, bf16[48,1536]{1,0:T(8,128)(2,1)S(1)}, u32[]{:S(2)}, u32[]{:S(2)}) collective-permute-start(bf16[48,1536]{1,0:T(8,128)(2,1)S(1)} %constant_dynamic-slice_fusion), channel_id=1, source_target_pairs={{0,1},{1,2},{2,3},{3,0},{4,5},{5,6},{6,7},{7,4},{8,9},{9,10},{10,1... | collective-permute-start | bytes 442376 | tf_op jit(solution)/shard_map/ppermute | solution.py:34
  112.5 33.1 %collective-permute-start.29 = (bf16[48,1536]{1,0:T(8,128)(2,1)S(1)}, bf16[48,1536]{1,0:T(8,128)(2,1)S(1)}, u32[]{:S(2)}, u32[]{:S(2)}) collective-permute-start(bf16[48,1536]{1,0:T(8,128)(2,1)S(1)} %constant_dynamic-slice_fusion), channel_id=1, source_target_pairs={{0,2},{1,3},{2,0},{3,1},{4,6},{5,7},{6,4},{7,5},{8,10},{9,11},{10,... | collective-permute-start | bytes 442376 | tf_op jit(solution)/shard_map/ppermute | solution.py:34
  116.2 29.4 %collective-permute-start.30 = (bf16[48,1536]{1,0:T(8,128)(2,1)S(1)}, bf16[48,1536]{1,0:T(8,128)(2,1)S(1)}, u32[]{:S(2)}, u32[]{:S(2)}) collective-permute-start(bf16[48,1536]{1,0:T(8,128)(2,1)S(1)} %constant_dynamic-slice_fusion), channel_id=1, source_target_pairs={{0,3},{1,0},{2,1},{3,2},{4,7},{5,4},{6,5},{7,6},{8,11},{9,8},{10,9... | collective-permute-start | bytes 442376 | tf_op jit(solution)/shard_map/ppermute | solution.py:34
  146.5 7.3 %collective-permute-start.14 = (bf16[224,384]{1,0:T(8,128)(2,1)S(1)}, bf16[224,384]{1,0:T(8,128)(2,1)S(1)}, u32[]{:S(2)}, u32[]{:S(2)}) collective-permute-start(bf16[224,384]{1,0:T(8,128)(2,1)S(1)} %get-tuple-element.38.a0), channel_id=1, source_target_pairs={{0,1},{1,2},{2,3},{3,0},{4,5},{5,6},{6,7},{7,4},{8,9},{9,10},{10,1... | collective-permute-start | bytes 516104 | tf_op jit(solution)/shard_map/ppermute | solution.py:34
  146.6 15.1 %collective-permute-start.15 = (bf16[224,384]{1,0:T(8,128)(2,1)S(1)}, bf16[224,384]{1,0:T(8,128)(2,1)S(1)}, u32[]{:S(2)}, u32[]{:S(2)}) collective-permute-start(bf16[224,384]{1,0:T(8,128)(2,1)S(1)} %get-tuple-element.38.a0), channel_id=1, source_target_pairs={{0,2},{1,3},{2,0},{3,1},{4,6},{5,7},{6,4},{7,5},{8,10},{9,11},{10,... | collective-permute-start | bytes 516104 | tf_op jit(solution)/shard_map/ppermute | solution.py:34
  146.7 15.0 %collective-permute-start.16 = (bf16[224,384]{1,0:T(8,128)(2,1)S(1)}, bf16[224,384]{1,0:T(8,128)(2,1)S(1)}, u32[]{:S(2)}, u32[]{:S(2)}) collective-permute-start(bf16[224,384]{1,0:T(8,128)(2,1)S(1)} %get-tuple-element.38.a0), channel_id=1, source_target_pairs={{0,3},{1,0},{2,1},{3,2},{4,7},{5,4},{6,5},{7,6},{8,11},{9,8},{10,9... | collective-permute-start | bytes 516104 | tf_op jit(solution)/shard_map/ppermute | solution.py:34
  176.1 5.6 %collective-permute-start.20 = (bf16[192,384]{1,0:T(8,128)(2,1)S(1)}, bf16[192,384]{1,0:T(8,128)(2,1)S(1)}, u32[]{:S(2)}, u32[]{:S(2)}) collective-permute-start(bf16[192,384]{1,0:T(8,128)(2,1)S(1)} %get-tuple-element.45.a0), channel_id=1, source_target_pairs={{0,1},{1,2},{2,3},{3,0},{4,5},{5,6},{6,7},{7,4},{8,9},{9,10},{10,1... | collective-permute-start | bytes 442376 | tf_op jit(solution)/shard_map/ppermute | solution.py:34
  176.1 12.6 %collective-permute-start.21 = (bf16[192,384]{1,0:T(8,128)(2,1)S(1)}, bf16[192,384]{1,0:T(8,128)(2,1)S(1)}, u32[]{:S(2)}, u32[]{:S(2)}) collective-permute-start(bf16[192,384]{1,0:T(8,128)(2,1)S(1)} %get-tuple-element.45.a0), channel_id=1, source_target_pairs={{0,2},{1,3},{2,0},{3,1},{4,6},{5,7},{6,4},{7,5},{8,10},{9,11},{10,... | collective-permute-start | bytes 442376 | tf_op jit(solution)/shard_map/ppermute | solution.py:34
  179.6 12.8 %collective-permute-start.22 = (bf16[192,384]{1,0:T(8,128)(2,1)S(1)}, bf16[192,384]{1,0:T(8,128)(2,1)S(1)}, u32[]{:S(2)}, u32[]{:S(2)}) collective-permute-start(bf16[192,384]{1,0:T(8,128)(2,1)S(1)} %get-tuple-element.45.a0), channel_id=1, source_target_pairs={{0,3},{1,0},{2,1},{3,2},{4,7},{5,4},{6,5},{7,6},{8,11},{9,8},{10,9... | collective-permute-start | bytes 442376 | tf_op jit(solution)/shard_map/ppermute | solution.py:34
  209.6 7.7 %collective-permute-start.26 = (bf16[192,384]{1,0:T(8,128)(2,1)S(1)}, bf16[192,384]{1,0:T(8,128)(2,1)S(1)}, u32[]{:S(2)}, u32[]{:S(2)}) collective-permute-start(bf16[192,384]{1,0:T(8,128)(2,1)S(1)} %shard_map.100.a0), channel_id=1, source_target_pairs={{0,2},{1,3},{2,0},{3,1},{4,6},{5,7},{6,4},{7,5},{8,10},{9,11},{10,... | collective-permute-start | bytes 442376 | tf_op jit(solution)/shard_map/ppermute | solution.py:34
  210.3 14.7 %collective-permute-start.27 = (bf16[192,384]{1,0:T(8,128)(2,1)S(1)}, bf16[192,384]{1,0:T(8,128)(2,1)S(1)}, u32[]{:S(2)}, u32[]{:S(2)}) collective-permute-start(bf16[192,384]{1,0:T(8,128)(2,1)S(1)} %shard_map.100.a0), channel_id=1, source_target_pairs={{0,3},{1,0},{2,1},{3,2},{4,7},{5,4},{6,5},{7,6},{8,11},{9,8},{10,9... | collective-permute-start | bytes 442376 | tf_op jit(solution)/shard_map/ppermute | solution.py:34
  246.2 6.2 %collective-permute-start.34 = (bf16[192,384]{1,0:T(8,128)(2,1)S(1)}, bf16[192,384]{1,0:T(8,128)(2,1)S(1)}, u32[]{:S(2)}, u32[]{:S(2)}) collective-permute-start(bf16[192,384]{1,0:T(8,128)(2,1)S(1)} %shard_map.102.a0), channel_id=1, source_target_pairs={{0,2},{1,3},{2,0},{3,1},{4,6},{5,7},{6,4},{7,5},{8,10},{9,11},{10,... | collective-permute-start | bytes 442376 | tf_op jit(solution)/shard_map/ppermute | solution.py:34
  246.9 13.3 %collective-permute-start.35 = (bf16[192,384]{1,0:T(8,128)(2,1)S(1)}, bf16[192,384]{1,0:T(8,128)(2,1)S(1)}, u32[]{:S(2)}, u32[]{:S(2)}) collective-permute-start(bf16[192,384]{1,0:T(8,128)(2,1)S(1)} %shard_map.102.a0), channel_id=1, source_target_pairs={{0,3},{1,0},{2,1},{3,2},{4,7},{5,4},{6,5},{7,6},{8,11},{9,8},{10,9... | collective-permute-start | bytes 442376 | tf_op jit(solution)/shard_map/ppermute | solution.py:34
  267.4 13.9 %all-to-all-start = ((bf16[8,8,1024]{2,1,0:T(8,128)(2,1)}), bf16[8,8,1024]{2,1,0:T(8,128)(2,1)S(1)}, u32[]{:S(2)}, u32[]{:S(2)}) async-start(bf16[8,8,1024]{2,1,0:T(8,128)(2,1)} %bitcast.9), calls=%async_computation | async-start | bytes 262144 | tf_op jit(solution)/shard_map/all_to_all | solution.py:505
  (30 other events, 205.0 us)
Sparse Core Ops, SparseCore 0:
  27.5 39.1 all-gather.6
  108.9 38.0 all-gather.8
  149.5 40.5 all-gather.10

commit v6 on v2

v6 whole, which is shorter than its diff:
```python
import functools
import math

import jax
import jax.numpy as jnp
from jax import lax
from jax.experimental import pallas as pl
from jax.experimental.pallas import tpu as pltpu
from jax.sharding import PartitionSpec as P

RESIDUAL_BLOCKS = 6
BASE_DILATION = 2
BLOCKS_PER_LOAD = 2
FRAMED_BLOCKS = 4
DIGIT = 128
VMEM_BYTES = 20 * 2**20
STAGE_BYTES = 40 * 2**20


def dilation(block):
    return BASE_DILATION * 2**block


def after(cells, *earlier):
    return lax.optimization_barrier((cells,) + earlier)[0]


def after_all(cells, *earlier):
    return list(lax.optimization_barrier(tuple(cells) + earlier)[: len(cells)])


def from_others(cells):
    count = lax.axis_size("trk")
    return [cells] + [
        lax.ppermute(cells, "trk", [(i, (i + k) % count) for i in range(count)])
        for k in range(1, count)
    ]


def halo(cells, width):
    count = lax.axis_size("seq")
    head = cells[:width]
    tail = cells[cells.shape[0] - width :]
    above = lax.ppermute(tail, "seq", [(i, i + 1) for i in range(count - 1)])
    below = lax.ppermute(head, "seq", [(i + 1, i) for i in range(count - 1)])
    return above, below


def group_size(rows, count):
    size = 1
    for g in range(1, count + 1):
        if count % g == 0 and rows % (16 * g) == 0:
            size = g
    return size


def tile_of(channels):
    for width in (512, 256, 384, 128):
        if channels % width == 0:
            return width
    return channels


def dot(a, b):
    return jnp.dot(a, b, preferred_element_type=jnp.float32)


def dot_last(a, b):
    return lax.dot_general(a, b, (((1,), (1,)), ((), ())), preferred_element_type=jnp.float32)


def gelu(x):
    cubic = x + 0.044715 * (x * x * x)
    return 0.5 * x * (1.0 + jnp.tanh(math.sqrt(2.0 / math.pi) * cubic))


def pack(act):
    half = act.shape[0] // 2
    return jnp.concatenate([act[:half], act[half:]], axis=1)


def unpack(cells):
    half = cells.shape[1] // 2
    return jnp.concatenate([cells[:, :half], cells[:, half:]], axis=0)


def columns(tile, width):
    return pl.ds(tile * width, width)


def project_all(acts, weight, trunk, margin, bias, target):
    rows, channels = target.shape
    width = tile_of(channels)
    cells = jnp.concatenate([unpack(act[...]) for act in acts], axis=1)
    for c in range(channels // width):
        cols = columns(c, width)
        total = dot(cells, weight[:, cols]) + bias[:, cols].astype(jnp.float32)
        total = total + trunk[pl.ds(margin, rows), cols].astype(jnp.float32)
        target[:, cols] = total.astype(BF16)


def convolve(cells, taps, bias, step, act_ref):
    rows = cells.shape[0]
    sums = [dot_last(cells, taps[t]) for t in range(3)]
    inner = sums[1] + pltpu.roll(sums[0], step, 0) + pltpu.roll(sums[2], rows - step, 0)
    keep = 2 * act_ref.shape[0]
    margin = (rows - keep) // 2
    inner = inner[margin : margin + keep] + bias.astype(jnp.float32)
    act_ref[...] = pack(gelu(inner).astype(BF16))


BF16 = jnp.bfloat16
ANY = pl.BlockSpec(memory_space=pl.ANY)
SMEM = pl.BlockSpec(memory_space=pltpu.SMEM)
VMEM = pl.BlockSpec(memory_space=pltpu.VMEM)


def shape(*dims):
    return jax.ShapeDtypeStruct(dims, BF16)


def kernel_call(body, ins, outs, flops, moved, special=0, scalars=0, scratch=(), limit=VMEM_BYTES, specs=None):
    return pl.pallas_call(
        body,
        in_specs=specs or [SMEM] * scalars + [VMEM] * (len(ins) - scalars),
        out_specs=[VMEM] * len(outs),
        out_shape=list(outs),
        scratch_shapes=list(scratch),
        compiler_params=pltpu.CompilerParams(vmem_limit_bytes=limit),
        cost_estimate=pl.CostEstimate(
            flops=flops, bytes_accessed=2 * moved, transcendentals=special
        ),
    )(*ins)


def stage_kernel(plan, *refs):
    sems = refs[-1]
    used = 0
    copies = []
    for source, target, cuts in plan:
        for src, dst in cuts(refs[source], refs[target]):
            copies.append(pltpu.make_async_copy(src, dst, sems.at[used]))
            used += 1
    for copy in copies:
        copy.start()
    for copy in copies:
        copy.wait()


def projection_cuts(part, per_block, share, load, target):
    return [
        (
            load.at[part * per_block + i, pl.ds(j * share, share)],
            target.at[pl.ds((j * per_block + i) * share, share)],
        )
        for j in range(target.shape[0] // (per_block * share))
        for i in range(per_block)
    ]


def tap_cuts(block, conv_in, target):
    return [(conv_in.at[block, t], target.at[t]) for t in range(3)]


def whole_cuts(source, target):
    return [(source, target)]


def stage(sources, targets, cuts):
    count = len(sources)
    plan = [(i, count + i, cut) for i, cut in enumerate(cuts)]
    return kernel_call(
        functools.partial(stage_kernel, plan),
        sources,
        targets,
        0,
        sum(math.prod(t.shape) for t in targets),
        scratch=[pltpu.SemaphoreType.DMA((32,))],
        specs=[ANY] * count,
        limit=STAGE_BYTES,
    )


def first_kernel(step, order_ref, c0, c1, c2, c3, taps, bias_ref, act_ref, trunk, pbias):
    width = c0.shape[1]
    rows = trunk.shape[0]
    for k, cell in enumerate((c0, c1, c2, c3)):
        cols = pl.ds(pl.multiple_of(order_ref[k] * width, 128), width)
        trunk[:, cols] = cell[:rows]
        pbias[:, cols] = cell[rows:]
    convolve(trunk[...], taps, bias_ref[0:1], step, act_ref)


def first_conv(cells, rows, order, taps, conv_bias, step):
    _, hidden, channels = taps.shape
    return kernel_call(
        functools.partial(first_kernel, step),
        (order, *cells, taps, conv_bias),
        [
            shape(rows // 2, 2 * hidden),
            shape(rows, channels),
            shape(cells[0].shape[0] - rows, channels),
        ],
        6 * rows * hidden * channels,
        3 * hidden * channels + 2 * rows * channels,
        rows * hidden,
        scalars=1,
    )


def fused_kernel(
    block, edge_ref, a0, a1, a2, a3, weight, trunk_in, pbias_ref, taps, bias_ref, act_ref, trunk
):
    pbias = pbias_ref[block : block + 1]
    project_all((a0, a1, a2, a3), weight, trunk_in, 0, pbias, trunk)
    rows = trunk.shape[0]
    margin = dilation(FRAMED_BLOCKS)

    @pl.when(edge_ref[0] == 1)
    def _():
        trunk[:margin] = jnp.zeros((margin, trunk.shape[1]), BF16)

    @pl.when(edge_ref[1] == 1)
    def _():
        trunk[rows - margin :] = jnp.zeros((margin, trunk.shape[1]), BF16)

    bias = bias_ref[block + 1 : block + 2]
    convolve(trunk[...], taps, bias, dilation(block + 1), act_ref)


def fused(acts, weight, trunk, pbias, taps, conv_bias, block, edge, rows_out):
    rows, channels = trunk.shape
    hidden = taps.shape[1]
    return kernel_call(
        functools.partial(fused_kernel, block),
        (edge, *acts, weight, trunk, pbias, taps, conv_bias),
        [shape(rows_out // 2, 2 * hidden), shape(rows, channels)],
        14 * rows * hidden * channels,
        7 * hidden * channels + 2 * rows * channels,
        rows * hidden,
        scalars=1,
    )


def projection_kernel(block, a0, a1, a2, a3, weight, trunk_in, pbias_ref, trunk):
    margin = (trunk_in.shape[0] - trunk.shape[0]) // 2
    pbias = pbias_ref[block : block + 1]
    project_all((a0, a1, a2, a3), weight, trunk_in, margin, pbias, trunk)


def projection(acts, weight, trunk, pbias, block):
    channels = trunk.shape[1]
    rows, hidden = 2 * acts[0].shape[0], acts[0].shape[1] // 2
    return kernel_call(
        functools.partial(projection_kernel, block),
        (*acts, weight, trunk, pbias),
        [shape(rows, channels)],
        8 * rows * hidden * channels,
        4 * hidden * channels + 2 * rows * channels,
    )[0]


def conv_kernel(block, above, trunk, below, taps, bias_ref, act_ref):
    cells = jnp.concatenate([above[...], trunk[...], below[...]], axis=0)
    convolve(cells, taps, bias_ref[block : block + 1], dilation(block), act_ref)


def conv(above, trunk, below, taps, conv_bias, block):
    rows, channels = trunk.shape
    hidden = taps.shape[1]
    frame = rows + 2 * dilation(block)
    return kernel_call(
        functools.partial(conv_kernel, block),
        (above, trunk, below, taps, conv_bias),
        [shape(rows // 2, 2 * hidden)],
        6 * frame * hidden * channels,
        3 * hidden * channels + frame * channels,
        rows * hidden,
    )[0]


def head_kernel(
    block, a0, a1, a2, a3, weight, trunk_in, pbias_ref, head_ref, hbias_ref, onehot_ref,
    cover_ref, gene_ref, trunk
):
    pbias = pbias_ref[block : block + 1]
    project_all((a0, a1, a2, a3), weight, trunk_in, 0, pbias, trunk)
    tracks = head_ref.shape[1]
    width = tile_of(tracks)
    for c in range(tracks // width):
        cols = columns(c, width)
        x = dot(trunk[...], head_ref[:, cols]) + hbias_ref[:, cols].astype(jnp.float32)
        tile = (jnp.maximum(x, 0.0) + jnp.log1p(jnp.exp(-jnp.abs(x)))).astype(BF16)
        cover_ref[:, cols] = tile
        gene_ref[:, cols] = dot(onehot_ref[...], tile).astype(BF16)


def head(acts, weight, trunk, pbias, block, head_weight, head_bias, onehot):
    rows, channels = trunk.shape
    hidden = acts[0].shape[1] // 2
    tracks = head_weight.shape[1]
    genes = onehot.shape[0]
    return kernel_call(
        functools.partial(head_kernel, block),
        (*acts, weight, trunk, pbias, head_weight, head_bias, onehot),
        [shape(rows, tracks), shape(genes, tracks)],
        8 * rows * hidden * channels + 2 * rows * channels * tracks,
        4 * hidden * channels + rows * channels + channels * tracks,
        2 * rows * tracks,
        scratch=[pltpu.VMEM((rows, channels), BF16)],
    )


def exon_digits(exon_bins, channels):
    digits = jnp.concatenate([exon_bins >> 7, exon_bins & (DIGIT - 1)], axis=1)
    genes, width = digits.shape
    return jnp.pad(digits.astype(jnp.bfloat16), ((0, -genes % 16), (0, channels - width)))


def exon_lists(rows, genes, entries):
    digits = rows[:, :genes, : 2 * entries].astype(jnp.int32)
    lists = digits[:, :, :entries] * DIGIT + digits[:, :, entries:]
    return lists.reshape(-1, entries)


def exon_onehot(gene_block, first_bin, width_now):
    exon_matches = (
        gene_block[:, :, None] - first_bin == jnp.arange(width_now, dtype=jnp.int32)[None, None, :]
    )
    return jnp.sum(exon_matches.astype(jnp.float32), axis=1).astype(jnp.bfloat16)


def shards(
    trunk_input, conv_in, conv_bias, conv_out, projection_bias, head_weight, head_bias, exon_bins
):
    quarters = lax.axis_size("trk")
    place = lax.axis_index("trk")
    count = lax.axis_size("seq")
    lane = lax.axis_index("seq")
    bin_rows, channels_here = trunk_input.shape
    blocks, hidden, channels = conv_out.shape
    genes_here, entries = exon_bins.shape

    load_rows = BLOCKS_PER_LOAD * hidden
    size = group_size(load_rows, count)
    share = load_rows // size
    per_block = hidden // share
    groups = [[g * size + i for i in range(size)] for g in range(count // size)]
    mine = lax.rem(lane, size)
    packed = size == count and 2 * entries <= channels

    def column(load):
        first = load * BLOCKS_PER_LOAD
        flat = conv_out[first : first + BLOCKS_PER_LOAD].reshape(load_rows, channels)
        return lax.dynamic_slice_in_dim(flat, mine * share, share, 0)

    def gather(parts):
        return lax.all_gather(
            jnp.concatenate(parts, axis=0), "seq", axis=0, tiled=False, axis_index_groups=groups
        )

    margin = dilation(FRAMED_BLOCKS)
    frame = bin_rows + 2 * margin
    order = lax.rem(place - jnp.arange(quarters, dtype=jnp.int32) + quarters, quarters)
    edge = jnp.stack([lane == 0, lane == count - 1]).astype(jnp.int32)

    above, below = halo(trunk_input, margin)
    first_column = from_others(column(0))
    loads = [gather(after_all(first_column, above, below))]
    own = jnp.concatenate(
        [above, trunk_input, below, jnp.pad(projection_bias, ((0, -blocks % 16), (0, 0)))], axis=0
    )
    own = after(own, *first_column)
    cells = from_others(own)
    second = from_others(after(column(1), *cells))

    taps_shape = shape(3, hidden, channels)
    weight_shape = shape(quarters * hidden, channels)
    (taps,) = stage((after(conv_in, own),), (taps_shape,), (functools.partial(tap_cuts, 0),))
    act, trunk, biases = first_conv(cells, frame, order, taps, conv_bias, dilation(0))

    onehot = None
    for block in range(RESIDUAL_BLOCKS):
        others = from_others(act)
        if block == 0:
            third = from_others(after(column(2), *others))
        if block == 1:
            loads.append(gather(after_all(second, act)))
        if block == 2:
            tail = [exon_digits(exon_bins, channels)] if packed else []
            loads.append(gather(after_all(third, act) + tail))
        if block == 4:
            if packed:
                gene_lists = exon_lists(loads[2][:, quarters * share :], genes_here, entries)
            else:
                gene_lists = lax.all_gather(exon_bins, "seq", axis=0, tiled=True)
            onehot = exon_onehot(gene_lists, lane * bin_rows, bin_rows)
        later = block + 1
        part = functools.partial(projection_cuts, block % BLOCKS_PER_LOAD, per_block, share)
        load = after(loads[block // BLOCKS_PER_LOAD], act)
        if later < RESIDUAL_BLOCKS:
            weight, taps = stage(
                (load, conv_in),
                (weight_shape, taps_shape),
                (part, functools.partial(tap_cuts, later)),
            )
        else:
            weight, head_rows = stage(
                (load, head_weight), (weight_shape, shape(*head_weight.shape)), (part, whole_cuts)
            )
        if later < FRAMED_BLOCKS:
            rows_out = frame if later < FRAMED_BLOCKS - 1 else bin_rows
            act, trunk = fused(
                others, weight, trunk, biases, taps, conv_bias, block, edge, rows_out
            )
        elif later < RESIDUAL_BLOCKS:
            trunk = projection(others, weight, trunk, biases, block)
            above, below = halo(trunk, dilation(later))
            act = conv(above, trunk, below, taps, conv_bias, later)
        else:
            coverage, partial = head(
                others, weight, trunk, biases, block, head_rows, head_bias[None, :], onehot
            )

    parts = lax.all_to_all(
        partial.reshape(count, genes_here, partial.shape[1]), "seq", 0, 0, tiled=False
    )
    gene_sum = jnp.sum(parts.astype(jnp.float32), axis=0)
    counts = jnp.sum((exon_bins >= 0).astype(jnp.float32), axis=1)
    gene_cov = gene_sum / counts[:, None]
    return (coverage, gene_cov)


def solution(mesh):
    in_specs = (
        P("seq", "trk"),
        P(None, None, "trk", None),
        P(None, "trk"),
        P(None, "trk", None),
        P(None, "trk"),
        P(None, "trk"),
        P("trk"),
        P("seq", None),
    )
    out_specs = (P("seq", "trk"), P("seq", "trk"))
    return jax.shard_map(shards, mesh=mesh, in_specs=in_specs, out_specs=out_specs, check_vma=False)
```

time: 296 us -> 238 us (0.80); the launches traced: 291 us -> 237 us
  matrix products: 62.4 us -> 0 us
  Pallas kernels: 0 us -> 52 us
  waiting for transfers between devices: 121 us -> 88.1 us
  starting transfers between devices: 61.8 us -> 55.8 us
  other arithmetic: 9.77 us -> 3.94 us
    dot_general x43 -> x0, matrix products: 62.4 us -> none  [the longest x18 31.1 us: contract_last(): lax.dot_general(rows, kernel, (((1,), (1,)), ((), ())), preferred_element...]
    pallas_call x0 -> x16, Pallas kernels: none -> 52 us  [kernel_call(): pl.pallas_call(body, in_specs=specs or [SMEM] * scalars + [VMEM] * (len(i...]
    ppermute x30, waiting for transfers between devices: 115 us -> 66 us  [from_others(): lax.ppermute(cells, 'trk', [(i, (i + k) % count) for i in range(count)])]
    unnamed x76 -> x36, local copies, waits for them, and re-layouts: 4.39 us -> 17.1 us
    ppermute x3, waiting for transfers between devices: 0.01 us -> 9.4 us  [halo(): below = lax.ppermute(head, 'seq', [(i + 1, i) for i in range(count - 1)])]
    slice x3 -> x2, local copies, waits for them, and re-layouts: 8.69 us -> 0.04 us  [halo(): head = cells[:width]]
    all_gather x3, waiting for transfers between devices: 0.02 us -> 6.42 us  [gather(): lax.all_gather(jnp.concatenate(parts, axis=0), 'seq', axis=0, tiled=False...]
    ppermute x30, starting transfers between devices: 40.5 us -> 36.5 us  [from_others(): lax.ppermute(cells, 'trk', [(i, (i + k) % count) for i in range(count)])]
  transfers between devices with their start and end apart: 40 -> 40, of which waited for: 24 -> 24; matrix products, arithmetic and copies ran while one was open for 24% -> 1% of each run, Pallas kernels for 0% -> 19%
where the time goes in v6:
time: 238 us; the launch traced here: 237 us
  waiting for transfers between devices  88.1 us (37%)
  starting transfers between devices  55.8 us (23%)
  Pallas kernels  52 us (22%)
  local copies, waits for them, and re-layouts  22.7 us (10%)
  between operations  14.2 us (6%)
  other arithmetic  3.94 us (2%)
    ppermute x30, waiting for transfers between devices, from_others(): lax.ppermute(cells, 'trk', [(i, (i + k) % count) for i in range(count)])  66 us
    pallas_call x16, Pallas kernels, kernel_call(): pl.pallas_call(body, in_specs=specs or [SMEM] * scalars + [VMEM] * (len(i...  52 us
    ppermute x30, starting transfers between devices, from_others(): lax.ppermute(cells, 'trk', [(i, (i + k) % count) for i in range(count)])  36.5 us
    unnamed x36, local copies, waits for them, and re-layouts  17.1 us
    ppermute x3, waiting for transfers between devices, halo(): below = lax.ppermute(head, 'seq', [(i + 1, i) for i in range(count - 1)])  9.4 us
    ppermute x3, starting transfers between devices, halo(): above = lax.ppermute(tail, 'seq', [(i, i + 1) for i in range(count - 1)])  9.14 us
    all_gather x3, waiting for transfers between devices, gather(): lax.all_gather(jnp.concatenate(parts, axis=0), 'seq', axis=0, tiled=False...  6.42 us
    all_to_all x1, starting transfers between devices, shards(): lax.all_to_all(partial.reshape(count, genes_here, partial.shape[1]), 'seq...  6.21 us
  transfers between devices with their start and end apart: 40, of which 24 were waited for; matrix products, arithmetic and copies ran while one was open for 1% of the time, Pallas kernels for 19%

profile of v6, /device:TPU:8, one launch (start us, length us, event | category | flops | bytes accessed | tf_op | source)
XLA Modules:
  0.0 236.9 jit_solution(2911882872194203061)
XLA Ops:
  7.2 3.8 %fusion.12 = (bf16[2,192,1536]{2,1,0:T(8,128)(2,1)}, bf16[2,192,1536]{2,1,0:T(8,128)(2,1)S(1)}, bf16[2,192,1536]{2,1,0:T(8,128)(2,1)}) fusion(bf16[6,192,1536]{2,1,0:T(8,128)(2,1)} %param.11), kind=kLoop, calls=%fused_computation.37 | loop fusion | bytes 7077888 | tf_op jit(solution)/shard_map/slice | solution.py:354
  17.0 3.0 %collective-permute-start = (bf16[32,384]{1,0:T(8,128)(2,1)S(1)}, bf16[32,384]{1,0:T(8,128)(2,1)S(1)}, u32[]{:S(2)}, u32[]{:S(2)}) collective-permute-start(bf16[32,384]{1,0:T(8,128)(2,1)S(1)} %get-tuple-element.99), channel_id=1, source_target_pairs={{0,4},{4,8},{8,12},{12,16},{16,20},{20,24},{24,28},{1,5},{5,9},{9,... | collective-permute-start | bytes 73736 | tf_op jit(solution)/shard_map/ppermute | solution.py:44
  20.9 2.4 collective-permute-done.2
  31.8 4.2 %copy-done = bf16[6,3,192,1536]{3,2,1,0:T(8,128)(2,1)S(1)} copy-done((bf16[6,3,192,1536]{3,2,1,0:T(8,128)(2,1)S(1)}, bf16[6,3,192,1536]{3,2,1,0:T(8,128)(2,1)}, u32[]{:S(2)}) %copy-start) | copy-done | bytes 10616856
  36.6 2.6 %collective-permute-done.5.c1 = bf16[464,384]{1,0:T(8,128)(2,1)S(1)} collective-permute-done((bf16[464,384]{1,0:T(8,128)(2,1)S(1)}, bf16[464,384]{1,0:T(8,128)(2,1)S(1)}, u32[]{:S(2)}, u32[]{:S(2)}) %collective-permute-start.5) | collective-permute-done | bytes 356384 | tf_op jit(solution)/shard_map/ppermute | solution.py:35
  39.2 19.8 %collective-permute-done.6.c2 = bf16[464,384]{1,0:T(8,128)(2,1)S(1)} collective-permute-done((bf16[464,384]{1,0:T(8,128)(2,1)S(1)}, bf16[464,384]{1,0:T(8,128)(2,1)S(1)}, u32[]{:S(2)}, u32[]{:S(2)}) %collective-permute-start.6) | collective-permute-done | bytes 356384 | tf_op jit(solution)/shard_map/ppermute | solution.py:35
  62.1 2.4 %collective-permute-start.9 = (bf16[224,384]{1,0:T(8,128)(2,1)S(1)}, bf16[224,384]{1,0:T(8,128)(2,1)S(1)}, u32[]{:S(2)}, u32[]{:S(2)}) collective-permute-start(bf16[224,384]{1,0:T(8,128)(2,1)S(1)} %get-tuple-element.49.a0), channel_id=1, source_target_pairs={{0,2},{1,3},{2,0},{3,1},{4,6},{5,7},{6,4},{7,5},{8,10},{9,11},{10,... | collective-permute-start | bytes 516104 | tf_op jit(solution)/shard_map/ppermute | solution.py:35
  67.5 2.4 %collective-permute-start.18 = (bf16[48,1536]{1,0:T(8,128)(2,1)S(1)}, bf16[48,1536]{1,0:T(8,128)(2,1)S(1)}, u32[]{:S(2)}, u32[]{:S(2)}) collective-permute-start(bf16[48,1536]{1,0:T(8,128)(2,1)S(1)} %constant_dynamic-slice_fusion.1), channel_id=1, source_target_pairs={{0,2},{1,3},{2,0},{3,1},{4,6},{5,7},{6,4},{7,5},{8,10},{9,11},{10,... | collective-permute-start | bytes 442376 | tf_op jit(solution)/shard_map/ppermute | solution.py:35
  72.3 4.7 %shard_map.97 = (bf16[768,1536]{1,0:T(8,128)(2,1)S(1)}, bf16[3,192,1536]{2,1,0:T(8,128)(2,1)S(1)}) custom-call(bf16[8,192,1536]{2,1,0:T(8,128)(2,1)S(1)} %bitcast.14, bf16[6,3,192,1536]{3,2,1,0:T(8,128)(2,1)} %refs_1_.10), custom_call_target="tpu_custom_call" | custom-call | bytes 4128768 | tf_op jit(solution)/shard_map/pallas_call | solution.py:123
  78.0 7.9 %collective-permute-done.10.a3 = bf16[224,384]{1,0:T(8,128)(2,1)S(1)} collective-permute-done((bf16[224,384]{1,0:T(8,128)(2,1)S(1)}, bf16[224,384]{1,0:T(8,128)(2,1)S(1)}, u32[]{:S(2)}, u32[]{:S(2)}) %collective-permute-start.10) | collective-permute-done | bytes 172064 | tf_op jit(solution)/shard_map/ppermute | solution.py:35
  85.9 4.0 %shard_map.98 = (bf16[224,384]{1,0:T(8,128)(2,1)S(1)}, bf16[448,1536]{1,0:T(8,128)(2,1)S(1)}) custom-call(s32[2]{0:T(128)S(1)} %add_convert_fusion.edge_ref, bf16[224,384]{1,0:T(8,128)(2,1)S(1)} %get-tuple-element.49.a0, bf16[224,384]{1,0:T(8,128)(2,1)S(1)} %collective-permute-done.8.a1, bf16[224,384]{1,0:T(8,128)(2,1)S(1)} %collective-permute-done.9.a2, ...), custom_call_target="tpu_custom_call" | custom-call | flops 1849688064 | bytes 6881280 | tf_op jit(solution)/shard_map/pallas_call | solution.py:123
  97.6 3.3 %collective-permute-start.29 = (bf16[48,1536]{1,0:T(8,128)(2,1)S(1)}, bf16[48,1536]{1,0:T(8,128)(2,1)S(1)}, u32[]{:S(2)}, u32[]{:S(2)}) collective-permute-start(bf16[48,1536]{1,0:T(8,128)(2,1)S(1)} %constant_dynamic-slice_fusion), channel_id=1, source_target_pairs={{0,2},{1,3},{2,0},{3,1},{4,6},{5,7},{6,4},{7,5},{8,10},{9,11},{10,... | collective-permute-start | bytes 442376 | tf_op jit(solution)/shard_map/ppermute | solution.py:35
  100.9 2.5 %copy-done.3 = bf16[1536,1536]{1,0:T(8,128)(2,1)S(1)} copy-done((bf16[1536,1536]{1,0:T(8,128)(2,1)S(1)}, bf16[1536,1536]{1,0:T(8,128)(2,1)}, u32[]{:S(2)}) %copy-start.3) | copy-done | bytes 4718616
  103.4 4.7 %shard_map.99 = (bf16[768,1536]{1,0:T(8,128)(2,1)S(1)}, bf16[3,192,1536]{2,1,0:T(8,128)(2,1)S(1)}) custom-call(bf16[8,192,1536]{2,1,0:T(8,128)(2,1)S(1)} %bitcast.15, bf16[6,3,192,1536]{3,2,1,0:T(8,128)(2,1)} %refs_1_.10), custom_call_target="tpu_custom_call" | custom-call | bytes 4128768 | tf_op jit(solution)/shard_map/pallas_call | solution.py:123
  110.2 6.7 %collective-permute-done.13.a3 = bf16[224,384]{1,0:T(8,128)(2,1)S(1)} collective-permute-done((bf16[224,384]{1,0:T(8,128)(2,1)S(1)}, bf16[224,384]{1,0:T(8,128)(2,1)S(1)}, u32[]{:S(2)}, u32[]{:S(2)}) %collective-permute-start.13) | collective-permute-done | bytes 172064 | tf_op jit(solution)/shard_map/ppermute | solution.py:35
  116.9 3.7 %shard_map.100 = (bf16[224,384]{1,0:T(8,128)(2,1)S(1)}, bf16[448,1536]{1,0:T(8,128)(2,1)S(1)}) custom-call(s32[2]{0:T(128)S(1)} %add_convert_fusion.edge_ref, bf16[224,384]{1,0:T(8,128)(2,1)S(1)} %get-tuple-element.59.a0, bf16[224,384]{1,0:T(8,128)(2,1)S(1)} %collective-permute-done.11.a1, bf16[224,384]{1,0:T(8,128)(2,1)S(1)} %collective-permute-done.12.a2, ...), custom_call_target="tpu_custom_call" | custom-call | flops 1849688064 | bytes 6881280 | tf_op jit(solution)/shard_map/pallas_call | solution.py:123
  128.3 3.6 %all-gather.9.cloned.1.call-done = bf16[1536,1536]{1,0:T(8,128)(2,1)} async-done(((bf16[192,1536]{1,0:T(8,128)(2,1)}), bf16[1536,1536]{1,0:T(8,128)(2,1)}) %all-gather.9.cloned.1.call-update) | async-done | bytes 4718608 | tf_op jit(solution)/shard_map/all_gather | solution.py:358
  134.3 4.7 %shard_map.101 = (bf16[768,1536]{1,0:T(8,128)(2,1)S(1)}, bf16[3,192,1536]{2,1,0:T(8,128)(2,1)S(1)}) custom-call(bf16[8,192,1536]{2,1,0:T(8,128)(2,1)S(1)} %bitcast.16, bf16[6,3,192,1536]{3,2,1,0:T(8,128)(2,1)} %refs_1_.10), custom_call_target="tpu_custom_call" | custom-call | bytes 4128768 | tf_op jit(solution)/shard_map/pallas_call | solution.py:123
  141.4 5.1 %shard_map.102 = (bf16[192,384]{1,0:T(8,128)(2,1)S(1)}, bf16[448,1536]{1,0:T(8,128)(2,1)S(1)}) custom-call(s32[2]{0:T(128)S(1)} %add_convert_fusion.edge_ref, bf16[224,384]{1,0:T(8,128)(2,1)S(1)} %get-tuple-element.64.a0, bf16[224,384]{1,0:T(8,128)(2,1)S(1)} %collective-permute-done.14.a1, bf16[224,384]{1,0:T(8,128)(2,1)S(1)} %collective-permute-done.15.a2, ...), custom_call_target="tpu_custom_call" | custom-call | flops 1849688064 | bytes 6881280 | tf_op jit(solution)/shard_map/pallas_call | solution.py:123
  150.2 4.7 %shard_map.103 = (bf16[768,1536]{1,0:T(8,128)(2,1)S(1)}, bf16[3,192,1536]{2,1,0:T(8,128)(2,1)S(1)}) custom-call(bf16[8,192,1536]{2,1,0:T(8,128)(2,1)S(1)} %bitcast.17, bf16[6,3,192,1536]{3,2,1,0:T(8,128)(2,1)} %refs_1_.10), custom_call_target="tpu_custom_call" | custom-call | bytes 4128768 | tf_op jit(solution)/shard_map/pallas_call | solution.py:123
  155.0 4.8 %collective-permute-done.21.a2 = bf16[192,384]{1,0:T(8,128)(2,1)S(1)} collective-permute-done((bf16[192,384]{1,0:T(8,128)(2,1)S(1)}, bf16[192,384]{1,0:T(8,128)(2,1)S(1)}, u32[]{:S(2)}, u32[]{:S(2)}) %collective-permute-start.21) | collective-permute-done | bytes 147488 | tf_op jit(solution)/shard_map/ppermute | solution.py:35
  165.9 2.8 %collective-permute-done.24.below = bf16[32,1536]{1,0:T(8,128)(2,1)S(1)} collective-permute-done((bf16[32,1536]{1,0:T(8,128)(2,1)S(1)}, bf16[32,1536]{1,0:T(8,128)(2,1)S(1)}, u32[]{:S(2)}, u32[]{:S(2)}) %collective-permute-start.24) | collective-permute-done | bytes 98336 | tf_op jit(solution)/shard_map/ppermute | solution.py:45
  174.1 2.8 %all-gather.11.cloned.1.call-done = bf16[1664,1536]{1,0:T(8,128)(2,1)} async-done(((bf16[208,1536]{1,0:T(8,128)(2,1)}), bf16[1664,1536]{1,0:T(8,128)(2,1)}) %all-gather.11.cloned.1.call-update) | async-done | bytes 5111824 | tf_op jit(solution)/shard_map/all_gather | solution.py:358
  176.9 2.4 %copy-done.1 = bf16[1664,1536]{1,0:T(8,128)(2,1)S(1)} copy-done((bf16[1664,1536]{1,0:T(8,128)(2,1)S(1)}, bf16[1664,1536]{1,0:T(8,128)(2,1)}, u32[]{:S(2)}) %copy-start.1) | copy-done | bytes 5111832
  179.3 4.7 %shard_map.106 = (bf16[768,1536]{1,0:T(8,128)(2,1)S(1)}, bf16[3,192,1536]{2,1,0:T(8,128)(2,1)S(1)}) custom-call(bf16[8,208,1536]{2,1,0:T(8,128)(2,1)S(1)} %bitcast.11, bf16[6,3,192,1536]{3,2,1,0:T(8,128)(2,1)} %refs_1_.10), custom_call_target="tpu_custom_call" | custom-call | bytes 4128768 | tf_op jit(solution)/shard_map/pallas_call | solution.py:123
  185.4 4.1 %collective-permute-start.31 = (bf16[64,1536]{1,0:T(8,128)(2,1)S(1)}, bf16[64,1536]{1,0:T(8,128)(2,1)S(1)}, u32[]{:S(2)}, u32[]{:S(2)}) collective-permute-start(bf16[64,1536]{1,0:T(8,128)(2,1)S(1)} %get-tuple-element.96), channel_id=1, source_target_pairs={{0,4},{4,8},{8,12},{12,16},{16,20},{20,24},{24,28},{1,5},{5,9},{9,... | collective-permute-start | bytes 589832 | tf_op jit(solution)/shard_map/ppermute | solution.py:44
  190.9 6.6 %collective-permute-done.32.below = bf16[64,1536]{1,0:T(8,128)(2,1)S(1)} collective-permute-done((bf16[64,1536]{1,0:T(8,128)(2,1)S(1)}, bf16[64,1536]{1,0:T(8,128)(2,1)S(1)}, u32[]{:S(2)}, u32[]{:S(2)}) %collective-permute-start.32) | collective-permute-done | bytes 196640 | tf_op jit(solution)/shard_map/ppermute | solution.py:45
  202.2 3.6 %shard_map.109 = (bf16[768,1536]{1,0:T(8,128)(2,1)S(1)}, bf16[1536,1024]{1,0:T(8,128)(2,1)S(1)}) custom-call(bf16[8,208,1536]{2,1,0:T(8,128)(2,1)S(1)} %bitcast.13, bf16[1536,1024]{1,0:T(8,128)(2,1)S(1)} %copy-done.5), custom_call_target="tpu_custom_call" | custom-call | bytes 5505024 | tf_op jit(solution)/shard_map/pallas_call | solution.py:123
  205.7 7.9 %collective-permute-done.35.a3 = bf16[192,384]{1,0:T(8,128)(2,1)S(1)} collective-permute-done((bf16[192,384]{1,0:T(8,128)(2,1)S(1)}, bf16[192,384]{1,0:T(8,128)(2,1)S(1)}, u32[]{:S(2)}, u32[]{:S(2)}) %collective-permute-start.35) | collective-permute-done | bytes 147488 | tf_op jit(solution)/shard_map/ppermute | solution.py:35
  213.7 4.2 %shard_map.110 = (bf16[384,1024]{1,0:T(8,128)(2,1)}, bf16[64,1024]{1,0:T(8,128)(2,1)}) custom-call(bf16[192,384]{1,0:T(8,128)(2,1)S(1)} %shard_map.108.a0, bf16[192,384]{1,0:T(8,128)(2,1)S(1)} %collective-permute-done.33.a1, bf16[192,384]{1,0:T(8,128)(2,1)S(1)} %collective-permute-done.34.a2, bf16[192,384]{1,0:T(8,128)(2,1)S(1)} %collective-permute-done.35.a3, ...), custom_call_target="tpu_custom_call" | custom-call | flops 2113929216 | bytes 6684672 | tf_op jit(solution)/shard_map/pallas_call | solution.py:123
  217.9 6.2 %all-to-all-start = ((bf16[8,8,1024]{2,1,0:T(8,128)(2,1)}), bf16[8,8,1024]{2,1,0:T(8,128)(2,1)S(1)}, u32[]{:S(2)}, u32[]{:S(2)}) async-start(bf16[8,8,1024]{2,1,0:T(8,128)(2,1)} %bitcast.9), calls=%async_computation | async-start | bytes 262144 | tf_op jit(solution)/shard_map/all_to_all | solution.py:425
  224.2 5.4 %all-to-all-done = bf16[8,8,1024]{2,1,0:T(8,128)(2,1)S(1)} async-done(((bf16[8,8,1024]{2,1,0:T(8,128)(2,1)}), bf16[8,8,1024]{2,1,0:T(8,128)(2,1)S(1)}, u32[]{:S(2)}, u32[]{:S(2)}) %all-to-all-start) | async-done | bytes 131104 | tf_op jit(solution)/shard_map/all_to_all | solution.py:425
  (124 shorter events, 70.9 us)
Async XLA Ops:
  7.2 62.7 %all-gather.7.cloned.1.call-start = ((), (), s32[]{:S(2)}) async-start(), calls=%async_computation.1 | async-start | bytes 5308416 | tf_op jit(solution)/shard_map/all_gather | solution.py:358
  11.0 12.2 %collective-permute-start.2 = (bf16[48,1536]{1,0:T(8,128)(2,1)S(1)}, bf16[48,1536]{1,0:T(8,128)(2,1)S(1)}, u32[]{:S(2)}, u32[]{:S(2)}) collective-permute-start(bf16[48,1536]{1,0:T(8,128)(2,1)S(1)} %constant_dynamic-slice_fusion.2), channel_id=1, source_target_pairs={{0,1},{1,2},{2,3},{3,0},{4,5},{5,6},{6,7},{7,4},{8,9},{9,10},{10,1... | collective-permute-start | bytes 442376 | tf_op jit(solution)/shard_map/ppermute | solution.py:35
  12.6 12.6 %collective-permute-start.3 = (bf16[48,1536]{1,0:T(8,128)(2,1)S(1)}, bf16[48,1536]{1,0:T(8,128)(2,1)S(1)}, u32[]{:S(2)}, u32[]{:S(2)}) collective-permute-start(bf16[48,1536]{1,0:T(8,128)(2,1)S(1)} %constant_dynamic-slice_fusion.2), channel_id=1, source_target_pairs={{0,2},{1,3},{2,0},{3,1},{4,6},{5,7},{6,4},{7,5},{8,10},{9,11},{10,... | collective-permute-start | bytes 442376 | tf_op jit(solution)/shard_map/ppermute | solution.py:35
  13.7 13.2 %collective-permute-start.4 = (bf16[48,1536]{1,0:T(8,128)(2,1)S(1)}, bf16[48,1536]{1,0:T(8,128)(2,1)S(1)}, u32[]{:S(2)}, u32[]{:S(2)}) collective-permute-start(bf16[48,1536]{1,0:T(8,128)(2,1)S(1)} %constant_dynamic-slice_fusion.2), channel_id=1, source_target_pairs={{0,3},{1,0},{2,1},{3,2},{4,7},{5,4},{6,5},{7,6},{8,11},{9,8},{10,9... | collective-permute-start | bytes 442376 | tf_op jit(solution)/shard_map/ppermute | solution.py:35
  27.8 104.1 %all-gather.9.cloned.1.call-start = ((), (), s32[]{:S(2)}) async-start(), calls=%async_computation.2 | async-start | bytes 5308416 | tf_op jit(solution)/shard_map/all_gather | solution.py:358
  28.0 11.2 %collective-permute-start.5 = (bf16[464,384]{1,0:T(8,128)(2,1)S(1)}, bf16[464,384]{1,0:T(8,128)(2,1)S(1)}, u32[]{:S(2)}, u32[]{:S(2)}) collective-permute-start(bf16[464,384]{1,0:T(8,128)(2,1)S(1)} %fusion.1.c0), channel_id=1, source_target_pairs={{0,1},{1,2},{2,3},{3,0},{4,5},{5,6},{6,7},{7,4},{8,9},{9,10},{10,1... | collective-permute-start | bytes 1069064 | tf_op jit(solution)/shard_map/ppermute | solution.py:35
  28.0 30.9 %collective-permute-start.6 = (bf16[464,384]{1,0:T(8,128)(2,1)S(1)}, bf16[464,384]{1,0:T(8,128)(2,1)S(1)}, u32[]{:S(2)}, u32[]{:S(2)}) collective-permute-start(bf16[464,384]{1,0:T(8,128)(2,1)S(1)} %fusion.1.c0), channel_id=1, source_target_pairs={{0,2},{1,3},{2,0},{3,1},{4,6},{5,7},{6,4},{7,5},{8,10},{9,11},{10,... | collective-permute-start | bytes 1069064 | tf_op jit(solution)/shard_map/ppermute | solution.py:35
  29.7 30.3 %collective-permute-start.7 = (bf16[464,384]{1,0:T(8,128)(2,1)S(1)}, bf16[464,384]{1,0:T(8,128)(2,1)S(1)}, u32[]{:S(2)}, u32[]{:S(2)}) collective-permute-start(bf16[464,384]{1,0:T(8,128)(2,1)S(1)} %fusion.1.c0), channel_id=1, source_target_pairs={{0,3},{1,0},{2,1},{3,2},{4,7},{5,4},{6,5},{7,6},{8,11},{9,8},{10,9... | collective-permute-start | bytes 1069064 | tf_op jit(solution)/shard_map/ppermute | solution.py:35
  62.1 14.9 %collective-permute-start.8 = (bf16[224,384]{1,0:T(8,128)(2,1)S(1)}, bf16[224,384]{1,0:T(8,128)(2,1)S(1)}, u32[]{:S(2)}, u32[]{:S(2)}) collective-permute-start(bf16[224,384]{1,0:T(8,128)(2,1)S(1)} %get-tuple-element.49.a0), channel_id=1, source_target_pairs={{0,1},{1,2},{2,3},{3,0},{4,5},{5,6},{6,7},{7,4},{8,9},{9,10},{10,1... | collective-permute-start | bytes 516104 | tf_op jit(solution)/shard_map/ppermute | solution.py:35
  62.1 15.9 %collective-permute-start.9 = (bf16[224,384]{1,0:T(8,128)(2,1)S(1)}, bf16[224,384]{1,0:T(8,128)(2,1)S(1)}, u32[]{:S(2)}, u32[]{:S(2)}) collective-permute-start(bf16[224,384]{1,0:T(8,128)(2,1)S(1)} %get-tuple-element.49.a0), channel_id=1, source_target_pairs={{0,2},{1,3},{2,0},{3,1},{4,6},{5,7},{6,4},{7,5},{8,10},{9,11},{10,... | collective-permute-start | bytes 516104 | tf_op jit(solution)/shard_map/ppermute | solution.py:35
  64.5 21.4 %collective-permute-start.10 = (bf16[224,384]{1,0:T(8,128)(2,1)S(1)}, bf16[224,384]{1,0:T(8,128)(2,1)S(1)}, u32[]{:S(2)}, u32[]{:S(2)}) collective-permute-start(bf16[224,384]{1,0:T(8,128)(2,1)S(1)} %get-tuple-element.49.a0), channel_id=1, source_target_pairs={{0,3},{1,0},{2,1},{3,2},{4,7},{5,4},{6,5},{7,6},{8,11},{9,8},{10,9... | collective-permute-start | bytes 516104 | tf_op jit(solution)/shard_map/ppermute | solution.py:35
  67.4 23.7 %collective-permute-start.17 = (bf16[48,1536]{1,0:T(8,128)(2,1)S(1)}, bf16[48,1536]{1,0:T(8,128)(2,1)S(1)}, u32[]{:S(2)}, u32[]{:S(2)}) collective-permute-start(bf16[48,1536]{1,0:T(8,128)(2,1)S(1)} %constant_dynamic-slice_fusion.1), channel_id=1, source_target_pairs={{0,1},{1,2},{2,3},{3,0},{4,5},{5,6},{6,7},{7,4},{8,9},{9,10},{10,1... | collective-permute-start | bytes 442376 | tf_op jit(solution)/shard_map/ppermute | solution.py:35
  67.5 23.6 %collective-permute-start.18 = (bf16[48,1536]{1,0:T(8,128)(2,1)S(1)}, bf16[48,1536]{1,0:T(8,128)(2,1)S(1)}, u32[]{:S(2)}, u32[]{:S(2)}) collective-permute-start(bf16[48,1536]{1,0:T(8,128)(2,1)S(1)} %constant_dynamic-slice_fusion.1), channel_id=1, source_target_pairs={{0,2},{1,3},{2,0},{3,1},{4,6},{5,7},{6,4},{7,5},{8,10},{9,11},{10,... | collective-permute-start | bytes 442376 | tf_op jit(solution)/shard_map/ppermute | solution.py:35
  77.0 15.2 %collective-permute-start.19 = (bf16[48,1536]{1,0:T(8,128)(2,1)S(1)}, bf16[48,1536]{1,0:T(8,128)(2,1)S(1)}, u32[]{:S(2)}, u32[]{:S(2)}) collective-permute-start(bf16[48,1536]{1,0:T(8,128)(2,1)S(1)} %constant_dynamic-slice_fusion.1), channel_id=1, source_target_pairs={{0,3},{1,0},{2,1},{3,2},{4,7},{5,4},{6,5},{7,6},{8,11},{9,8},{10,9... | collective-permute-start | bytes 442376 | tf_op jit(solution)/shard_map/ppermute | solution.py:35
  93.0 83.9 %all-gather.11.cloned.1.call-start = ((), (), s32[]{:S(2)}) async-start(), calls=%async_computation.3 | async-start | bytes 5750784 | tf_op jit(solution)/shard_map/all_gather | solution.py:358
  94.0 14.2 %collective-permute-start.11 = (bf16[224,384]{1,0:T(8,128)(2,1)S(1)}, bf16[224,384]{1,0:T(8,128)(2,1)S(1)}, u32[]{:S(2)}, u32[]{:S(2)}) collective-permute-start(bf16[224,384]{1,0:T(8,128)(2,1)S(1)} %get-tuple-element.59.a0), channel_id=1, source_target_pairs={{0,1},{1,2},{2,3},{3,0},{4,5},{5,6},{6,7},{7,4},{8,9},{9,10},{10,1... | collective-permute-start | bytes 516104 | tf_op jit(solution)/shard_map/ppermute | solution.py:35
  94.1 16.1 %collective-permute-start.12 = (bf16[224,384]{1,0:T(8,128)(2,1)S(1)}, bf16[224,384]{1,0:T(8,128)(2,1)S(1)}, u32[]{:S(2)}, u32[]{:S(2)}) collective-permute-start(bf16[224,384]{1,0:T(8,128)(2,1)S(1)} %get-tuple-element.59.a0), channel_id=1, source_target_pairs={{0,2},{1,3},{2,0},{3,1},{4,6},{5,7},{6,4},{7,5},{8,10},{9,11},{10,... | collective-permute-start | bytes 516104 | tf_op jit(solution)/shard_map/ppermute | solution.py:35
  95.4 21.5 %collective-permute-start.13 = (bf16[224,384]{1,0:T(8,128)(2,1)S(1)}, bf16[224,384]{1,0:T(8,128)(2,1)S(1)}, u32[]{:S(2)}, u32[]{:S(2)}) collective-permute-start(bf16[224,384]{1,0:T(8,128)(2,1)S(1)} %get-tuple-element.59.a0), channel_id=1, source_target_pairs={{0,3},{1,0},{2,1},{3,2},{4,7},{5,4},{6,5},{7,6},{8,11},{9,8},{10,9... | collective-permute-start | bytes 516104 | tf_op jit(solution)/shard_map/ppermute | solution.py:35
  97.3 24.4 %collective-permute-start.28 = (bf16[48,1536]{1,0:T(8,128)(2,1)S(1)}, bf16[48,1536]{1,0:T(8,128)(2,1)S(1)}, u32[]{:S(2)}, u32[]{:S(2)}) collective-permute-start(bf16[48,1536]{1,0:T(8,128)(2,1)S(1)} %constant_dynamic-slice_fusion), channel_id=1, source_target_pairs={{0,1},{1,2},{2,3},{3,0},{4,5},{5,6},{6,7},{7,4},{8,9},{9,10},{10,1... | collective-permute-start | bytes 442376 | tf_op jit(solution)/shard_map/ppermute | solution.py:35
  97.6 24.2 %collective-permute-start.29 = (bf16[48,1536]{1,0:T(8,128)(2,1)S(1)}, bf16[48,1536]{1,0:T(8,128)(2,1)S(1)}, u32[]{:S(2)}, u32[]{:S(2)}) collective-permute-start(bf16[48,1536]{1,0:T(8,128)(2,1)S(1)} %constant_dynamic-slice_fusion), channel_id=1, source_target_pairs={{0,2},{1,3},{2,0},{3,1},{4,6},{5,7},{6,4},{7,5},{8,10},{9,11},{10,... | collective-permute-start | bytes 442376 | tf_op jit(solution)/shard_map/ppermute | solution.py:35
  108.2 15.0 %collective-permute-start.30 = (bf16[48,1536]{1,0:T(8,128)(2,1)S(1)}, bf16[48,1536]{1,0:T(8,128)(2,1)S(1)}, u32[]{:S(2)}, u32[]{:S(2)}) collective-permute-start(bf16[48,1536]{1,0:T(8,128)(2,1)S(1)} %constant_dynamic-slice_fusion), channel_id=1, source_target_pairs={{0,3},{1,0},{2,1},{3,2},{4,7},{5,4},{6,5},{7,6},{8,11},{9,8},{10,9... | collective-permute-start | bytes 442376 | tf_op jit(solution)/shard_map/ppermute | solution.py:35
  124.2 14.8 %collective-permute-start.14 = (bf16[224,384]{1,0:T(8,128)(2,1)S(1)}, bf16[224,384]{1,0:T(8,128)(2,1)S(1)}, u32[]{:S(2)}, u32[]{:S(2)}) collective-permute-start(bf16[224,384]{1,0:T(8,128)(2,1)S(1)} %get-tuple-element.64.a0), channel_id=1, source_target_pairs={{0,1},{1,2},{2,3},{3,0},{4,5},{5,6},{6,7},{7,4},{8,9},{9,10},{10,1... | collective-permute-start | bytes 516104 | tf_op jit(solution)/shard_map/ppermute | solution.py:35
  124.2 15.3 %collective-permute-start.15 = (bf16[224,384]{1,0:T(8,128)(2,1)S(1)}, bf16[224,384]{1,0:T(8,128)(2,1)S(1)}, u32[]{:S(2)}, u32[]{:S(2)}) collective-permute-start(bf16[224,384]{1,0:T(8,128)(2,1)S(1)} %get-tuple-element.64.a0), channel_id=1, source_target_pairs={{0,2},{1,3},{2,0},{3,1},{4,6},{5,7},{6,4},{7,5},{8,10},{9,11},{10,... | collective-permute-start | bytes 516104 | tf_op jit(solution)/shard_map/ppermute | solution.py:35
  126.4 15.0 %collective-permute-start.16 = (bf16[224,384]{1,0:T(8,128)(2,1)S(1)}, bf16[224,384]{1,0:T(8,128)(2,1)S(1)}, u32[]{:S(2)}, u32[]{:S(2)}) collective-permute-start(bf16[224,384]{1,0:T(8,128)(2,1)S(1)} %get-tuple-element.64.a0), channel_id=1, source_target_pairs={{0,3},{1,0},{2,1},{3,2},{4,7},{5,4},{6,5},{7,6},{8,11},{9,8},{10,9... | collective-permute-start | bytes 516104 | tf_op jit(solution)/shard_map/ppermute | solution.py:35
  146.5 8.5 %collective-permute-start.20 = (bf16[192,384]{1,0:T(8,128)(2,1)S(1)}, bf16[192,384]{1,0:T(8,128)(2,1)S(1)}, u32[]{:S(2)}, u32[]{:S(2)}) collective-permute-start(bf16[192,384]{1,0:T(8,128)(2,1)S(1)} %get-tuple-element.74.a0), channel_id=1, source_target_pairs={{0,1},{1,2},{2,3},{3,0},{4,5},{5,6},{6,7},{7,4},{8,9},{9,10},{10,1... | collective-permute-start | bytes 442376 | tf_op jit(solution)/shard_map/ppermute | solution.py:35
  146.8 13.0 %collective-permute-start.21 = (bf16[192,384]{1,0:T(8,128)(2,1)S(1)}, bf16[192,384]{1,0:T(8,128)(2,1)S(1)}, u32[]{:S(2)}, u32[]{:S(2)}) collective-permute-start(bf16[192,384]{1,0:T(8,128)(2,1)S(1)} %get-tuple-element.74.a0), channel_id=1, source_target_pairs={{0,2},{1,3},{2,0},{3,1},{4,6},{5,7},{6,4},{7,5},{8,10},{9,11},{10,... | collective-permute-start | bytes 442376 | tf_op jit(solution)/shard_map/ppermute | solution.py:35
  148.3 13.0 %collective-permute-start.22 = (bf16[192,384]{1,0:T(8,128)(2,1)S(1)}, bf16[192,384]{1,0:T(8,128)(2,1)S(1)}, u32[]{:S(2)}, u32[]{:S(2)}) collective-permute-start(bf16[192,384]{1,0:T(8,128)(2,1)S(1)} %get-tuple-element.74.a0), channel_id=1, source_target_pairs={{0,3},{1,0},{2,1},{3,2},{4,7},{5,4},{6,5},{7,6},{8,11},{9,8},{10,9... | collective-permute-start | bytes 442376 | tf_op jit(solution)/shard_map/ppermute | solution.py:35
  170.1 14.0 %collective-permute-start.25 = (bf16[192,384]{1,0:T(8,128)(2,1)S(1)}, bf16[192,384]{1,0:T(8,128)(2,1)S(1)}, u32[]{:S(2)}, u32[]{:S(2)}) collective-permute-start(bf16[192,384]{1,0:T(8,128)(2,1)S(1)} %shard_map.105.a0), channel_id=1, source_target_pairs={{0,1},{1,2},{2,3},{3,0},{4,5},{5,6},{6,7},{7,4},{8,9},{9,10},{10,1... | collective-permute-start | bytes 442376 | tf_op jit(solution)/shard_map/ppermute | solution.py:35
  170.2 13.9 %collective-permute-start.26 = (bf16[192,384]{1,0:T(8,128)(2,1)S(1)}, bf16[192,384]{1,0:T(8,128)(2,1)S(1)}, u32[]{:S(2)}, u32[]{:S(2)}) collective-permute-start(bf16[192,384]{1,0:T(8,128)(2,1)S(1)} %shard_map.105.a0), channel_id=1, source_target_pairs={{0,2},{1,3},{2,0},{3,1},{4,6},{5,7},{6,4},{7,5},{8,10},{9,11},{10,... | collective-permute-start | bytes 442376 | tf_op jit(solution)/shard_map/ppermute | solution.py:35
  172.1 12.0 %collective-permute-start.27 = (bf16[192,384]{1,0:T(8,128)(2,1)S(1)}, bf16[192,384]{1,0:T(8,128)(2,1)S(1)}, u32[]{:S(2)}, u32[]{:S(2)}) collective-permute-start(bf16[192,384]{1,0:T(8,128)(2,1)S(1)} %shard_map.105.a0), channel_id=1, source_target_pairs={{0,3},{1,0},{2,1},{3,2},{4,7},{5,4},{6,5},{7,6},{8,11},{9,8},{10,9... | collective-permute-start | bytes 442376 | tf_op jit(solution)/shard_map/ppermute | solution.py:35
  199.9 13.8 %collective-permute-start.35 = (bf16[192,384]{1,0:T(8,128)(2,1)S(1)}, bf16[192,384]{1,0:T(8,128)(2,1)S(1)}, u32[]{:S(2)}, u32[]{:S(2)}) collective-permute-start(bf16[192,384]{1,0:T(8,128)(2,1)S(1)} %shard_map.108.a0), channel_id=1, source_target_pairs={{0,3},{1,0},{2,1},{3,2},{4,7},{5,4},{6,5},{7,6},{8,11},{9,8},{10,9... | collective-permute-start | bytes 442376 | tf_op jit(solution)/shard_map/ppermute | solution.py:35
  217.9 11.7 %all-to-all-start = ((bf16[8,8,1024]{2,1,0:T(8,128)(2,1)}), bf16[8,8,1024]{2,1,0:T(8,128)(2,1)S(1)}, u32[]{:S(2)}, u32[]{:S(2)}) async-start(bf16[8,8,1024]{2,1,0:T(8,128)(2,1)} %bitcast.9), calls=%async_computation | async-start | bytes 262144 | tf_op jit(solution)/shard_map/all_to_all | solution.py:425
  (24 other events, 145.4 us)
Sparse Core Ops, SparseCore 0:
  28.0 39.1 all-gather.6
  93.1 38.7 all-gather.8
  134.4 42.4 all-gather.10

commit v7 on v6

--- a/solution.py
+++ b/solution.py
@@ -88,10 +88,9 @@
     return pl.ds(tile * width, width)
 
 
-def project_all(acts, weight, trunk, margin, bias, target):
+def project_all(cells, weight, trunk, margin, bias, target):
     rows, channels = target.shape
     width = tile_of(channels)
-    cells = jnp.concatenate([unpack(act[...]) for act in acts], axis=1)
     for c in range(channels // width):
         cols = columns(c, width)
         total = dot(cells, weight[:, cols]) + bias[:, cols].astype(jnp.float32)
@@ -99,13 +98,16 @@
         target[:, cols] = total.astype(BF16)
 
 
-def convolve(cells, taps, bias, step, act_ref):
+def dilated(cells, taps, step):
     rows = cells.shape[0]
     sums = [dot_last(cells, taps[t]) for t in range(3)]
-    inner = sums[1] + pltpu.roll(sums[0], step, 0) + pltpu.roll(sums[2], rows - step, 0)
+    return sums[1] + pltpu.roll(sums[0], step, 0) + pltpu.roll(sums[2], rows - step, 0)
+
+
+def convolve(cells, taps, bias, step, act_ref):
     keep = 2 * act_ref.shape[0]
-    margin = (rows - keep) // 2
-    inner = inner[margin : margin + keep] + bias.astype(jnp.float32)
+    margin = (cells.shape[0] - keep) // 2
+    inner = dilated(cells, taps, step)[margin : margin + keep] + bias.astype(jnp.float32)
     act_ref[...] = pack(gelu(inner).astype(BF16))
 
 
@@ -181,6 +183,35 @@
     )
 
 
+def join_kernel(*refs):
+    parts, target, sems = refs[:-2], refs[-2], refs[-1]
+    copies = []
+    row = 0
+    for k, part in enumerate(parts):
+        rows = part.shape[0]
+        copies.append(pltpu.make_async_copy(part, target.at[pl.ds(row, rows)], sems.at[k]))
+        row += rows
+    for copy in copies:
+        copy.start()
+    for copy in copies:
+        copy.wait()
+
+
+def join(parts):
+    rows = sum(part.shape[0] for part in parts)
+    return pl.pallas_call(
+        join_kernel,
+        in_specs=[ANY] * len(parts),
+        out_specs=pl.BlockSpec(memory_space=pltpu.HBM),
+        out_shape=shape(rows, parts[0].shape[1]),
+        scratch_shapes=[pltpu.SemaphoreType.DMA((len(parts),))],
+        compiler_params=pltpu.CompilerParams(vmem_limit_bytes=2**22),
+        cost_estimate=pl.CostEstimate(
+            flops=0, bytes_accessed=4 * rows * parts[0].shape[1], transcendentals=0
+        ),
+    )(*parts)
+
+
 def first_kernel(step, order_ref, c0, c1, c2, c3, taps, bias_ref, act_ref, trunk, pbias):
     width = c0.shape[1]
     rows = trunk.shape[0]
@@ -208,31 +239,45 @@
     )
 
 
+def gather_acts(acts, edges=()):
+    cells = []
+    for j, act in enumerate(acts):
+        parts = [unpack(act[...])]
+        if edges:
+            half = edges[j].shape[1] // 2
+            parts = [edges[j][:, :half]] + parts + [edges[j][:, half:]]
+        cells.append(jnp.concatenate(parts, axis=0))
+    return jnp.concatenate(cells, axis=1)
+
+
+def close_window(edge_ref, trunk, margin):
+    rows, channels = trunk.shape
+
+    @pl.when(edge_ref[0] == 1)
+    def _():
+        trunk[:margin] = jnp.zeros((margin, channels), BF16)
+
+    @pl.when(edge_ref[1] == 1)
+    def _():
+        trunk[rows - margin :] = jnp.zeros((margin, channels), BF16)
+
+
 def fused_kernel(
-    block, edge_ref, a0, a1, a2, a3, weight, trunk_in, pbias_ref, taps, bias_ref, act_ref, trunk
+    block, margin, edge_ref, a0, a1, a2, a3, weight, trunk_in, pbias_ref, taps, bias_ref, act_ref,
+    trunk
 ):
     pbias = pbias_ref[block : block + 1]
-    project_all((a0, a1, a2, a3), weight, trunk_in, 0, pbias, trunk)
-    rows = trunk.shape[0]
-    margin = dilation(FRAMED_BLOCKS)
-
-    @pl.when(edge_ref[0] == 1)
-    def _():
-        trunk[:margin] = jnp.zeros((margin, trunk.shape[1]), BF16)
-
-    @pl.when(edge_ref[1] == 1)
-    def _():
-        trunk[rows - margin :] = jnp.zeros((margin, trunk.shape[1]), BF16)
-
+    project_all(gather_acts((a0, a1, a2, a3)), weight, trunk_in, 0, pbias, trunk)
+    close_window(edge_ref, trunk, margin)
     bias = bias_ref[block + 1 : block + 2]
     convolve(trunk[...], taps, bias, dilation(block + 1), act_ref)
 
 
-def fused(acts, weight, trunk, pbias, taps, conv_bias, block, edge, rows_out):
+def fused(acts, weight, trunk, pbias, taps, conv_bias, block, edge, rows_out, margin):
     rows, channels = trunk.shape
     hidden = taps.shape[1]
     return kernel_call(
-        functools.partial(fused_kernel, block),
+        functools.partial(fused_kernel, block, margin),
         (edge, *acts, weight, trunk, pbias, taps, conv_bias),
         [shape(rows_out // 2, 2 * hidden), shape(rows, channels)],
         14 * rows * hidden * channels,
@@ -242,10 +287,43 @@
     )
 
 
+def edged_kernel(
+    block, margin, edge_ref, a0, a1, a2, a3, e0, e1, e2, e3, weight, above, trunk_in, below,
+    pbias_ref, taps, bias_ref, act_ref, trunk, frame
+):
+    rows = trunk_in.shape[0]
+    frame[:margin] = above[above.shape[0] - margin :]
+    frame[margin : margin + rows] = trunk_in[...]
+    frame[margin + rows :] = below[:margin]
+    pbias = pbias_ref[block : block + 1]
+    cells = gather_acts((a0, a1, a2, a3), (e0, e1, e2, e3))
+    project_all(cells, weight, frame, 0, pbias, trunk)
+    close_window(edge_ref, trunk, margin)
+    bias = bias_ref[block + 1 : block + 2]
+    convolve(trunk[...], taps, bias, dilation(block + 1), act_ref)
+
+
+def edged(acts, edges, weight, above, trunk, below, pbias, taps, conv_bias, block, edge):
+    rows, channels = trunk.shape
+    hidden = taps.shape[1]
+    margin = dilation(block + 1)
+    frame = rows + 2 * margin
+    return kernel_call(
+        functools.partial(edged_kernel, block, margin),
+        (edge, *acts, *edges, weight, above, trunk, below, pbias, taps, conv_bias),
+        [shape(rows // 2, 2 * hidden), shape(frame, channels)],
+        14 * frame * hidden * channels,
+        7 * hidden * channels + 2 * frame * channels,
+        rows * hidden,
+        scalars=1,
+        scratch=[pltpu.VMEM((frame, channels), BF16)],
+    )
+
+
 def projection_kernel(block, a0, a1, a2, a3, weight, trunk_in, pbias_ref, trunk):
     margin = (trunk_in.shape[0] - trunk.shape[0]) // 2
     pbias = pbias_ref[block : block + 1]
-    project_all((a0, a1, a2, a3), weight, trunk_in, margin, pbias, trunk)
+    project_all(gather_acts((a0, a1, a2, a3)), weight, trunk_in, margin, pbias, trunk)
 
 
 def projection(acts, weight, trunk, pbias, block):
@@ -260,21 +338,50 @@
     )[0]
 
 
-def conv_kernel(block, above, trunk, below, taps, bias_ref, act_ref):
-    cells = jnp.concatenate([above[...], trunk[...], below[...]], axis=0)
-    convolve(cells, taps, bias_ref[block : block + 1], dilation(block), act_ref)
-
-
-def conv(above, trunk, below, taps, conv_bias, block):
+def center_kernel(block, trunk, taps, bias_ref, act_ref):
+    convolve(trunk[...], taps, bias_ref[block : block + 1], dilation(block), act_ref)
+
+
+def center_conv(trunk, taps, conv_bias, block):
     rows, channels = trunk.shape
     hidden = taps.shape[1]
-    frame = rows + 2 * dilation(block)
-    return kernel_call(
-        functools.partial(conv_kernel, block),
+    return kernel_call(
+        functools.partial(center_kernel, block),
+        (trunk, taps, conv_bias),
+        [shape((rows - 2 * dilation(block)) // 2, 2 * hidden)],
+        6 * rows * hidden * channels,
+        3 * hidden * channels + rows * channels,
+        rows * hidden,
+    )[0]
+
+
+def edge_kernel(block, above, trunk, below, taps, bias_ref, act_ref):
+    step = dilation(block)
+    rows = trunk.shape[0]
+    keep = act_ref.shape[0]
+    part = keep + 2 * step
+    inner_rows = part - above.shape[0]
+    cells = jnp.concatenate(
+        [above[...], trunk[:inner_rows], trunk[rows - inner_rows :], below[...]], axis=0
+    )
+    inner = dilated(cells, taps, step) + bias_ref[block : block + 1].astype(jnp.float32)
+    top = inner[step : step + keep]
+    bottom = inner[part + step : part + step + keep]
+    act_ref[...] = jnp.concatenate([gelu(top).astype(BF16), gelu(bottom).astype(BF16)], axis=1)
+
+
+def edge_conv(above, trunk, below, taps, conv_bias, block):
+    channels = trunk.shape[1]
+    hidden = taps.shape[1]
+    step = dilation(block)
+    keep = above.shape[0]
+    rows = 2 * (keep + 2 * step)
+    return kernel_call(
+        functools.partial(edge_kernel, block),
         (above, trunk, below, taps, conv_bias),
-        [shape(rows // 2, 2 * hidden)],
-        6 * frame * hidden * channels,
-        3 * hidden * channels + frame * channels,
+        [shape(keep, 2 * hidden)],
+        6 * rows * hidden * channels,
+        3 * hidden * channels + rows * channels,
         rows * hidden,
     )[0]
 
@@ -284,7 +391,8 @@
     cover_ref, gene_ref, trunk
 ):
     pbias = pbias_ref[block : block + 1]
-    project_all((a0, a1, a2, a3), weight, trunk_in, 0, pbias, trunk)
+    margin = (trunk_in.shape[0] - trunk.shape[0]) // 2
+    project_all(gather_acts((a0, a1, a2, a3)), weight, trunk_in, margin, pbias, trunk)
     tracks = head_ref.shape[1]
     width = tile_of(tracks)
     for c in range(tracks // width):
@@ -296,8 +404,8 @@
 
 
 def head(acts, weight, trunk, pbias, block, head_weight, head_bias, onehot):
-    rows, channels = trunk.shape
-    hidden = acts[0].shape[1] // 2
+    channels = trunk.shape[1]
+    rows, hidden = 2 * acts[0].shape[0], acts[0].shape[1] // 2
     tracks = head_weight.shape[1]
     genes = onehot.shape[0]
     return kernel_call(
@@ -349,14 +457,14 @@
     mine = lax.rem(lane, size)
     packed = size == count and 2 * entries <= channels
 
+    flat = conv_out.reshape(blocks * hidden, channels)
+
     def column(load):
-        first = load * BLOCKS_PER_LOAD
-        flat = conv_out[first : first + BLOCKS_PER_LOAD].reshape(load_rows, channels)
-        return lax.dynamic_slice_in_dim(flat, mine * share, share, 0)
+        return lax.dynamic_slice_in_dim(flat, load * load_rows + mine * share, share, 0)
 
     def gather(parts):
         return lax.all_gather(
-            jnp.concatenate(parts, axis=0), "seq", axis=0, tiled=False, axis_index_groups=groups
+            join(parts), "seq", axis=0, tiled=False, axis_index_groups=groups
         )
 
     margin = dilation(FRAMED_BLOCKS)
@@ -365,12 +473,12 @@
     edge = jnp.stack([lane == 0, lane == count - 1]).astype(jnp.int32)
 
     above, below = halo(trunk_input, margin)
-    first_column = from_others(column(0))
-    loads = [gather(after_all(first_column, above, below))]
+    first = from_others(column(0))
+    loads = [gather(after_all(first, above, below))]
     own = jnp.concatenate(
         [above, trunk_input, below, jnp.pad(projection_bias, ((0, -blocks % 16), (0, 0)))], axis=0
     )
-    own = after(own, *first_column)
+    own = after(own, *first)
     cells = from_others(own)
     second = from_others(after(column(1), *cells))
 
@@ -379,8 +487,13 @@
     (taps,) = stage((after(conv_in, own),), (taps_shape,), (functools.partial(tap_cuts, 0),))
     act, trunk, biases = first_conv(cells, frame, order, taps, conv_bias, dilation(0))
 
-    onehot = None
-    for block in range(RESIDUAL_BLOCKS):
+    def staged(block, extra, extra_shape, extra_cut, token):
+        part = functools.partial(projection_cuts, block % BLOCKS_PER_LOAD, per_block, share)
+        load = after(loads[block // BLOCKS_PER_LOAD], token)
+        return stage((load, extra), (weight_shape, extra_shape), (part, extra_cut))
+
+    for block in range(FRAMED_BLOCKS):
+        later = block + 1
         others = from_others(act)
         if block == 0:
             third = from_others(after(column(2), *others))
@@ -389,38 +502,40 @@
         if block == 2:
             tail = [exon_digits(exon_bins, channels)] if packed else []
             loads.append(gather(after_all(third, act) + tail))
-        if block == 4:
-            if packed:
-                gene_lists = exon_lists(loads[2][:, quarters * share :], genes_here, entries)
-            else:
-                gene_lists = lax.all_gather(exon_bins, "seq", axis=0, tiled=True)
-            onehot = exon_onehot(gene_lists, lane * bin_rows, bin_rows)
-        later = block + 1
-        part = functools.partial(projection_cuts, block % BLOCKS_PER_LOAD, per_block, share)
-        load = after(loads[block // BLOCKS_PER_LOAD], act)
-        if later < RESIDUAL_BLOCKS:
-            weight, taps = stage(
-                (load, conv_in),
-                (weight_shape, taps_shape),
-                (part, functools.partial(tap_cuts, later)),
-            )
-        else:
-            weight, head_rows = stage(
-                (load, head_weight), (weight_shape, shape(*head_weight.shape)), (part, whole_cuts)
-            )
+        weight, taps = staged(
+            block, conv_in, taps_shape, functools.partial(tap_cuts, later), act
+        )
         if later < FRAMED_BLOCKS:
             rows_out = frame if later < FRAMED_BLOCKS - 1 else bin_rows
             act, trunk = fused(
-                others, weight, trunk, biases, taps, conv_bias, block, edge, rows_out
+                others, weight, trunk, biases, taps, conv_bias, block, edge, rows_out, margin
             )
-        elif later < RESIDUAL_BLOCKS:
+        else:
             trunk = projection(others, weight, trunk, biases, block)
-            above, below = halo(trunk, dilation(later))
-            act = conv(above, trunk, below, taps, conv_bias, later)
-        else:
-            coverage, partial = head(
-                others, weight, trunk, biases, block, head_rows, head_bias[None, :], onehot
-            )
+
+    block = FRAMED_BLOCKS
+    later = block + 1
+    act = center_conv(trunk, taps, conv_bias, block)
+    others = from_others(act)
+    above, below = halo(trunk, dilation(block) + dilation(later))
+    edges = from_others(edge_conv(above, trunk, below, taps, conv_bias, block))
+    weight, taps = staged(block, conv_in, taps_shape, functools.partial(tap_cuts, later), act)
+    act, trunk = edged(
+        others, edges, weight, above, trunk, below, biases, taps, conv_bias, block, edge
+    )
+
+    others = from_others(act)
+    weight, head_rows = staged(
+        later, head_weight, shape(*head_weight.shape), whole_cuts, act
+    )
+    if packed:
+        gene_lists = exon_lists(loads[2][:, quarters * share :], genes_here, entries)
+    else:
+        gene_lists = lax.all_gather(exon_bins, "seq", axis=0, tiled=True)
+    onehot = exon_onehot(gene_lists, lane * bin_rows, bin_rows)
+    coverage, partial = head(
+        others, weight, trunk, biases, later, head_rows, head_bias[None, :], onehot
+    )
 
     parts = lax.all_to_all(
         partial.reshape(count, genes_here, partial.shape[1]), "seq", 0, 0, tiled=False

time: 238 us -> 232 us (0.975)
  waiting for transfers between devices: 88.1 us -> 81.1 us
  Pallas kernels: 52 us -> 58.5 us
  local copies, waits for them, and re-layouts: 22.7 us -> 18.1 us
    ppermute x3 -> x2, waiting for transfers between devices: 9.4 us -> 0.01 us  [halo(): below = lax.ppermute(head, 'seq', [(i + 1, i) for i in range(count - 1)])]
    ppermute x30 -> x33, starting transfers between devices: 36.5 us -> 42.4 us  [from_others(): lax.ppermute(cells, 'trk', [(i, (i + k) % count) for i in range(count)])]
    ppermute x3 -> x2, starting transfers between devices: 9.14 us -> 5.07 us  [halo(): above = lax.ppermute(tail, 'seq', [(i, i + 1) for i in range(count - 1)])]
    pallas_call x16, Pallas kernels: 52 us -> 56 us  [kernel_call(): pl.pallas_call(body, in_specs=specs or [SMEM] * scalars + [VMEM] * (len(i...]
    slice x1 -> x0, local copies, waits for them, and re-layouts: 3.76 us -> none  [column(): flat = conv_out[first:first + BLOCKS_PER_LOAD].reshape(load_rows, channels)]
    all_gather x3, waiting for transfers between devices: 6.42 us -> 9.92 us  [gather(): lax.all_gather(join(parts), 'seq', axis=0, tiled=False, axis_index_groups...]
    pallas_call x0 -> x3, Pallas kernels: none -> 2.58 us  [join(): pl.pallas_call(join_kernel, in_specs=[ANY] * len(parts), out_specs=pl.Blo...]
    ppermute x30 -> x33, waiting for transfers between devices: 66 us -> 64.9 us  [from_others(): lax.ppermute(cells, 'trk', [(i, (i + k) % count) for i in range(count)])]
  transfers between devices with their start and end apart: 40 -> 41, of which waited for: 24 -> 22; matrix products, arithmetic and copies ran while one was open for 1% -> 1% of each run, Pallas kernels for 19% -> 20%
where the time goes in v7:
time: 232 us; the launch traced here: 231 us
  waiting for transfers between devices  81.1 us (35%)
  Pallas kernels  58.5 us (25%)
  starting transfers between devices  56.8 us (24%)
  local copies, waits for them, and re-layouts  18.1 us (8%)
  between operations  14.2 us (6%)
    ppermute x33, waiting for transfers between devices, from_others(): lax.ppermute(cells, 'trk', [(i, (i + k) % count) for i in range(count)])  64.9 us
    pallas_call x16, Pallas kernels, kernel_call(): pl.pallas_call(body, in_specs=specs or [SMEM] * scalars + [VMEM] * (len(i...  56 us
    ppermute x33, starting transfers between devices, from_others(): lax.ppermute(cells, 'trk', [(i, (i + k) % count) for i in range(count)])  42.4 us
    unnamed x30, local copies, waits for them, and re-layouts  16.2 us
    all_gather x3, waiting for transfers between devices, gather(): lax.all_gather(join(parts), 'seq', axis=0, tiled=False, axis_index_groups...  9.92 us
    all_to_all x1, starting transfers between devices, shards(): lax.all_to_all(partial.reshape(count, genes_here, partial.shape[1]), 'seq...  6.7 us
    all_to_all x1, waiting for transfers between devices, shards(): lax.all_to_all(partial.reshape(count, genes_here, partial.shape[1]), 'seq...  5.42 us
    ppermute x2, starting transfers between devices, halo(): above = lax.ppermute(tail, 'seq', [(i, i + 1) for i in range(count - 1)])  5.07 us
  transfers between devices with their start and end apart: 41, of which 22 were waited for; matrix products, arithmetic and copies ran while one was open for 1% of the time, Pallas kernels for 20%

profile of v7, /device:TPU:8, one launch (start us, length us, event | category | flops | bytes accessed | tf_op | source)
XLA Modules:
  0.0 231.0 jit_solution(16296118739104259875)
XLA Ops:
  15.1 3.0 %collective-permute-start = (bf16[32,384]{1,0:T(8,128)(2,1)S(1)}, bf16[32,384]{1,0:T(8,128)(2,1)S(1)}, u32[]{:S(2)}, u32[]{:S(2)}) collective-permute-start(bf16[32,384]{1,0:T(8,128)(2,1)S(1)} %get-tuple-element.101), channel_id=1, source_target_pairs={{0,4},{4,8},{8,12},{12,16},{16,20},{20,24},{24,28},{1,5},{5,9},{9,... | collective-permute-start | bytes 73736 | tf_op jit(solution)/shard_map/ppermute | solution.py:44
  29.0 4.2 %copy-done = bf16[6,3,192,1536]{3,2,1,0:T(8,128)(2,1)S(1)} copy-done((bf16[6,3,192,1536]{3,2,1,0:T(8,128)(2,1)S(1)}, bf16[6,3,192,1536]{3,2,1,0:T(8,128)(2,1)}, u32[]{:S(2)}) %copy-start) | copy-done | bytes 10616856
  33.9 2.7 %collective-permute-done.5.c1 = bf16[464,384]{1,0:T(8,128)(2,1)S(1)} collective-permute-done((bf16[464,384]{1,0:T(8,128)(2,1)S(1)}, bf16[464,384]{1,0:T(8,128)(2,1)S(1)}, u32[]{:S(2)}, u32[]{:S(2)}) %collective-permute-start.5) | collective-permute-done | bytes 356384 | tf_op jit(solution)/shard_map/ppermute | solution.py:35
  36.6 19.8 %collective-permute-done.6.c2 = bf16[464,384]{1,0:T(8,128)(2,1)S(1)} collective-permute-done((bf16[464,384]{1,0:T(8,128)(2,1)S(1)}, bf16[464,384]{1,0:T(8,128)(2,1)S(1)}, u32[]{:S(2)}, u32[]{:S(2)}) %collective-permute-start.6) | collective-permute-done | bytes 356384 | tf_op jit(solution)/shard_map/ppermute | solution.py:35
  59.5 2.4 %collective-permute-start.9 = (bf16[224,384]{1,0:T(8,128)(2,1)S(1)}, bf16[224,384]{1,0:T(8,128)(2,1)S(1)}, u32[]{:S(2)}, u32[]{:S(2)}) collective-permute-start(bf16[224,384]{1,0:T(8,128)(2,1)S(1)} %get-tuple-element.51.a0), channel_id=1, source_target_pairs={{0,2},{1,3},{2,0},{3,1},{4,6},{5,7},{6,4},{7,5},{8,10},{9,11},{10,... | collective-permute-start | bytes 516104 | tf_op jit(solution)/shard_map/ppermute | solution.py:35
  64.0 2.4 %collective-permute-start.18 = (bf16[48,1536]{1,0:T(8,128)(2,1)S(1)}, bf16[48,1536]{1,0:T(8,128)(2,1)S(1)}, u32[]{:S(2)}, u32[]{:S(2)}) collective-permute-start(bf16[48,1536]{1,0:T(8,128)(2,1)S(1)} %get-tuple-element.68.refs_0_), channel_id=1, source_target_pairs={{0,2},{1,3},{2,0},{3,1},{4,6},{5,7},{6,4},{7,5},{8,10},{9,11},{10,... | collective-permute-start | bytes 442376 | tf_op jit(solution)/shard_map/ppermute | solution.py:35
  66.4 2.3 %copy-done.2 = bf16[1536,1536]{1,0:T(8,128)(2,1)S(1)} copy-done((bf16[1536,1536]{1,0:T(8,128)(2,1)S(1)}, bf16[1536,1536]{1,0:T(8,128)(2,1)}, u32[]{:S(2)}) %copy-start.2) | copy-done | bytes 4718616
  68.7 4.7 %shard_map.98 = (bf16[768,1536]{1,0:T(8,128)(2,1)S(1)}, bf16[3,192,1536]{2,1,0:T(8,128)(2,1)S(1)}) custom-call(bf16[8,192,1536]{2,1,0:T(8,128)(2,1)S(1)} %bitcast.12, bf16[6,3,192,1536]{3,2,1,0:T(8,128)(2,1)} %refs_1_.10), custom_call_target="tpu_custom_call" | custom-call | bytes 4128768 | tf_op jit(solution)/shard_map/pallas_call | solution.py:125
  75.4 7.9 %collective-permute-done.10.a3 = bf16[224,384]{1,0:T(8,128)(2,1)S(1)} collective-permute-done((bf16[224,384]{1,0:T(8,128)(2,1)S(1)}, bf16[224,384]{1,0:T(8,128)(2,1)S(1)}, u32[]{:S(2)}, u32[]{:S(2)}) %collective-permute-start.10) | collective-permute-done | bytes 172064 | tf_op jit(solution)/shard_map/ppermute | solution.py:35
  83.3 4.0 %shard_map.99 = (bf16[224,384]{1,0:T(8,128)(2,1)S(1)}, bf16[448,1536]{1,0:T(8,128)(2,1)S(1)}) custom-call(s32[2]{0:T(128)S(1)} %add_convert_fusion.edge_ref, bf16[224,384]{1,0:T(8,128)(2,1)S(1)} %get-tuple-element.51.a0, bf16[224,384]{1,0:T(8,128)(2,1)S(1)} %collective-permute-done.8.a1, bf16[224,384]{1,0:T(8,128)(2,1)S(1)} %collective-permute-done.9.a2, ...), custom_call_target="tpu_custom_call" | custom-call | flops 1849688064 | bytes 6881280 | tf_op jit(solution)/shard_map/pallas_call | solution.py:125
  94.1 3.3 %collective-permute-start.32 = (bf16[48,1536]{1,0:T(8,128)(2,1)S(1)}, bf16[48,1536]{1,0:T(8,128)(2,1)S(1)}, u32[]{:S(2)}, u32[]{:S(2)}) collective-permute-start(bf16[48,1536]{1,0:T(8,128)(2,1)S(1)} %get-tuple-element.82.refs_0_), channel_id=1, source_target_pairs={{0,2},{1,3},{2,0},{3,1},{4,6},{5,7},{6,4},{7,5},{8,10},{9,11},{10,... | collective-permute-start | bytes 442376 | tf_op jit(solution)/shard_map/ppermute | solution.py:35
  97.5 2.7 %copy-done.3 = bf16[1536,1536]{1,0:T(8,128)(2,1)S(1)} copy-done((bf16[1536,1536]{1,0:T(8,128)(2,1)S(1)}, bf16[1536,1536]{1,0:T(8,128)(2,1)}, u32[]{:S(2)}) %copy-start.3) | copy-done | bytes 4718616
  100.2 4.7 %shard_map.100 = (bf16[768,1536]{1,0:T(8,128)(2,1)S(1)}, bf16[3,192,1536]{2,1,0:T(8,128)(2,1)S(1)}) custom-call(bf16[8,192,1536]{2,1,0:T(8,128)(2,1)S(1)} %bitcast.13, bf16[6,3,192,1536]{3,2,1,0:T(8,128)(2,1)} %refs_1_.10), custom_call_target="tpu_custom_call" | custom-call | bytes 4128768 | tf_op jit(solution)/shard_map/pallas_call | solution.py:125
  106.7 6.7 %collective-permute-done.13.a3 = bf16[224,384]{1,0:T(8,128)(2,1)S(1)} collective-permute-done((bf16[224,384]{1,0:T(8,128)(2,1)S(1)}, bf16[224,384]{1,0:T(8,128)(2,1)S(1)}, u32[]{:S(2)}, u32[]{:S(2)}) %collective-permute-start.13) | collective-permute-done | bytes 172064 | tf_op jit(solution)/shard_map/ppermute | solution.py:35
  113.4 3.7 %shard_map.101 = (bf16[224,384]{1,0:T(8,128)(2,1)S(1)}, bf16[448,1536]{1,0:T(8,128)(2,1)S(1)}) custom-call(s32[2]{0:T(128)S(1)} %add_convert_fusion.edge_ref, bf16[224,384]{1,0:T(8,128)(2,1)S(1)} %get-tuple-element.61.a0, bf16[224,384]{1,0:T(8,128)(2,1)S(1)} %collective-permute-done.11.a1, bf16[224,384]{1,0:T(8,128)(2,1)S(1)} %collective-permute-done.12.a2, ...), custom_call_target="tpu_custom_call" | custom-call | flops 1849688064 | bytes 6881280 | tf_op jit(solution)/shard_map/pallas_call | solution.py:125
  124.7 4.6 %all-gather.9.cloned.1.call-done = bf16[1536,1536]{1,0:T(8,128)(2,1)} async-done(((bf16[192,1536]{1,0:T(8,128)(2,1)}), bf16[1536,1536]{1,0:T(8,128)(2,1)}) %all-gather.9.cloned.1.call-update) | async-done | bytes 4718608 | tf_op jit(solution)/shard_map/all_gather | solution.py:466
  129.3 2.3 %copy-done.4 = bf16[1536,1536]{1,0:T(8,128)(2,1)S(1)} copy-done((bf16[1536,1536]{1,0:T(8,128)(2,1)S(1)}, bf16[1536,1536]{1,0:T(8,128)(2,1)}, u32[]{:S(2)}) %copy-start.4) | copy-done | bytes 4718616
  131.7 4.7 %shard_map.103 = (bf16[768,1536]{1,0:T(8,128)(2,1)S(1)}, bf16[3,192,1536]{2,1,0:T(8,128)(2,1)S(1)}) custom-call(bf16[8,192,1536]{2,1,0:T(8,128)(2,1)S(1)} %bitcast.14, bf16[6,3,192,1536]{3,2,1,0:T(8,128)(2,1)} %refs_1_.10), custom_call_target="tpu_custom_call" | custom-call | bytes 4128768 | tf_op jit(solution)/shard_map/pallas_call | solution.py:125
  137.8 5.1 %shard_map.104 = (bf16[192,384]{1,0:T(8,128)(2,1)S(1)}, bf16[448,1536]{1,0:T(8,128)(2,1)S(1)}) custom-call(s32[2]{0:T(128)S(1)} %add_convert_fusion.edge_ref, bf16[224,384]{1,0:T(8,128)(2,1)S(1)} %get-tuple-element.66.a0, bf16[224,384]{1,0:T(8,128)(2,1)S(1)} %collective-permute-done.14.a1, bf16[224,384]{1,0:T(8,128)(2,1)S(1)} %collective-permute-done.15.a2, ...), custom_call_target="tpu_custom_call" | custom-call | flops 1849688064 | bytes 6881280 | tf_op jit(solution)/shard_map/pallas_call | solution.py:125
  146.4 4.7 %shard_map.105 = (bf16[768,1536]{1,0:T(8,128)(2,1)S(1)}, bf16[3,192,1536]{2,1,0:T(8,128)(2,1)S(1)}) custom-call(bf16[8,192,1536]{2,1,0:T(8,128)(2,1)S(1)} %bitcast.15, bf16[6,3,192,1536]{3,2,1,0:T(8,128)(2,1)} %refs_1_.10), custom_call_target="tpu_custom_call" | custom-call | bytes 4128768 | tf_op jit(solution)/shard_map/pallas_call | solution.py:125
  151.2 4.9 %collective-permute-done.21.a2 = bf16[192,384]{1,0:T(8,128)(2,1)S(1)} collective-permute-done((bf16[192,384]{1,0:T(8,128)(2,1)S(1)}, bf16[192,384]{1,0:T(8,128)(2,1)S(1)}, u32[]{:S(2)}, u32[]{:S(2)}) %collective-permute-start.21) | collective-permute-done | bytes 147488 | tf_op jit(solution)/shard_map/ppermute | solution.py:35
  168.4 3.3 %collective-permute-start.29 = (bf16[96,384]{1,0:T(8,128)(2,1)S(1)}, bf16[96,384]{1,0:T(8,128)(2,1)S(1)}, u32[]{:S(2)}, u32[]{:S(2)}) collective-permute-start(bf16[96,384]{1,0:T(8,128)(2,1)S(1)} %shard_map.108.e0), channel_id=1, source_target_pairs={{0,2},{1,3},{2,0},{3,1},{4,6},{5,7},{6,4},{7,5},{8,10},{9,11},{10,... | collective-permute-start | bytes 221192 | tf_op jit(solution)/shard_map/ppermute | solution.py:35
  171.9 5.3 %all-gather.11.cloned.1.call-done = bf16[1664,1536]{1,0:T(8,128)(2,1)} async-done(((bf16[208,1536]{1,0:T(8,128)(2,1)}), bf16[1664,1536]{1,0:T(8,128)(2,1)}) %all-gather.11.cloned.1.call-update) | async-done | bytes 5111824 | tf_op jit(solution)/shard_map/all_gather | solution.py:466
  177.2 2.4 %copy-done.1 = bf16[1664,1536]{1,0:T(8,128)(2,1)S(1)} copy-done((bf16[1664,1536]{1,0:T(8,128)(2,1)S(1)}, bf16[1664,1536]{1,0:T(8,128)(2,1)}, u32[]{:S(2)}) %copy-start.1) | copy-done | bytes 5111832
  179.7 4.7 %shard_map.110 = (bf16[768,1536]{1,0:T(8,128)(2,1)S(1)}, bf16[3,192,1536]{2,1,0:T(8,128)(2,1)S(1)}) custom-call(bf16[8,208,1536]{2,1,0:T(8,128)(2,1)S(1)} %bitcast.9, bf16[6,3,192,1536]{3,2,1,0:T(8,128)(2,1)} %refs_1_.10), custom_call_target="tpu_custom_call" | custom-call | bytes 4128768 | tf_op jit(solution)/shard_map/pallas_call | solution.py:125
  184.5 5.7 %shard_map.111 = (bf16[192,384]{1,0:T(8,128)(2,1)S(1)}, bf16[512,1536]{1,0:T(8,128)(2,1)S(1)}) custom-call(s32[2]{0:T(128)S(1)} %add_convert_fusion.edge_ref, bf16[160,384]{1,0:T(8,128)(2,1)S(1)} %shard_map.107.a0, bf16[160,384]{1,0:T(8,128)(2,1)S(1)} %collective-permute-done.23.a1, bf16[160,384]{1,0:T(8,128)(2,1)S(1)} %collective-permute-done.24.a2, ...), custom_call_target="tpu_custom_call" | custom-call | flops 2113929216 | bytes 7274496 | tf_op jit(solution)/shard_map/pallas_call | solution.py:125
  190.2 2.7 %collective-permute-start.34 = (bf16[192,384]{1,0:T(8,128)(2,1)S(1)}, bf16[192,384]{1,0:T(8,128)(2,1)S(1)}, u32[]{:S(2)}, u32[]{:S(2)}) collective-permute-start(bf16[192,384]{1,0:T(8,128)(2,1)S(1)} %get-tuple-element.89.a0), channel_id=1, source_target_pairs={{0,1},{1,2},{2,3},{3,0},{4,5},{5,6},{6,7},{7,4},{8,9},{9,10},{10,1... | collective-permute-start | bytes 442376 | tf_op jit(solution)/shard_map/ppermute | solution.py:35
  195.3 3.6 %shard_map.112 = (bf16[768,1536]{1,0:T(8,128)(2,1)S(1)}, bf16[1536,1024]{1,0:T(8,128)(2,1)S(1)}) custom-call(bf16[8,208,1536]{2,1,0:T(8,128)(2,1)S(1)} %bitcast.11, bf16[1536,1024]{1,0:T(8,128)(2,1)S(1)} %copy-done.5), custom_call_target="tpu_custom_call" | custom-call | bytes 5505024 | tf_op jit(solution)/shard_map/pallas_call | solution.py:125
  200.1 4.9 %collective-permute-done.35.a2 = bf16[192,384]{1,0:T(8,128)(2,1)S(1)} collective-permute-done((bf16[192,384]{1,0:T(8,128)(2,1)S(1)}, bf16[192,384]{1,0:T(8,128)(2,1)S(1)}, u32[]{:S(2)}, u32[]{:S(2)}) %collective-permute-start.35) | collective-permute-done | bytes 147488 | tf_op jit(solution)/shard_map/ppermute | solution.py:35
  207.3 4.2 %shard_map.113 = (bf16[384,1024]{1,0:T(8,128)(2,1)}, bf16[64,1024]{1,0:T(8,128)(2,1)}) custom-call(bf16[192,384]{1,0:T(8,128)(2,1)S(1)} %get-tuple-element.89.a0, bf16[192,384]{1,0:T(8,128)(2,1)S(1)} %collective-permute-done.34.a1, bf16[192,384]{1,0:T(8,128)(2,1)S(1)} %collective-permute-done.35.a2, bf16[192,384]{1,0:T(8,128)(2,1)S(1)} %collective-permute-done.36.a3, ...), custom_call_target="tpu_custom_call" | custom-call | flops 2113929216 | bytes 6684672 | tf_op jit(solution)/shard_map/pallas_call | solution.py:125
  211.5 6.7 %all-to-all-start = ((bf16[8,8,1024]{2,1,0:T(8,128)(2,1)}), bf16[8,8,1024]{2,1,0:T(8,128)(2,1)S(1)}, u32[]{:S(2)}, u32[]{:S(2)}) async-start(bf16[8,8,1024]{2,1,0:T(8,128)(2,1)} %bitcast.7), calls=%async_computation | async-start | bytes 262144 | tf_op jit(solution)/shard_map/all_to_all | solution.py:540
  218.3 5.4 %all-to-all-done = bf16[8,8,1024]{2,1,0:T(8,128)(2,1)S(1)} async-done(((bf16[8,8,1024]{2,1,0:T(8,128)(2,1)}), bf16[8,8,1024]{2,1,0:T(8,128)(2,1)S(1)}, u32[]{:S(2)}, u32[]{:S(2)}) %all-to-all-start) | async-done | bytes 131104 | tf_op jit(solution)/shard_map/all_to_all | solution.py:540
  (117 shorter events, 66.8 us)
Async XLA Ops:
  7.2 59.2 %all-gather.7.cloned.1.call-start = ((), (), s32[]{:S(2)}) async-start(), calls=%async_computation.1 | async-start | bytes 5308416 | tf_op jit(solution)/shard_map/all_gather | solution.py:466
  8.4 12.2 %collective-permute-start.2 = (bf16[48,1536]{1,0:T(8,128)(2,1)S(1)}, bf16[48,1536]{1,0:T(8,128)(2,1)S(1)}, u32[]{:S(2)}, u32[]{:S(2)}) collective-permute-start(bf16[48,1536]{1,0:T(8,128)(2,1)S(1)} %get-tuple-element.52.refs_0_), channel_id=1, source_target_pairs={{0,1},{1,2},{2,3},{3,0},{4,5},{5,6},{6,7},{7,4},{8,9},{9,10},{10,1... | collective-permute-start | bytes 442376 | tf_op jit(solution)/shard_map/ppermute | solution.py:35
  10.0 12.6 %collective-permute-start.3 = (bf16[48,1536]{1,0:T(8,128)(2,1)S(1)}, bf16[48,1536]{1,0:T(8,128)(2,1)S(1)}, u32[]{:S(2)}, u32[]{:S(2)}) collective-permute-start(bf16[48,1536]{1,0:T(8,128)(2,1)S(1)} %get-tuple-element.52.refs_0_), channel_id=1, source_target_pairs={{0,2},{1,3},{2,0},{3,1},{4,6},{5,7},{6,4},{7,5},{8,10},{9,11},{10,... | collective-permute-start | bytes 442376 | tf_op jit(solution)/shard_map/ppermute | solution.py:35
  11.1 13.2 %collective-permute-start.4 = (bf16[48,1536]{1,0:T(8,128)(2,1)S(1)}, bf16[48,1536]{1,0:T(8,128)(2,1)S(1)}, u32[]{:S(2)}, u32[]{:S(2)}) collective-permute-start(bf16[48,1536]{1,0:T(8,128)(2,1)S(1)} %get-tuple-element.52.refs_0_), channel_id=1, source_target_pairs={{0,3},{1,0},{2,1},{3,2},{4,7},{5,4},{6,5},{7,6},{8,11},{9,8},{10,9... | collective-permute-start | bytes 442376 | tf_op jit(solution)/shard_map/ppermute | solution.py:35
  25.2 104.1 %all-gather.9.cloned.1.call-start = ((), (), s32[]{:S(2)}) async-start(), calls=%async_computation.2 | async-start | bytes 5308416 | tf_op jit(solution)/shard_map/all_gather | solution.py:466
  25.4 30.9 %collective-permute-start.6 = (bf16[464,384]{1,0:T(8,128)(2,1)S(1)}, bf16[464,384]{1,0:T(8,128)(2,1)S(1)}, u32[]{:S(2)}, u32[]{:S(2)}) collective-permute-start(bf16[464,384]{1,0:T(8,128)(2,1)S(1)} %fusion.1.c0), channel_id=1, source_target_pairs={{0,2},{1,3},{2,0},{3,1},{4,6},{5,7},{6,4},{7,5},{8,10},{9,11},{10,... | collective-permute-start | bytes 1069064 | tf_op jit(solution)/shard_map/ppermute | solution.py:35
  27.1 30.3 %collective-permute-start.7 = (bf16[464,384]{1,0:T(8,128)(2,1)S(1)}, bf16[464,384]{1,0:T(8,128)(2,1)S(1)}, u32[]{:S(2)}, u32[]{:S(2)}) collective-permute-start(bf16[464,384]{1,0:T(8,128)(2,1)S(1)} %fusion.1.c0), channel_id=1, source_target_pairs={{0,3},{1,0},{2,1},{3,2},{4,7},{5,4},{6,5},{7,6},{8,11},{9,8},{10,9... | collective-permute-start | bytes 1069064 | tf_op jit(solution)/shard_map/ppermute | solution.py:35
  59.4 14.0 %collective-permute-start.8 = (bf16[224,384]{1,0:T(8,128)(2,1)S(1)}, bf16[224,384]{1,0:T(8,128)(2,1)S(1)}, u32[]{:S(2)}, u32[]{:S(2)}) collective-permute-start(bf16[224,384]{1,0:T(8,128)(2,1)S(1)} %get-tuple-element.51.a0), channel_id=1, source_target_pairs={{0,1},{1,2},{2,3},{3,0},{4,5},{5,6},{6,7},{7,4},{8,9},{9,10},{10,1... | collective-permute-start | bytes 516104 | tf_op jit(solution)/shard_map/ppermute | solution.py:35
  59.5 15.9 %collective-permute-start.9 = (bf16[224,384]{1,0:T(8,128)(2,1)S(1)}, bf16[224,384]{1,0:T(8,128)(2,1)S(1)}, u32[]{:S(2)}, u32[]{:S(2)}) collective-permute-start(bf16[224,384]{1,0:T(8,128)(2,1)S(1)} %get-tuple-element.51.a0), channel_id=1, source_target_pairs={{0,2},{1,3},{2,0},{3,1},{4,6},{5,7},{6,4},{7,5},{8,10},{9,11},{10,... | collective-permute-start | bytes 516104 | tf_op jit(solution)/shard_map/ppermute | solution.py:35
  61.9 21.4 %collective-permute-start.10 = (bf16[224,384]{1,0:T(8,128)(2,1)S(1)}, bf16[224,384]{1,0:T(8,128)(2,1)S(1)}, u32[]{:S(2)}, u32[]{:S(2)}) collective-permute-start(bf16[224,384]{1,0:T(8,128)(2,1)S(1)} %get-tuple-element.51.a0), channel_id=1, source_target_pairs={{0,3},{1,0},{2,1},{3,2},{4,7},{5,4},{6,5},{7,6},{8,11},{9,8},{10,9... | collective-permute-start | bytes 516104 | tf_op jit(solution)/shard_map/ppermute | solution.py:35
  63.9 24.5 %collective-permute-start.17 = (bf16[48,1536]{1,0:T(8,128)(2,1)S(1)}, bf16[48,1536]{1,0:T(8,128)(2,1)S(1)}, u32[]{:S(2)}, u32[]{:S(2)}) collective-permute-start(bf16[48,1536]{1,0:T(8,128)(2,1)S(1)} %get-tuple-element.68.refs_0_), channel_id=1, source_target_pairs={{0,1},{1,2},{2,3},{3,0},{4,5},{5,6},{6,7},{7,4},{8,9},{9,10},{10,1... | collective-permute-start | bytes 442376 | tf_op jit(solution)/shard_map/ppermute | solution.py:35
  64.0 24.4 %collective-permute-start.18 = (bf16[48,1536]{1,0:T(8,128)(2,1)S(1)}, bf16[48,1536]{1,0:T(8,128)(2,1)S(1)}, u32[]{:S(2)}, u32[]{:S(2)}) collective-permute-start(bf16[48,1536]{1,0:T(8,128)(2,1)S(1)} %get-tuple-element.68.refs_0_), channel_id=1, source_target_pairs={{0,2},{1,3},{2,0},{3,1},{4,6},{5,7},{6,4},{7,5},{8,10},{9,11},{10,... | collective-permute-start | bytes 442376 | tf_op jit(solution)/shard_map/ppermute | solution.py:35
  73.4 16.1 %collective-permute-start.19 = (bf16[48,1536]{1,0:T(8,128)(2,1)S(1)}, bf16[48,1536]{1,0:T(8,128)(2,1)S(1)}, u32[]{:S(2)}, u32[]{:S(2)}) collective-permute-start(bf16[48,1536]{1,0:T(8,128)(2,1)S(1)} %get-tuple-element.68.refs_0_), channel_id=1, source_target_pairs={{0,3},{1,0},{2,1},{3,2},{4,7},{5,4},{6,5},{7,6},{8,11},{9,8},{10,9... | collective-permute-start | bytes 442376 | tf_op jit(solution)/shard_map/ppermute | solution.py:35
  90.4 86.8 %all-gather.11.cloned.1.call-start = ((), (), s32[]{:S(2)}) async-start(), calls=%async_computation.3 | async-start | bytes 5750784 | tf_op jit(solution)/shard_map/all_gather | solution.py:466
  90.5 14.4 %collective-permute-start.11 = (bf16[224,384]{1,0:T(8,128)(2,1)S(1)}, bf16[224,384]{1,0:T(8,128)(2,1)S(1)}, u32[]{:S(2)}, u32[]{:S(2)}) collective-permute-start(bf16[224,384]{1,0:T(8,128)(2,1)S(1)} %get-tuple-element.61.a0), channel_id=1, source_target_pairs={{0,1},{1,2},{2,3},{3,0},{4,5},{5,6},{6,7},{7,4},{8,9},{9,10},{10,1... | collective-permute-start | bytes 516104 | tf_op jit(solution)/shard_map/ppermute | solution.py:35
  90.6 16.1 %collective-permute-start.12 = (bf16[224,384]{1,0:T(8,128)(2,1)S(1)}, bf16[224,384]{1,0:T(8,128)(2,1)S(1)}, u32[]{:S(2)}, u32[]{:S(2)}) collective-permute-start(bf16[224,384]{1,0:T(8,128)(2,1)S(1)} %get-tuple-element.61.a0), channel_id=1, source_target_pairs={{0,2},{1,3},{2,0},{3,1},{4,6},{5,7},{6,4},{7,5},{8,10},{9,11},{10,... | collective-permute-start | bytes 516104 | tf_op jit(solution)/shard_map/ppermute | solution.py:35
  91.9 21.5 %collective-permute-start.13 = (bf16[224,384]{1,0:T(8,128)(2,1)S(1)}, bf16[224,384]{1,0:T(8,128)(2,1)S(1)}, u32[]{:S(2)}, u32[]{:S(2)}) collective-permute-start(bf16[224,384]{1,0:T(8,128)(2,1)S(1)} %get-tuple-element.61.a0), channel_id=1, source_target_pairs={{0,3},{1,0},{2,1},{3,2},{4,7},{5,4},{6,5},{7,6},{8,11},{9,8},{10,9... | collective-permute-start | bytes 516104 | tf_op jit(solution)/shard_map/ppermute | solution.py:35
  93.9 24.3 %collective-permute-start.31 = (bf16[48,1536]{1,0:T(8,128)(2,1)S(1)}, bf16[48,1536]{1,0:T(8,128)(2,1)S(1)}, u32[]{:S(2)}, u32[]{:S(2)}) collective-permute-start(bf16[48,1536]{1,0:T(8,128)(2,1)S(1)} %get-tuple-element.82.refs_0_), channel_id=1, source_target_pairs={{0,1},{1,2},{2,3},{3,0},{4,5},{5,6},{6,7},{7,4},{8,9},{9,10},{10,1... | collective-permute-start | bytes 442376 | tf_op jit(solution)/shard_map/ppermute | solution.py:35
  94.1 24.2 %collective-permute-start.32 = (bf16[48,1536]{1,0:T(8,128)(2,1)S(1)}, bf16[48,1536]{1,0:T(8,128)(2,1)S(1)}, u32[]{:S(2)}, u32[]{:S(2)}) collective-permute-start(bf16[48,1536]{1,0:T(8,128)(2,1)S(1)} %get-tuple-element.82.refs_0_), channel_id=1, source_target_pairs={{0,2},{1,3},{2,0},{3,1},{4,6},{5,7},{6,4},{7,5},{8,10},{9,11},{10,... | collective-permute-start | bytes 442376 | tf_op jit(solution)/shard_map/ppermute | solution.py:35
  104.9 14.8 %collective-permute-start.33 = (bf16[48,1536]{1,0:T(8,128)(2,1)S(1)}, bf16[48,1536]{1,0:T(8,128)(2,1)S(1)}, u32[]{:S(2)}, u32[]{:S(2)}) collective-permute-start(bf16[48,1536]{1,0:T(8,128)(2,1)S(1)} %get-tuple-element.82.refs_0_), channel_id=1, source_target_pairs={{0,3},{1,0},{2,1},{3,2},{4,7},{5,4},{6,5},{7,6},{8,11},{9,8},{10,9... | collective-permute-start | bytes 442376 | tf_op jit(solution)/shard_map/ppermute | solution.py:35
  120.5 15.9 %collective-permute-start.14 = (bf16[224,384]{1,0:T(8,128)(2,1)S(1)}, bf16[224,384]{1,0:T(8,128)(2,1)S(1)}, u32[]{:S(2)}, u32[]{:S(2)}) collective-permute-start(bf16[224,384]{1,0:T(8,128)(2,1)S(1)} %get-tuple-element.66.a0), channel_id=1, source_target_pairs={{0,1},{1,2},{2,3},{3,0},{4,5},{5,6},{6,7},{7,4},{8,9},{9,10},{10,1... | collective-permute-start | bytes 516104 | tf_op jit(solution)/shard_map/ppermute | solution.py:35
  120.6 15.8 %collective-permute-start.15 = (bf16[224,384]{1,0:T(8,128)(2,1)S(1)}, bf16[224,384]{1,0:T(8,128)(2,1)S(1)}, u32[]{:S(2)}, u32[]{:S(2)}) collective-permute-start(bf16[224,384]{1,0:T(8,128)(2,1)S(1)} %get-tuple-element.66.a0), channel_id=1, source_target_pairs={{0,2},{1,3},{2,0},{3,1},{4,6},{5,7},{6,4},{7,5},{8,10},{9,11},{10,... | collective-permute-start | bytes 516104 | tf_op jit(solution)/shard_map/ppermute | solution.py:35
  122.8 15.0 %collective-permute-start.16 = (bf16[224,384]{1,0:T(8,128)(2,1)S(1)}, bf16[224,384]{1,0:T(8,128)(2,1)S(1)}, u32[]{:S(2)}, u32[]{:S(2)}) collective-permute-start(bf16[224,384]{1,0:T(8,128)(2,1)S(1)} %get-tuple-element.66.a0), channel_id=1, source_target_pairs={{0,3},{1,0},{2,1},{3,2},{4,7},{5,4},{6,5},{7,6},{8,11},{9,8},{10,9... | collective-permute-start | bytes 516104 | tf_op jit(solution)/shard_map/ppermute | solution.py:35
  143.1 13.0 %collective-permute-start.21 = (bf16[192,384]{1,0:T(8,128)(2,1)S(1)}, bf16[192,384]{1,0:T(8,128)(2,1)S(1)}, u32[]{:S(2)}, u32[]{:S(2)}) collective-permute-start(bf16[192,384]{1,0:T(8,128)(2,1)S(1)} %get-tuple-element.76.a0), channel_id=1, source_target_pairs={{0,2},{1,3},{2,0},{3,1},{4,6},{5,7},{6,4},{7,5},{8,10},{9,11},{10,... | collective-permute-start | bytes 442376 | tf_op jit(solution)/shard_map/ppermute | solution.py:35
  144.5 13.5 %collective-permute-start.22 = (bf16[192,384]{1,0:T(8,128)(2,1)S(1)}, bf16[192,384]{1,0:T(8,128)(2,1)S(1)}, u32[]{:S(2)}, u32[]{:S(2)}) collective-permute-start(bf16[192,384]{1,0:T(8,128)(2,1)S(1)} %get-tuple-element.76.a0), channel_id=1, source_target_pairs={{0,3},{1,0},{2,1},{3,2},{4,7},{5,4},{6,5},{7,6},{8,11},{9,8},{10,9... | collective-permute-start | bytes 442376 | tf_op jit(solution)/shard_map/ppermute | solution.py:35
  163.9 20.5 %collective-permute-start.24 = (bf16[160,384]{1,0:T(8,128)(2,1)S(1)}, bf16[160,384]{1,0:T(8,128)(2,1)S(1)}, u32[]{:S(2)}, u32[]{:S(2)}) collective-permute-start(bf16[160,384]{1,0:T(8,128)(2,1)S(1)} %shard_map.107.a0), channel_id=1, source_target_pairs={{0,2},{1,3},{2,0},{3,1},{4,6},{5,7},{6,4},{7,5},{8,10},{9,11},{10,... | collective-permute-start | bytes 368648 | tf_op jit(solution)/shard_map/ppermute | solution.py:35
  164.8 19.7 %collective-permute-start.25 = (bf16[160,384]{1,0:T(8,128)(2,1)S(1)}, bf16[160,384]{1,0:T(8,128)(2,1)S(1)}, u32[]{:S(2)}, u32[]{:S(2)}) collective-permute-start(bf16[160,384]{1,0:T(8,128)(2,1)S(1)} %shard_map.107.a0), channel_id=1, source_target_pairs={{0,3},{1,0},{2,1},{3,2},{4,7},{5,4},{6,5},{7,6},{8,11},{9,8},{10,9... | collective-permute-start | bytes 368648 | tf_op jit(solution)/shard_map/ppermute | solution.py:35
  167.8 16.7 %collective-permute-start.28 = (bf16[96,384]{1,0:T(8,128)(2,1)S(1)}, bf16[96,384]{1,0:T(8,128)(2,1)S(1)}, u32[]{:S(2)}, u32[]{:S(2)}) collective-permute-start(bf16[96,384]{1,0:T(8,128)(2,1)S(1)} %shard_map.108.e0), channel_id=1, source_target_pairs={{0,1},{1,2},{2,3},{3,0},{4,5},{5,6},{6,7},{7,4},{8,9},{9,10},{10,1... | collective-permute-start | bytes 221192 | tf_op jit(solution)/shard_map/ppermute | solution.py:35
  168.4 16.0 %collective-permute-start.29 = (bf16[96,384]{1,0:T(8,128)(2,1)S(1)}, bf16[96,384]{1,0:T(8,128)(2,1)S(1)}, u32[]{:S(2)}, u32[]{:S(2)}) collective-permute-start(bf16[96,384]{1,0:T(8,128)(2,1)S(1)} %shard_map.108.e0), channel_id=1, source_target_pairs={{0,2},{1,3},{2,0},{3,1},{4,6},{5,7},{6,4},{7,5},{8,10},{9,11},{10,... | collective-permute-start | bytes 221192 | tf_op jit(solution)/shard_map/ppermute | solution.py:35
  171.8 12.7 %collective-permute-start.30 = (bf16[96,384]{1,0:T(8,128)(2,1)S(1)}, bf16[96,384]{1,0:T(8,128)(2,1)S(1)}, u32[]{:S(2)}, u32[]{:S(2)}) collective-permute-start(bf16[96,384]{1,0:T(8,128)(2,1)S(1)} %shard_map.108.e0), channel_id=1, source_target_pairs={{0,3},{1,0},{2,1},{3,2},{4,7},{5,4},{6,5},{7,6},{8,11},{9,8},{10,9... | collective-permute-start | bytes 221192 | tf_op jit(solution)/shard_map/ppermute | solution.py:35
  194.3 12.9 %collective-permute-start.36 = (bf16[192,384]{1,0:T(8,128)(2,1)S(1)}, bf16[192,384]{1,0:T(8,128)(2,1)S(1)}, u32[]{:S(2)}, u32[]{:S(2)}) collective-permute-start(bf16[192,384]{1,0:T(8,128)(2,1)S(1)} %get-tuple-element.89.a0), channel_id=1, source_target_pairs={{0,3},{1,0},{2,1},{3,2},{4,7},{5,4},{6,5},{7,6},{8,11},{9,8},{10,9... | collective-permute-start | bytes 442376 | tf_op jit(solution)/shard_map/ppermute | solution.py:35
  211.5 12.2 %all-to-all-start = ((bf16[8,8,1024]{2,1,0:T(8,128)(2,1)}), bf16[8,8,1024]{2,1,0:T(8,128)(2,1)S(1)}, u32[]{:S(2)}, u32[]{:S(2)}) async-start(bf16[8,8,1024]{2,1,0:T(8,128)(2,1)} %bitcast.7), calls=%async_computation | async-start | bytes 262144 | tf_op jit(solution)/shard_map/all_to_all | solution.py:540
  (24 other events, 192.6 us)
Sparse Core Ops, SparseCore 0:
  25.3 39.1 all-gather.6
  90.5 38.7 all-gather.8
  131.8 45.4 all-gather.10

commit v8 on v7

--- a/solution.py
+++ b/solution.py
@@ -37,6 +37,16 @@
     ]
 
 
+def relayed(cells):
+    count = lax.axis_size("trk")
+    last = count - 1
+    across = lax.ppermute(cells, "trk", [(i, (i + 2) % count) for i in range(count)])
+    up = lax.ppermute(cells, "trk", [(i, i + 1) for i in range(last)])
+    down = lax.ppermute(cells, "trk", [(i + 1, i) for i in range(last)])
+    far = lax.ppermute(across, "trk", [(last - 1, last), (1, 0)])
+    return [cells, up, across, down, far]
+
+
 def halo(cells, width):
     count = lax.axis_size("seq")
     head = cells[:width]
@@ -93,7 +103,7 @@
     width = tile_of(channels)
     for c in range(channels // width):
         cols = columns(c, width)
-        total = dot(cells, weight[:, cols]) + bias[:, cols].astype(jnp.float32)
+        total = dot(cells, weight[:, :, :, cols].reshape(-1, width)) + bias[:, cols].astype(jnp.float32)
         total = total + trunk[pl.ds(margin, rows), cols].astype(jnp.float32)
         target[:, cols] = total.astype(BF16)
 
@@ -135,11 +145,13 @@
     )(*ins)
 
 
-def stage_kernel(plan, *refs):
+def stage_kernel(plan, order_ref, *refs):
     sems = refs[-1]
     used = 0
     copies = []
     for source, target, cuts in plan:
+        if cuts.func is direct_cuts:
+            cuts = functools.partial(cuts, order_ref)
         for src, dst in cuts(refs[source], refs[target]):
             copies.append(pltpu.make_async_copy(src, dst, sems.at[used]))
             used += 1
@@ -151,12 +163,15 @@
 
 def projection_cuts(part, per_block, share, load, target):
     return [
-        (
-            load.at[part * per_block + i, pl.ds(j * share, share)],
-            target.at[pl.ds((j * per_block + i) * share, share)],
-        )
-        for j in range(target.shape[0] // (per_block * share))
-        for i in range(per_block)
+        (load.at[pl.ds(part * per_block, per_block), pl.ds(j * share, share)], target.at[j])
+        for j in range(target.shape[0])
+    ]
+
+
+def direct_cuts(part, per_block, order_ref, load, target):
+    return [
+        (load.at[order_ref[j], pl.ds(part * per_block, per_block)], target.at[j])
+        for j in range(target.shape[0])
     ]
 
 
@@ -164,21 +179,21 @@
     return [(conv_in.at[block, t], target.at[t]) for t in range(3)]
 
 
-def whole_cuts(source, target):
+def whole_cuts(_, source, target):
     return [(source, target)]
 
 
-def stage(sources, targets, cuts):
+def stage(order, sources, targets, cuts):
     count = len(sources)
     plan = [(i, count + i, cut) for i, cut in enumerate(cuts)]
     return kernel_call(
         functools.partial(stage_kernel, plan),
-        sources,
+        (order, *sources),
         targets,
         0,
         sum(math.prod(t.shape) for t in targets),
         scratch=[pltpu.SemaphoreType.DMA((32,))],
-        specs=[ANY] * count,
+        specs=[SMEM] + [ANY] * count,
         limit=STAGE_BYTES,
     )
 
@@ -212,13 +227,17 @@
     )(*parts)
 
 
-def first_kernel(step, order_ref, c0, c1, c2, c3, taps, bias_ref, act_ref, trunk, pbias):
+def first_kernel(step, owner_ref, c0, c1, c2, c3, c4, taps, bias_ref, act_ref, trunk, pbias):
     width = c0.shape[1]
     rows = trunk.shape[0]
-    for k, cell in enumerate((c0, c1, c2, c3)):
-        cols = pl.ds(pl.multiple_of(order_ref[k] * width, 128), width)
-        trunk[:, cols] = cell[:rows]
-        pbias[:, cols] = cell[rows:]
+    for k, cell in enumerate((c0, c1, c2, c3, c4)):
+
+        @pl.when(owner_ref[k] >= 0)
+        def _():
+            cols = pl.ds(pl.multiple_of(owner_ref[k] * width, 128), width)
+            trunk[:, cols] = cell[:rows]
+            pbias[:, cols] = cell[rows:]
+
     convolve(trunk[...], taps, bias_ref[0:1], step, act_ref)
 
 
@@ -267,14 +286,17 @@
     trunk
 ):
     pbias = pbias_ref[block : block + 1]
-    project_all(gather_acts((a0, a1, a2, a3)), weight, trunk_in, 0, pbias, trunk)
-    close_window(edge_ref, trunk, margin)
+    skip = (trunk_in.shape[0] - trunk.shape[0]) // 2
+    project_all(gather_acts((a0, a1, a2, a3)), weight, trunk_in, skip, pbias, trunk)
+    close_window(edge_ref, trunk, margin - skip)
     bias = bias_ref[block + 1 : block + 2]
     convolve(trunk[...], taps, bias, dilation(block + 1), act_ref)
 
 
-def fused(acts, weight, trunk, pbias, taps, conv_bias, block, edge, rows_out, margin):
-    rows, channels = trunk.shape
+def fused(acts, weight, trunk, pbias, taps, conv_bias, block, edge, rows_out):
+    channels = trunk.shape[1]
+    rows = 2 * acts[0].shape[0]
+    margin = dilation(FRAMED_BLOCKS)
     hidden = taps.shape[1]
     return kernel_call(
         functools.partial(fused_kernel, block, margin),
@@ -470,6 +492,16 @@
     margin = dilation(FRAMED_BLOCKS)
     frame = bin_rows + 2 * margin
     order = lax.rem(place - jnp.arange(quarters, dtype=jnp.int32) + quarters, quarters)
+    last_place = quarters - 1
+    owners = jnp.stack(
+        [
+            place,
+            place - 1,
+            lax.rem(place + 2, quarters),
+            jnp.where(place == last_place, -1, place + 1),
+            jnp.where((place == 0) | (place == last_place), last_place - place, -1),
+        ]
+    ).astype(jnp.int32)
     edge = jnp.stack([lane == 0, lane == count - 1]).astype(jnp.int32)
 
     above, below = halo(trunk_input, margin)
@@ -478,37 +510,40 @@
     own = jnp.concatenate(
         [above, trunk_input, below, jnp.pad(projection_bias, ((0, -blocks % 16), (0, 0)))], axis=0
     )
-    own = after(own, *first)
-    cells = from_others(own)
-    second = from_others(after(column(1), *cells))
-
+    own = after(own, first[1])
+    cells = relayed(own)
+    exon_rows = [exon_digits(exon_bins, channels)] if packed else []
+    exon_rows = [exon_digits(exon_bins, channels)] if packed else []
+    second = from_others(after(column(1), cells[2]))
     taps_shape = shape(3, hidden, channels)
-    weight_shape = shape(quarters * hidden, channels)
-    (taps,) = stage((after(conv_in, own),), (taps_shape,), (functools.partial(tap_cuts, 0),))
-    act, trunk, biases = first_conv(cells, frame, order, taps, conv_bias, dilation(0))
+    weight_shape = shape(quarters, per_block, share, channels)
+    (taps,) = stage(order, (after(conv_in, own),), (taps_shape,), (functools.partial(tap_cuts, 0),))
+    act, trunk, biases = first_conv(cells, frame, owners, taps, conv_bias, dilation(0))
 
     def staged(block, extra, extra_shape, extra_cut, token):
-        part = functools.partial(projection_cuts, block % BLOCKS_PER_LOAD, per_block, share)
-        load = after(loads[block // BLOCKS_PER_LOAD], token)
-        return stage((load, extra), (weight_shape, extra_shape), (part, extra_cut))
+        place = block // BLOCKS_PER_LOAD
+        part = block % BLOCKS_PER_LOAD
+        cut = functools.partial(projection_cuts, part, per_block, share)
+        load = after(loads[place], token)
+        return stage(order, (load, extra), (weight_shape, extra_shape), (cut, extra_cut))
 
     for block in range(FRAMED_BLOCKS):
         later = block + 1
         others = from_others(act)
         if block == 0:
-            third = from_others(after(column(2), *others))
-        if block == 1:
-            loads.append(gather(after_all(second, act)))
+            loads.append(gather(after_all(second, act) + exon_rows))
         if block == 2:
-            tail = [exon_digits(exon_bins, channels)] if packed else []
-            loads.append(gather(after_all(third, act) + tail))
+            loads.append(gather(after_all(third, act)))
         weight, taps = staged(
             block, conv_in, taps_shape, functools.partial(tap_cuts, later), act
         )
+        if block == 1:
+            third = from_others(after(column(2), weight))
         if later < FRAMED_BLOCKS:
-            rows_out = frame if later < FRAMED_BLOCKS - 1 else bin_rows
+            reach = sum(dilation(b) for b in range(later + 1, FRAMED_BLOCKS))
+            rows_out = bin_rows + 2 * (-(-reach // 16) * 16)
             act, trunk = fused(
-                others, weight, trunk, biases, taps, conv_bias, block, edge, rows_out, margin
+                others, weight, trunk, biases, taps, conv_bias, block, edge, rows_out
             )
         else:
             trunk = projection(others, weight, trunk, biases, block)
@@ -526,10 +561,10 @@
 
     others = from_others(act)
     weight, head_rows = staged(
-        later, head_weight, shape(*head_weight.shape), whole_cuts, act
+        later, head_weight, shape(*head_weight.shape), functools.partial(whole_cuts, 0), act
     )
     if packed:
-        gene_lists = exon_lists(loads[2][:, quarters * share :], genes_here, entries)
+        gene_lists = exon_lists(loads[1][:, quarters * share :], genes_here, entries)
     else:
         gene_lists = lax.all_gather(exon_bins, "seq", axis=0, tiled=True)
     onehot = exon_onehot(gene_lists, lane * bin_rows, bin_rows)

time: 232 us -> 225 us (0.970); the launches traced: 231 us -> 222 us
  starting transfers between devices: 56.8 us -> 71.3 us
  waiting for transfers between devices: 81.1 us -> 67.9 us
  Pallas kernels: 58.5 us -> 47.7 us
    ppermute x33 -> x30, waiting for transfers between devices: 64.9 us -> 45.2 us  [from_others(): lax.ppermute(cells, 'trk', [(i, (i + k) % count) for i in range(count)])]
    ppermute x0 -> x4, waiting for transfers between devices: none -> 13.7 us  [the longest x1 9.75 us: relayed(): lax.ppermute(cells, 'trk', [(i, (i + 2) % count) for i in range(count)])]
    ppermute x0 -> x4, starting transfers between devices: none -> 12.2 us  [the longest x1 4.75 us: relayed(): down = lax.ppermute(cells, 'trk', [(i + 1, i) for i in range(last)])]
    pallas_call x16, Pallas kernels: 56 us -> 45 us  [kernel_call(): pl.pallas_call(body, in_specs=specs or [SMEM] * scalars + [VMEM] * (len(i...]
    all_gather x3, waiting for transfers between devices: 9.92 us -> 0.01 us  [gather(): lax.all_gather(join(parts), 'seq', axis=0, tiled=False, axis_index_groups...]
    ppermute x33 -> x30, starting transfers between devices: 42.4 us -> 48.7 us  [from_others(): lax.ppermute(cells, 'trk', [(i, (i + k) % count) for i in range(count)])]
    ppermute x2, waiting for transfers between devices: 0.01 us -> 3.51 us  [halo(): below = lax.ppermute(head, 'seq', [(i + 1, i) for i in range(count - 1)])]
    all_to_all x1, starting transfers between devices: 6.7 us -> 3.42 us  [shards(): lax.all_to_all(partial.reshape(count, genes_here, partial.shape[1]), 'seq...]
  transfers between devices with their start and end apart: 41 -> 42, of which waited for: 22 -> 23; matrix products, arithmetic and copies ran while one was open for 1% -> 2% of each run, Pallas kernels for 20% -> 16%
where the time goes in v8:
time: 225 us; the launch traced here: 222 us
  starting transfers between devices  71.3 us (32%)
  waiting for transfers between devices  67.9 us (30%)
  Pallas kernels  47.7 us (21%)
  local copies, waits for them, and re-layouts  17.6 us (8%)
  between operations  14.2 us (6%)
  other arithmetic  2.94 us (1%)
    ppermute x30, starting transfers between devices, from_others(): lax.ppermute(cells, 'trk', [(i, (i + k) % count) for i in range(count)])  48.7 us
    ppermute x30, waiting for transfers between devices, from_others(): lax.ppermute(cells, 'trk', [(i, (i + k) % count) for i in range(count)])  45.2 us
    pallas_call x16, Pallas kernels, kernel_call(): pl.pallas_call(body, in_specs=specs or [SMEM] * scalars + [VMEM] * (len(i...  45 us
    unnamed x36, local copies, waits for them, and re-layouts  14.1 us
    ppermute x1, waiting for transfers between devices, relayed(): lax.ppermute(cells, 'trk', [(i, (i + 2) % count) for i in range(count)])  9.75 us
    all_to_all x1, waiting for transfers between devices, shards(): lax.all_to_all(partial.reshape(count, genes_here, partial.shape[1]), 'seq...  5.41 us
    ppermute x1, starting transfers between devices, relayed(): down = lax.ppermute(cells, 'trk', [(i + 1, i) for i in range(last)])  4.75 us
  transfers between devices with their start and end apart: 42, of which 23 were waited for; matrix products, arithmetic and copies ran while one was open for 2% of the time, Pallas kernels for 16%

profile of v8, /device:TPU:8, one launch (start us, length us, event | category | flops | bytes accessed | tf_op | source)
XLA Modules:
  0.0 221.6 jit_solution(10727620529534184495)
XLA Ops:
  8.4 3.0 %collective-permute-start.10 = (bf16[48,1536]{1,0:T(8,128)(2,1)S(1)}, bf16[48,1536]{1,0:T(8,128)(2,1)S(1)}, u32[]{:S(2)}, u32[]{:S(2)}) collective-permute-start(bf16[48,1536]{1,0:T(8,128)(2,1)S(1)} %get-tuple-element.52.refs_0_), channel_id=1, source_target_pairs={{0,2},{1,3},{2,0},{3,1},{4,6},{5,7},{6,4},{7,5},{8,10},{9,11},{10,... | collective-permute-start | bytes 442376 | tf_op jit(solution)/shard_map/ppermute | solution.py:35
  17.3 3.5 %collective-permute-done.1 = bf16[32,384]{1,0:T(8,128)(2,1)S(1)} collective-permute-done((bf16[32,384]{1,0:T(8,128)(2,1)S(1)}, bf16[32,384]{1,0:T(8,128)(2,1)S(1)}, u32[]{:S(2)}, u32[]{:S(2)}) %collective-permute-start.1) | collective-permute-done | bytes 24608 | tf_op jit(solution)/shard_map/ppermute | solution.py:55
  26.0 4.8 %collective-permute-start.5 = (bf16[464,384]{1,0:T(8,128)(2,1)S(1)}, bf16[464,384]{1,0:T(8,128)(2,1)S(1)}, u32[]{:S(2)}, u32[]{:S(2)}) collective-permute-start(bf16[464,384]{1,0:T(8,128)(2,1)S(1)} %fusion.1.c0), channel_id=1, source_target_pairs={{1,0},{2,1},{3,2},{5,4},{6,5},{7,6},{9,8},{10,9},{11,10},{13,12},{... | collective-permute-start | bytes 1069064 | tf_op jit(solution)/shard_map/ppermute | solution.py:45
  32.7 9.8 %collective-permute-done.4.c2 = bf16[464,384]{1,0:T(8,128)(2,1)S(1)} collective-permute-done((bf16[464,384]{1,0:T(8,128)(2,1)S(1)}, bf16[464,384]{1,0:T(8,128)(2,1)S(1)}, u32[]{:S(2)}, u32[]{:S(2)}) %collective-permute-start.4) | collective-permute-done | bytes 356384 | tf_op jit(solution)/shard_map/ppermute | solution.py:43
  42.4 4.4 %collective-permute-start.6 = (bf16[464,384]{1,0:T(8,128)(2,1)S(1)}, bf16[464,384]{1,0:T(8,128)(2,1)S(1)}, u32[]{:S(2)}, u32[]{:S(2)}) collective-permute-start(bf16[464,384]{1,0:T(8,128)(2,1)S(1)} %collective-permute-done.4.c2), channel_id=1, source_target_pairs={{2,3},{1,0},{6,7},{5,4},{10,11},{9,8},{14,15},{13,12},{18,19},{17,... | collective-permute-start | bytes 1069064 | tf_op jit(solution)/shard_map/ppermute | solution.py:46
  47.0 3.0 %collective-permute-start.19 = (bf16[48,1536]{1,0:T(8,128)(2,1)S(1)}, bf16[48,1536]{1,0:T(8,128)(2,1)S(1)}, u32[]{:S(2)}, u32[]{:S(2)}) collective-permute-start(bf16[48,1536]{1,0:T(8,128)(2,1)S(1)} %get-tuple-element.68.refs_0_), channel_id=1, source_target_pairs={{0,2},{1,3},{2,0},{3,1},{4,6},{5,7},{6,4},{7,5},{8,10},{9,11},{10,... | collective-permute-start | bytes 442376 | tf_op jit(solution)/shard_map/ppermute | solution.py:35
  50.0 4.0 %collective-permute-done.5.c3 = bf16[464,384]{1,0:T(8,128)(2,1)S(1)} collective-permute-done((bf16[464,384]{1,0:T(8,128)(2,1)S(1)}, bf16[464,384]{1,0:T(8,128)(2,1)S(1)}, u32[]{:S(2)}, u32[]{:S(2)}) %collective-permute-start.5) | collective-permute-done | bytes 356384 | tf_op jit(solution)/shard_map/ppermute | solution.py:45
  54.0 4.1 %copy-done = bf16[6,3,192,1536]{3,2,1,0:T(8,128)(2,1)S(1)} copy-done((bf16[6,3,192,1536]{3,2,1,0:T(8,128)(2,1)S(1)}, bf16[6,3,192,1536]{3,2,1,0:T(8,128)(2,1)}, u32[]{:S(2)}) %copy-start) | copy-done | bytes 10616856
  67.5 2.8 %collective-permute-start.7 = (bf16[224,384]{1,0:T(8,128)(2,1)S(1)}, bf16[224,384]{1,0:T(8,128)(2,1)S(1)}, u32[]{:S(2)}, u32[]{:S(2)}) collective-permute-start(bf16[224,384]{1,0:T(8,128)(2,1)S(1)} %get-tuple-element.51.a0), channel_id=1, source_target_pairs={{0,1},{1,2},{2,3},{3,0},{4,5},{5,6},{6,7},{7,4},{8,9},{9,10},{10,1... | collective-permute-start | bytes 516104 | tf_op jit(solution)/shard_map/ppermute | solution.py:35
  72.8 2.6 %shard_map.98 = (bf16[4,4,48,1536]{3,2,1,0:T(8,128)(2,1)S(1)}, bf16[3,192,1536]{2,1,0:T(8,128)(2,1)S(1)}) custom-call(s32[4]{0:T(128)S(1)} %compare_select_fusion.order_ref, bf16[8,192,1536]{2,1,0:T(8,128)(2,1)S(1)} %bitcast.17, bf16[6,3,192,1536]{3,2,1,0:T(8,128)(2,1)} %refs_1_.10), custom_call_target="tpu_custom_call" | custom-call | bytes 4128768 | tf_op jit(solution)/shard_map/pallas_call | solution.py:135
  75.4 2.8 %collective-permute-done.9.a3 = bf16[224,384]{1,0:T(8,128)(2,1)S(1)} collective-permute-done((bf16[224,384]{1,0:T(8,128)(2,1)S(1)}, bf16[224,384]{1,0:T(8,128)(2,1)S(1)}, u32[]{:S(2)}, u32[]{:S(2)}) %collective-permute-start.9) | collective-permute-done | bytes 172064 | tf_op jit(solution)/shard_map/ppermute | solution.py:35
  79.7 4.0 %shard_map.99 = (bf16[224,384]{1,0:T(8,128)(2,1)S(1)}, bf16[448,1536]{1,0:T(8,128)(2,1)S(1)}) custom-call(s32[2]{0:T(128)S(1)} %add_convert_fusion.edge_ref, bf16[224,384]{1,0:T(8,128)(2,1)S(1)} %get-tuple-element.51.a0, bf16[224,384]{1,0:T(8,128)(2,1)S(1)} %collective-permute-done.7.a1, bf16[224,384]{1,0:T(8,128)(2,1)S(1)} %collective-permute-done.8.a2, ...), custom_call_target="tpu_custom_call" | custom-call | flops 1849688064 | bytes 6881280 | tf_op jit(solution)/shard_map/pallas_call | solution.py:135
  90.1 2.6 %collective-permute-start.34 = (bf16[48,1536]{1,0:T(8,128)(2,1)S(1)}, bf16[48,1536]{1,0:T(8,128)(2,1)S(1)}, u32[]{:S(2)}, u32[]{:S(2)}) collective-permute-start(bf16[48,1536]{1,0:T(8,128)(2,1)S(1)} %get-tuple-element.82.refs_0_), channel_id=1, source_target_pairs={{0,3},{1,0},{2,1},{3,2},{4,7},{5,4},{6,5},{7,6},{8,11},{9,8},{10,9... | collective-permute-start | bytes 442376 | tf_op jit(solution)/shard_map/ppermute | solution.py:35
  93.0 2.5 %collective-permute-start.32 = (bf16[48,1536]{1,0:T(8,128)(2,1)S(1)}, bf16[48,1536]{1,0:T(8,128)(2,1)S(1)}, u32[]{:S(2)}, u32[]{:S(2)}) collective-permute-start(bf16[48,1536]{1,0:T(8,128)(2,1)S(1)} %get-tuple-element.82.refs_0_), channel_id=1, source_target_pairs={{0,1},{1,2},{2,3},{3,0},{4,5},{5,6},{6,7},{7,4},{8,9},{9,10},{10,1... | collective-permute-start | bytes 442376 | tf_op jit(solution)/shard_map/ppermute | solution.py:35
  96.6 9.0 %collective-permute-done.12.a1 = bf16[224,384]{1,0:T(8,128)(2,1)S(1)} collective-permute-done((bf16[224,384]{1,0:T(8,128)(2,1)S(1)}, bf16[224,384]{1,0:T(8,128)(2,1)S(1)}, u32[]{:S(2)}, u32[]{:S(2)}) %collective-permute-start.12) | collective-permute-done | bytes 172064 | tf_op jit(solution)/shard_map/ppermute | solution.py:35
  105.6 3.7 %shard_map.101 = (bf16[208,384]{1,0:T(8,128)(2,1)S(1)}, bf16[448,1536]{1,0:T(8,128)(2,1)S(1)}) custom-call(s32[2]{0:T(128)S(1)} %add_convert_fusion.edge_ref, bf16[224,384]{1,0:T(8,128)(2,1)S(1)} %get-tuple-element.61.a0, bf16[224,384]{1,0:T(8,128)(2,1)S(1)} %collective-permute-done.12.a1, bf16[224,384]{1,0:T(8,128)(2,1)S(1)} %collective-permute-done.13.a2, ...), custom_call_target="tpu_custom_call" | custom-call | flops 1849688064 | bytes 6881280 | tf_op jit(solution)/shard_map/pallas_call | solution.py:135
  112.8 4.2 %collective-permute-start.17 = (bf16[208,384]{1,0:T(8,128)(2,1)S(1)}, bf16[208,384]{1,0:T(8,128)(2,1)S(1)}, u32[]{:S(2)}, u32[]{:S(2)}) collective-permute-start(bf16[208,384]{1,0:T(8,128)(2,1)S(1)} %get-tuple-element.66.a0), channel_id=1, source_target_pairs={{0,3},{1,0},{2,1},{3,2},{4,7},{5,4},{6,5},{7,6},{8,11},{9,8},{10,9... | collective-permute-start | bytes 479240 | tf_op jit(solution)/shard_map/ppermute | solution.py:35
  121.0 2.6 %shard_map.103 = (bf16[4,4,48,1536]{3,2,1,0:T(8,128)(2,1)S(1)}, bf16[3,192,1536]{2,1,0:T(8,128)(2,1)S(1)}) custom-call(s32[4]{0:T(128)S(1)} %compare_select_fusion.order_ref, bf16[8,208,1536]{2,1,0:T(8,128)(2,1)S(1)} %bitcast.15, bf16[6,3,192,1536]{3,2,1,0:T(8,128)(2,1)} %refs_1_.10), custom_call_target="tpu_custom_call" | custom-call | bytes 4128768 | tf_op jit(solution)/shard_map/pallas_call | solution.py:135
  123.6 3.2 %collective-permute-done.16.a2 = bf16[208,384]{1,0:T(8,128)(2,1)S(1)} collective-permute-done((bf16[208,384]{1,0:T(8,128)(2,1)S(1)}, bf16[208,384]{1,0:T(8,128)(2,1)S(1)}, u32[]{:S(2)}, u32[]{:S(2)}) %collective-permute-start.16) | collective-permute-done | bytes 159776 | tf_op jit(solution)/shard_map/ppermute | solution.py:35
  126.8 3.3 %collective-permute-done.15.a1 = bf16[208,384]{1,0:T(8,128)(2,1)S(1)} collective-permute-done((bf16[208,384]{1,0:T(8,128)(2,1)S(1)}, bf16[208,384]{1,0:T(8,128)(2,1)S(1)}, u32[]{:S(2)}, u32[]{:S(2)}) %collective-permute-start.15) | collective-permute-done | bytes 159776 | tf_op jit(solution)/shard_map/ppermute | solution.py:35
  130.1 4.8 %shard_map.104 = (bf16[192,384]{1,0:T(8,128)(2,1)S(1)}, bf16[416,1536]{1,0:T(8,128)(2,1)S(1)}) custom-call(s32[2]{0:T(128)S(1)} %add_convert_fusion.edge_ref, bf16[208,384]{1,0:T(8,128)(2,1)S(1)} %get-tuple-element.66.a0, bf16[208,384]{1,0:T(8,128)(2,1)S(1)} %collective-permute-done.15.a1, bf16[208,384]{1,0:T(8,128)(2,1)S(1)} %collective-permute-done.16.a2, ...), custom_call_target="tpu_custom_call" | custom-call | flops 1717567488 | bytes 6684672 | tf_op jit(solution)/shard_map/pallas_call | solution.py:135
  136.2 2.7 %collective-permute-start.22 = (bf16[192,384]{1,0:T(8,128)(2,1)S(1)}, bf16[192,384]{1,0:T(8,128)(2,1)S(1)}, u32[]{:S(2)}, u32[]{:S(2)}) collective-permute-start(bf16[192,384]{1,0:T(8,128)(2,1)S(1)} %get-tuple-element.76.a0), channel_id=1, source_target_pairs={{0,2},{1,3},{2,0},{3,1},{4,6},{5,7},{6,4},{7,5},{8,10},{9,11},{10,... | collective-permute-start | bytes 442376 | tf_op jit(solution)/shard_map/ppermute | solution.py:35
  142.3 4.6 %collective-permute-done.22.a2 = bf16[192,384]{1,0:T(8,128)(2,1)S(1)} collective-permute-done((bf16[192,384]{1,0:T(8,128)(2,1)S(1)}, bf16[192,384]{1,0:T(8,128)(2,1)S(1)}, u32[]{:S(2)}, u32[]{:S(2)}) %collective-permute-start.22) | collective-permute-done | bytes 147488 | tf_op jit(solution)/shard_map/ppermute | solution.py:35
  152.0 3.0 %collective-permute-start.27 = (bf16[96,1536]{1,0:T(8,128)(2,1)}, bf16[96,1536]{1,0:T(8,128)(2,1)S(1)}, u32[]{:S(2)}, u32[]{:S(2)}) collective-permute-start(bf16[96,1536]{1,0:T(8,128)(2,1)} %get-tuple-element.100), channel_id=1, source_target_pairs={{0,4},{4,8},{8,12},{12,16},{16,20},{20,24},{24,28},{1,5},{5,9},{9,... | collective-permute-start | bytes 884744 | tf_op jit(solution)/shard_map/ppermute | solution.py:54
  157.6 3.9 %collective-permute-start.26 = (bf16[160,384]{1,0:T(8,128)(2,1)}, bf16[160,384]{1,0:T(8,128)(2,1)S(1)}, u32[]{:S(2)}, u32[]{:S(2)}) collective-permute-start(bf16[160,384]{1,0:T(8,128)(2,1)} %shard_map.107.a0), channel_id=1, source_target_pairs={{0,3},{1,0},{2,1},{3,2},{4,7},{5,4},{6,5},{7,6},{8,11},{9,8},{10,9... | collective-permute-start | bytes 368648 | tf_op jit(solution)/shard_map/ppermute | solution.py:35
  166.0 2.9 %collective-permute-start.30 = (bf16[96,384]{1,0:T(8,128)(2,1)}, bf16[96,384]{1,0:T(8,128)(2,1)S(1)}, u32[]{:S(2)}, u32[]{:S(2)}) collective-permute-start(bf16[96,384]{1,0:T(8,128)(2,1)} %shard_map.108.e0), channel_id=1, source_target_pairs={{0,2},{1,3},{2,0},{3,1},{4,6},{5,7},{6,4},{7,5},{8,10},{9,11},{10,... | collective-permute-start | bytes 221192 | tf_op jit(solution)/shard_map/ppermute | solution.py:35
  179.2 6.3 %shard_map.111 = (bf16[192,384]{1,0:T(8,128)(2,1)S(1)}, bf16[512,1536]{1,0:T(8,128)(2,1)S(1)}) custom-call(s32[2]{0:T(128)S(1)} %add_convert_fusion.edge_ref, bf16[160,384]{1,0:T(8,128)(2,1)} %shard_map.107.a0, bf16[160,384]{1,0:T(8,128)(2,1)} %collective-permute-done.24.a1, bf16[160,384]{1,0:T(8,128)(2,1)} %collective-permute-done.25.a2, ...), custom_call_target="tpu_custom_call" | custom-call | flops 2113929216 | bytes 7274496 | tf_op jit(solution)/shard_map/pallas_call | solution.py:135
  192.8 5.2 %collective-permute-done.36.a2 = bf16[192,384]{1,0:T(8,128)(2,1)S(1)} collective-permute-done((bf16[192,384]{1,0:T(8,128)(2,1)S(1)}, bf16[192,384]{1,0:T(8,128)(2,1)S(1)}, u32[]{:S(2)}, u32[]{:S(2)}) %collective-permute-start.36) | collective-permute-done | bytes 147488 | tf_op jit(solution)/shard_map/ppermute | solution.py:35
  198.1 3.1 %collective-permute-done.35.a1 = bf16[192,384]{1,0:T(8,128)(2,1)S(1)} collective-permute-done((bf16[192,384]{1,0:T(8,128)(2,1)S(1)}, bf16[192,384]{1,0:T(8,128)(2,1)S(1)}, u32[]{:S(2)}, u32[]{:S(2)}) %collective-permute-start.35) | collective-permute-done | bytes 147488 | tf_op jit(solution)/shard_map/ppermute | solution.py:35
  201.1 4.2 %shard_map.113 = (bf16[384,1024]{1,0:T(8,128)(2,1)}, bf16[64,1024]{1,0:T(8,128)(2,1)}) custom-call(bf16[192,384]{1,0:T(8,128)(2,1)S(1)} %get-tuple-element.89.a0, bf16[192,384]{1,0:T(8,128)(2,1)S(1)} %collective-permute-done.35.a1, bf16[192,384]{1,0:T(8,128)(2,1)S(1)} %collective-permute-done.36.a2, bf16[192,384]{1,0:T(8,128)(2,1)S(1)} %collective-permute-done.37.a3, ...), custom_call_target="tpu_custom_call" | custom-call | flops 2113929216 | bytes 6684672 | tf_op jit(solution)/shard_map/pallas_call | solution.py:135
  205.4 3.4 %all-to-all-start = ((bf16[8,8,1024]{2,1,0:T(8,128)(2,1)}), bf16[8,8,1024]{2,1,0:T(8,128)(2,1)S(1)}, u32[]{:S(2)}, u32[]{:S(2)}) async-start(bf16[8,8,1024]{2,1,0:T(8,128)(2,1)} %bitcast.12), calls=%async_computation | async-start | bytes 262144 | tf_op jit(solution)/shard_map/all_to_all | solution.py:575
  208.9 5.4 %all-to-all-done = bf16[8,8,1024]{2,1,0:T(8,128)(2,1)S(1)} async-done(((bf16[8,8,1024]{2,1,0:T(8,128)(2,1)}), bf16[8,8,1024]{2,1,0:T(8,128)(2,1)S(1)}, u32[]{:S(2)}, u32[]{:S(2)}) %all-to-all-start) | async-done | bytes 131104 | tf_op jit(solution)/shard_map/all_to_all | solution.py:575
  (126 shorter events, 78.0 us)
Async XLA Ops:
  7.2 63.3 %all-gather.7.cloned.1.call-start = ((), (), s32[]{:S(2)}) async-start(), calls=%async_computation.1 | async-start | bytes 5308416 | tf_op jit(solution)/shard_map/all_gather | solution.py:488
  8.4 12.4 %collective-permute-start.11 = (bf16[48,1536]{1,0:T(8,128)(2,1)S(1)}, bf16[48,1536]{1,0:T(8,128)(2,1)S(1)}, u32[]{:S(2)}, u32[]{:S(2)}) collective-permute-start(bf16[48,1536]{1,0:T(8,128)(2,1)S(1)} %get-tuple-element.52.refs_0_), channel_id=1, source_target_pairs={{0,3},{1,0},{2,1},{3,2},{4,7},{5,4},{6,5},{7,6},{8,11},{9,8},{10,9... | collective-permute-start | bytes 442376 | tf_op jit(solution)/shard_map/ppermute | solution.py:35
  8.4 13.1 %collective-permute-start.10 = (bf16[48,1536]{1,0:T(8,128)(2,1)S(1)}, bf16[48,1536]{1,0:T(8,128)(2,1)S(1)}, u32[]{:S(2)}, u32[]{:S(2)}) collective-permute-start(bf16[48,1536]{1,0:T(8,128)(2,1)S(1)} %get-tuple-element.52.refs_0_), channel_id=1, source_target_pairs={{0,2},{1,3},{2,0},{3,1},{4,6},{5,7},{6,4},{7,5},{8,10},{9,11},{10,... | collective-permute-start | bytes 442376 | tf_op jit(solution)/shard_map/ppermute | solution.py:35
  11.5 12.3 %collective-permute-start.2 = (bf16[48,1536]{1,0:T(8,128)(2,1)S(1)}, bf16[48,1536]{1,0:T(8,128)(2,1)S(1)}, u32[]{:S(2)}, u32[]{:S(2)}) collective-permute-start(bf16[48,1536]{1,0:T(8,128)(2,1)S(1)} %get-tuple-element.52.refs_0_), channel_id=1, source_target_pairs={{0,1},{1,2},{2,3},{3,0},{4,5},{5,6},{6,7},{7,4},{8,9},{9,10},{10,1... | collective-permute-start | bytes 442376 | tf_op jit(solution)/shard_map/ppermute | solution.py:35
  24.7 93.8 %all-gather.9.cloned.1.call-start = ((), (), s32[]{:S(2)}) async-start(), calls=%async_computation.2 | async-start | bytes 5750784 | tf_op jit(solution)/shard_map/all_gather | solution.py:488
  24.8 17.6 %collective-permute-start.4 = (bf16[464,384]{1,0:T(8,128)(2,1)S(1)}, bf16[464,384]{1,0:T(8,128)(2,1)S(1)}, u32[]{:S(2)}, u32[]{:S(2)}) collective-permute-start(bf16[464,384]{1,0:T(8,128)(2,1)S(1)} %fusion.1.c0), channel_id=1, source_target_pairs={{0,2},{1,3},{2,0},{3,1},{4,6},{5,7},{6,4},{7,5},{8,10},{9,11},{10,... | collective-permute-start | bytes 1069064 | tf_op jit(solution)/shard_map/ppermute | solution.py:43
  26.0 27.9 %collective-permute-start.5 = (bf16[464,384]{1,0:T(8,128)(2,1)S(1)}, bf16[464,384]{1,0:T(8,128)(2,1)S(1)}, u32[]{:S(2)}, u32[]{:S(2)}) collective-permute-start(bf16[464,384]{1,0:T(8,128)(2,1)S(1)} %fusion.1.c0), channel_id=1, source_target_pairs={{1,0},{2,1},{3,2},{5,4},{6,5},{7,6},{9,8},{10,9},{11,10},{13,12},{... | collective-permute-start | bytes 1069064 | tf_op jit(solution)/shard_map/ppermute | solution.py:45
  30.8 28.5 %collective-permute-start.3 = (bf16[464,384]{1,0:T(8,128)(2,1)S(1)}, bf16[464,384]{1,0:T(8,128)(2,1)S(1)}, u32[]{:S(2)}, u32[]{:S(2)}) collective-permute-start(bf16[464,384]{1,0:T(8,128)(2,1)S(1)} %fusion.1.c0), channel_id=1, source_target_pairs={{0,1},{1,2},{2,3},{4,5},{5,6},{6,7},{8,9},{9,10},{10,11},{12,13},{... | collective-permute-start | bytes 1069064 | tf_op jit(solution)/shard_map/ppermute | solution.py:44
  42.4 16.9 %collective-permute-start.6 = (bf16[464,384]{1,0:T(8,128)(2,1)S(1)}, bf16[464,384]{1,0:T(8,128)(2,1)S(1)}, u32[]{:S(2)}, u32[]{:S(2)}) collective-permute-start(bf16[464,384]{1,0:T(8,128)(2,1)S(1)} %collective-permute-done.4.c2), channel_id=1, source_target_pairs={{2,3},{1,0},{6,7},{5,4},{10,11},{9,8},{14,15},{13,12},{18,19},{17,... | collective-permute-start | bytes 1069064 | tf_op jit(solution)/shard_map/ppermute | solution.py:46
  47.0 15.8 %collective-permute-start.20 = (bf16[48,1536]{1,0:T(8,128)(2,1)S(1)}, bf16[48,1536]{1,0:T(8,128)(2,1)S(1)}, u32[]{:S(2)}, u32[]{:S(2)}) collective-permute-start(bf16[48,1536]{1,0:T(8,128)(2,1)S(1)} %get-tuple-element.68.refs_0_), channel_id=1, source_target_pairs={{0,3},{1,0},{2,1},{3,2},{4,7},{5,4},{6,5},{7,6},{8,11},{9,8},{10,9... | collective-permute-start | bytes 442376 | tf_op jit(solution)/shard_map/ppermute | solution.py:35
  47.0 15.8 %collective-permute-start.19 = (bf16[48,1536]{1,0:T(8,128)(2,1)S(1)}, bf16[48,1536]{1,0:T(8,128)(2,1)S(1)}, u32[]{:S(2)}, u32[]{:S(2)}) collective-permute-start(bf16[48,1536]{1,0:T(8,128)(2,1)S(1)} %get-tuple-element.68.refs_0_), channel_id=1, source_target_pairs={{0,2},{1,3},{2,0},{3,1},{4,6},{5,7},{6,4},{7,5},{8,10},{9,11},{10,... | collective-permute-start | bytes 442376 | tf_op jit(solution)/shard_map/ppermute | solution.py:35
  63.8 106.8 %all-gather.11.cloned.1.call-start = ((), (), s32[]{:S(2)}) async-start(), calls=%async_computation.3 | async-start | bytes 5308416 | tf_op jit(solution)/shard_map/all_gather | solution.py:488
  63.8 14.4 %collective-permute-start.9 = (bf16[224,384]{1,0:T(8,128)(2,1)S(1)}, bf16[224,384]{1,0:T(8,128)(2,1)S(1)}, u32[]{:S(2)}, u32[]{:S(2)}) collective-permute-start(bf16[224,384]{1,0:T(8,128)(2,1)S(1)} %get-tuple-element.51.a0), channel_id=1, source_target_pairs={{0,3},{1,0},{2,1},{3,2},{4,7},{5,4},{6,5},{7,6},{8,11},{9,8},{10,9... | collective-permute-start | bytes 516104 | tf_op jit(solution)/shard_map/ppermute | solution.py:35
  66.3 11.9 %collective-permute-start.8 = (bf16[224,384]{1,0:T(8,128)(2,1)S(1)}, bf16[224,384]{1,0:T(8,128)(2,1)S(1)}, u32[]{:S(2)}, u32[]{:S(2)}) collective-permute-start(bf16[224,384]{1,0:T(8,128)(2,1)S(1)} %get-tuple-element.51.a0), channel_id=1, source_target_pairs={{0,2},{1,3},{2,0},{3,1},{4,6},{5,7},{6,4},{7,5},{8,10},{9,11},{10,... | collective-permute-start | bytes 516104 | tf_op jit(solution)/shard_map/ppermute | solution.py:35
  67.5 12.1 %collective-permute-start.7 = (bf16[224,384]{1,0:T(8,128)(2,1)S(1)}, bf16[224,384]{1,0:T(8,128)(2,1)S(1)}, u32[]{:S(2)}, u32[]{:S(2)}) collective-permute-start(bf16[224,384]{1,0:T(8,128)(2,1)S(1)} %get-tuple-element.51.a0), channel_id=1, source_target_pairs={{0,1},{1,2},{2,3},{3,0},{4,5},{5,6},{6,7},{7,4},{8,9},{9,10},{10,1... | collective-permute-start | bytes 516104 | tf_op jit(solution)/shard_map/ppermute | solution.py:35
  85.6 11.1 %collective-permute-start.13 = (bf16[224,384]{1,0:T(8,128)(2,1)S(1)}, bf16[224,384]{1,0:T(8,128)(2,1)S(1)}, u32[]{:S(2)}, u32[]{:S(2)}) collective-permute-start(bf16[224,384]{1,0:T(8,128)(2,1)S(1)} %get-tuple-element.61.a0), channel_id=1, source_target_pairs={{0,2},{1,3},{2,0},{3,1},{4,6},{5,7},{6,4},{7,5},{8,10},{9,11},{10,... | collective-permute-start | bytes 516104 | tf_op jit(solution)/shard_map/ppermute | solution.py:35
  87.6 18.0 %collective-permute-start.12 = (bf16[224,384]{1,0:T(8,128)(2,1)S(1)}, bf16[224,384]{1,0:T(8,128)(2,1)S(1)}, u32[]{:S(2)}, u32[]{:S(2)}) collective-permute-start(bf16[224,384]{1,0:T(8,128)(2,1)S(1)} %get-tuple-element.61.a0), channel_id=1, source_target_pairs={{0,1},{1,2},{2,3},{3,0},{4,5},{5,6},{6,7},{7,4},{8,9},{9,10},{10,1... | collective-permute-start | bytes 516104 | tf_op jit(solution)/shard_map/ppermute | solution.py:35
  90.1 21.8 %collective-permute-start.34 = (bf16[48,1536]{1,0:T(8,128)(2,1)S(1)}, bf16[48,1536]{1,0:T(8,128)(2,1)S(1)}, u32[]{:S(2)}, u32[]{:S(2)}) collective-permute-start(bf16[48,1536]{1,0:T(8,128)(2,1)S(1)} %get-tuple-element.82.refs_0_), channel_id=1, source_target_pairs={{0,3},{1,0},{2,1},{3,2},{4,7},{5,4},{6,5},{7,6},{8,11},{9,8},{10,9... | collective-permute-start | bytes 442376 | tf_op jit(solution)/shard_map/ppermute | solution.py:35
  92.7 19.3 %collective-permute-start.33 = (bf16[48,1536]{1,0:T(8,128)(2,1)S(1)}, bf16[48,1536]{1,0:T(8,128)(2,1)S(1)}, u32[]{:S(2)}, u32[]{:S(2)}) collective-permute-start(bf16[48,1536]{1,0:T(8,128)(2,1)S(1)} %get-tuple-element.82.refs_0_), channel_id=1, source_target_pairs={{0,2},{1,3},{2,0},{3,1},{4,6},{5,7},{6,4},{7,5},{8,10},{9,11},{10,... | collective-permute-start | bytes 442376 | tf_op jit(solution)/shard_map/ppermute | solution.py:35
  93.0 18.9 %collective-permute-start.32 = (bf16[48,1536]{1,0:T(8,128)(2,1)S(1)}, bf16[48,1536]{1,0:T(8,128)(2,1)S(1)}, u32[]{:S(2)}, u32[]{:S(2)}) collective-permute-start(bf16[48,1536]{1,0:T(8,128)(2,1)S(1)} %get-tuple-element.82.refs_0_), channel_id=1, source_target_pairs={{0,1},{1,2},{2,3},{3,0},{4,5},{5,6},{6,7},{7,4},{8,9},{9,10},{10,1... | collective-permute-start | bytes 442376 | tf_op jit(solution)/shard_map/ppermute | solution.py:35
  112.8 10.8 %collective-permute-start.17 = (bf16[208,384]{1,0:T(8,128)(2,1)S(1)}, bf16[208,384]{1,0:T(8,128)(2,1)S(1)}, u32[]{:S(2)}, u32[]{:S(2)}) collective-permute-start(bf16[208,384]{1,0:T(8,128)(2,1)S(1)} %get-tuple-element.66.a0), channel_id=1, source_target_pairs={{0,3},{1,0},{2,1},{3,2},{4,7},{5,4},{6,5},{7,6},{8,11},{9,8},{10,9... | collective-permute-start | bytes 479240 | tf_op jit(solution)/shard_map/ppermute | solution.py:35
  117.0 13.1 %collective-permute-start.15 = (bf16[208,384]{1,0:T(8,128)(2,1)S(1)}, bf16[208,384]{1,0:T(8,128)(2,1)S(1)}, u32[]{:S(2)}, u32[]{:S(2)}) collective-permute-start(bf16[208,384]{1,0:T(8,128)(2,1)S(1)} %get-tuple-element.66.a0), channel_id=1, source_target_pairs={{0,1},{1,2},{2,3},{3,0},{4,5},{5,6},{6,7},{7,4},{8,9},{9,10},{10,1... | collective-permute-start | bytes 479240 | tf_op jit(solution)/shard_map/ppermute | solution.py:35
  136.2 10.7 %collective-permute-start.22 = (bf16[192,384]{1,0:T(8,128)(2,1)S(1)}, bf16[192,384]{1,0:T(8,128)(2,1)S(1)}, u32[]{:S(2)}, u32[]{:S(2)}) collective-permute-start(bf16[192,384]{1,0:T(8,128)(2,1)S(1)} %get-tuple-element.76.a0), channel_id=1, source_target_pairs={{0,2},{1,3},{2,0},{3,1},{4,6},{5,7},{6,4},{7,5},{8,10},{9,11},{10,... | collective-permute-start | bytes 442376 | tf_op jit(solution)/shard_map/ppermute | solution.py:35
  150.7 13.0 %collective-permute-start.28 = (bf16[96,1536]{1,0:T(8,128)(2,1)}, bf16[96,1536]{1,0:T(8,128)(2,1)S(1)}, u32[]{:S(2)}, u32[]{:S(2)}) collective-permute-start(bf16[96,1536]{1,0:T(8,128)(2,1)} %get-tuple-element.99), channel_id=1, source_target_pairs={{4,0},{8,4},{12,8},{16,12},{20,16},{24,20},{28,24},{5,1},{9,5},{13... | collective-permute-start | bytes 884744 | tf_op jit(solution)/shard_map/ppermute | solution.py:55
  152.0 11.7 %collective-permute-start.27 = (bf16[96,1536]{1,0:T(8,128)(2,1)}, bf16[96,1536]{1,0:T(8,128)(2,1)S(1)}, u32[]{:S(2)}, u32[]{:S(2)}) collective-permute-start(bf16[96,1536]{1,0:T(8,128)(2,1)} %get-tuple-element.100), channel_id=1, source_target_pairs={{0,4},{4,8},{8,12},{12,16},{16,20},{20,24},{24,28},{1,5},{5,9},{9,... | collective-permute-start | bytes 884744 | tf_op jit(solution)/shard_map/ppermute | solution.py:54
  157.6 11.3 %collective-permute-start.26 = (bf16[160,384]{1,0:T(8,128)(2,1)}, bf16[160,384]{1,0:T(8,128)(2,1)S(1)}, u32[]{:S(2)}, u32[]{:S(2)}) collective-permute-start(bf16[160,384]{1,0:T(8,128)(2,1)} %shard_map.107.a0), channel_id=1, source_target_pairs={{0,3},{1,0},{2,1},{3,2},{4,7},{5,4},{6,5},{7,6},{8,11},{9,8},{10,9... | collective-permute-start | bytes 368648 | tf_op jit(solution)/shard_map/ppermute | solution.py:35
  162.3 13.1 %collective-permute-start.25 = (bf16[160,384]{1,0:T(8,128)(2,1)}, bf16[160,384]{1,0:T(8,128)(2,1)}, u32[]{:S(2)}, u32[]{:S(2)}) collective-permute-start(bf16[160,384]{1,0:T(8,128)(2,1)} %shard_map.107.a0), channel_id=1, source_target_pairs={{0,2},{1,3},{2,0},{3,1},{4,6},{5,7},{6,4},{7,5},{8,10},{9,11},{10,... | collective-permute-start | bytes 368648 | tf_op jit(solution)/shard_map/ppermute | solution.py:35
  162.3 13.8 %collective-permute-start.24 = (bf16[160,384]{1,0:T(8,128)(2,1)}, bf16[160,384]{1,0:T(8,128)(2,1)}, u32[]{:S(2)}, u32[]{:S(2)}) collective-permute-start(bf16[160,384]{1,0:T(8,128)(2,1)} %shard_map.107.a0), channel_id=1, source_target_pairs={{0,1},{1,2},{2,3},{3,0},{4,5},{5,6},{6,7},{7,4},{8,9},{9,10},{10,1... | collective-permute-start | bytes 368648 | tf_op jit(solution)/shard_map/ppermute | solution.py:35
  165.4 12.2 %collective-permute-start.31 = (bf16[96,384]{1,0:T(8,128)(2,1)}, bf16[96,384]{1,0:T(8,128)(2,1)S(1)}, u32[]{:S(2)}, u32[]{:S(2)}) collective-permute-start(bf16[96,384]{1,0:T(8,128)(2,1)} %shard_map.108.e0), channel_id=1, source_target_pairs={{0,3},{1,0},{2,1},{3,2},{4,7},{5,4},{6,5},{7,6},{8,11},{9,8},{10,9... | collective-permute-start | bytes 221192 | tf_op jit(solution)/shard_map/ppermute | solution.py:35
  166.0 11.6 %collective-permute-start.30 = (bf16[96,384]{1,0:T(8,128)(2,1)}, bf16[96,384]{1,0:T(8,128)(2,1)S(1)}, u32[]{:S(2)}, u32[]{:S(2)}) collective-permute-start(bf16[96,384]{1,0:T(8,128)(2,1)} %shard_map.108.e0), channel_id=1, source_target_pairs={{0,2},{1,3},{2,0},{3,1},{4,6},{5,7},{6,4},{7,5},{8,10},{9,11},{10,... | collective-permute-start | bytes 221192 | tf_op jit(solution)/shard_map/ppermute | solution.py:35
  187.1 11.0 %collective-permute-start.36 = (bf16[192,384]{1,0:T(8,128)(2,1)S(1)}, bf16[192,384]{1,0:T(8,128)(2,1)S(1)}, u32[]{:S(2)}, u32[]{:S(2)}) collective-permute-start(bf16[192,384]{1,0:T(8,128)(2,1)S(1)} %get-tuple-element.89.a0), channel_id=1, source_target_pairs={{0,2},{1,3},{2,0},{3,1},{4,6},{5,7},{6,4},{7,5},{8,10},{9,11},{10,... | collective-permute-start | bytes 442376 | tf_op jit(solution)/shard_map/ppermute | solution.py:35
  189.5 11.7 %collective-permute-start.35 = (bf16[192,384]{1,0:T(8,128)(2,1)S(1)}, bf16[192,384]{1,0:T(8,128)(2,1)S(1)}, u32[]{:S(2)}, u32[]{:S(2)}) collective-permute-start(bf16[192,384]{1,0:T(8,128)(2,1)S(1)} %get-tuple-element.89.a0), channel_id=1, source_target_pairs={{0,1},{1,2},{2,3},{3,0},{4,5},{5,6},{6,7},{7,4},{8,9},{9,10},{10,1... | collective-permute-start | bytes 442376 | tf_op jit(solution)/shard_map/ppermute | solution.py:35
  (28 other events, 303.2 us)
Sparse Core Ops, SparseCore 0:
  24.8 39.9 all-gather.6
  67.3 40.5 all-gather.8
  113.0 41.0 all-gather.10

commit v9 on v8

--- a/solution.py
+++ b/solution.py
@@ -98,19 +98,30 @@
     return pl.ds(tile * width, width)
 
 
-def project_all(cells, weight, trunk, margin, bias, target):
+def project_all(cells, weight, trunk, margin, bias, target, edge=None, closed=0):
     rows, channels = target.shape
     width = tile_of(channels)
+    if closed:
+        keep_top = (1 - edge[0]).astype(jnp.float32)
+        keep_bottom = (1 - edge[1]).astype(jnp.float32)
     for c in range(channels // width):
         cols = columns(c, width)
-        total = dot(cells, weight[:, :, :, cols].reshape(-1, width)) + bias[:, cols].astype(jnp.float32)
+        total = dot(cells, weight[:, :, :, cols].reshape(-1, width))
+        total = total + bias[:, cols].astype(jnp.float32)
         total = total + trunk[pl.ds(margin, rows), cols].astype(jnp.float32)
-        target[:, cols] = total.astype(BF16)
+        if closed:
+            target[:closed, cols] = (total[:closed] * keep_top).astype(BF16)
+            target[closed : rows - closed, cols] = total[closed : rows - closed].astype(BF16)
+            target[rows - closed :, cols] = (total[rows - closed :] * keep_bottom).astype(BF16)
+        else:
+            target[:, cols] = total.astype(BF16)
 
 
 def dilated(cells, taps, step):
     rows = cells.shape[0]
-    sums = [dot_last(cells, taps[t]) for t in range(3)]
+    hidden = taps.shape[1]
+    joint = dot_last(cells, taps[...].reshape(3 * hidden, -1))
+    sums = [joint[:, t * hidden : (t + 1) * hidden] for t in range(3)]
     return sums[1] + pltpu.roll(sums[0], step, 0) + pltpu.roll(sums[2], rows - step, 0)
 
 
@@ -269,26 +280,14 @@
     return jnp.concatenate(cells, axis=1)
 
 
-def close_window(edge_ref, trunk, margin):
-    rows, channels = trunk.shape
-
-    @pl.when(edge_ref[0] == 1)
-    def _():
-        trunk[:margin] = jnp.zeros((margin, channels), BF16)
-
-    @pl.when(edge_ref[1] == 1)
-    def _():
-        trunk[rows - margin :] = jnp.zeros((margin, channels), BF16)
-
-
 def fused_kernel(
     block, margin, edge_ref, a0, a1, a2, a3, weight, trunk_in, pbias_ref, taps, bias_ref, act_ref,
     trunk
 ):
     pbias = pbias_ref[block : block + 1]
     skip = (trunk_in.shape[0] - trunk.shape[0]) // 2
-    project_all(gather_acts((a0, a1, a2, a3)), weight, trunk_in, skip, pbias, trunk)
-    close_window(edge_ref, trunk, margin - skip)
+    cells = gather_acts((a0, a1, a2, a3))
+    project_all(cells, weight, trunk_in, skip, pbias, trunk, edge_ref, margin - skip)
     bias = bias_ref[block + 1 : block + 2]
     convolve(trunk[...], taps, bias, dilation(block + 1), act_ref)
 
@@ -319,8 +318,7 @@
     frame[margin + rows :] = below[:margin]
     pbias = pbias_ref[block : block + 1]
     cells = gather_acts((a0, a1, a2, a3), (e0, e1, e2, e3))
-    project_all(cells, weight, frame, 0, pbias, trunk)
-    close_window(edge_ref, trunk, margin)
+    project_all(cells, weight, frame, 0, pbias, trunk, edge_ref, margin)
     bias = bias_ref[block + 1 : block + 2]
     convolve(trunk[...], taps, bias, dilation(block + 1), act_ref)
 
@@ -517,7 +515,8 @@
     second = from_others(after(column(1), cells[2]))
     taps_shape = shape(3, hidden, channels)
     weight_shape = shape(quarters, per_block, share, channels)
-    (taps,) = stage(order, (after(conv_in, own),), (taps_shape,), (functools.partial(tap_cuts, 0),))
+    head_row = head_bias[None, :]
+    (taps,) = stage(order, (after(conv_in, own, head_row),), (taps_shape,), (functools.partial(tap_cuts, 0),))
     act, trunk, biases = first_conv(cells, frame, owners, taps, conv_bias, dilation(0))
 
     def staged(block, extra, extra_shape, extra_cut, token):
@@ -531,14 +530,20 @@
         later = block + 1
         others = from_others(act)
         if block == 0:
+            third = from_others(after(column(2), others[2]))
             loads.append(gather(after_all(second, act) + exon_rows))
         if block == 2:
             loads.append(gather(after_all(third, act)))
+        if block == 3:
+            if packed:
+                gene_lists = exon_lists(loads[1][:, quarters * share :], genes_here, entries)
+            else:
+                gene_lists = lax.all_gather(exon_bins, "seq", axis=0, tiled=True)
+            onehot = exon_onehot(gene_lists, lane * bin_rows, bin_rows)
+            loads[1] = after(loads[1], onehot)
         weight, taps = staged(
             block, conv_in, taps_shape, functools.partial(tap_cuts, later), act
         )
-        if block == 1:
-            third = from_others(after(column(2), weight))
         if later < FRAMED_BLOCKS:
             reach = sum(dilation(b) for b in range(later + 1, FRAMED_BLOCKS))
             rows_out = bin_rows + 2 * (-(-reach // 16) * 16)
@@ -552,7 +557,7 @@
     later = block + 1
     act = center_conv(trunk, taps, conv_bias, block)
     others = from_others(act)
-    above, below = halo(trunk, dilation(block) + dilation(later))
+    above, below = halo(after(trunk, act), dilation(block) + dilation(later))
     edges = from_others(edge_conv(above, trunk, below, taps, conv_bias, block))
     weight, taps = staged(block, conv_in, taps_shape, functools.partial(tap_cuts, later), act)
     act, trunk = edged(
@@ -563,13 +568,8 @@
     weight, head_rows = staged(
         later, head_weight, shape(*head_weight.shape), functools.partial(whole_cuts, 0), act
     )
-    if packed:
-        gene_lists = exon_lists(loads[1][:, quarters * share :], genes_here, entries)
-    else:
-        gene_lists = lax.all_gather(exon_bins, "seq", axis=0, tiled=True)
-    onehot = exon_onehot(gene_lists, lane * bin_rows, bin_rows)
     coverage, partial = head(
-        others, weight, trunk, biases, later, head_rows, head_bias[None, :], onehot
+        others, weight, trunk, biases, later, head_rows, head_row, onehot
     )
 
     parts = lax.all_to_all(

time: 225 us -> 217 us (0.964); the launches traced: 222 us -> 216 us
  waiting for transfers between devices: 67.9 us -> 83.6 us
  starting transfers between devices: 71.3 us -> 61.7 us
  Pallas kernels: 47.7 us -> 40.7 us
  local copies, waits for them, and re-layouts: 17.6 us -> 13.9 us
    ppermute x30, waiting for transfers between devices: 45.2 us -> 62.3 us  [from_others(): lax.ppermute(cells, 'trk', [(i, (i + k) % count) for i in range(count)])]
    ppermute x30, starting transfers between devices: 48.7 us -> 37.6 us  [from_others(): lax.ppermute(cells, 'trk', [(i, (i + k) % count) for i in range(count)])]
    pallas_call x16, Pallas kernels: 45 us -> 38.1 us  [kernel_call(): pl.pallas_call(body, in_specs=specs or [SMEM] * scalars + [VMEM] * (len(i...]
    ppermute x2, waiting for transfers between devices: 3.51 us -> 0.01 us  [halo(): below = lax.ppermute(head, 'seq', [(i + 1, i) for i in range(count - 1)])]
    ppermute x1, waiting for transfers between devices: 0.01 us -> 3.19 us  [relayed(): far = lax.ppermute(across, 'trk', [(last - 1, last), (1, 0)])]
    ppermute x1, waiting for transfers between devices: 3.98 us -> 1.22 us  [relayed(): down = lax.ppermute(cells, 'trk', [(i + 1, i) for i in range(last)])]
    unnamed x36 -> x24, local copies, waits for them, and re-layouts: 14.1 us -> 11.8 us
  transfers between devices with their start and end apart: 42 -> 42, of which waited for: 23 -> 27; matrix products, arithmetic and copies ran while one was open for 2% -> 1% of each run, Pallas kernels for 16% -> 15%
where the time goes in v9:
time: 217 us; the launch traced here: 216 us
  waiting for transfers between devices  83.6 us (39%)
  starting transfers between devices  61.7 us (28%)
  Pallas kernels  40.7 us (19%)
  between operations  14.2 us (7%)
  local copies, waits for them, and re-layouts  13.9 us (6%)
  other arithmetic  2.25 us (1%)
    ppermute x30, waiting for transfers between devices, from_others(): lax.ppermute(cells, 'trk', [(i, (i + k) % count) for i in range(count)])  62.3 us
    pallas_call x16, Pallas kernels, kernel_call(): pl.pallas_call(body, in_specs=specs or [SMEM] * scalars + [VMEM] * (len(i...  38.1 us
    ppermute x30, starting transfers between devices, from_others(): lax.ppermute(cells, 'trk', [(i, (i + k) % count) for i in range(count)])  37.6 us
    unnamed x24, local copies, waits for them, and re-layouts  11.8 us
    ppermute x1, waiting for transfers between devices, relayed(): lax.ppermute(cells, 'trk', [(i, (i + 2) % count) for i in range(count)])  8.49 us
    all_to_all x1, waiting for transfers between devices, shards(): lax.all_to_all(partial.reshape(count, genes_here, partial.shape[1]), 'seq...  5.42 us
    ppermute x2, starting transfers between devices, halo(): above = lax.ppermute(tail, 'seq', [(i, i + 1) for i in range(count - 1)])  5.08 us
    all_to_all x1, starting transfers between devices, shards(): lax.all_to_all(partial.reshape(count, genes_here, partial.shape[1]), 'seq...  4.66 us
  transfers between devices with their start and end apart: 42, of which 27 were waited for; matrix products, arithmetic and copies ran while one was open for 1% of the time, Pallas kernels for 15%

profile of v9, /device:TPU:8, one launch (start us, length us, event | category | flops | bytes accessed | tf_op | source)
XLA Modules:
  0.0 216.3 jit_solution(15173112554722082775)
XLA Ops:
  15.1 3.0 %collective-permute-start = (bf16[32,384]{1,0:T(8,128)(2,1)S(1)}, bf16[32,384]{1,0:T(8,128)(2,1)S(1)}, u32[]{:S(2)}, u32[]{:S(2)}) collective-permute-start(bf16[32,384]{1,0:T(8,128)(2,1)S(1)} %get-tuple-element.105), channel_id=1, source_target_pairs={{0,4},{4,8},{8,12},{12,16},{16,20},{20,24},{24,28},{1,5},{5,9},{9,... | collective-permute-start | bytes 73736 | tf_op jit(solution)/shard_map/ppermute | solution.py:54
  29.0 3.9 %collective-permute-start.5 = (bf16[464,384]{1,0:T(8,128)(2,1)S(1)}, bf16[464,384]{1,0:T(8,128)(2,1)S(1)}, u32[]{:S(2)}, u32[]{:S(2)}) collective-permute-start(bf16[464,384]{1,0:T(8,128)(2,1)S(1)} %fusion.1.c0), channel_id=1, source_target_pairs={{1,0},{2,1},{3,2},{5,4},{6,5},{7,6},{9,8},{10,9},{11,10},{13,12},{... | collective-permute-start | bytes 1069064 | tf_op jit(solution)/shard_map/ppermute | solution.py:45
  32.9 8.5 %collective-permute-done.4.c2 = bf16[464,384]{1,0:T(8,128)(2,1)S(1)} collective-permute-done((bf16[464,384]{1,0:T(8,128)(2,1)S(1)}, bf16[464,384]{1,0:T(8,128)(2,1)S(1)}, u32[]{:S(2)}, u32[]{:S(2)}) %collective-permute-start.4) | collective-permute-done | bytes 356384 | tf_op jit(solution)/shard_map/ppermute | solution.py:43
  41.4 4.1 %collective-permute-start.6 = (bf16[464,384]{1,0:T(8,128)(2,1)S(1)}, bf16[464,384]{1,0:T(8,128)(2,1)S(1)}, u32[]{:S(2)}, u32[]{:S(2)}) collective-permute-start(bf16[464,384]{1,0:T(8,128)(2,1)S(1)} %collective-permute-done.4.c2), channel_id=1, source_target_pairs={{2,3},{1,0},{6,7},{5,4},{10,11},{9,8},{14,15},{13,12},{18,19},{17,... | collective-permute-start | bytes 1069064 | tf_op jit(solution)/shard_map/ppermute | solution.py:46
  49.6 4.0 %copy-done = bf16[6,3,192,1536]{3,2,1,0:T(8,128)(2,1)S(1)} copy-done((bf16[6,3,192,1536]{3,2,1,0:T(8,128)(2,1)S(1)}, bf16[6,3,192,1536]{3,2,1,0:T(8,128)(2,1)}, u32[]{:S(2)}) %copy-start) | copy-done | bytes 10616856
  56.1 3.2 %collective-permute-done.6.c4 = bf16[464,384]{1,0:T(8,128)(2,1)S(1)} collective-permute-done((bf16[464,384]{1,0:T(8,128)(2,1)S(1)}, bf16[464,384]{1,0:T(8,128)(2,1)S(1)}, u32[]{:S(2)}, u32[]{:S(2)}) %collective-permute-start.6) | collective-permute-done | bytes 356384 | tf_op jit(solution)/shard_map/ppermute | solution.py:46
  65.4 2.6 %collective-permute-start.8 = (bf16[224,384]{1,0:T(8,128)(2,1)}, bf16[224,384]{1,0:T(8,128)(2,1)S(1)}, u32[]{:S(2)}, u32[]{:S(2)}) collective-permute-start(bf16[224,384]{1,0:T(8,128)(2,1)} %copy-done.6), channel_id=1, source_target_pairs={{0,2},{1,3},{2,0},{3,1},{4,6},{5,7},{6,4},{7,5},{8,10},{9,11},{10,... | collective-permute-start | bytes 516104 | tf_op jit(solution)/shard_map/ppermute | solution.py:35
  71.8 2.5 %shard_map.98 = (bf16[4,4,48,1536]{3,2,1,0:T(8,128)(2,1)S(1)}, bf16[3,192,1536]{2,1,0:T(8,128)(2,1)S(1)}) custom-call(s32[4]{0:T(128)S(1)} %compare_select_fusion.order_ref, bf16[8,192,1536]{2,1,0:T(8,128)(2,1)S(1)} %bitcast.17, bf16[6,3,192,1536]{3,2,1,0:T(8,128)(2,1)} %refs_1_.10), custom_call_target="tpu_custom_call" | custom-call | bytes 4128768 | tf_op jit(solution)/shard_map/pallas_call | solution.py:146
  74.3 3.4 %collective-permute-done.7.a1 = bf16[224,384]{1,0:T(8,128)(2,1)S(1)} collective-permute-done((bf16[224,384]{1,0:T(8,128)(2,1)}, bf16[224,384]{1,0:T(8,128)(2,1)S(1)}, u32[]{:S(2)}, u32[]{:S(2)}) %collective-permute-start.7) | collective-permute-done | bytes 172064 | tf_op jit(solution)/shard_map/ppermute | solution.py:35
  79.7 2.6 %collective-permute-done.9.a3 = bf16[224,384]{1,0:T(8,128)(2,1)S(1)} collective-permute-done((bf16[224,384]{1,0:T(8,128)(2,1)}, bf16[224,384]{1,0:T(8,128)(2,1)S(1)}, u32[]{:S(2)}, u32[]{:S(2)}) %collective-permute-start.9) | collective-permute-done | bytes 172064 | tf_op jit(solution)/shard_map/ppermute | solution.py:35
  82.3 3.2 %shard_map.99 = (bf16[224,384]{1,0:T(8,128)(2,1)S(1)}, bf16[448,1536]{1,0:T(8,128)(2,1)S(1)}) custom-call(s32[2]{0:T(128)S(1)} %add_convert_fusion.edge_ref, bf16[224,384]{1,0:T(8,128)(2,1)S(1)} %copy-done.7, bf16[224,384]{1,0:T(8,128)(2,1)S(1)} %collective-permute-done.7.a1, bf16[224,384]{1,0:T(8,128)(2,1)S(1)} %collective-permute-done.8.a2, ...), custom_call_target="tpu_custom_call" | custom-call | flops 1849688064 | bytes 6881280 | tf_op jit(solution)/shard_map/pallas_call | solution.py:146
  89.1 3.3 %collective-permute-start.33 = (bf16[48,1536]{1,0:T(8,128)(2,1)S(1)}, bf16[48,1536]{1,0:T(8,128)(2,1)S(1)}, u32[]{:S(2)}, u32[]{:S(2)}) collective-permute-start(bf16[48,1536]{1,0:T(8,128)(2,1)S(1)} %get-tuple-element.86.refs_0_), channel_id=1, source_target_pairs={{0,2},{1,3},{2,0},{3,1},{4,6},{5,7},{6,4},{7,5},{8,10},{9,11},{10,... | collective-permute-start | bytes 442376 | tf_op jit(solution)/shard_map/ppermute | solution.py:35
  95.1 6.4 %collective-permute-done.13.a2 = bf16[224,384]{1,0:T(8,128)(2,1)S(1)} collective-permute-done((bf16[224,384]{1,0:T(8,128)(2,1)S(1)}, bf16[224,384]{1,0:T(8,128)(2,1)S(1)}, u32[]{:S(2)}, u32[]{:S(2)}) %collective-permute-start.13) | collective-permute-done | bytes 172064 | tf_op jit(solution)/shard_map/ppermute | solution.py:35
  101.5 6.0 %collective-permute-done.14.a3 = bf16[224,384]{1,0:T(8,128)(2,1)S(1)} collective-permute-done((bf16[224,384]{1,0:T(8,128)(2,1)S(1)}, bf16[224,384]{1,0:T(8,128)(2,1)S(1)}, u32[]{:S(2)}, u32[]{:S(2)}) %collective-permute-start.14) | collective-permute-done | bytes 172064 | tf_op jit(solution)/shard_map/ppermute | solution.py:35
  107.5 3.2 %shard_map.101 = (bf16[208,384]{1,0:T(8,128)(2,1)S(1)}, bf16[448,1536]{1,0:T(8,128)(2,1)S(1)}) custom-call(s32[2]{0:T(128)S(1)} %add_convert_fusion.edge_ref, bf16[224,384]{1,0:T(8,128)(2,1)S(1)} %get-tuple-element.63.a0, bf16[224,384]{1,0:T(8,128)(2,1)S(1)} %collective-permute-done.12.a1, bf16[224,384]{1,0:T(8,128)(2,1)S(1)} %collective-permute-done.13.a2, ...), custom_call_target="tpu_custom_call" | custom-call | flops 1849688064 | bytes 6881280 | tf_op jit(solution)/shard_map/pallas_call | solution.py:146
  110.8 2.7 %collective-permute-done.33.refs_2_ = bf16[48,1536]{1,0:T(8,128)(2,1)S(1)} collective-permute-done((bf16[48,1536]{1,0:T(8,128)(2,1)S(1)}, bf16[48,1536]{1,0:T(8,128)(2,1)S(1)}, u32[]{:S(2)}, u32[]{:S(2)}) %collective-permute-start.33) | collective-permute-done | bytes 147488 | tf_op jit(solution)/shard_map/ppermute | solution.py:35
  114.7 3.2 %collective-permute-start.16 = (bf16[208,384]{1,0:T(8,128)(2,1)S(1)}, bf16[208,384]{1,0:T(8,128)(2,1)S(1)}, u32[]{:S(2)}, u32[]{:S(2)}) collective-permute-start(bf16[208,384]{1,0:T(8,128)(2,1)S(1)} %get-tuple-element.68.a0), channel_id=1, source_target_pairs={{0,2},{1,3},{2,0},{3,1},{4,6},{5,7},{6,4},{7,5},{8,10},{9,11},{10,... | collective-permute-start | bytes 479240 | tf_op jit(solution)/shard_map/ppermute | solution.py:35
  122.3 2.6 %shard_map.103 = (bf16[4,4,48,1536]{3,2,1,0:T(8,128)(2,1)S(1)}, bf16[3,192,1536]{2,1,0:T(8,128)(2,1)S(1)}) custom-call(s32[4]{0:T(128)S(1)} %compare_select_fusion.order_ref, bf16[8,208,1536]{2,1,0:T(8,128)(2,1)S(1)} %bitcast.14, bf16[6,3,192,1536]{3,2,1,0:T(8,128)(2,1)} %refs_1_.10), custom_call_target="tpu_custom_call" | custom-call | bytes 4128768 | tf_op jit(solution)/shard_map/pallas_call | solution.py:146
  124.9 3.8 %collective-permute-done.16.a2 = bf16[208,384]{1,0:T(8,128)(2,1)S(1)} collective-permute-done((bf16[208,384]{1,0:T(8,128)(2,1)S(1)}, bf16[208,384]{1,0:T(8,128)(2,1)S(1)}, u32[]{:S(2)}, u32[]{:S(2)}) %collective-permute-start.16) | collective-permute-done | bytes 159776 | tf_op jit(solution)/shard_map/ppermute | solution.py:35
  128.8 3.2 %collective-permute-done.17.a3 = bf16[208,384]{1,0:T(8,128)(2,1)S(1)} collective-permute-done((bf16[208,384]{1,0:T(8,128)(2,1)S(1)}, bf16[208,384]{1,0:T(8,128)(2,1)S(1)}, u32[]{:S(2)}, u32[]{:S(2)}) %collective-permute-start.17) | collective-permute-done | bytes 159776 | tf_op jit(solution)/shard_map/ppermute | solution.py:35
  132.0 3.1 %shard_map.104 = (bf16[192,384]{1,0:T(8,128)(2,1)S(1)}, bf16[416,1536]{1,0:T(8,128)(2,1)S(1)}) custom-call(s32[2]{0:T(128)S(1)} %add_convert_fusion.edge_ref, bf16[208,384]{1,0:T(8,128)(2,1)S(1)} %get-tuple-element.68.a0, bf16[208,384]{1,0:T(8,128)(2,1)S(1)} %collective-permute-done.15.a1, bf16[208,384]{1,0:T(8,128)(2,1)S(1)} %collective-permute-done.16.a2, ...), custom_call_target="tpu_custom_call" | custom-call | flops 1717567488 | bytes 6684672 | tf_op jit(solution)/shard_map/pallas_call | solution.py:146
  138.6 2.5 %shard_map.105 = (bf16[4,4,48,1536]{3,2,1,0:T(8,128)(2,1)S(1)}, bf16[3,192,1536]{2,1,0:T(8,128)(2,1)S(1)}) custom-call(s32[4]{0:T(128)S(1)} %compare_select_fusion.order_ref, bf16[8,208,1536]{2,1,0:T(8,128)(2,1)S(1)} %bitcast.16, bf16[6,3,192,1536]{3,2,1,0:T(8,128)(2,1)} %refs_1_.10), custom_call_target="tpu_custom_call" | custom-call | bytes 4128768 | tf_op jit(solution)/shard_map/pallas_call | solution.py:146
  141.8 6.5 %collective-permute-done.22.a2 = bf16[192,384]{1,0:T(8,128)(2,1)S(1)} collective-permute-done((bf16[192,384]{1,0:T(8,128)(2,1)S(1)}, bf16[192,384]{1,0:T(8,128)(2,1)S(1)}, u32[]{:S(2)}, u32[]{:S(2)}) %collective-permute-start.22) | collective-permute-done | bytes 147488 | tf_op jit(solution)/shard_map/ppermute | solution.py:35
  154.7 2.5 %collective-permute-start.25 = (bf16[160,384]{1,0:T(8,128)(2,1)S(1)}, bf16[160,384]{1,0:T(8,128)(2,1)S(1)}, u32[]{:S(2)}, u32[]{:S(2)}) collective-permute-start(bf16[160,384]{1,0:T(8,128)(2,1)S(1)} %shard_map.107.a0), channel_id=1, source_target_pairs={{0,2},{1,3},{2,0},{3,1},{4,6},{5,7},{6,4},{7,5},{8,10},{9,11},{10,... | collective-permute-start | bytes 368648 | tf_op jit(solution)/shard_map/ppermute | solution.py:35
  168.7 3.6 %collective-permute-done.26.a3 = bf16[160,384]{1,0:T(8,128)(2,1)S(1)} collective-permute-done((bf16[160,384]{1,0:T(8,128)(2,1)S(1)}, bf16[160,384]{1,0:T(8,128)(2,1)S(1)}, u32[]{:S(2)}, u32[]{:S(2)}) %collective-permute-start.26) | collective-permute-done | bytes 122912 | tf_op jit(solution)/shard_map/ppermute | solution.py:35
  172.3 3.2 %collective-permute-done.31.e3 = bf16[96,384]{1,0:T(8,128)(2,1)S(1)} collective-permute-done((bf16[96,384]{1,0:T(8,128)(2,1)S(1)}, bf16[96,384]{1,0:T(8,128)(2,1)S(1)}, u32[]{:S(2)}, u32[]{:S(2)}) %collective-permute-start.31) | collective-permute-done | bytes 73760 | tf_op jit(solution)/shard_map/ppermute | solution.py:35
  175.4 3.6 %shard_map.111 = (bf16[192,384]{1,0:T(8,128)(2,1)S(1)}, bf16[512,1536]{1,0:T(8,128)(2,1)S(1)}) custom-call(s32[2]{0:T(128)S(1)} %add_convert_fusion.edge_ref, bf16[160,384]{1,0:T(8,128)(2,1)S(1)} %shard_map.107.a0, bf16[160,384]{1,0:T(8,128)(2,1)S(1)} %collective-permute-done.24.a1, bf16[160,384]{1,0:T(8,128)(2,1)S(1)} %collective-permute-done.25.a2, ...), custom_call_target="tpu_custom_call" | custom-call | flops 2113929216 | bytes 7274496 | tf_op jit(solution)/shard_map/pallas_call | solution.py:146
  182.6 3.2 %collective-permute-done.35.a1 = bf16[192,384]{1,0:T(8,128)(2,1)S(1)} collective-permute-done((bf16[192,384]{1,0:T(8,128)(2,1)S(1)}, bf16[192,384]{1,0:T(8,128)(2,1)S(1)}, u32[]{:S(2)}, u32[]{:S(2)}) %collective-permute-start.35) | collective-permute-done | bytes 147488 | tf_op jit(solution)/shard_map/ppermute | solution.py:35
  185.8 6.4 %collective-permute-done.36.a2 = bf16[192,384]{1,0:T(8,128)(2,1)S(1)} collective-permute-done((bf16[192,384]{1,0:T(8,128)(2,1)S(1)}, bf16[192,384]{1,0:T(8,128)(2,1)S(1)}, u32[]{:S(2)}, u32[]{:S(2)}) %collective-permute-start.36) | collective-permute-done | bytes 147488 | tf_op jit(solution)/shard_map/ppermute | solution.py:35
  194.7 4.2 %shard_map.113 = (bf16[384,1024]{1,0:T(8,128)(2,1)}, bf16[64,1024]{1,0:T(8,128)(2,1)}) custom-call(bf16[192,384]{1,0:T(8,128)(2,1)S(1)} %get-tuple-element.93.a0, bf16[192,384]{1,0:T(8,128)(2,1)S(1)} %collective-permute-done.35.a1, bf16[192,384]{1,0:T(8,128)(2,1)S(1)} %collective-permute-done.36.a2, bf16[192,384]{1,0:T(8,128)(2,1)S(1)} %collective-permute-done.37.a3, ...), custom_call_target="tpu_custom_call" | custom-call | flops 2113929216 | bytes 6684672 | tf_op jit(solution)/shard_map/pallas_call | solution.py:146
  198.9 4.7 %all-to-all-start = ((bf16[8,8,1024]{2,1,0:T(8,128)(2,1)}), bf16[8,8,1024]{2,1,0:T(8,128)(2,1)S(1)}, u32[]{:S(2)}, u32[]{:S(2)}) async-start(bf16[8,8,1024]{2,1,0:T(8,128)(2,1)} %bitcast.12), calls=%async_computation | async-start | bytes 262144 | tf_op jit(solution)/shard_map/all_to_all | solution.py:575
  203.7 5.4 %all-to-all-done = bf16[8,8,1024]{2,1,0:T(8,128)(2,1)S(1)} async-done(((bf16[8,8,1024]{2,1,0:T(8,128)(2,1)}), bf16[8,8,1024]{2,1,0:T(8,128)(2,1)S(1)}, u32[]{:S(2)}, u32[]{:S(2)}) %all-to-all-start) | async-done | bytes 131104 | tf_op jit(solution)/shard_map/all_to_all | solution.py:575
  (114 shorter events, 77.8 us)
Async XLA Ops:
  7.2 62.2 %all-gather.7.cloned.1.call-start = ((), (), s32[]{:S(2)}) async-start(), calls=%async_computation.1 | async-start | bytes 5308416 | tf_op jit(solution)/shard_map/all_gather | solution.py:486
  8.4 12.2 %collective-permute-start.2 = (bf16[48,1536]{1,0:T(8,128)(2,1)S(1)}, bf16[48,1536]{1,0:T(8,128)(2,1)S(1)}, u32[]{:S(2)}, u32[]{:S(2)}) collective-permute-start(bf16[48,1536]{1,0:T(8,128)(2,1)S(1)} %get-tuple-element.54.refs_0_), channel_id=1, source_target_pairs={{0,1},{1,2},{2,3},{3,0},{4,5},{5,6},{6,7},{7,4},{8,9},{9,10},{10,1... | collective-permute-start | bytes 442376 | tf_op jit(solution)/shard_map/ppermute | solution.py:35
  10.0 12.6 %collective-permute-start.10 = (bf16[48,1536]{1,0:T(8,128)(2,1)S(1)}, bf16[48,1536]{1,0:T(8,128)(2,1)S(1)}, u32[]{:S(2)}, u32[]{:S(2)}) collective-permute-start(bf16[48,1536]{1,0:T(8,128)(2,1)S(1)} %get-tuple-element.54.refs_0_), channel_id=1, source_target_pairs={{0,2},{1,3},{2,0},{3,1},{4,6},{5,7},{6,4},{7,5},{8,10},{9,11},{10,... | collective-permute-start | bytes 442376 | tf_op jit(solution)/shard_map/ppermute | solution.py:35
  11.1 13.2 %collective-permute-start.11 = (bf16[48,1536]{1,0:T(8,128)(2,1)S(1)}, bf16[48,1536]{1,0:T(8,128)(2,1)S(1)}, u32[]{:S(2)}, u32[]{:S(2)}) collective-permute-start(bf16[48,1536]{1,0:T(8,128)(2,1)S(1)} %get-tuple-element.54.refs_0_), channel_id=1, source_target_pairs={{0,3},{1,0},{2,1},{3,2},{4,7},{5,4},{6,5},{7,6},{8,11},{9,8},{10,9... | collective-permute-start | bytes 442376 | tf_op jit(solution)/shard_map/ppermute | solution.py:35
  25.2 94.6 %all-gather.9.cloned.1.call-start = ((), (), s32[]{:S(2)}) async-start(), calls=%async_computation.2 | async-start | bytes 5750784 | tf_op jit(solution)/shard_map/all_gather | solution.py:486
  25.4 16.1 %collective-permute-start.4 = (bf16[464,384]{1,0:T(8,128)(2,1)S(1)}, bf16[464,384]{1,0:T(8,128)(2,1)S(1)}, u32[]{:S(2)}, u32[]{:S(2)}) collective-permute-start(bf16[464,384]{1,0:T(8,128)(2,1)S(1)} %fusion.1.c0), channel_id=1, source_target_pairs={{0,2},{1,3},{2,0},{3,1},{4,6},{5,7},{6,4},{7,5},{8,10},{9,11},{10,... | collective-permute-start | bytes 1069064 | tf_op jit(solution)/shard_map/ppermute | solution.py:43
  27.1 22.6 %collective-permute-start.3 = (bf16[464,384]{1,0:T(8,128)(2,1)S(1)}, bf16[464,384]{1,0:T(8,128)(2,1)S(1)}, u32[]{:S(2)}, u32[]{:S(2)}) collective-permute-start(bf16[464,384]{1,0:T(8,128)(2,1)S(1)} %fusion.1.c0), channel_id=1, source_target_pairs={{0,1},{1,2},{2,3},{4,5},{5,6},{6,7},{8,9},{9,10},{10,11},{12,13},{... | collective-permute-start | bytes 1069064 | tf_op jit(solution)/shard_map/ppermute | solution.py:44
  29.0 27.1 %collective-permute-start.5 = (bf16[464,384]{1,0:T(8,128)(2,1)S(1)}, bf16[464,384]{1,0:T(8,128)(2,1)S(1)}, u32[]{:S(2)}, u32[]{:S(2)}) collective-permute-start(bf16[464,384]{1,0:T(8,128)(2,1)S(1)} %fusion.1.c0), channel_id=1, source_target_pairs={{1,0},{2,1},{3,2},{5,4},{6,5},{7,6},{9,8},{10,9},{11,10},{13,12},{... | collective-permute-start | bytes 1069064 | tf_op jit(solution)/shard_map/ppermute | solution.py:45
  41.4 17.9 %collective-permute-start.6 = (bf16[464,384]{1,0:T(8,128)(2,1)S(1)}, bf16[464,384]{1,0:T(8,128)(2,1)S(1)}, u32[]{:S(2)}, u32[]{:S(2)}) collective-permute-start(bf16[464,384]{1,0:T(8,128)(2,1)S(1)} %collective-permute-done.4.c2), channel_id=1, source_target_pairs={{2,3},{1,0},{6,7},{5,4},{10,11},{9,8},{14,15},{13,12},{18,19},{17,... | collective-permute-start | bytes 1069064 | tf_op jit(solution)/shard_map/ppermute | solution.py:46
  45.8 16.4 %collective-permute-start.18 = (bf16[48,1536]{1,0:T(8,128)(2,1)S(1)}, bf16[48,1536]{1,0:T(8,128)(2,1)S(1)}, u32[]{:S(2)}, u32[]{:S(2)}) collective-permute-start(bf16[48,1536]{1,0:T(8,128)(2,1)S(1)} %get-tuple-element.70.refs_0_), channel_id=1, source_target_pairs={{0,1},{1,2},{2,3},{3,0},{4,5},{5,6},{6,7},{7,4},{8,9},{9,10},{10,1... | collective-permute-start | bytes 442376 | tf_op jit(solution)/shard_map/ppermute | solution.py:35
  47.5 14.6 %collective-permute-start.19 = (bf16[48,1536]{1,0:T(8,128)(2,1)S(1)}, bf16[48,1536]{1,0:T(8,128)(2,1)S(1)}, u32[]{:S(2)}, u32[]{:S(2)}) collective-permute-start(bf16[48,1536]{1,0:T(8,128)(2,1)S(1)} %get-tuple-element.70.refs_0_), channel_id=1, source_target_pairs={{0,2},{1,3},{2,0},{3,1},{4,6},{5,7},{6,4},{7,5},{8,10},{9,11},{10,... | collective-permute-start | bytes 442376 | tf_op jit(solution)/shard_map/ppermute | solution.py:35
  49.6 12.5 %collective-permute-start.20 = (bf16[48,1536]{1,0:T(8,128)(2,1)S(1)}, bf16[48,1536]{1,0:T(8,128)(2,1)S(1)}, u32[]{:S(2)}, u32[]{:S(2)}) collective-permute-start(bf16[48,1536]{1,0:T(8,128)(2,1)S(1)} %get-tuple-element.70.refs_0_), channel_id=1, source_target_pairs={{0,3},{1,0},{2,1},{3,2},{4,7},{5,4},{6,5},{7,6},{8,11},{9,8},{10,9... | collective-permute-start | bytes 442376 | tf_op jit(solution)/shard_map/ppermute | solution.py:35
  63.0 100.8 %all-gather.11.cloned.1.call-start = ((), (), s32[]{:S(2)}) async-start(), calls=%async_computation.3 | async-start | bytes 5308416 | tf_op jit(solution)/shard_map/all_gather | solution.py:486
  63.1 14.6 %collective-permute-start.7 = (bf16[224,384]{1,0:T(8,128)(2,1)}, bf16[224,384]{1,0:T(8,128)(2,1)S(1)}, u32[]{:S(2)}, u32[]{:S(2)}) collective-permute-start(bf16[224,384]{1,0:T(8,128)(2,1)} %copy-done.6), channel_id=1, source_target_pairs={{0,1},{1,2},{2,3},{3,0},{4,5},{5,6},{6,7},{7,4},{8,9},{9,10},{10,1... | collective-permute-start | bytes 516104 | tf_op jit(solution)/shard_map/ppermute | solution.py:35
  65.4 14.3 %collective-permute-start.8 = (bf16[224,384]{1,0:T(8,128)(2,1)}, bf16[224,384]{1,0:T(8,128)(2,1)S(1)}, u32[]{:S(2)}, u32[]{:S(2)}) collective-permute-start(bf16[224,384]{1,0:T(8,128)(2,1)} %copy-done.6), channel_id=1, source_target_pairs={{0,2},{1,3},{2,0},{3,1},{4,6},{5,7},{6,4},{7,5},{8,10},{9,11},{10,... | collective-permute-start | bytes 516104 | tf_op jit(solution)/shard_map/ppermute | solution.py:35
  68.0 14.3 %collective-permute-start.9 = (bf16[224,384]{1,0:T(8,128)(2,1)}, bf16[224,384]{1,0:T(8,128)(2,1)S(1)}, u32[]{:S(2)}, u32[]{:S(2)}) collective-permute-start(bf16[224,384]{1,0:T(8,128)(2,1)} %copy-done.6), channel_id=1, source_target_pairs={{0,3},{1,0},{2,1},{3,2},{4,7},{5,4},{6,5},{7,6},{8,11},{9,8},{10,9... | collective-permute-start | bytes 516104 | tf_op jit(solution)/shard_map/ppermute | solution.py:35
  85.6 15.9 %collective-permute-start.13 = (bf16[224,384]{1,0:T(8,128)(2,1)S(1)}, bf16[224,384]{1,0:T(8,128)(2,1)S(1)}, u32[]{:S(2)}, u32[]{:S(2)}) collective-permute-start(bf16[224,384]{1,0:T(8,128)(2,1)S(1)} %get-tuple-element.63.a0), channel_id=1, source_target_pairs={{0,2},{1,3},{2,0},{3,1},{4,6},{5,7},{6,4},{7,5},{8,10},{9,11},{10,... | collective-permute-start | bytes 516104 | tf_op jit(solution)/shard_map/ppermute | solution.py:35
  86.3 21.2 %collective-permute-start.14 = (bf16[224,384]{1,0:T(8,128)(2,1)S(1)}, bf16[224,384]{1,0:T(8,128)(2,1)S(1)}, u32[]{:S(2)}, u32[]{:S(2)}) collective-permute-start(bf16[224,384]{1,0:T(8,128)(2,1)S(1)} %get-tuple-element.63.a0), channel_id=1, source_target_pairs={{0,3},{1,0},{2,1},{3,2},{4,7},{5,4},{6,5},{7,6},{8,11},{9,8},{10,9... | collective-permute-start | bytes 516104 | tf_op jit(solution)/shard_map/ppermute | solution.py:35
  88.3 22.5 %collective-permute-start.32 = (bf16[48,1536]{1,0:T(8,128)(2,1)S(1)}, bf16[48,1536]{1,0:T(8,128)(2,1)S(1)}, u32[]{:S(2)}, u32[]{:S(2)}) collective-permute-start(bf16[48,1536]{1,0:T(8,128)(2,1)S(1)} %get-tuple-element.86.refs_0_), channel_id=1, source_target_pairs={{0,1},{1,2},{2,3},{3,0},{4,5},{5,6},{6,7},{7,4},{8,9},{9,10},{10,1... | collective-permute-start | bytes 442376 | tf_op jit(solution)/shard_map/ppermute | solution.py:35
  89.1 24.4 %collective-permute-start.33 = (bf16[48,1536]{1,0:T(8,128)(2,1)S(1)}, bf16[48,1536]{1,0:T(8,128)(2,1)S(1)}, u32[]{:S(2)}, u32[]{:S(2)}) collective-permute-start(bf16[48,1536]{1,0:T(8,128)(2,1)S(1)} %get-tuple-element.86.refs_0_), channel_id=1, source_target_pairs={{0,2},{1,3},{2,0},{3,1},{4,6},{5,7},{6,4},{7,5},{8,10},{9,11},{10,... | collective-permute-start | bytes 442376 | tf_op jit(solution)/shard_map/ppermute | solution.py:35
  94.9 18.8 %collective-permute-start.34 = (bf16[48,1536]{1,0:T(8,128)(2,1)S(1)}, bf16[48,1536]{1,0:T(8,128)(2,1)S(1)}, u32[]{:S(2)}, u32[]{:S(2)}) collective-permute-start(bf16[48,1536]{1,0:T(8,128)(2,1)S(1)} %get-tuple-element.86.refs_0_), channel_id=1, source_target_pairs={{0,3},{1,0},{2,1},{3,2},{4,7},{5,4},{6,5},{7,6},{8,11},{9,8},{10,9... | collective-permute-start | bytes 442376 | tf_op jit(solution)/shard_map/ppermute | solution.py:35
  114.7 14.1 %collective-permute-start.16 = (bf16[208,384]{1,0:T(8,128)(2,1)S(1)}, bf16[208,384]{1,0:T(8,128)(2,1)S(1)}, u32[]{:S(2)}, u32[]{:S(2)}) collective-permute-start(bf16[208,384]{1,0:T(8,128)(2,1)S(1)} %get-tuple-element.68.a0), channel_id=1, source_target_pairs={{0,2},{1,3},{2,0},{3,1},{4,6},{5,7},{6,4},{7,5},{8,10},{9,11},{10,... | collective-permute-start | bytes 479240 | tf_op jit(solution)/shard_map/ppermute | solution.py:35
  117.9 14.1 %collective-permute-start.17 = (bf16[208,384]{1,0:T(8,128)(2,1)S(1)}, bf16[208,384]{1,0:T(8,128)(2,1)S(1)}, u32[]{:S(2)}, u32[]{:S(2)}) collective-permute-start(bf16[208,384]{1,0:T(8,128)(2,1)S(1)} %get-tuple-element.68.a0), channel_id=1, source_target_pairs={{0,3},{1,0},{2,1},{3,2},{4,7},{5,4},{6,5},{7,6},{8,11},{9,8},{10,9... | collective-permute-start | bytes 479240 | tf_op jit(solution)/shard_map/ppermute | solution.py:35
  135.1 13.1 %collective-permute-start.22 = (bf16[192,384]{1,0:T(8,128)(2,1)S(1)}, bf16[192,384]{1,0:T(8,128)(2,1)S(1)}, u32[]{:S(2)}, u32[]{:S(2)}) collective-permute-start(bf16[192,384]{1,0:T(8,128)(2,1)S(1)} %get-tuple-element.78.a0), channel_id=1, source_target_pairs={{0,2},{1,3},{2,0},{3,1},{4,6},{5,7},{6,4},{7,5},{8,10},{9,11},{10,... | collective-permute-start | bytes 442376 | tf_op jit(solution)/shard_map/ppermute | solution.py:35
  135.6 13.1 %collective-permute-start.23 = (bf16[192,384]{1,0:T(8,128)(2,1)S(1)}, bf16[192,384]{1,0:T(8,128)(2,1)S(1)}, u32[]{:S(2)}, u32[]{:S(2)}) collective-permute-start(bf16[192,384]{1,0:T(8,128)(2,1)S(1)} %get-tuple-element.78.a0), channel_id=1, source_target_pairs={{0,3},{1,0},{2,1},{3,2},{4,7},{5,4},{6,5},{7,6},{8,11},{9,8},{10,9... | collective-permute-start | bytes 442376 | tf_op jit(solution)/shard_map/ppermute | solution.py:35
  154.7 14.0 %collective-permute-start.25 = (bf16[160,384]{1,0:T(8,128)(2,1)S(1)}, bf16[160,384]{1,0:T(8,128)(2,1)S(1)}, u32[]{:S(2)}, u32[]{:S(2)}) collective-permute-start(bf16[160,384]{1,0:T(8,128)(2,1)S(1)} %shard_map.107.a0), channel_id=1, source_target_pairs={{0,2},{1,3},{2,0},{3,1},{4,6},{5,7},{6,4},{7,5},{8,10},{9,11},{10,... | collective-permute-start | bytes 368648 | tf_op jit(solution)/shard_map/ppermute | solution.py:35
  157.2 15.1 %collective-permute-start.26 = (bf16[160,384]{1,0:T(8,128)(2,1)S(1)}, bf16[160,384]{1,0:T(8,128)(2,1)S(1)}, u32[]{:S(2)}, u32[]{:S(2)}) collective-permute-start(bf16[160,384]{1,0:T(8,128)(2,1)S(1)} %shard_map.107.a0), channel_id=1, source_target_pairs={{0,3},{1,0},{2,1},{3,2},{4,7},{5,4},{6,5},{7,6},{8,11},{9,8},{10,9... | collective-permute-start | bytes 368648 | tf_op jit(solution)/shard_map/ppermute | solution.py:35
  160.2 12.1 %collective-permute-start.29 = (bf16[96,384]{1,0:T(8,128)(2,1)S(1)}, bf16[96,384]{1,0:T(8,128)(2,1)S(1)}, u32[]{:S(2)}, u32[]{:S(2)}) collective-permute-start(bf16[96,384]{1,0:T(8,128)(2,1)S(1)} %shard_map.108.e0), channel_id=1, source_target_pairs={{0,1},{1,2},{2,3},{3,0},{4,5},{5,6},{6,7},{7,4},{8,9},{9,10},{10,1... | collective-permute-start | bytes 221192 | tf_op jit(solution)/shard_map/ppermute | solution.py:35
  160.4 11.9 %collective-permute-start.30 = (bf16[96,384]{1,0:T(8,128)(2,1)S(1)}, bf16[96,384]{1,0:T(8,128)(2,1)S(1)}, u32[]{:S(2)}, u32[]{:S(2)}) collective-permute-start(bf16[96,384]{1,0:T(8,128)(2,1)S(1)} %shard_map.108.e0), channel_id=1, source_target_pairs={{0,2},{1,3},{2,0},{3,1},{4,6},{5,7},{6,4},{7,5},{8,10},{9,11},{10,... | collective-permute-start | bytes 221192 | tf_op jit(solution)/shard_map/ppermute | solution.py:35
  162.7 12.8 %collective-permute-start.31 = (bf16[96,384]{1,0:T(8,128)(2,1)S(1)}, bf16[96,384]{1,0:T(8,128)(2,1)S(1)}, u32[]{:S(2)}, u32[]{:S(2)}) collective-permute-start(bf16[96,384]{1,0:T(8,128)(2,1)S(1)} %shard_map.108.e0), channel_id=1, source_target_pairs={{0,3},{1,0},{2,1},{3,2},{4,7},{5,4},{6,5},{7,6},{8,11},{9,8},{10,9... | collective-permute-start | bytes 221192 | tf_op jit(solution)/shard_map/ppermute | solution.py:35
  179.1 13.1 %collective-permute-start.36 = (bf16[192,384]{1,0:T(8,128)(2,1)S(1)}, bf16[192,384]{1,0:T(8,128)(2,1)S(1)}, u32[]{:S(2)}, u32[]{:S(2)}) collective-permute-start(bf16[192,384]{1,0:T(8,128)(2,1)S(1)} %get-tuple-element.93.a0), channel_id=1, source_target_pairs={{0,2},{1,3},{2,0},{3,1},{4,6},{5,7},{6,4},{7,5},{8,10},{9,11},{10,... | collective-permute-start | bytes 442376 | tf_op jit(solution)/shard_map/ppermute | solution.py:35
  181.3 13.4 %collective-permute-start.37 = (bf16[192,384]{1,0:T(8,128)(2,1)S(1)}, bf16[192,384]{1,0:T(8,128)(2,1)S(1)}, u32[]{:S(2)}, u32[]{:S(2)}) collective-permute-start(bf16[192,384]{1,0:T(8,128)(2,1)S(1)} %get-tuple-element.93.a0), channel_id=1, source_target_pairs={{0,3},{1,0},{2,1},{3,2},{4,7},{5,4},{6,5},{7,6},{8,11},{9,8},{10,9... | collective-permute-start | bytes 442376 | tf_op jit(solution)/shard_map/ppermute | solution.py:35
  (22 other events, 220.1 us)
Sparse Core Ops, SparseCore 0:
  25.4 39.1 all-gather.6
  67.0 40.5 all-gather.8
  114.8 40.5 all-gather.10

commit v10 on v9

--- a/solution.py
+++ b/solution.py
@@ -512,7 +512,7 @@
     cells = relayed(own)
     exon_rows = [exon_digits(exon_bins, channels)] if packed else []
     exon_rows = [exon_digits(exon_bins, channels)] if packed else []
-    second = from_others(after(column(1), cells[2]))
+    second = from_others(after(column(1), cells[3]))
     taps_shape = shape(3, hidden, channels)
     weight_shape = shape(quarters, per_block, share, channels)
     head_row = head_bias[None, :]
@@ -530,7 +530,6 @@
         later = block + 1
         others = from_others(act)
         if block == 0:
-            third = from_others(after(column(2), others[2]))
             loads.append(gather(after_all(second, act) + exon_rows))
         if block == 2:
             loads.append(gather(after_all(third, act)))
@@ -544,6 +543,8 @@
         weight, taps = staged(
             block, conv_in, taps_shape, functools.partial(tap_cuts, later), act
         )
+        if block == 1:
+            third = from_others(after(column(2), weight))
         if later < FRAMED_BLOCKS:
             reach = sum(dilation(b) for b in range(later + 1, FRAMED_BLOCKS))
             rows_out = bin_rows + 2 * (-(-reach // 16) * 16)

time: 217 us -> 214 us (0.986)
  waiting for transfers between devices: 83.6 us -> 80.8 us
    ppermute x1, waiting for transfers between devices: 1.22 us -> 6.21 us  [relayed(): down = lax.ppermute(cells, 'trk', [(i + 1, i) for i in range(last)])]
    ppermute x1, waiting for transfers between devices: 3.19 us -> 0.01 us  [relayed(): far = lax.ppermute(across, 'trk', [(last - 1, last), (1, 0)])]
    ppermute x30, waiting for transfers between devices: 62.3 us -> 59.8 us  [from_others(): lax.ppermute(cells, 'trk', [(i, (i + k) % count) for i in range(count)])]
  transfers between devices with their start and end apart: 42 -> 42, of which waited for: 27 -> 26; matrix products, arithmetic and copies ran while one was open for 1% -> 1% of each run, Pallas kernels for 15% -> 15%
where the time goes in v10:
time: 214 us
  waiting for transfers between devices  80.8 us (38%)
  starting transfers between devices  61.8 us (29%)
  Pallas kernels  40.7 us (19%)
  between operations  14.2 us (7%)
  local copies, waits for them, and re-layouts  13.9 us (6%)
  other arithmetic  2.25 us (1%)
    ppermute x30, waiting for transfers between devices, from_others(): lax.ppermute(cells, 'trk', [(i, (i + k) % count) for i in range(count)])  59.8 us
    pallas_call x16, Pallas kernels, kernel_call(): pl.pallas_call(body, in_specs=specs or [SMEM] * scalars + [VMEM] * (len(i...  38.2 us
    ppermute x30, starting transfers between devices, from_others(): lax.ppermute(cells, 'trk', [(i, (i + k) % count) for i in range(count)])  37.9 us
    unnamed x24, local copies, waits for them, and re-layouts  11.9 us
    ppermute x1, waiting for transfers between devices, relayed(): lax.ppermute(cells, 'trk', [(i, (i + 2) % count) for i in range(count)])  8.49 us
    ppermute x1, waiting for transfers between devices, relayed(): down = lax.ppermute(cells, 'trk', [(i + 1, i) for i in range(last)])  6.21 us
    all_to_all x1, waiting for transfers between devices, shards(): lax.all_to_all(partial.reshape(count, genes_here, partial.shape[1]), 'seq...  5.42 us
    ppermute x2, starting transfers between devices, halo(): above = lax.ppermute(tail, 'seq', [(i, i + 1) for i in range(count - 1)])  5.08 us
  transfers between devices with their start and end apart: 42, of which 26 were waited for; matrix products, arithmetic and copies ran while one was open for 1% of the time, Pallas kernels for 15%

profile of v10, /device:TPU:8, one launch (start us, length us, event | category | flops | bytes accessed | tf_op | source)
XLA Modules:
  0.0 213.7 jit_solution(11426450115867277898)
XLA Ops:
  15.1 3.0 %collective-permute-start = (bf16[32,384]{1,0:T(8,128)(2,1)S(1)}, bf16[32,384]{1,0:T(8,128)(2,1)S(1)}, u32[]{:S(2)}, u32[]{:S(2)}) collective-permute-start(bf16[32,384]{1,0:T(8,128)(2,1)S(1)} %get-tuple-element.105), channel_id=1, source_target_pairs={{0,4},{4,8},{8,12},{12,16},{16,20},{20,24},{24,28},{1,5},{5,9},{9,... | collective-permute-start | bytes 73736 | tf_op jit(solution)/shard_map/ppermute | solution.py:54
  29.0 3.9 %collective-permute-start.5 = (bf16[464,384]{1,0:T(8,128)(2,1)S(1)}, bf16[464,384]{1,0:T(8,128)(2,1)S(1)}, u32[]{:S(2)}, u32[]{:S(2)}) collective-permute-start(bf16[464,384]{1,0:T(8,128)(2,1)S(1)} %fusion.1.c0), channel_id=1, source_target_pairs={{1,0},{2,1},{3,2},{5,4},{6,5},{7,6},{9,8},{10,9},{11,10},{13,12},{... | collective-permute-start | bytes 1069064 | tf_op jit(solution)/shard_map/ppermute | solution.py:45
  32.9 8.5 %collective-permute-done.4.c2 = bf16[464,384]{1,0:T(8,128)(2,1)S(1)} collective-permute-done((bf16[464,384]{1,0:T(8,128)(2,1)S(1)}, bf16[464,384]{1,0:T(8,128)(2,1)S(1)}, u32[]{:S(2)}, u32[]{:S(2)}) %collective-permute-start.4) | collective-permute-done | bytes 356384 | tf_op jit(solution)/shard_map/ppermute | solution.py:43
  41.4 4.1 %collective-permute-start.6 = (bf16[464,384]{1,0:T(8,128)(2,1)S(1)}, bf16[464,384]{1,0:T(8,128)(2,1)S(1)}, u32[]{:S(2)}, u32[]{:S(2)}) collective-permute-start(bf16[464,384]{1,0:T(8,128)(2,1)S(1)} %collective-permute-done.4.c2), channel_id=1, source_target_pairs={{2,3},{1,0},{6,7},{5,4},{10,11},{9,8},{14,15},{13,12},{18,19},{17,... | collective-permute-start | bytes 1069064 | tf_op jit(solution)/shard_map/ppermute | solution.py:46
  45.8 6.2 %collective-permute-done.5.c3 = bf16[464,384]{1,0:T(8,128)(2,1)S(1)} collective-permute-done((bf16[464,384]{1,0:T(8,128)(2,1)S(1)}, bf16[464,384]{1,0:T(8,128)(2,1)S(1)}, u32[]{:S(2)}, u32[]{:S(2)}) %collective-permute-start.5) | collective-permute-done | bytes 356384 | tf_op jit(solution)/shard_map/ppermute | solution.py:45
  54.0 4.1 %copy-done = bf16[6,3,192,1536]{3,2,1,0:T(8,128)(2,1)S(1)} copy-done((bf16[6,3,192,1536]{3,2,1,0:T(8,128)(2,1)S(1)}, bf16[6,3,192,1536]{3,2,1,0:T(8,128)(2,1)}, u32[]{:S(2)}) %copy-start) | copy-done | bytes 10616856
  65.4 2.5 %collective-permute-start.8 = (bf16[224,384]{1,0:T(8,128)(2,1)}, bf16[224,384]{1,0:T(8,128)(2,1)S(1)}, u32[]{:S(2)}, u32[]{:S(2)}) collective-permute-start(bf16[224,384]{1,0:T(8,128)(2,1)} %copy-done.6), channel_id=1, source_target_pairs={{0,2},{1,3},{2,0},{3,1},{4,6},{5,7},{6,4},{7,5},{8,10},{9,11},{10,... | collective-permute-start | bytes 516104 | tf_op jit(solution)/shard_map/ppermute | solution.py:35
  71.9 2.6 %shard_map.98 = (bf16[4,4,48,1536]{3,2,1,0:T(8,128)(2,1)S(1)}, bf16[3,192,1536]{2,1,0:T(8,128)(2,1)S(1)}) custom-call(s32[4]{0:T(128)S(1)} %compare_select_fusion.order_ref, bf16[8,192,1536]{2,1,0:T(8,128)(2,1)S(1)} %bitcast.17, bf16[6,3,192,1536]{3,2,1,0:T(8,128)(2,1)} %refs_1_.10), custom_call_target="tpu_custom_call" | custom-call | bytes 4128768 | tf_op jit(solution)/shard_map/pallas_call | solution.py:146
  78.0 2.5 %collective-permute-done.9.a3 = bf16[224,384]{1,0:T(8,128)(2,1)S(1)} collective-permute-done((bf16[224,384]{1,0:T(8,128)(2,1)}, bf16[224,384]{1,0:T(8,128)(2,1)S(1)}, u32[]{:S(2)}, u32[]{:S(2)}) %collective-permute-start.9) | collective-permute-done | bytes 172064 | tf_op jit(solution)/shard_map/ppermute | solution.py:35
  80.4 3.2 %shard_map.99 = (bf16[224,384]{1,0:T(8,128)(2,1)S(1)}, bf16[448,1536]{1,0:T(8,128)(2,1)S(1)}) custom-call(s32[2]{0:T(128)S(1)} %add_convert_fusion.edge_ref, bf16[224,384]{1,0:T(8,128)(2,1)S(1)} %copy-done.7, bf16[224,384]{1,0:T(8,128)(2,1)S(1)} %collective-permute-done.7.a1, bf16[224,384]{1,0:T(8,128)(2,1)S(1)} %collective-permute-done.8.a2, ...), custom_call_target="tpu_custom_call" | custom-call | flops 1849688064 | bytes 6881280 | tf_op jit(solution)/shard_map/pallas_call | solution.py:146
  86.6 2.5 %shard_map.100 = (bf16[4,4,48,1536]{3,2,1,0:T(8,128)(2,1)S(1)}, bf16[3,192,1536]{2,1,0:T(8,128)(2,1)S(1)}) custom-call(s32[4]{0:T(128)S(1)} %compare_select_fusion.order_ref, bf16[8,192,1536]{2,1,0:T(8,128)(2,1)S(1)} %bitcast.18, bf16[6,3,192,1536]{3,2,1,0:T(8,128)(2,1)} %refs_1_.10), custom_call_target="tpu_custom_call" | custom-call | bytes 4128768 | tf_op jit(solution)/shard_map/pallas_call | solution.py:146
  89.7 3.3 %collective-permute-start.33 = (bf16[48,1536]{1,0:T(8,128)(2,1)S(1)}, bf16[48,1536]{1,0:T(8,128)(2,1)S(1)}, u32[]{:S(2)}, u32[]{:S(2)}) collective-permute-start(bf16[48,1536]{1,0:T(8,128)(2,1)S(1)} %get-tuple-element.86.refs_0_), channel_id=1, source_target_pairs={{0,2},{1,3},{2,0},{3,1},{4,6},{5,7},{6,4},{7,5},{8,10},{9,11},{10,... | collective-permute-start | bytes 442376 | tf_op jit(solution)/shard_map/ppermute | solution.py:35
  93.2 7.3 %collective-permute-done.13.a2 = bf16[224,384]{1,0:T(8,128)(2,1)S(1)} collective-permute-done((bf16[224,384]{1,0:T(8,128)(2,1)S(1)}, bf16[224,384]{1,0:T(8,128)(2,1)S(1)}, u32[]{:S(2)}, u32[]{:S(2)}) %collective-permute-start.13) | collective-permute-done | bytes 172064 | tf_op jit(solution)/shard_map/ppermute | solution.py:35
  100.6 4.9 %collective-permute-done.14.a3 = bf16[224,384]{1,0:T(8,128)(2,1)S(1)} collective-permute-done((bf16[224,384]{1,0:T(8,128)(2,1)S(1)}, bf16[224,384]{1,0:T(8,128)(2,1)S(1)}, u32[]{:S(2)}, u32[]{:S(2)}) %collective-permute-start.14) | collective-permute-done | bytes 172064 | tf_op jit(solution)/shard_map/ppermute | solution.py:35
  105.4 3.2 %shard_map.101 = (bf16[208,384]{1,0:T(8,128)(2,1)S(1)}, bf16[448,1536]{1,0:T(8,128)(2,1)S(1)}) custom-call(s32[2]{0:T(128)S(1)} %add_convert_fusion.edge_ref, bf16[224,384]{1,0:T(8,128)(2,1)S(1)} %get-tuple-element.63.a0, bf16[224,384]{1,0:T(8,128)(2,1)S(1)} %collective-permute-done.12.a1, bf16[224,384]{1,0:T(8,128)(2,1)S(1)} %collective-permute-done.13.a2, ...), custom_call_target="tpu_custom_call" | custom-call | flops 1849688064 | bytes 6881280 | tf_op jit(solution)/shard_map/pallas_call | solution.py:146
  112.6 3.1 %collective-permute-start.16 = (bf16[208,384]{1,0:T(8,128)(2,1)S(1)}, bf16[208,384]{1,0:T(8,128)(2,1)S(1)}, u32[]{:S(2)}, u32[]{:S(2)}) collective-permute-start(bf16[208,384]{1,0:T(8,128)(2,1)S(1)} %get-tuple-element.68.a0), channel_id=1, source_target_pairs={{0,2},{1,3},{2,0},{3,1},{4,6},{5,7},{6,4},{7,5},{8,10},{9,11},{10,... | collective-permute-start | bytes 479240 | tf_op jit(solution)/shard_map/ppermute | solution.py:35
  120.1 2.6 %shard_map.103 = (bf16[4,4,48,1536]{3,2,1,0:T(8,128)(2,1)S(1)}, bf16[3,192,1536]{2,1,0:T(8,128)(2,1)S(1)}) custom-call(s32[4]{0:T(128)S(1)} %compare_select_fusion.order_ref, bf16[8,208,1536]{2,1,0:T(8,128)(2,1)S(1)} %bitcast.14, bf16[6,3,192,1536]{3,2,1,0:T(8,128)(2,1)} %refs_1_.10), custom_call_target="tpu_custom_call" | custom-call | bytes 4128768 | tf_op jit(solution)/shard_map/pallas_call | solution.py:146
  122.8 3.9 %collective-permute-done.16.a2 = bf16[208,384]{1,0:T(8,128)(2,1)S(1)} collective-permute-done((bf16[208,384]{1,0:T(8,128)(2,1)S(1)}, bf16[208,384]{1,0:T(8,128)(2,1)S(1)}, u32[]{:S(2)}, u32[]{:S(2)}) %collective-permute-start.16) | collective-permute-done | bytes 159776 | tf_op jit(solution)/shard_map/ppermute | solution.py:35
  126.7 2.7 %collective-permute-done.17.a3 = bf16[208,384]{1,0:T(8,128)(2,1)S(1)} collective-permute-done((bf16[208,384]{1,0:T(8,128)(2,1)S(1)}, bf16[208,384]{1,0:T(8,128)(2,1)S(1)}, u32[]{:S(2)}, u32[]{:S(2)}) %collective-permute-start.17) | collective-permute-done | bytes 159776 | tf_op jit(solution)/shard_map/ppermute | solution.py:35
  129.4 3.1 %shard_map.104 = (bf16[192,384]{1,0:T(8,128)(2,1)S(1)}, bf16[416,1536]{1,0:T(8,128)(2,1)S(1)}) custom-call(s32[2]{0:T(128)S(1)} %add_convert_fusion.edge_ref, bf16[208,384]{1,0:T(8,128)(2,1)S(1)} %get-tuple-element.68.a0, bf16[208,384]{1,0:T(8,128)(2,1)S(1)} %collective-permute-done.15.a1, bf16[208,384]{1,0:T(8,128)(2,1)S(1)} %collective-permute-done.16.a2, ...), custom_call_target="tpu_custom_call" | custom-call | flops 1717567488 | bytes 6684672 | tf_op jit(solution)/shard_map/pallas_call | solution.py:146
  136.5 2.5 %shard_map.105 = (bf16[4,4,48,1536]{3,2,1,0:T(8,128)(2,1)S(1)}, bf16[3,192,1536]{2,1,0:T(8,128)(2,1)S(1)}) custom-call(s32[4]{0:T(128)S(1)} %compare_select_fusion.order_ref, bf16[8,208,1536]{2,1,0:T(8,128)(2,1)S(1)} %bitcast.16, bf16[6,3,192,1536]{3,2,1,0:T(8,128)(2,1)} %refs_1_.10), custom_call_target="tpu_custom_call" | custom-call | bytes 4128768 | tf_op jit(solution)/shard_map/pallas_call | solution.py:146
  139.2 6.5 %collective-permute-done.22.a2 = bf16[192,384]{1,0:T(8,128)(2,1)S(1)} collective-permute-done((bf16[192,384]{1,0:T(8,128)(2,1)S(1)}, bf16[192,384]{1,0:T(8,128)(2,1)S(1)}, u32[]{:S(2)}, u32[]{:S(2)}) %collective-permute-start.22) | collective-permute-done | bytes 147488 | tf_op jit(solution)/shard_map/ppermute | solution.py:35
  163.7 2.5 %shard_map.110 = (bf16[4,4,48,1536]{3,2,1,0:T(8,128)(2,1)S(1)}, bf16[3,192,1536]{2,1,0:T(8,128)(2,1)S(1)}) custom-call(s32[4]{0:T(128)S(1)} %compare_select_fusion.order_ref, bf16[8,192,1536]{2,1,0:T(8,128)(2,1)S(1)} %bitcast.19, bf16[6,3,192,1536]{3,2,1,0:T(8,128)(2,1)} %refs_1_.10), custom_call_target="tpu_custom_call" | custom-call | bytes 4128768 | tf_op jit(solution)/shard_map/pallas_call | solution.py:146
  166.1 3.6 %collective-permute-done.26.a3 = bf16[160,384]{1,0:T(8,128)(2,1)S(1)} collective-permute-done((bf16[160,384]{1,0:T(8,128)(2,1)S(1)}, bf16[160,384]{1,0:T(8,128)(2,1)S(1)}, u32[]{:S(2)}, u32[]{:S(2)}) %collective-permute-start.26) | collective-permute-done | bytes 122912 | tf_op jit(solution)/shard_map/ppermute | solution.py:35
  169.7 3.2 %collective-permute-done.31.e3 = bf16[96,384]{1,0:T(8,128)(2,1)S(1)} collective-permute-done((bf16[96,384]{1,0:T(8,128)(2,1)S(1)}, bf16[96,384]{1,0:T(8,128)(2,1)S(1)}, u32[]{:S(2)}, u32[]{:S(2)}) %collective-permute-start.31) | collective-permute-done | bytes 73760 | tf_op jit(solution)/shard_map/ppermute | solution.py:35
  172.9 3.5 %shard_map.111 = (bf16[192,384]{1,0:T(8,128)(2,1)S(1)}, bf16[512,1536]{1,0:T(8,128)(2,1)S(1)}) custom-call(s32[2]{0:T(128)S(1)} %add_convert_fusion.edge_ref, bf16[160,384]{1,0:T(8,128)(2,1)S(1)} %shard_map.107.a0, bf16[160,384]{1,0:T(8,128)(2,1)S(1)} %collective-permute-done.24.a1, bf16[160,384]{1,0:T(8,128)(2,1)S(1)} %collective-permute-done.25.a2, ...), custom_call_target="tpu_custom_call" | custom-call | flops 2113929216 | bytes 7274496 | tf_op jit(solution)/shard_map/pallas_call | solution.py:146
  180.0 3.2 %collective-permute-done.35.a1 = bf16[192,384]{1,0:T(8,128)(2,1)S(1)} collective-permute-done((bf16[192,384]{1,0:T(8,128)(2,1)S(1)}, bf16[192,384]{1,0:T(8,128)(2,1)S(1)}, u32[]{:S(2)}, u32[]{:S(2)}) %collective-permute-start.35) | collective-permute-done | bytes 147488 | tf_op jit(solution)/shard_map/ppermute | solution.py:35
  183.2 6.5 %collective-permute-done.36.a2 = bf16[192,384]{1,0:T(8,128)(2,1)S(1)} collective-permute-done((bf16[192,384]{1,0:T(8,128)(2,1)S(1)}, bf16[192,384]{1,0:T(8,128)(2,1)S(1)}, u32[]{:S(2)}, u32[]{:S(2)}) %collective-permute-start.36) | collective-permute-done | bytes 147488 | tf_op jit(solution)/shard_map/ppermute | solution.py:35
  189.6 2.5 %collective-permute-done.37.a3 = bf16[192,384]{1,0:T(8,128)(2,1)S(1)} collective-permute-done((bf16[192,384]{1,0:T(8,128)(2,1)S(1)}, bf16[192,384]{1,0:T(8,128)(2,1)S(1)}, u32[]{:S(2)}, u32[]{:S(2)}) %collective-permute-start.37) | collective-permute-done | bytes 147488 | tf_op jit(solution)/shard_map/ppermute | solution.py:35
  192.1 4.2 %shard_map.113 = (bf16[384,1024]{1,0:T(8,128)(2,1)}, bf16[64,1024]{1,0:T(8,128)(2,1)}) custom-call(bf16[192,384]{1,0:T(8,128)(2,1)S(1)} %get-tuple-element.93.a0, bf16[192,384]{1,0:T(8,128)(2,1)S(1)} %collective-permute-done.35.a1, bf16[192,384]{1,0:T(8,128)(2,1)S(1)} %collective-permute-done.36.a2, bf16[192,384]{1,0:T(8,128)(2,1)S(1)} %collective-permute-done.37.a3, ...), custom_call_target="tpu_custom_call" | custom-call | flops 2113929216 | bytes 6684672 | tf_op jit(solution)/shard_map/pallas_call | solution.py:146
  196.3 4.5 %all-to-all-start = ((bf16[8,8,1024]{2,1,0:T(8,128)(2,1)}), bf16[8,8,1024]{2,1,0:T(8,128)(2,1)S(1)}, u32[]{:S(2)}, u32[]{:S(2)}) async-start(bf16[8,8,1024]{2,1,0:T(8,128)(2,1)} %bitcast.12), calls=%async_computation | async-start | bytes 262144 | tf_op jit(solution)/shard_map/all_to_all | solution.py:576
  201.0 5.4 %all-to-all-done = bf16[8,8,1024]{2,1,0:T(8,128)(2,1)S(1)} async-done(((bf16[8,8,1024]{2,1,0:T(8,128)(2,1)}), bf16[8,8,1024]{2,1,0:T(8,128)(2,1)S(1)}, u32[]{:S(2)}, u32[]{:S(2)}) %all-to-all-start) | async-done | bytes 131104 | tf_op jit(solution)/shard_map/all_to_all | solution.py:576
  (114 shorter events, 74.2 us)
Async XLA Ops:
  7.2 62.3 %all-gather.7.cloned.1.call-start = ((), (), s32[]{:S(2)}) async-start(), calls=%async_computation.1 | async-start | bytes 5308416 | tf_op jit(solution)/shard_map/all_gather | solution.py:486
  8.4 12.2 %collective-permute-start.2 = (bf16[48,1536]{1,0:T(8,128)(2,1)S(1)}, bf16[48,1536]{1,0:T(8,128)(2,1)S(1)}, u32[]{:S(2)}, u32[]{:S(2)}) collective-permute-start(bf16[48,1536]{1,0:T(8,128)(2,1)S(1)} %get-tuple-element.54.refs_0_), channel_id=1, source_target_pairs={{0,1},{1,2},{2,3},{3,0},{4,5},{5,6},{6,7},{7,4},{8,9},{9,10},{10,1... | collective-permute-start | bytes 442376 | tf_op jit(solution)/shard_map/ppermute | solution.py:35
  10.0 12.6 %collective-permute-start.10 = (bf16[48,1536]{1,0:T(8,128)(2,1)S(1)}, bf16[48,1536]{1,0:T(8,128)(2,1)S(1)}, u32[]{:S(2)}, u32[]{:S(2)}) collective-permute-start(bf16[48,1536]{1,0:T(8,128)(2,1)S(1)} %get-tuple-element.54.refs_0_), channel_id=1, source_target_pairs={{0,2},{1,3},{2,0},{3,1},{4,6},{5,7},{6,4},{7,5},{8,10},{9,11},{10,... | collective-permute-start | bytes 442376 | tf_op jit(solution)/shard_map/ppermute | solution.py:35
  11.1 13.2 %collective-permute-start.11 = (bf16[48,1536]{1,0:T(8,128)(2,1)S(1)}, bf16[48,1536]{1,0:T(8,128)(2,1)S(1)}, u32[]{:S(2)}, u32[]{:S(2)}) collective-permute-start(bf16[48,1536]{1,0:T(8,128)(2,1)S(1)} %get-tuple-element.54.refs_0_), channel_id=1, source_target_pairs={{0,3},{1,0},{2,1},{3,2},{4,7},{5,4},{6,5},{7,6},{8,11},{9,8},{10,9... | collective-permute-start | bytes 442376 | tf_op jit(solution)/shard_map/ppermute | solution.py:35
  25.2 92.4 %all-gather.9.cloned.1.call-start = ((), (), s32[]{:S(2)}) async-start(), calls=%async_computation.2 | async-start | bytes 5750784 | tf_op jit(solution)/shard_map/all_gather | solution.py:486
  25.4 16.1 %collective-permute-start.4 = (bf16[464,384]{1,0:T(8,128)(2,1)S(1)}, bf16[464,384]{1,0:T(8,128)(2,1)S(1)}, u32[]{:S(2)}, u32[]{:S(2)}) collective-permute-start(bf16[464,384]{1,0:T(8,128)(2,1)S(1)} %fusion.1.c0), channel_id=1, source_target_pairs={{0,2},{1,3},{2,0},{3,1},{4,6},{5,7},{6,4},{7,5},{8,10},{9,11},{10,... | collective-permute-start | bytes 1069064 | tf_op jit(solution)/shard_map/ppermute | solution.py:43
  27.1 32.2 %collective-permute-start.3 = (bf16[464,384]{1,0:T(8,128)(2,1)S(1)}, bf16[464,384]{1,0:T(8,128)(2,1)S(1)}, u32[]{:S(2)}, u32[]{:S(2)}) collective-permute-start(bf16[464,384]{1,0:T(8,128)(2,1)S(1)} %fusion.1.c0), channel_id=1, source_target_pairs={{0,1},{1,2},{2,3},{4,5},{5,6},{6,7},{8,9},{9,10},{10,11},{12,13},{... | collective-permute-start | bytes 1069064 | tf_op jit(solution)/shard_map/ppermute | solution.py:44
  29.0 23.0 %collective-permute-start.5 = (bf16[464,384]{1,0:T(8,128)(2,1)S(1)}, bf16[464,384]{1,0:T(8,128)(2,1)S(1)}, u32[]{:S(2)}, u32[]{:S(2)}) collective-permute-start(bf16[464,384]{1,0:T(8,128)(2,1)S(1)} %fusion.1.c0), channel_id=1, source_target_pairs={{1,0},{2,1},{3,2},{5,4},{6,5},{7,6},{9,8},{10,9},{11,10},{13,12},{... | collective-permute-start | bytes 1069064 | tf_op jit(solution)/shard_map/ppermute | solution.py:45
  41.4 17.9 %collective-permute-start.6 = (bf16[464,384]{1,0:T(8,128)(2,1)S(1)}, bf16[464,384]{1,0:T(8,128)(2,1)S(1)}, u32[]{:S(2)}, u32[]{:S(2)}) collective-permute-start(bf16[464,384]{1,0:T(8,128)(2,1)S(1)} %collective-permute-done.4.c2), channel_id=1, source_target_pairs={{2,3},{1,0},{6,7},{5,4},{10,11},{9,8},{14,15},{13,12},{18,19},{17,... | collective-permute-start | bytes 1069064 | tf_op jit(solution)/shard_map/ppermute | solution.py:46
  52.0 10.8 %collective-permute-start.19 = (bf16[48,1536]{1,0:T(8,128)(2,1)S(1)}, bf16[48,1536]{1,0:T(8,128)(2,1)S(1)}, u32[]{:S(2)}, u32[]{:S(2)}) collective-permute-start(bf16[48,1536]{1,0:T(8,128)(2,1)S(1)} %get-tuple-element.70.refs_0_), channel_id=1, source_target_pairs={{0,2},{1,3},{2,0},{3,1},{4,6},{5,7},{6,4},{7,5},{8,10},{9,11},{10,... | collective-permute-start | bytes 442376 | tf_op jit(solution)/shard_map/ppermute | solution.py:35
  52.0 10.8 %collective-permute-start.20 = (bf16[48,1536]{1,0:T(8,128)(2,1)S(1)}, bf16[48,1536]{1,0:T(8,128)(2,1)S(1)}, u32[]{:S(2)}, u32[]{:S(2)}) collective-permute-start(bf16[48,1536]{1,0:T(8,128)(2,1)S(1)} %get-tuple-element.70.refs_0_), channel_id=1, source_target_pairs={{0,3},{1,0},{2,1},{3,2},{4,7},{5,4},{6,5},{7,6},{8,11},{9,8},{10,9... | collective-permute-start | bytes 442376 | tf_op jit(solution)/shard_map/ppermute | solution.py:35
  63.6 97.7 %all-gather.11.cloned.1.call-start = ((), (), s32[]{:S(2)}) async-start(), calls=%async_computation.3 | async-start | bytes 5308416 | tf_op jit(solution)/shard_map/all_gather | solution.py:486
  63.7 12.4 %collective-permute-start.7 = (bf16[224,384]{1,0:T(8,128)(2,1)}, bf16[224,384]{1,0:T(8,128)(2,1)S(1)}, u32[]{:S(2)}, u32[]{:S(2)}) collective-permute-start(bf16[224,384]{1,0:T(8,128)(2,1)} %copy-done.6), channel_id=1, source_target_pairs={{0,1},{1,2},{2,3},{3,0},{4,5},{5,6},{6,7},{7,4},{8,9},{9,10},{10,1... | collective-permute-start | bytes 516104 | tf_op jit(solution)/shard_map/ppermute | solution.py:35
  65.4 12.5 %collective-permute-start.8 = (bf16[224,384]{1,0:T(8,128)(2,1)}, bf16[224,384]{1,0:T(8,128)(2,1)S(1)}, u32[]{:S(2)}, u32[]{:S(2)}) collective-permute-start(bf16[224,384]{1,0:T(8,128)(2,1)} %copy-done.6), channel_id=1, source_target_pairs={{0,2},{1,3},{2,0},{3,1},{4,6},{5,7},{6,4},{7,5},{8,10},{9,11},{10,... | collective-permute-start | bytes 516104 | tf_op jit(solution)/shard_map/ppermute | solution.py:35
  67.9 12.5 %collective-permute-start.9 = (bf16[224,384]{1,0:T(8,128)(2,1)}, bf16[224,384]{1,0:T(8,128)(2,1)S(1)}, u32[]{:S(2)}, u32[]{:S(2)}) collective-permute-start(bf16[224,384]{1,0:T(8,128)(2,1)} %copy-done.6), channel_id=1, source_target_pairs={{0,3},{1,0},{2,1},{3,2},{4,7},{5,4},{6,5},{7,6},{8,11},{9,8},{10,9... | collective-permute-start | bytes 516104 | tf_op jit(solution)/shard_map/ppermute | solution.py:35
  83.7 16.8 %collective-permute-start.13 = (bf16[224,384]{1,0:T(8,128)(2,1)S(1)}, bf16[224,384]{1,0:T(8,128)(2,1)S(1)}, u32[]{:S(2)}, u32[]{:S(2)}) collective-permute-start(bf16[224,384]{1,0:T(8,128)(2,1)S(1)} %get-tuple-element.63.a0), channel_id=1, source_target_pairs={{0,2},{1,3},{2,0},{3,1},{4,6},{5,7},{6,4},{7,5},{8,10},{9,11},{10,... | collective-permute-start | bytes 516104 | tf_op jit(solution)/shard_map/ppermute | solution.py:35
  84.6 20.8 %collective-permute-start.14 = (bf16[224,384]{1,0:T(8,128)(2,1)S(1)}, bf16[224,384]{1,0:T(8,128)(2,1)S(1)}, u32[]{:S(2)}, u32[]{:S(2)}) collective-permute-start(bf16[224,384]{1,0:T(8,128)(2,1)S(1)} %get-tuple-element.63.a0), channel_id=1, source_target_pairs={{0,3},{1,0},{2,1},{3,2},{4,7},{5,4},{6,5},{7,6},{8,11},{9,8},{10,9... | collective-permute-start | bytes 516104 | tf_op jit(solution)/shard_map/ppermute | solution.py:35
  89.0 20.0 %collective-permute-start.32 = (bf16[48,1536]{1,0:T(8,128)(2,1)S(1)}, bf16[48,1536]{1,0:T(8,128)(2,1)S(1)}, u32[]{:S(2)}, u32[]{:S(2)}) collective-permute-start(bf16[48,1536]{1,0:T(8,128)(2,1)S(1)} %get-tuple-element.86.refs_0_), channel_id=1, source_target_pairs={{0,1},{1,2},{2,3},{3,0},{4,5},{5,6},{6,7},{7,4},{8,9},{9,10},{10,1... | collective-permute-start | bytes 442376 | tf_op jit(solution)/shard_map/ppermute | solution.py:35
  89.7 21.6 %collective-permute-start.33 = (bf16[48,1536]{1,0:T(8,128)(2,1)S(1)}, bf16[48,1536]{1,0:T(8,128)(2,1)S(1)}, u32[]{:S(2)}, u32[]{:S(2)}) collective-permute-start(bf16[48,1536]{1,0:T(8,128)(2,1)S(1)} %get-tuple-element.86.refs_0_), channel_id=1, source_target_pairs={{0,2},{1,3},{2,0},{3,1},{4,6},{5,7},{6,4},{7,5},{8,10},{9,11},{10,... | collective-permute-start | bytes 442376 | tf_op jit(solution)/shard_map/ppermute | solution.py:35
  93.1 18.6 %collective-permute-start.34 = (bf16[48,1536]{1,0:T(8,128)(2,1)S(1)}, bf16[48,1536]{1,0:T(8,128)(2,1)S(1)}, u32[]{:S(2)}, u32[]{:S(2)}) collective-permute-start(bf16[48,1536]{1,0:T(8,128)(2,1)S(1)} %get-tuple-element.86.refs_0_), channel_id=1, source_target_pairs={{0,3},{1,0},{2,1},{3,2},{4,7},{5,4},{6,5},{7,6},{8,11},{9,8},{10,9... | collective-permute-start | bytes 442376 | tf_op jit(solution)/shard_map/ppermute | solution.py:35
  112.5 10.2 %collective-permute-start.15 = (bf16[208,384]{1,0:T(8,128)(2,1)S(1)}, bf16[208,384]{1,0:T(8,128)(2,1)S(1)}, u32[]{:S(2)}, u32[]{:S(2)}) collective-permute-start(bf16[208,384]{1,0:T(8,128)(2,1)S(1)} %get-tuple-element.68.a0), channel_id=1, source_target_pairs={{0,1},{1,2},{2,3},{3,0},{4,5},{5,6},{6,7},{7,4},{8,9},{9,10},{10,1... | collective-permute-start | bytes 479240 | tf_op jit(solution)/shard_map/ppermute | solution.py:35
  112.6 14.1 %collective-permute-start.16 = (bf16[208,384]{1,0:T(8,128)(2,1)S(1)}, bf16[208,384]{1,0:T(8,128)(2,1)S(1)}, u32[]{:S(2)}, u32[]{:S(2)}) collective-permute-start(bf16[208,384]{1,0:T(8,128)(2,1)S(1)} %get-tuple-element.68.a0), channel_id=1, source_target_pairs={{0,2},{1,3},{2,0},{3,1},{4,6},{5,7},{6,4},{7,5},{8,10},{9,11},{10,... | collective-permute-start | bytes 479240 | tf_op jit(solution)/shard_map/ppermute | solution.py:35
  115.7 13.7 %collective-permute-start.17 = (bf16[208,384]{1,0:T(8,128)(2,1)S(1)}, bf16[208,384]{1,0:T(8,128)(2,1)S(1)}, u32[]{:S(2)}, u32[]{:S(2)}) collective-permute-start(bf16[208,384]{1,0:T(8,128)(2,1)S(1)} %get-tuple-element.68.a0), channel_id=1, source_target_pairs={{0,3},{1,0},{2,1},{3,2},{4,7},{5,4},{6,5},{7,6},{8,11},{9,8},{10,9... | collective-permute-start | bytes 479240 | tf_op jit(solution)/shard_map/ppermute | solution.py:35
  132.6 13.2 %collective-permute-start.22 = (bf16[192,384]{1,0:T(8,128)(2,1)S(1)}, bf16[192,384]{1,0:T(8,128)(2,1)S(1)}, u32[]{:S(2)}, u32[]{:S(2)}) collective-permute-start(bf16[192,384]{1,0:T(8,128)(2,1)S(1)} %get-tuple-element.78.a0), channel_id=1, source_target_pairs={{0,2},{1,3},{2,0},{3,1},{4,6},{5,7},{6,4},{7,5},{8,10},{9,11},{10,... | collective-permute-start | bytes 442376 | tf_op jit(solution)/shard_map/ppermute | solution.py:35
  133.3 12.9 %collective-permute-start.23 = (bf16[192,384]{1,0:T(8,128)(2,1)S(1)}, bf16[192,384]{1,0:T(8,128)(2,1)S(1)}, u32[]{:S(2)}, u32[]{:S(2)}) collective-permute-start(bf16[192,384]{1,0:T(8,128)(2,1)S(1)} %get-tuple-element.78.a0), channel_id=1, source_target_pairs={{0,3},{1,0},{2,1},{3,2},{4,7},{5,4},{6,5},{7,6},{8,11},{9,8},{10,9... | collective-permute-start | bytes 442376 | tf_op jit(solution)/shard_map/ppermute | solution.py:35
  152.2 14.0 %collective-permute-start.25 = (bf16[160,384]{1,0:T(8,128)(2,1)S(1)}, bf16[160,384]{1,0:T(8,128)(2,1)S(1)}, u32[]{:S(2)}, u32[]{:S(2)}) collective-permute-start(bf16[160,384]{1,0:T(8,128)(2,1)S(1)} %shard_map.107.a0), channel_id=1, source_target_pairs={{0,2},{1,3},{2,0},{3,1},{4,6},{5,7},{6,4},{7,5},{8,10},{9,11},{10,... | collective-permute-start | bytes 368648 | tf_op jit(solution)/shard_map/ppermute | solution.py:35
  154.6 15.1 %collective-permute-start.26 = (bf16[160,384]{1,0:T(8,128)(2,1)S(1)}, bf16[160,384]{1,0:T(8,128)(2,1)S(1)}, u32[]{:S(2)}, u32[]{:S(2)}) collective-permute-start(bf16[160,384]{1,0:T(8,128)(2,1)S(1)} %shard_map.107.a0), channel_id=1, source_target_pairs={{0,3},{1,0},{2,1},{3,2},{4,7},{5,4},{6,5},{7,6},{8,11},{9,8},{10,9... | collective-permute-start | bytes 368648 | tf_op jit(solution)/shard_map/ppermute | solution.py:35
  157.7 12.1 %collective-permute-start.29 = (bf16[96,384]{1,0:T(8,128)(2,1)S(1)}, bf16[96,384]{1,0:T(8,128)(2,1)S(1)}, u32[]{:S(2)}, u32[]{:S(2)}) collective-permute-start(bf16[96,384]{1,0:T(8,128)(2,1)S(1)} %shard_map.108.e0), channel_id=1, source_target_pairs={{0,1},{1,2},{2,3},{3,0},{4,5},{5,6},{6,7},{7,4},{8,9},{9,10},{10,1... | collective-permute-start | bytes 221192 | tf_op jit(solution)/shard_map/ppermute | solution.py:35
  157.8 11.9 %collective-permute-start.30 = (bf16[96,384]{1,0:T(8,128)(2,1)S(1)}, bf16[96,384]{1,0:T(8,128)(2,1)S(1)}, u32[]{:S(2)}, u32[]{:S(2)}) collective-permute-start(bf16[96,384]{1,0:T(8,128)(2,1)S(1)} %shard_map.108.e0), channel_id=1, source_target_pairs={{0,2},{1,3},{2,0},{3,1},{4,6},{5,7},{6,4},{7,5},{8,10},{9,11},{10,... | collective-permute-start | bytes 221192 | tf_op jit(solution)/shard_map/ppermute | solution.py:35
  160.1 12.7 %collective-permute-start.31 = (bf16[96,384]{1,0:T(8,128)(2,1)S(1)}, bf16[96,384]{1,0:T(8,128)(2,1)S(1)}, u32[]{:S(2)}, u32[]{:S(2)}) collective-permute-start(bf16[96,384]{1,0:T(8,128)(2,1)S(1)} %shard_map.108.e0), channel_id=1, source_target_pairs={{0,3},{1,0},{2,1},{3,2},{4,7},{5,4},{6,5},{7,6},{8,11},{9,8},{10,9... | collective-permute-start | bytes 221192 | tf_op jit(solution)/shard_map/ppermute | solution.py:35
  176.5 13.1 %collective-permute-start.36 = (bf16[192,384]{1,0:T(8,128)(2,1)S(1)}, bf16[192,384]{1,0:T(8,128)(2,1)S(1)}, u32[]{:S(2)}, u32[]{:S(2)}) collective-permute-start(bf16[192,384]{1,0:T(8,128)(2,1)S(1)} %get-tuple-element.93.a0), channel_id=1, source_target_pairs={{0,2},{1,3},{2,0},{3,1},{4,6},{5,7},{6,4},{7,5},{8,10},{9,11},{10,... | collective-permute-start | bytes 442376 | tf_op jit(solution)/shard_map/ppermute | solution.py:35
  178.7 13.4 %collective-permute-start.37 = (bf16[192,384]{1,0:T(8,128)(2,1)S(1)}, bf16[192,384]{1,0:T(8,128)(2,1)S(1)}, u32[]{:S(2)}, u32[]{:S(2)}) collective-permute-start(bf16[192,384]{1,0:T(8,128)(2,1)S(1)} %get-tuple-element.93.a0), channel_id=1, source_target_pairs={{0,3},{1,0},{2,1},{3,2},{4,7},{5,4},{6,5},{7,6},{8,11},{9,8},{10,9... | collective-permute-start | bytes 442376 | tf_op jit(solution)/shard_map/ppermute | solution.py:35
  (22 other events, 213.4 us)
Sparse Core Ops, SparseCore 0:
  25.4 39.1 all-gather.6
  67.0 40.5 all-gather.8
  112.7 40.5 all-gather.10

commit v11 on v10

--- a/solution.py
+++ b/solution.py
@@ -414,7 +414,7 @@
     margin = (trunk_in.shape[0] - trunk.shape[0]) // 2
     project_all(gather_acts((a0, a1, a2, a3)), weight, trunk_in, margin, pbias, trunk)
     tracks = head_ref.shape[1]
-    width = tile_of(tracks)
+    width = tracks
     for c in range(tracks // width):
         cols = columns(c, width)
         x = dot(trunk[...], head_ref[:, cols]) + hbias_ref[:, cols].astype(jnp.float32)
@@ -508,7 +508,6 @@
     own = jnp.concatenate(
         [above, trunk_input, below, jnp.pad(projection_bias, ((0, -blocks % 16), (0, 0)))], axis=0
     )
-    own = after(own, first[1])
     cells = relayed(own)
     exon_rows = [exon_digits(exon_bins, channels)] if packed else []
     exon_rows = [exon_digits(exon_bins, channels)] if packed else []

time: 214 us -> 214 us (level)
  no operation moved by 1% of the time
where the time goes in v11:
time: 214 us; the launch traced here: 213 us
  waiting for transfers between devices  80.8 us (38%)
  starting transfers between devices  61.8 us (29%)
  Pallas kernels  40.5 us (19%)
  between operations  14.2 us (7%)
  local copies, waits for them, and re-layouts  13.9 us (6%)
  other arithmetic  2.25 us (1%)
    ppermute x30, waiting for transfers between devices, from_others(): lax.ppermute(cells, 'trk', [(i, (i + k) % count) for i in range(count)])  59.8 us
    pallas_call x16, Pallas kernels, kernel_call(): pl.pallas_call(body, in_specs=specs or [SMEM] * scalars + [VMEM] * (len(i...  37.9 us
    ppermute x30, starting transfers between devices, from_others(): lax.ppermute(cells, 'trk', [(i, (i + k) % count) for i in range(count)])  37.9 us
    unnamed x24, local copies, waits for them, and re-layouts  11.9 us
    ppermute x1, waiting for transfers between devices, relayed(): lax.ppermute(cells, 'trk', [(i, (i + 2) % count) for i in range(count)])  8.49 us
    ppermute x1, waiting for transfers between devices, relayed(): down = lax.ppermute(cells, 'trk', [(i + 1, i) for i in range(last)])  6.21 us
    all_to_all x1, waiting for transfers between devices, shards(): lax.all_to_all(partial.reshape(count, genes_here, partial.shape[1]), 'seq...  5.42 us
    ppermute x2, starting transfers between devices, halo(): above = lax.ppermute(tail, 'seq', [(i, i + 1) for i in range(count - 1)])  5.08 us
  transfers between devices with their start and end apart: 42, of which 26 were waited for; matrix products, arithmetic and copies ran while one was open for 1% of the time, Pallas kernels for 15%

profile of v11, /device:TPU:8, one launch (start us, length us, event | category | flops | bytes accessed | tf_op | source)
XLA Modules:
  0.0 213.4 jit_solution(7854548261578714373)
XLA Ops:
  15.1 3.0 %collective-permute-start = (bf16[32,384]{1,0:T(8,128)(2,1)S(1)}, bf16[32,384]{1,0:T(8,128)(2,1)S(1)}, u32[]{:S(2)}, u32[]{:S(2)}) collective-permute-start(bf16[32,384]{1,0:T(8,128)(2,1)S(1)} %get-tuple-element.103), channel_id=1, source_target_pairs={{0,4},{4,8},{8,12},{12,16},{16,20},{20,24},{24,28},{1,5},{5,9},{9,... | collective-permute-start | bytes 73736 | tf_op jit(solution)/shard_map/ppermute | solution.py:54
  29.0 3.9 %collective-permute-start.4 = (bf16[464,384]{1,0:T(8,128)(2,1)S(1)}, bf16[464,384]{1,0:T(8,128)(2,1)S(1)}, u32[]{:S(2)}, u32[]{:S(2)}) collective-permute-start(bf16[464,384]{1,0:T(8,128)(2,1)S(1)} %fusion.1.c0), channel_id=1, source_target_pairs={{1,0},{2,1},{3,2},{5,4},{6,5},{7,6},{9,8},{10,9},{11,10},{13,12},{... | collective-permute-start | bytes 1069064 | tf_op jit(solution)/shard_map/ppermute | solution.py:45
  32.9 8.5 %collective-permute-done.3.c2 = bf16[464,384]{1,0:T(8,128)(2,1)S(1)} collective-permute-done((bf16[464,384]{1,0:T(8,128)(2,1)S(1)}, bf16[464,384]{1,0:T(8,128)(2,1)S(1)}, u32[]{:S(2)}, u32[]{:S(2)}) %collective-permute-start.3) | collective-permute-done | bytes 356384 | tf_op jit(solution)/shard_map/ppermute | solution.py:43
  41.4 4.1 %collective-permute-start.5 = (bf16[464,384]{1,0:T(8,128)(2,1)S(1)}, bf16[464,384]{1,0:T(8,128)(2,1)S(1)}, u32[]{:S(2)}, u32[]{:S(2)}) collective-permute-start(bf16[464,384]{1,0:T(8,128)(2,1)S(1)} %collective-permute-done.3.c2), channel_id=1, source_target_pairs={{2,3},{1,0},{6,7},{5,4},{10,11},{9,8},{14,15},{13,12},{18,19},{17,... | collective-permute-start | bytes 1069064 | tf_op jit(solution)/shard_map/ppermute | solution.py:46
  45.8 6.2 %collective-permute-done.4.c3 = bf16[464,384]{1,0:T(8,128)(2,1)S(1)} collective-permute-done((bf16[464,384]{1,0:T(8,128)(2,1)S(1)}, bf16[464,384]{1,0:T(8,128)(2,1)S(1)}, u32[]{:S(2)}, u32[]{:S(2)}) %collective-permute-start.4) | collective-permute-done | bytes 356384 | tf_op jit(solution)/shard_map/ppermute | solution.py:45
  54.0 4.1 %copy-done = bf16[6,3,192,1536]{3,2,1,0:T(8,128)(2,1)S(1)} copy-done((bf16[6,3,192,1536]{3,2,1,0:T(8,128)(2,1)S(1)}, bf16[6,3,192,1536]{3,2,1,0:T(8,128)(2,1)}, u32[]{:S(2)}) %copy-start) | copy-done | bytes 10616856
  65.4 2.5 %collective-permute-start.7 = (bf16[224,384]{1,0:T(8,128)(2,1)}, bf16[224,384]{1,0:T(8,128)(2,1)S(1)}, u32[]{:S(2)}, u32[]{:S(2)}) collective-permute-start(bf16[224,384]{1,0:T(8,128)(2,1)} %copy-done.6), channel_id=1, source_target_pairs={{0,2},{1,3},{2,0},{3,1},{4,6},{5,7},{6,4},{7,5},{8,10},{9,11},{10,... | collective-permute-start | bytes 516104 | tf_op jit(solution)/shard_map/ppermute | solution.py:35
  71.9 2.6 %shard_map.98 = (bf16[4,4,48,1536]{3,2,1,0:T(8,128)(2,1)S(1)}, bf16[3,192,1536]{2,1,0:T(8,128)(2,1)S(1)}) custom-call(s32[4]{0:T(128)S(1)} %compare_select_fusion.order_ref, bf16[8,192,1536]{2,1,0:T(8,128)(2,1)S(1)} %bitcast.17, bf16[6,3,192,1536]{3,2,1,0:T(8,128)(2,1)} %refs_1_.10), custom_call_target="tpu_custom_call" | custom-call | bytes 4128768 | tf_op jit(solution)/shard_map/pallas_call | solution.py:146
  78.0 2.5 %collective-permute-done.8.a3 = bf16[224,384]{1,0:T(8,128)(2,1)S(1)} collective-permute-done((bf16[224,384]{1,0:T(8,128)(2,1)}, bf16[224,384]{1,0:T(8,128)(2,1)S(1)}, u32[]{:S(2)}, u32[]{:S(2)}) %collective-permute-start.8) | collective-permute-done | bytes 172064 | tf_op jit(solution)/shard_map/ppermute | solution.py:35
  80.4 3.2 %shard_map.99 = (bf16[224,384]{1,0:T(8,128)(2,1)S(1)}, bf16[448,1536]{1,0:T(8,128)(2,1)S(1)}) custom-call(s32[2]{0:T(128)S(1)} %add_convert_fusion.edge_ref, bf16[224,384]{1,0:T(8,128)(2,1)S(1)} %copy-done.7, bf16[224,384]{1,0:T(8,128)(2,1)S(1)} %collective-permute-done.6.a1, bf16[224,384]{1,0:T(8,128)(2,1)S(1)} %collective-permute-done.7.a2, ...), custom_call_target="tpu_custom_call" | custom-call | flops 1849688064 | bytes 6881280 | tf_op jit(solution)/shard_map/pallas_call | solution.py:146
  86.6 2.5 %shard_map.100 = (bf16[4,4,48,1536]{3,2,1,0:T(8,128)(2,1)S(1)}, bf16[3,192,1536]{2,1,0:T(8,128)(2,1)S(1)}) custom-call(s32[4]{0:T(128)S(1)} %compare_select_fusion.order_ref, bf16[8,192,1536]{2,1,0:T(8,128)(2,1)S(1)} %bitcast.18, bf16[6,3,192,1536]{3,2,1,0:T(8,128)(2,1)} %refs_1_.10), custom_call_target="tpu_custom_call" | custom-call | bytes 4128768 | tf_op jit(solution)/shard_map/pallas_call | solution.py:146
  89.7 3.3 %collective-permute-start.33 = (bf16[48,1536]{1,0:T(8,128)(2,1)S(1)}, bf16[48,1536]{1,0:T(8,128)(2,1)S(1)}, u32[]{:S(2)}, u32[]{:S(2)}) collective-permute-start(bf16[48,1536]{1,0:T(8,128)(2,1)S(1)} %get-tuple-element.84.refs_0_), channel_id=1, source_target_pairs={{0,2},{1,3},{2,0},{3,1},{4,6},{5,7},{6,4},{7,5},{8,10},{9,11},{10,... | collective-permute-start | bytes 442376 | tf_op jit(solution)/shard_map/ppermute | solution.py:35
  93.2 7.3 %collective-permute-done.13.a2 = bf16[224,384]{1,0:T(8,128)(2,1)S(1)} collective-permute-done((bf16[224,384]{1,0:T(8,128)(2,1)S(1)}, bf16[224,384]{1,0:T(8,128)(2,1)S(1)}, u32[]{:S(2)}, u32[]{:S(2)}) %collective-permute-start.13) | collective-permute-done | bytes 172064 | tf_op jit(solution)/shard_map/ppermute | solution.py:35
  100.6 4.9 %collective-permute-done.14.a3 = bf16[224,384]{1,0:T(8,128)(2,1)S(1)} collective-permute-done((bf16[224,384]{1,0:T(8,128)(2,1)S(1)}, bf16[224,384]{1,0:T(8,128)(2,1)S(1)}, u32[]{:S(2)}, u32[]{:S(2)}) %collective-permute-start.14) | collective-permute-done | bytes 172064 | tf_op jit(solution)/shard_map/ppermute | solution.py:35
  105.4 3.2 %shard_map.101 = (bf16[208,384]{1,0:T(8,128)(2,1)S(1)}, bf16[448,1536]{1,0:T(8,128)(2,1)S(1)}) custom-call(s32[2]{0:T(128)S(1)} %add_convert_fusion.edge_ref, bf16[224,384]{1,0:T(8,128)(2,1)S(1)} %get-tuple-element.61.a0, bf16[224,384]{1,0:T(8,128)(2,1)S(1)} %collective-permute-done.12.a1, bf16[224,384]{1,0:T(8,128)(2,1)S(1)} %collective-permute-done.13.a2, ...), custom_call_target="tpu_custom_call" | custom-call | flops 1849688064 | bytes 6881280 | tf_op jit(solution)/shard_map/pallas_call | solution.py:146
  112.6 3.1 %collective-permute-start.16 = (bf16[208,384]{1,0:T(8,128)(2,1)S(1)}, bf16[208,384]{1,0:T(8,128)(2,1)S(1)}, u32[]{:S(2)}, u32[]{:S(2)}) collective-permute-start(bf16[208,384]{1,0:T(8,128)(2,1)S(1)} %get-tuple-element.66.a0), channel_id=1, source_target_pairs={{0,2},{1,3},{2,0},{3,1},{4,6},{5,7},{6,4},{7,5},{8,10},{9,11},{10,... | collective-permute-start | bytes 479240 | tf_op jit(solution)/shard_map/ppermute | solution.py:35
  120.1 2.6 %shard_map.103 = (bf16[4,4,48,1536]{3,2,1,0:T(8,128)(2,1)S(1)}, bf16[3,192,1536]{2,1,0:T(8,128)(2,1)S(1)}) custom-call(s32[4]{0:T(128)S(1)} %compare_select_fusion.order_ref, bf16[8,208,1536]{2,1,0:T(8,128)(2,1)S(1)} %bitcast.14, bf16[6,3,192,1536]{3,2,1,0:T(8,128)(2,1)} %refs_1_.10), custom_call_target="tpu_custom_call" | custom-call | bytes 4128768 | tf_op jit(solution)/shard_map/pallas_call | solution.py:146
  122.8 3.9 %collective-permute-done.16.a2 = bf16[208,384]{1,0:T(8,128)(2,1)S(1)} collective-permute-done((bf16[208,384]{1,0:T(8,128)(2,1)S(1)}, bf16[208,384]{1,0:T(8,128)(2,1)S(1)}, u32[]{:S(2)}, u32[]{:S(2)}) %collective-permute-start.16) | collective-permute-done | bytes 159776 | tf_op jit(solution)/shard_map/ppermute | solution.py:35
  126.7 2.7 %collective-permute-done.17.a3 = bf16[208,384]{1,0:T(8,128)(2,1)S(1)} collective-permute-done((bf16[208,384]{1,0:T(8,128)(2,1)S(1)}, bf16[208,384]{1,0:T(8,128)(2,1)S(1)}, u32[]{:S(2)}, u32[]{:S(2)}) %collective-permute-start.17) | collective-permute-done | bytes 159776 | tf_op jit(solution)/shard_map/ppermute | solution.py:35
  129.4 3.1 %shard_map.104 = (bf16[192,384]{1,0:T(8,128)(2,1)S(1)}, bf16[416,1536]{1,0:T(8,128)(2,1)S(1)}) custom-call(s32[2]{0:T(128)S(1)} %add_convert_fusion.edge_ref, bf16[208,384]{1,0:T(8,128)(2,1)S(1)} %get-tuple-element.66.a0, bf16[208,384]{1,0:T(8,128)(2,1)S(1)} %collective-permute-done.15.a1, bf16[208,384]{1,0:T(8,128)(2,1)S(1)} %collective-permute-done.16.a2, ...), custom_call_target="tpu_custom_call" | custom-call | flops 1717567488 | bytes 6684672 | tf_op jit(solution)/shard_map/pallas_call | solution.py:146
  136.5 2.5 %shard_map.105 = (bf16[4,4,48,1536]{3,2,1,0:T(8,128)(2,1)S(1)}, bf16[3,192,1536]{2,1,0:T(8,128)(2,1)S(1)}) custom-call(s32[4]{0:T(128)S(1)} %compare_select_fusion.order_ref, bf16[8,208,1536]{2,1,0:T(8,128)(2,1)S(1)} %bitcast.16, bf16[6,3,192,1536]{3,2,1,0:T(8,128)(2,1)} %refs_1_.10), custom_call_target="tpu_custom_call" | custom-call | bytes 4128768 | tf_op jit(solution)/shard_map/pallas_call | solution.py:146
  139.2 6.5 %collective-permute-done.22.a2 = bf16[192,384]{1,0:T(8,128)(2,1)S(1)} collective-permute-done((bf16[192,384]{1,0:T(8,128)(2,1)S(1)}, bf16[192,384]{1,0:T(8,128)(2,1)S(1)}, u32[]{:S(2)}, u32[]{:S(2)}) %collective-permute-start.22) | collective-permute-done | bytes 147488 | tf_op jit(solution)/shard_map/ppermute | solution.py:35
  163.7 2.5 %shard_map.110 = (bf16[4,4,48,1536]{3,2,1,0:T(8,128)(2,1)S(1)}, bf16[3,192,1536]{2,1,0:T(8,128)(2,1)S(1)}) custom-call(s32[4]{0:T(128)S(1)} %compare_select_fusion.order_ref, bf16[8,192,1536]{2,1,0:T(8,128)(2,1)S(1)} %bitcast.19, bf16[6,3,192,1536]{3,2,1,0:T(8,128)(2,1)} %refs_1_.10), custom_call_target="tpu_custom_call" | custom-call | bytes 4128768 | tf_op jit(solution)/shard_map/pallas_call | solution.py:146
  166.1 3.6 %collective-permute-done.26.a3 = bf16[160,384]{1,0:T(8,128)(2,1)S(1)} collective-permute-done((bf16[160,384]{1,0:T(8,128)(2,1)S(1)}, bf16[160,384]{1,0:T(8,128)(2,1)S(1)}, u32[]{:S(2)}, u32[]{:S(2)}) %collective-permute-start.26) | collective-permute-done | bytes 122912 | tf_op jit(solution)/shard_map/ppermute | solution.py:35
  169.7 3.2 %collective-permute-done.31.e3 = bf16[96,384]{1,0:T(8,128)(2,1)S(1)} collective-permute-done((bf16[96,384]{1,0:T(8,128)(2,1)S(1)}, bf16[96,384]{1,0:T(8,128)(2,1)S(1)}, u32[]{:S(2)}, u32[]{:S(2)}) %collective-permute-start.31) | collective-permute-done | bytes 73760 | tf_op jit(solution)/shard_map/ppermute | solution.py:35
  172.9 3.5 %shard_map.111 = (bf16[192,384]{1,0:T(8,128)(2,1)S(1)}, bf16[512,1536]{1,0:T(8,128)(2,1)S(1)}) custom-call(s32[2]{0:T(128)S(1)} %add_convert_fusion.edge_ref, bf16[160,384]{1,0:T(8,128)(2,1)S(1)} %shard_map.107.a0, bf16[160,384]{1,0:T(8,128)(2,1)S(1)} %collective-permute-done.24.a1, bf16[160,384]{1,0:T(8,128)(2,1)S(1)} %collective-permute-done.25.a2, ...), custom_call_target="tpu_custom_call" | custom-call | flops 2113929216 | bytes 7274496 | tf_op jit(solution)/shard_map/pallas_call | solution.py:146
  180.0 3.2 %collective-permute-done.35.a1 = bf16[192,384]{1,0:T(8,128)(2,1)S(1)} collective-permute-done((bf16[192,384]{1,0:T(8,128)(2,1)S(1)}, bf16[192,384]{1,0:T(8,128)(2,1)S(1)}, u32[]{:S(2)}, u32[]{:S(2)}) %collective-permute-start.35) | collective-permute-done | bytes 147488 | tf_op jit(solution)/shard_map/ppermute | solution.py:35
  183.2 6.5 %collective-permute-done.36.a2 = bf16[192,384]{1,0:T(8,128)(2,1)S(1)} collective-permute-done((bf16[192,384]{1,0:T(8,128)(2,1)S(1)}, bf16[192,384]{1,0:T(8,128)(2,1)S(1)}, u32[]{:S(2)}, u32[]{:S(2)}) %collective-permute-start.36) | collective-permute-done | bytes 147488 | tf_op jit(solution)/shard_map/ppermute | solution.py:35
  189.6 2.5 %collective-permute-done.37.a3 = bf16[192,384]{1,0:T(8,128)(2,1)S(1)} collective-permute-done((bf16[192,384]{1,0:T(8,128)(2,1)S(1)}, bf16[192,384]{1,0:T(8,128)(2,1)S(1)}, u32[]{:S(2)}, u32[]{:S(2)}) %collective-permute-start.37) | collective-permute-done | bytes 147488 | tf_op jit(solution)/shard_map/ppermute | solution.py:35
  192.1 4.0 %shard_map.113 = (bf16[384,1024]{1,0:T(8,128)(2,1)}, bf16[64,1024]{1,0:T(8,128)(2,1)}) custom-call(bf16[192,384]{1,0:T(8,128)(2,1)S(1)} %get-tuple-element.91.a0, bf16[192,384]{1,0:T(8,128)(2,1)S(1)} %collective-permute-done.35.a1, bf16[192,384]{1,0:T(8,128)(2,1)S(1)} %collective-permute-done.36.a2, bf16[192,384]{1,0:T(8,128)(2,1)S(1)} %collective-permute-done.37.a3, ...), custom_call_target="tpu_custom_call" | custom-call | flops 2113929216 | bytes 6684672 | tf_op jit(solution)/shard_map/pallas_call | solution.py:146
  196.1 4.6 %all-to-all-start = ((bf16[8,8,1024]{2,1,0:T(8,128)(2,1)}), bf16[8,8,1024]{2,1,0:T(8,128)(2,1)S(1)}, u32[]{:S(2)}, u32[]{:S(2)}) async-start(bf16[8,8,1024]{2,1,0:T(8,128)(2,1)} %bitcast.12), calls=%async_computation | async-start | bytes 262144 | tf_op jit(solution)/shard_map/all_to_all | solution.py:575
  200.8 5.4 %all-to-all-done = bf16[8,8,1024]{2,1,0:T(8,128)(2,1)S(1)} async-done(((bf16[8,8,1024]{2,1,0:T(8,128)(2,1)}), bf16[8,8,1024]{2,1,0:T(8,128)(2,1)S(1)}, u32[]{:S(2)}, u32[]{:S(2)}) %all-to-all-start) | async-done | bytes 131104 | tf_op jit(solution)/shard_map/all_to_all | solution.py:575
  (114 shorter events, 74.2 us)
Async XLA Ops:
  7.2 62.3 %all-gather.7.cloned.1.call-start = ((), (), s32[]{:S(2)}) async-start(), calls=%async_computation.1 | async-start | bytes 5308416 | tf_op jit(solution)/shard_map/all_gather | solution.py:486
  8.4 12.2 %collective-permute-start.9 = (bf16[48,1536]{1,0:T(8,128)(2,1)S(1)}, bf16[48,1536]{1,0:T(8,128)(2,1)S(1)}, u32[]{:S(2)}, u32[]{:S(2)}) collective-permute-start(bf16[48,1536]{1,0:T(8,128)(2,1)S(1)} %get-tuple-element.52.refs_0_), channel_id=1, source_target_pairs={{0,1},{1,2},{2,3},{3,0},{4,5},{5,6},{6,7},{7,4},{8,9},{9,10},{10,1... | collective-permute-start | bytes 442376 | tf_op jit(solution)/shard_map/ppermute | solution.py:35
  10.0 12.6 %collective-permute-start.10 = (bf16[48,1536]{1,0:T(8,128)(2,1)S(1)}, bf16[48,1536]{1,0:T(8,128)(2,1)S(1)}, u32[]{:S(2)}, u32[]{:S(2)}) collective-permute-start(bf16[48,1536]{1,0:T(8,128)(2,1)S(1)} %get-tuple-element.52.refs_0_), channel_id=1, source_target_pairs={{0,2},{1,3},{2,0},{3,1},{4,6},{5,7},{6,4},{7,5},{8,10},{9,11},{10,... | collective-permute-start | bytes 442376 | tf_op jit(solution)/shard_map/ppermute | solution.py:35
  11.1 13.2 %collective-permute-start.11 = (bf16[48,1536]{1,0:T(8,128)(2,1)S(1)}, bf16[48,1536]{1,0:T(8,128)(2,1)S(1)}, u32[]{:S(2)}, u32[]{:S(2)}) collective-permute-start(bf16[48,1536]{1,0:T(8,128)(2,1)S(1)} %get-tuple-element.52.refs_0_), channel_id=1, source_target_pairs={{0,3},{1,0},{2,1},{3,2},{4,7},{5,4},{6,5},{7,6},{8,11},{9,8},{10,9... | collective-permute-start | bytes 442376 | tf_op jit(solution)/shard_map/ppermute | solution.py:35
  25.2 92.4 %all-gather.9.cloned.1.call-start = ((), (), s32[]{:S(2)}) async-start(), calls=%async_computation.2 | async-start | bytes 5750784 | tf_op jit(solution)/shard_map/all_gather | solution.py:486
  25.4 16.1 %collective-permute-start.3 = (bf16[464,384]{1,0:T(8,128)(2,1)S(1)}, bf16[464,384]{1,0:T(8,128)(2,1)S(1)}, u32[]{:S(2)}, u32[]{:S(2)}) collective-permute-start(bf16[464,384]{1,0:T(8,128)(2,1)S(1)} %fusion.1.c0), channel_id=1, source_target_pairs={{0,2},{1,3},{2,0},{3,1},{4,6},{5,7},{6,4},{7,5},{8,10},{9,11},{10,... | collective-permute-start | bytes 1069064 | tf_op jit(solution)/shard_map/ppermute | solution.py:43
  27.1 32.2 %collective-permute-start.2 = (bf16[464,384]{1,0:T(8,128)(2,1)S(1)}, bf16[464,384]{1,0:T(8,128)(2,1)S(1)}, u32[]{:S(2)}, u32[]{:S(2)}) collective-permute-start(bf16[464,384]{1,0:T(8,128)(2,1)S(1)} %fusion.1.c0), channel_id=1, source_target_pairs={{0,1},{1,2},{2,3},{4,5},{5,6},{6,7},{8,9},{9,10},{10,11},{12,13},{... | collective-permute-start | bytes 1069064 | tf_op jit(solution)/shard_map/ppermute | solution.py:44
  29.0 23.0 %collective-permute-start.4 = (bf16[464,384]{1,0:T(8,128)(2,1)S(1)}, bf16[464,384]{1,0:T(8,128)(2,1)S(1)}, u32[]{:S(2)}, u32[]{:S(2)}) collective-permute-start(bf16[464,384]{1,0:T(8,128)(2,1)S(1)} %fusion.1.c0), channel_id=1, source_target_pairs={{1,0},{2,1},{3,2},{5,4},{6,5},{7,6},{9,8},{10,9},{11,10},{13,12},{... | collective-permute-start | bytes 1069064 | tf_op jit(solution)/shard_map/ppermute | solution.py:45
  41.4 17.9 %collective-permute-start.5 = (bf16[464,384]{1,0:T(8,128)(2,1)S(1)}, bf16[464,384]{1,0:T(8,128)(2,1)S(1)}, u32[]{:S(2)}, u32[]{:S(2)}) collective-permute-start(bf16[464,384]{1,0:T(8,128)(2,1)S(1)} %collective-permute-done.3.c2), channel_id=1, source_target_pairs={{2,3},{1,0},{6,7},{5,4},{10,11},{9,8},{14,15},{13,12},{18,19},{17,... | collective-permute-start | bytes 1069064 | tf_op jit(solution)/shard_map/ppermute | solution.py:46
  52.0 10.8 %collective-permute-start.19 = (bf16[48,1536]{1,0:T(8,128)(2,1)S(1)}, bf16[48,1536]{1,0:T(8,128)(2,1)S(1)}, u32[]{:S(2)}, u32[]{:S(2)}) collective-permute-start(bf16[48,1536]{1,0:T(8,128)(2,1)S(1)} %get-tuple-element.68.refs_0_), channel_id=1, source_target_pairs={{0,2},{1,3},{2,0},{3,1},{4,6},{5,7},{6,4},{7,5},{8,10},{9,11},{10,... | collective-permute-start | bytes 442376 | tf_op jit(solution)/shard_map/ppermute | solution.py:35
  52.0 10.8 %collective-permute-start.20 = (bf16[48,1536]{1,0:T(8,128)(2,1)S(1)}, bf16[48,1536]{1,0:T(8,128)(2,1)S(1)}, u32[]{:S(2)}, u32[]{:S(2)}) collective-permute-start(bf16[48,1536]{1,0:T(8,128)(2,1)S(1)} %get-tuple-element.68.refs_0_), channel_id=1, source_target_pairs={{0,3},{1,0},{2,1},{3,2},{4,7},{5,4},{6,5},{7,6},{8,11},{9,8},{10,9... | collective-permute-start | bytes 442376 | tf_op jit(solution)/shard_map/ppermute | solution.py:35
  63.6 97.7 %all-gather.11.cloned.1.call-start = ((), (), s32[]{:S(2)}) async-start(), calls=%async_computation.3 | async-start | bytes 5308416 | tf_op jit(solution)/shard_map/all_gather | solution.py:486
  63.7 12.4 %collective-permute-start.6 = (bf16[224,384]{1,0:T(8,128)(2,1)}, bf16[224,384]{1,0:T(8,128)(2,1)S(1)}, u32[]{:S(2)}, u32[]{:S(2)}) collective-permute-start(bf16[224,384]{1,0:T(8,128)(2,1)} %copy-done.6), channel_id=1, source_target_pairs={{0,1},{1,2},{2,3},{3,0},{4,5},{5,6},{6,7},{7,4},{8,9},{9,10},{10,1... | collective-permute-start | bytes 516104 | tf_op jit(solution)/shard_map/ppermute | solution.py:35
  65.4 12.5 %collective-permute-start.7 = (bf16[224,384]{1,0:T(8,128)(2,1)}, bf16[224,384]{1,0:T(8,128)(2,1)S(1)}, u32[]{:S(2)}, u32[]{:S(2)}) collective-permute-start(bf16[224,384]{1,0:T(8,128)(2,1)} %copy-done.6), channel_id=1, source_target_pairs={{0,2},{1,3},{2,0},{3,1},{4,6},{5,7},{6,4},{7,5},{8,10},{9,11},{10,... | collective-permute-start | bytes 516104 | tf_op jit(solution)/shard_map/ppermute | solution.py:35
  67.9 12.5 %collective-permute-start.8 = (bf16[224,384]{1,0:T(8,128)(2,1)}, bf16[224,384]{1,0:T(8,128)(2,1)S(1)}, u32[]{:S(2)}, u32[]{:S(2)}) collective-permute-start(bf16[224,384]{1,0:T(8,128)(2,1)} %copy-done.6), channel_id=1, source_target_pairs={{0,3},{1,0},{2,1},{3,2},{4,7},{5,4},{6,5},{7,6},{8,11},{9,8},{10,9... | collective-permute-start | bytes 516104 | tf_op jit(solution)/shard_map/ppermute | solution.py:35
  83.7 16.8 %collective-permute-start.13 = (bf16[224,384]{1,0:T(8,128)(2,1)S(1)}, bf16[224,384]{1,0:T(8,128)(2,1)S(1)}, u32[]{:S(2)}, u32[]{:S(2)}) collective-permute-start(bf16[224,384]{1,0:T(8,128)(2,1)S(1)} %get-tuple-element.61.a0), channel_id=1, source_target_pairs={{0,2},{1,3},{2,0},{3,1},{4,6},{5,7},{6,4},{7,5},{8,10},{9,11},{10,... | collective-permute-start | bytes 516104 | tf_op jit(solution)/shard_map/ppermute | solution.py:35
  84.6 20.8 %collective-permute-start.14 = (bf16[224,384]{1,0:T(8,128)(2,1)S(1)}, bf16[224,384]{1,0:T(8,128)(2,1)S(1)}, u32[]{:S(2)}, u32[]{:S(2)}) collective-permute-start(bf16[224,384]{1,0:T(8,128)(2,1)S(1)} %get-tuple-element.61.a0), channel_id=1, source_target_pairs={{0,3},{1,0},{2,1},{3,2},{4,7},{5,4},{6,5},{7,6},{8,11},{9,8},{10,9... | collective-permute-start | bytes 516104 | tf_op jit(solution)/shard_map/ppermute | solution.py:35
  89.0 20.0 %collective-permute-start.32 = (bf16[48,1536]{1,0:T(8,128)(2,1)S(1)}, bf16[48,1536]{1,0:T(8,128)(2,1)S(1)}, u32[]{:S(2)}, u32[]{:S(2)}) collective-permute-start(bf16[48,1536]{1,0:T(8,128)(2,1)S(1)} %get-tuple-element.84.refs_0_), channel_id=1, source_target_pairs={{0,1},{1,2},{2,3},{3,0},{4,5},{5,6},{6,7},{7,4},{8,9},{9,10},{10,1... | collective-permute-start | bytes 442376 | tf_op jit(solution)/shard_map/ppermute | solution.py:35
  89.7 21.6 %collective-permute-start.33 = (bf16[48,1536]{1,0:T(8,128)(2,1)S(1)}, bf16[48,1536]{1,0:T(8,128)(2,1)S(1)}, u32[]{:S(2)}, u32[]{:S(2)}) collective-permute-start(bf16[48,1536]{1,0:T(8,128)(2,1)S(1)} %get-tuple-element.84.refs_0_), channel_id=1, source_target_pairs={{0,2},{1,3},{2,0},{3,1},{4,6},{5,7},{6,4},{7,5},{8,10},{9,11},{10,... | collective-permute-start | bytes 442376 | tf_op jit(solution)/shard_map/ppermute | solution.py:35
  93.1 18.6 %collective-permute-start.34 = (bf16[48,1536]{1,0:T(8,128)(2,1)S(1)}, bf16[48,1536]{1,0:T(8,128)(2,1)S(1)}, u32[]{:S(2)}, u32[]{:S(2)}) collective-permute-start(bf16[48,1536]{1,0:T(8,128)(2,1)S(1)} %get-tuple-element.84.refs_0_), channel_id=1, source_target_pairs={{0,3},{1,0},{2,1},{3,2},{4,7},{5,4},{6,5},{7,6},{8,11},{9,8},{10,9... | collective-permute-start | bytes 442376 | tf_op jit(solution)/shard_map/ppermute | solution.py:35
  112.5 10.2 %collective-permute-start.15 = (bf16[208,384]{1,0:T(8,128)(2,1)S(1)}, bf16[208,384]{1,0:T(8,128)(2,1)S(1)}, u32[]{:S(2)}, u32[]{:S(2)}) collective-permute-start(bf16[208,384]{1,0:T(8,128)(2,1)S(1)} %get-tuple-element.66.a0), channel_id=1, source_target_pairs={{0,1},{1,2},{2,3},{3,0},{4,5},{5,6},{6,7},{7,4},{8,9},{9,10},{10,1... | collective-permute-start | bytes 479240 | tf_op jit(solution)/shard_map/ppermute | solution.py:35
  112.6 14.1 %collective-permute-start.16 = (bf16[208,384]{1,0:T(8,128)(2,1)S(1)}, bf16[208,384]{1,0:T(8,128)(2,1)S(1)}, u32[]{:S(2)}, u32[]{:S(2)}) collective-permute-start(bf16[208,384]{1,0:T(8,128)(2,1)S(1)} %get-tuple-element.66.a0), channel_id=1, source_target_pairs={{0,2},{1,3},{2,0},{3,1},{4,6},{5,7},{6,4},{7,5},{8,10},{9,11},{10,... | collective-permute-start | bytes 479240 | tf_op jit(solution)/shard_map/ppermute | solution.py:35
  115.7 13.7 %collective-permute-start.17 = (bf16[208,384]{1,0:T(8,128)(2,1)S(1)}, bf16[208,384]{1,0:T(8,128)(2,1)S(1)}, u32[]{:S(2)}, u32[]{:S(2)}) collective-permute-start(bf16[208,384]{1,0:T(8,128)(2,1)S(1)} %get-tuple-element.66.a0), channel_id=1, source_target_pairs={{0,3},{1,0},{2,1},{3,2},{4,7},{5,4},{6,5},{7,6},{8,11},{9,8},{10,9... | collective-permute-start | bytes 479240 | tf_op jit(solution)/shard_map/ppermute | solution.py:35
  132.6 13.2 %collective-permute-start.22 = (bf16[192,384]{1,0:T(8,128)(2,1)S(1)}, bf16[192,384]{1,0:T(8,128)(2,1)S(1)}, u32[]{:S(2)}, u32[]{:S(2)}) collective-permute-start(bf16[192,384]{1,0:T(8,128)(2,1)S(1)} %get-tuple-element.76.a0), channel_id=1, source_target_pairs={{0,2},{1,3},{2,0},{3,1},{4,6},{5,7},{6,4},{7,5},{8,10},{9,11},{10,... | collective-permute-start | bytes 442376 | tf_op jit(solution)/shard_map/ppermute | solution.py:35
  133.3 12.9 %collective-permute-start.23 = (bf16[192,384]{1,0:T(8,128)(2,1)S(1)}, bf16[192,384]{1,0:T(8,128)(2,1)S(1)}, u32[]{:S(2)}, u32[]{:S(2)}) collective-permute-start(bf16[192,384]{1,0:T(8,128)(2,1)S(1)} %get-tuple-element.76.a0), channel_id=1, source_target_pairs={{0,3},{1,0},{2,1},{3,2},{4,7},{5,4},{6,5},{7,6},{8,11},{9,8},{10,9... | collective-permute-start | bytes 442376 | tf_op jit(solution)/shard_map/ppermute | solution.py:35
  152.2 14.0 %collective-permute-start.25 = (bf16[160,384]{1,0:T(8,128)(2,1)S(1)}, bf16[160,384]{1,0:T(8,128)(2,1)S(1)}, u32[]{:S(2)}, u32[]{:S(2)}) collective-permute-start(bf16[160,384]{1,0:T(8,128)(2,1)S(1)} %shard_map.107.a0), channel_id=1, source_target_pairs={{0,2},{1,3},{2,0},{3,1},{4,6},{5,7},{6,4},{7,5},{8,10},{9,11},{10,... | collective-permute-start | bytes 368648 | tf_op jit(solution)/shard_map/ppermute | solution.py:35
  154.6 15.1 %collective-permute-start.26 = (bf16[160,384]{1,0:T(8,128)(2,1)S(1)}, bf16[160,384]{1,0:T(8,128)(2,1)S(1)}, u32[]{:S(2)}, u32[]{:S(2)}) collective-permute-start(bf16[160,384]{1,0:T(8,128)(2,1)S(1)} %shard_map.107.a0), channel_id=1, source_target_pairs={{0,3},{1,0},{2,1},{3,2},{4,7},{5,4},{6,5},{7,6},{8,11},{9,8},{10,9... | collective-permute-start | bytes 368648 | tf_op jit(solution)/shard_map/ppermute | solution.py:35
  157.7 12.1 %collective-permute-start.29 = (bf16[96,384]{1,0:T(8,128)(2,1)S(1)}, bf16[96,384]{1,0:T(8,128)(2,1)S(1)}, u32[]{:S(2)}, u32[]{:S(2)}) collective-permute-start(bf16[96,384]{1,0:T(8,128)(2,1)S(1)} %shard_map.108.e0), channel_id=1, source_target_pairs={{0,1},{1,2},{2,3},{3,0},{4,5},{5,6},{6,7},{7,4},{8,9},{9,10},{10,1... | collective-permute-start | bytes 221192 | tf_op jit(solution)/shard_map/ppermute | solution.py:35
  157.8 11.9 %collective-permute-start.30 = (bf16[96,384]{1,0:T(8,128)(2,1)S(1)}, bf16[96,384]{1,0:T(8,128)(2,1)S(1)}, u32[]{:S(2)}, u32[]{:S(2)}) collective-permute-start(bf16[96,384]{1,0:T(8,128)(2,1)S(1)} %shard_map.108.e0), channel_id=1, source_target_pairs={{0,2},{1,3},{2,0},{3,1},{4,6},{5,7},{6,4},{7,5},{8,10},{9,11},{10,... | collective-permute-start | bytes 221192 | tf_op jit(solution)/shard_map/ppermute | solution.py:35
  160.1 12.7 %collective-permute-start.31 = (bf16[96,384]{1,0:T(8,128)(2,1)S(1)}, bf16[96,384]{1,0:T(8,128)(2,1)S(1)}, u32[]{:S(2)}, u32[]{:S(2)}) collective-permute-start(bf16[96,384]{1,0:T(8,128)(2,1)S(1)} %shard_map.108.e0), channel_id=1, source_target_pairs={{0,3},{1,0},{2,1},{3,2},{4,7},{5,4},{6,5},{7,6},{8,11},{9,8},{10,9... | collective-permute-start | bytes 221192 | tf_op jit(solution)/shard_map/ppermute | solution.py:35
  176.5 13.1 %collective-permute-start.36 = (bf16[192,384]{1,0:T(8,128)(2,1)S(1)}, bf16[192,384]{1,0:T(8,128)(2,1)S(1)}, u32[]{:S(2)}, u32[]{:S(2)}) collective-permute-start(bf16[192,384]{1,0:T(8,128)(2,1)S(1)} %get-tuple-element.91.a0), channel_id=1, source_target_pairs={{0,2},{1,3},{2,0},{3,1},{4,6},{5,7},{6,4},{7,5},{8,10},{9,11},{10,... | collective-permute-start | bytes 442376 | tf_op jit(solution)/shard_map/ppermute | solution.py:35
  178.7 13.4 %collective-permute-start.37 = (bf16[192,384]{1,0:T(8,128)(2,1)S(1)}, bf16[192,384]{1,0:T(8,128)(2,1)S(1)}, u32[]{:S(2)}, u32[]{:S(2)}) collective-permute-start(bf16[192,384]{1,0:T(8,128)(2,1)S(1)} %get-tuple-element.91.a0), channel_id=1, source_target_pairs={{0,3},{1,0},{2,1},{3,2},{4,7},{5,4},{6,5},{7,6},{8,11},{9,8},{10,9... | collective-permute-start | bytes 442376 | tf_op jit(solution)/shard_map/ppermute | solution.py:35
  (22 other events, 213.4 us)
Sparse Core Ops, SparseCore 0:
  25.4 39.1 all-gather.6
  67.0 40.5 all-gather.8
  112.7 40.5 all-gather.10
